TPU v7x, 512 devices: a whole 4x4x16 slice. The times are simulated.
512 devices in a mesh: grp: 8 (over z_hi, x), exp: 64 (over y, z_lo, core).
Axes of the slice: x: 4, y: 4, z: 16 (z_hi: 2, z_lo: 8; z = z_hi * 8 + z_lo), core: 2. Of those that a mesh axis runs over, the one named last changes fastest.
Arguments:
- counts: int32 [64], P('exp'), may hold values from 1 to 4095
- up_weights: bfloat16 [64, 4096, 1536], P('exp', 'grp'), may hold values from -16 to 16
- sketch: bfloat16 [1536, 256], replicated, may hold values from -0.15625 to 0.15625
Outputs:
- base: bfloat16 [4096, 1536], P(('grp', 'exp'))
- basis: float32 [64, 4096, 256], P('exp', 'grp')
- coefficients: float32 [64, 256, 1536], P('exp')
All inputs are finite; a program needn't handle non-finite values.
Results may differ from a plain program's by a relative error of at most 0.001.
Values may be sent and summed in bfloat16 or wider, within the bound.
No kernel may reach another device: no remote copies, remote signals or barrier semaphores. Data moves between devices by JAX's collectives and lax.ppermute only.
A program may use at most 64 MiB of HBM per device.

v0:
```python
import math

import jax
import jax.numpy as jnp
from jax import lax
from jax.sharding import PartitionSpec as P

contract_rows = (((0,), (0,)), ((), ()))


def per_device(counts, up_weights, sketch):
    own = up_weights[0]
    freq = counts.astype(jnp.float32)
    total = lax.psum(jnp.sum(freq), "exp")
    factor = freq[0] / total
    weighted = factor * own.astype(jnp.float32)
    own_sketch = jnp.dot(own, sketch, preferred_element_type=jnp.float32)
    base_rows = lax.psum_scatter(weighted, "exp", scatter_dimension=0, tiled=True)
    base_piece = base_rows.astype(jnp.bfloat16)
    wide = lax.all_gather(base_rows, "exp", axis=0, tiled=True)
    base_sketch = jnp.dot(wide, sketch.astype(jnp.float32), precision=lax.Precision.HIGHEST)
    slab = wide.astype(jnp.bfloat16)
    range_rows = own_sketch - base_sketch
    local_gram = jnp.dot(range_rows.T, range_rows, precision=lax.Precision.HIGHEST)
    gram = lax.psum(local_gram, "grp")
    lower = jnp.linalg.cholesky(gram)
    ortho = lax.linalg.triangular_solve(
        lower, range_rows, left_side=False, lower=True, transpose_a=True
    )
    ortho_short = ortho.astype(jnp.bfloat16)
    ortho_back = lax.optimization_barrier(ortho_short).astype(jnp.float32)
    ortho_rest = (ortho - ortho_back).astype(jnp.bfloat16)
    both_parts = jnp.concatenate([ortho_short, ortho_rest], axis=1)
    own_term = lax.dot_general(both_parts, own, contract_rows, preferred_element_type=jnp.float32)
    base_term = lax.dot_general(both_parts, slab, contract_rows, preferred_element_type=jnp.float32)
    width = ortho.shape[1]
    local_coeff = own_term[:width] + own_term[width:] - (base_term[:width] + base_term[width:])
    coeff = lax.psum(local_coeff, "grp")
    width_total = own.shape[0] * lax.axis_size("grp")
    basis = ortho * math.sqrt(width_total)
    return (base_piece, basis[None], coeff[None])


def solution(mesh):
    placed = (P("exp"), P("exp", "grp", None), P())
    return jax.shard_map(
        per_device,
        mesh=mesh,
        in_specs=placed,
        out_specs=(P(("grp", "exp"), None), P("exp", "grp", None), P("exp", None, None)),
        check_vma=False,
    )
```

profile of v0, /device:TPU:6, one launch (start us, length us, event | category | flops | bytes accessed | tf_op | source)
XLA Modules:
  0.0 1217.9 jit_solution(3585406732648350116)
XLA Ops:
  7.9 224.5 %psum.21 = f32[]{:T(128)} all-reduce(f32[]{:T(128)} %bitcast), channel_id=1, replica_groups=mesh['grp'=8,'exp'=64] {'exp'}, use_global_device_ids=true, to_apply=%region_0.0 | all-reduce | flops 1 | bytes 8 | tf_op jit(solution)/shard_map/psum | solution.py:14
  233.1 3.5 convert_multiply_fusion
  236.7 435.7 %reduce-scatter.2.cloned.1.call-done = f32[8,1536]{1,0:T(8,128)} async-done(((f32[512,1536]{1,0:T(8,128)}), f32[8,1536]{1,0:T(8,128)}) %reduce-scatter.2.cloned.1.call-update) | async-done | bytes 49168 | tf_op jit(solution)/shard_map/reduce_scatter | solution.py:18
  673.1 115.2 %all-gather.2.cloned.1.call-done = f32[512,1536]{1,0:T(8,128)} async-done(((f32[8,1536]{1,0:T(8,128)}), f32[512,1536]{1,0:T(8,128)}) %all-gather.2.cloned.1.call-update) | async-done | bytes 3145744 | tf_op jit(solution)/shard_map/all_gather | solution.py:20
  788.3 3.4 convolution_subtract_fusion
  791.7 1.7 fusion.20
  793.7 145.0 %all-reduce.4.cloned.1.call-done = f32[256,256]{0,1:T(8,128)} async-done(((f32[256,256]{0,1:T(8,128)}), f32[256,256]{0,1:T(8,128)}) %all-reduce.4.cloned.1.call-update) | async-done | bytes 262160 | tf_op jit(solution)/shard_map/psum | solution.py:25
  938.6 1.1 copy.7
  939.7 1.0 fusion.11
  941.4 11.7 cholesky.50
  953.2 9.8 custom-call.14
  963.0 1.0 constant_dynamic-update-slice_fusion.1
  964.1 1.1 convolution_subtract_fusion.2
  965.2 11.7 cholesky.105
  979.0 4.2 while.1
  979.8 1.4 bitcast_dynamic-update-slice_fusion.2
  981.8 1.4 bitcast_dynamic-update-slice_fusion.2
  983.8 20.5 %custom-call.15 = f32[2,128,128]{1,2,0:T(8,128)S(1)} custom-call(f32[2,128,128]{2,1,0:T(8,128)} %copy-done.5), custom_call_target="InvertDiagBlocksLowerTriangular" | custom-call | tf_op jit(solution)/shard_map/triangular_solve | solution.py:27
  1005.9 1.0 fusion.2
  1007.8 1.0 fusion.6
  1008.8 1.8 fusion.1
  1012.0 1.0 copy.8
  1013.0 195.7 %all-reduce.6.cloned.1.call-done = f32[1,256,1536]{2,1,0:T(8,128)} async-done(((f32[1,256,1536]{2,1,0:T(8,128)}), f32[1,256,1536]{2,1,0:T(8,128)}) %all-reduce.6.cloned.1.call-update) | async-done | bytes 1572880 | tf_op jit(solution)/shard_map/psum | solution.py:38
  1208.7 2.7 copy.24
  (41 shorter events, 8.2 us)
Async XLA Ops:
  7.2 665.3 %copy-start = (bf16[1536,256]{1,0:T(8,128)(2,1)S(1)}, bf16[1536,256]{1,0:T(8,128)(2,1)}, u32[]{:S(2)}) copy-start(bf16[1536,256]{1,0:T(8,128)(2,1)} %param.5) | copy-start | bytes 2359300
  7.2 665.2 %reduce-scatter.2.cloned.1.call-start = ((), (), s32[]{:S(2)}) async-start(), calls=%async_computation.1 | async-start | bytes 3194880 | tf_op jit(solution)/shard_map/reduce_scatter | solution.py:18
  236.6 435.9 %copy-start.1 = (bf16[1,512,1536]{2,1,0:T(8,128)(2,1)S(1)}, bf16[1,512,1536]{2,1,0:T(8,128)(2,1)}, u32[]{:S(2)}) copy-start(bf16[1,512,1536]{2,1,0:T(8,128)(2,1)} %param.4) | copy-start | bytes 4718596
  236.6 551.6 %all-gather.2.cloned.1.call-start = ((), (), s32[]{:S(2)}) async-start(), calls=%async_computation.2 | async-start | bytes 3194880 | tf_op jit(solution)/shard_map/all_gather | solution.py:20
  672.4 266.2 %all-reduce.4.cloned.1.call-start = ((), (), s32[]{:S(2)}) async-start(), calls=%async_computation.3 | async-start | bytes 524288 | tf_op jit(solution)/shard_map/psum | solution.py:25
  793.4 415.3 %all-reduce.6.cloned.1.call-start = ((), (), s32[]{:S(2)}) async-start(), calls=%async_computation.4 | async-start | bytes 3145728 | tf_op jit(solution)/shard_map/psum | solution.py:38
  940.7 0.7 copy-start.3
  983.2 0.7 copy-start.5
  1005.9 1.9 copy-start.2
  1010.5 0.8 copy-start.4
Sparse Core Ops, SparseCore 0:
  236.8 435.5 reduce-scatter.1
  674.8 113.4 all-gather.1
  793.6 145.0 all-reduce.3
  1010.7 198.0 all-reduce.5
where the time goes:
time: 1220 us
  waiting for transfers between devices  892 us (73%)
  blocking collectives  224 us (18%)
  other arithmetic  61.5 us (5%)
  between operations  16.7 us (1%)
    reduce_scatter x1, waiting for transfers between devices, per_device(): lax.psum_scatter(weighted, 'exp', scatter_dimension=0, tiled=True)  436 us
    psum x1, blocking collectives, per_device(): total = lax.psum(jnp.sum(freq), 'exp')  224 us
    psum x1, waiting for transfers between devices, per_device(): coeff = lax.psum(local_coeff, 'grp')  196 us
    psum x1, waiting for transfers between devices, per_device(): gram = lax.psum(local_gram, 'grp')  145 us
    all_gather x1, waiting for transfers between devices, per_device(): wide = lax.all_gather(base_rows, 'exp', axis=0, tiled=True)  115 us
    another operation x6, other arithmetic, per_device(): lower = jnp.linalg.cholesky(gram)  34 us
  transfers between devices with their start and end apart: 4, of which 4 were waited for; matrix products, arithmetic and copies ran while one was open for 0% of the time, Pallas kernels for 0%

commit v1 on v0

v1 whole, which is shorter than its diff:
```python
import math

import jax
import jax.numpy as jnp
from jax import lax
from jax.sharding import PartitionSpec as P

F32, BF16 = jnp.float32, jnp.bfloat16
HIGHEST = lax.Precision.HIGHEST
contract_rows = (((0,), (0,)), ((), ()))

YN, ZN, CN, XN, HN = 4, 8, 2, 4, 2
YC_GROUPS = [[y * 16 + z * 2 + c for y in range(YN) for c in range(CN)] for z in range(ZN)]
Z_GROUPS = [[y * 16 + z * 2 + c for z in range(ZN)] for y in range(YN) for c in range(CN)]
Y_GROUPS = [[y * 16 + z * 2 + c for y in range(YN)] for z in range(ZN) for c in range(CN)]
OTHER_CORE = [(i, i ^ 1) for i in range(64)]
X_GROUPS = [[h * 4 + x for x in range(XN)] for h in range(HN)]
OTHER_HALF = [(i, i ^ 4) for i in range(8)]


def along_x(k):
    return [(i, i ^ k) for i in range(8)]


def parts_of(value):
    first = lax.reduce_precision(value, 8, 7)
    rest = value - first
    second = lax.reduce_precision(rest, 8, 7)
    return [first.astype(BF16), second.astype(BF16), (rest - second).astype(BF16)]


def per_device(counts, up_weights, sketch):
    rows, ff = up_weights.shape[1:]
    rank = sketch.shape[1]
    piece = rows // 64
    own = up_weights[0].reshape(YN, ZN, CN, piece, ff).transpose(0, 2, 1, 3, 4)
    own = own.reshape(YN * CN, ZN * piece, ff)

    lane = lax.broadcasted_iota(jnp.int32, (YN * CN, ZN * piece, 128), 2)
    count = counts[0]
    tag = jnp.where(lane == 0, count // 64, jnp.where(lane == 1, count % 64, 0)).astype(BF16)
    got = lax.all_to_all(
        jnp.concatenate([own, tag], axis=2), "exp", 0, 0, axis_index_groups=YC_GROUPS
    )
    freq = got[:, 0, ff].astype(F32) * 64 + got[:, 0, ff + 1].astype(F32)
    weighted = jnp.sum(freq[:, None, None] * got[:, :, :ff].astype(F32), axis=0)
    freq_sum = jnp.broadcast_to(jnp.sum(freq), (ZN, piece, 128))

    sums = lax.all_to_all(
        jnp.concatenate([weighted.reshape(ZN, piece, ff), freq_sum], axis=2),
        "exp", 0, 0, axis_index_groups=Z_GROUPS,
    )
    sums = jnp.sum(sums, axis=0)
    base_rows = sums[:, :ff] / sums[:, ff : ff + 1]
    base_piece = base_rows.astype(BF16)
    sketched = jnp.dot(base_rows, sketch.astype(F32), precision=HIGHEST)

    wide = ff + 3 * rank
    load = jnp.concatenate([base_piece] + parts_of(sketched), axis=1)
    load = lax.all_to_all(
        jnp.broadcast_to(load, (ZN, piece, wide)), "exp", 0, 0, axis_index_groups=Z_GROUPS
    ).reshape(ZN * piece, wide)
    load = lax.all_to_all(
        jnp.broadcast_to(load, (YN, ZN * piece, wide)), "exp", 0, 0, axis_index_groups=Y_GROUPS
    )
    other = lax.ppermute(load, "exp", OTHER_CORE)
    first = lax.axis_index("exp") % 2 == 0
    slab = jnp.stack([jnp.where(first, load, other), jnp.where(first, other, load)], axis=1)
    slab = slab.reshape(rows, wide)
    base = slab[:, :ff]
    base_sketch = (
        slab[:, ff : ff + rank].astype(F32)
        + slab[:, ff + rank : ff + 2 * rank].astype(F32)
        + slab[:, ff + 2 * rank :].astype(F32)
    )

    own = own.reshape(rows, ff)
    range_rows = jnp.dot(own, sketch, preferred_element_type=F32) - base_sketch
    gram = jnp.dot(range_rows.T, range_rows, precision=HIGHEST)
    three = jnp.concatenate(parts_of(range_rows), axis=1)
    delta = lax.dot_general(three, own, contract_rows, preferred_element_type=F32)
    delta = delta - lax.dot_general(three, base, contract_rows, preferred_element_type=F32)
    delta = delta[:rank] + delta[rank : 2 * rank] + delta[2 * rank :]

    both = jnp.concatenate([gram, delta], axis=1).reshape(XN, rank // XN, rank + ff)
    both = lax.all_to_all(both, "grp", 0, 0, axis_index_groups=X_GROUPS)
    both = jnp.sum(both, axis=0)
    both = both + lax.ppermute(both, "grp", OTHER_HALF)
    at_x = lax.axis_index("grp") % XN

    def gathered(block):
        whole = jnp.zeros((XN,) + block.shape, F32)
        whole = lax.dynamic_update_slice(whole, block[None], (at_x, 0, 0))
        for k in (1, 3, 2):
            came = lax.ppermute(block, "grp", along_x(k))
            whole = lax.dynamic_update_slice(whole, came[None], (at_x ^ k, 0, 0))
        return whole.reshape(XN * block.shape[0], block.shape[1])

    gram = gathered(both[:, :rank])
    delta = gathered(both[:, rank:])
    lower = jnp.linalg.cholesky(gram)
    inverse = lax.linalg.triangular_solve(
        lower, jnp.eye(rank, dtype=F32), left_side=True, lower=True
    )
    ortho = lax.dot_general(
        range_rows, inverse, (((1,), (1,)), ((), ())), precision=HIGHEST
    )
    coeff = jnp.dot(inverse, delta, precision=HIGHEST)
    width_total = rows * lax.axis_size("grp")
    basis = ortho * math.sqrt(width_total)
    basis = basis.reshape(YN, CN, ZN, piece, rank).transpose(0, 2, 1, 3, 4)
    return (base_piece, basis.reshape(1, rows, rank), coeff[None])


def solution(mesh):
    placed = (P("exp"), P("exp", "grp", None), P())
    return jax.shard_map(
        per_device,
        mesh=mesh,
        in_specs=placed,
        out_specs=(P(("grp", "exp"), None), P("exp", "grp", None), P("exp", None, None)),
        check_vma=False,
    )
```

time: 1220 us -> 306 us (0.25)
  the two profiles are of different devices: /device:TPU:6 before, /device:TPU:192 now
where the time goes in v1:
time: 306 us; the launch traced here: 305 us
  blocking collectives  126 us (41%)
  other arithmetic  60.4 us (20%)
  waiting for transfers between devices  58.4 us (19%)
  starting transfers between devices  28.2 us (9%)
  local copies, waits for them, and re-layouts  16.5 us (5%)
  matrix products  12.1 us (4%)
  between operations  3.22 us (1%)
    ppermute x1, waiting for transfers between devices, per_device(): both = both + lax.ppermute(both, 'grp', OTHER_HALF)  43.2 us
    another operation x6, other arithmetic, per_device(): lower = jnp.linalg.cholesky(gram)  34 us
    all_to_all x1, blocking collectives, per_device(): lax.all_to_all(jnp.concatenate([weighted.reshape(ZN, piece, ff), freq_sum...  27.9 us
    all_to_all x1, blocking collectives, per_device(): both = lax.all_to_all(both, 'grp', 0, 0, axis_index_groups=X_GROUPS)  27.9 us
    all_to_all x1, blocking collectives, per_device(): lax.all_to_all(jnp.concatenate([own, tag], axis=2), 'exp', 0, 0, axis_ind...  27.5 us
    all_to_all x1, blocking collectives, per_device(): lax.all_to_all(jnp.broadcast_to(load, (ZN, piece, wide)), 'exp', 0, 0, ax...  23.3 us
    another operation x3, other arithmetic, per_device(): lax.linalg.triangular_solve(lower, jnp.eye(rank, dtype=F32), left_side=Tr...  20.5 us
    all_to_all x1, blocking collectives, per_device(): lax.all_to_all(jnp.broadcast_to(load, (YN, ZN * piece, wide)), 'exp', 0,...  19.5 us
  transfers between devices with their start and end apart: 8, of which 5 were waited for; matrix products, arithmetic and copies ran while one was open for 22% of the time, Pallas kernels for 0%

profile of v1, /device:TPU:192, one launch (start us, length us, event | category | flops | bytes accessed | tf_op | source)
XLA Modules:
  0.0 305.1 jit_solution(494357040092444429)
XLA Ops:
  3.2 27.5 %all_to_all.25 = bf16[8,64,1664]{2,1,0:T(8,128)(2,1)S(1)} all-to-all(bf16[8,64,1664]{2,1,0:T(8,128)(2,1)S(1)} %pad_maximum_fusion.2), channel_id=1, replica_groups={{0,1,16,17,32,33,48,49},{2,3,18,19,34,35,50,51},{4,5,20,21,36,37,52,53}..., dimensions={0} | all-to-all | bytes 3407872 | tf_op jit(solution)/shard_map/all_to_all | solution.py:42
  32.4 27.9 %all_to_all.26 = f32[8,8,1664]{2,1,0:T(8,128)S(1)} all-to-all(f32[8,8,1664]{2,1,0:T(8,128)S(1)} %concatenate.18), channel_id=1, replica_groups={{0,2,4,6,8,10,12,14},{1,3,5,7,9,11,13,15},{16,18,20,22,24,26,28,30},{17..., dimensions={0} | all-to-all | bytes 851968 | tf_op jit(solution)/shard_map/all_to_all | solution.py:49
  61.1 23.3 %all_to_all.27 = bf16[8,8,2304]{2,1,0:T(8,128)(2,1)S(1)} all-to-all(bf16[8,8,2304]{2,1,0:T(8,128)(2,1)S(1)} %broadcast_in_dim.55), channel_id=1, replica_groups={{0,2,4,6,8,10,12,14},{1,3,5,7,9,11,13,15},{16,18,20,22,24,26,28,30},{17..., dimensions={0} | all-to-all | bytes 589824 | tf_op jit(solution)/shard_map/all_to_all | solution.py:60
  84.5 19.5 %all_to_all.28 = bf16[4,64,2304]{2,1,0:T(8,128)(2,1)} all-to-all(bf16[4,64,2304]{2,1,0:T(8,128)(2,1)S(1)} %broadcast_in_dim.56), channel_id=1, replica_groups={{0,16,32,48},{1,17,33,49},{2,18,34,50},{3,19,35,51},{4,20,36,52},{5,21,..., dimensions={0} | all-to-all | bytes 2359296 | tf_op jit(solution)/shard_map/all_to_all | solution.py:63
  106.0 3.1 %collective-permute-done = bf16[4,64,2304]{2,1,0:T(8,128)(2,1)} collective-permute-done((bf16[4,64,2304]{2,1,0:T(8,128)(2,1)}, bf16[4,64,2304]{2,1,0:T(8,128)(2,1)}, u32[]{:S(2)}, u32[]{:S(2)}) %collective-permute-start) | collective-permute-done | bytes 1179680 | tf_op jit(solution)/shard_map/ppermute | solution.py:66
  119.7 27.9 %all_to_all.29 = f32[4,64,1792]{2,1,0:T(8,128)S(1)} all-to-all(f32[4,64,1792]{2,1,0:T(8,128)S(1)} %bitcast.87), channel_id=1, replica_groups={{0,64,128,192},{256,320,384,448},{1,65,129,193},{257,321,385,449},{2,66..., dimensions={0} | all-to-all | bytes 3670016 | tf_op jit(solution)/shard_map/all_to_all | solution.py:86
  148.6 8.2 %collective-permute-start.1 = (f32[64,1792]{1,0:T(8,128)}, f32[64,1792]{1,0:T(8,128)S(1)}, u32[]{:S(2)}, u32[]{:S(2)}) collective-permute-start(f32[64,1792]{1,0:T(8,128)} %reduce_sum.39), channel_id=1, source_target_pairs={{0,256},{64,320},{128,384},{192,448},{256,0},{320,64},{384,128},{4... | collective-permute-start | bytes 1376264 | tf_op jit(solution)/shard_map/ppermute | solution.py:88
  156.9 43.2 %collective-permute-done.1 = f32[64,1792]{1,0:T(8,128)S(1)} collective-permute-done((f32[64,1792]{1,0:T(8,128)}, f32[64,1792]{1,0:T(8,128)S(1)}, u32[]{:S(2)}, u32[]{:S(2)}) %collective-permute-start.1) | collective-permute-done | bytes 458784 | tf_op jit(solution)/shard_map/ppermute | solution.py:88
  201.9 2.5 collective-permute-start.5
  204.4 2.8 collective-permute-start.6
  207.2 4.5 %collective-permute-start.7 = (f32[64,1536]{1,0:T(8,128)}, f32[64,1536]{1,0:T(8,128)}, u32[]{:S(2)}, u32[]{:S(2)}) collective-permute-start(f32[64,1536]{1,0:T(8,128)} %slice.123), channel_id=1, source_target_pairs={{0,128},{64,192},{128,0},{192,64},{256,384},{320,448},{384,256},{4... | collective-permute-start | bytes 1179656 | tf_op jit(solution)/shard_map/ppermute | solution.py:95
  211.8 2.5 collective-permute-start.2
  214.2 2.8 collective-permute-start.3
  217.3 7.4 %collective-permute-done.2 = f32[64,256]{1,0:T(8,128)S(1)} collective-permute-done((f32[64,256]{1,0:T(8,128)S(1)}, f32[64,256]{1,0:T(8,128)S(1)}, u32[]{:S(2)}, u32[]{:S(2)}) %collective-permute-start.2) | collective-permute-done | bytes 65568 | tf_op jit(solution)/shard_map/ppermute | solution.py:95
  224.7 3.0 collective-permute-start.4
  228.1 4.3 %collective-permute-done.4 = f32[64,256]{1,0:T(8,128)S(1)} collective-permute-done((f32[64,256]{1,0:T(8,128)S(1)}, f32[64,256]{1,0:T(8,128)S(1)}, u32[]{:S(2)}, u32[]{:S(2)}) %collective-permute-start.4) | collective-permute-done | bytes 65568 | tf_op jit(solution)/shard_map/ppermute | solution.py:95
  233.3 11.7 %cholesky.50 = f32[128,128]{1,0:T(8,128)S(1)} custom-call(f32[128,128]{1,0:T(8,128)S(1)} %cholesky.118), custom_call_target="Cholesky" | custom-call | tf_op jit(solution)/shard_map/jit(cholesky)/cholesky | solution.py:101
  245.0 9.8 %custom-call.14 = f32[1,128,128]{1,2,0:T(8,128)S(1)} custom-call(f32[1,128,128]{2,1,0:T(8,128)S(1)} %get-tuple-element.34), custom_call_target="InvertDiagBlocksLowerTriangular" | custom-call | tf_op jit(solution)/shard_map/jit(cholesky)/cholesky | solution.py:101
  257.0 11.7 %cholesky.105 = f32[128,128]{1,0:T(8,128)S(1)} custom-call(f32[128,128]{1,0:T(8,128)S(1)} %convolution_subtract_fusion.3), custom_call_target="Cholesky" | custom-call | tf_op jit(solution)/shard_map/jit(cholesky)/cholesky | solution.py:101
  270.8 5.3 %while.1 = (s32[]{:T(128)}, f32[256,256]{1,0:T(8,128)S(1)}, s32[2,2]{1,0:T(2,128)S(1)}, f32[2,128,128]{2,1,0:T(8,128)}, s32[]{:T(128)}) while((s32[]{:T(128)}, f32[256,256]{1,0:T(8,128)S(1)}, s32[2,2]{1,0:T(2,128)S(1)}, f32[2,128,128]{2,1,0:T(8,128)}, s32[]{:T(128)}) %tuple.36), condition=%wide.while_cond, body=%wide.while_body.sunk | while | flops 2 | bytes 132705 | solution.py:102
  271.6 2.0 bitcast_dynamic-update-slice_fusion.10
  274.2 2.0 bitcast_dynamic-update-slice_fusion.10
  276.2 20.5 %custom-call.15 = f32[2,128,128]{1,2,0:T(8,128)S(1)} custom-call(f32[2,128,128]{2,1,0:T(8,128)} %get-tuple-element.10), custom_call_target="InvertDiagBlocksLowerTriangular" | custom-call | tf_op jit(solution)/shard_map/triangular_solve | solution.py:102
  302.5 2.6 convolution_bitcast_fusion
  (80 shorter events, 31.0 us)
Async XLA Ops:
  0.6 59.9 %copy-start = (bf16[1536,256]{1,0:T(8,128)(2,1)S(1)}, bf16[1536,256]{1,0:T(8,128)(2,1)}, u32[]{:S(2)}) copy-start(bf16[1536,256]{1,0:T(8,128)(2,1)} %param.5) | copy-start | bytes 2359300
  60.6 23.9 %copy-start.4 = (bf16[8,1536]{1,0:T(8,128)(2,1)}, bf16[8,1536]{1,0:T(8,128)(2,1)S(1)}, u32[]{:S(2)}) copy-start(bf16[8,1536]{1,0:T(8,128)(2,1)S(1)} %fusion.13) | copy-start | bytes 73732
  104.0 5.1 %collective-permute-start = (bf16[4,64,2304]{2,1,0:T(8,128)(2,1)}, bf16[4,64,2304]{2,1,0:T(8,128)(2,1)}, u32[]{:S(2)}, u32[]{:S(2)}) collective-permute-start(bf16[4,64,2304]{2,1,0:T(8,128)(2,1)} %all_to_all.28), channel_id=1, source_target_pairs={{0,1},{1,0},{2,3},{3,2},{4,5},{5,4},{6,7},{7,6},{8,9},{9,8},{10,11... | collective-permute-start | bytes 3538952 | tf_op jit(solution)/shard_map/ppermute | solution.py:66
  111.3 1.4 copy-start.1
  115.5 1.7 copy-start.2
  148.6 51.5 %collective-permute-start.1 = (f32[64,1792]{1,0:T(8,128)}, f32[64,1792]{1,0:T(8,128)S(1)}, u32[]{:S(2)}, u32[]{:S(2)}) collective-permute-start(f32[64,1792]{1,0:T(8,128)} %reduce_sum.39), channel_id=1, source_target_pairs={{0,256},{64,320},{128,384},{192,448},{256,0},{320,64},{384,128},{4... | collective-permute-start | bytes 1376264 | tf_op jit(solution)/shard_map/ppermute | solution.py:88
  201.9 97.5 %collective-permute-start.5 = (f32[64,1536]{1,0:T(8,128)}, f32[64,1536]{1,0:T(8,128)}, u32[]{:S(2)}, u32[]{:S(2)}) collective-permute-start(f32[64,1536]{1,0:T(8,128)} %slice.123), channel_id=1, source_target_pairs={{0,64},{64,0},{128,192},{192,128},{256,320},{320,256},{384,448},{4... | collective-permute-start | bytes 1179656 | tf_op jit(solution)/shard_map/ppermute | solution.py:95
  204.4 96.0 %collective-permute-start.6 = (f32[64,1536]{1,0:T(8,128)}, f32[64,1536]{1,0:T(8,128)}, u32[]{:S(2)}, u32[]{:S(2)}) collective-permute-start(f32[64,1536]{1,0:T(8,128)} %slice.123), channel_id=1, source_target_pairs={{0,192},{64,128},{128,64},{192,0},{256,448},{320,384},{384,320},{4... | collective-permute-start | bytes 1179656 | tf_op jit(solution)/shard_map/ppermute | solution.py:95
  207.2 94.3 %collective-permute-start.7 = (f32[64,1536]{1,0:T(8,128)}, f32[64,1536]{1,0:T(8,128)}, u32[]{:S(2)}, u32[]{:S(2)}) collective-permute-start(f32[64,1536]{1,0:T(8,128)} %slice.123), channel_id=1, source_target_pairs={{0,128},{64,192},{128,0},{192,64},{256,384},{320,448},{384,256},{4... | collective-permute-start | bytes 1179656 | tf_op jit(solution)/shard_map/ppermute | solution.py:95
  211.8 13.0 %collective-permute-start.2 = (f32[64,256]{1,0:T(8,128)S(1)}, f32[64,256]{1,0:T(8,128)S(1)}, u32[]{:S(2)}, u32[]{:S(2)}) collective-permute-start(f32[64,256]{1,0:T(8,128)S(1)} %slice.122), channel_id=1, source_target_pairs={{0,64},{64,0},{128,192},{192,128},{256,320},{320,256},{384,448},{4... | collective-permute-start | bytes 196616 | tf_op jit(solution)/shard_map/ppermute | solution.py:95
  214.2 13.8 %collective-permute-start.3 = (f32[64,256]{1,0:T(8,128)S(1)}, f32[64,256]{1,0:T(8,128)S(1)}, u32[]{:S(2)}, u32[]{:S(2)}) collective-permute-start(f32[64,256]{1,0:T(8,128)S(1)} %slice.122), channel_id=1, source_target_pairs={{0,192},{64,128},{128,64},{192,0},{256,448},{320,384},{384,320},{4... | collective-permute-start | bytes 196616 | tf_op jit(solution)/shard_map/ppermute | solution.py:95
  224.7 7.7 %collective-permute-start.4 = (f32[64,256]{1,0:T(8,128)S(1)}, f32[64,256]{1,0:T(8,128)S(1)}, u32[]{:S(2)}, u32[]{:S(2)}) collective-permute-start(f32[64,256]{1,0:T(8,128)S(1)} %slice.122), channel_id=1, source_target_pairs={{0,128},{64,192},{128,0},{192,64},{256,384},{320,448},{384,256},{4... | collective-permute-start | bytes 196616 | tf_op jit(solution)/shard_map/ppermute | solution.py:95
  232.6 0.7 copy-start.3

commit v2 on v1

--- a/solution.py
+++ b/solution.py
@@ -14,7 +14,6 @@
 Z_GROUPS = [[y * 16 + z * 2 + c for z in range(ZN)] for y in range(YN) for c in range(CN)]
 Y_GROUPS = [[y * 16 + z * 2 + c for y in range(YN)] for z in range(ZN) for c in range(CN)]
 OTHER_CORE = [(i, i ^ 1) for i in range(64)]
-X_GROUPS = [[h * 4 + x for x in range(XN)] for h in range(HN)]
 OTHER_HALF = [(i, i ^ 4) for i in range(8)]
 
 
@@ -82,11 +81,15 @@
     delta = delta - lax.dot_general(three, base, contract_rows, preferred_element_type=F32)
     delta = delta[:rank] + delta[rank : 2 * rank] + delta[2 * rank :]
 
-    both = jnp.concatenate([gram, delta], axis=1).reshape(XN, rank // XN, rank + ff)
-    both = lax.all_to_all(both, "grp", 0, 0, axis_index_groups=X_GROUPS)
-    both = jnp.sum(both, axis=0)
-    both = both + lax.ppermute(both, "grp", OTHER_HALF)
     at_x = lax.axis_index("grp") % XN
+
+    def summed_along_x(whole):
+        blocks = whole.reshape(XN, rank // XN, whole.shape[1])
+        total = lax.dynamic_index_in_dim(blocks, at_x, 0, keepdims=False)
+        for k in (1, 3, 2):
+            block = lax.dynamic_index_in_dim(blocks, at_x ^ k, 0, keepdims=False)
+            total = total + lax.ppermute(block, "grp", along_x(k))
+        return total
 
     def gathered(block):
         whole = jnp.zeros((XN,) + block.shape, F32)
@@ -96,8 +99,13 @@
             whole = lax.dynamic_update_slice(whole, came[None], (at_x ^ k, 0, 0))
         return whole.reshape(XN * block.shape[0], block.shape[1])
 
-    gram = gathered(both[:, :rank])
-    delta = gathered(both[:, rank:])
+    gram = summed_along_x(gram)
+    delta = summed_along_x(delta)
+    gram = gram + lax.ppermute(gram, "grp", OTHER_HALF)
+    delta, gram = lax.optimization_barrier((delta, gram))
+    delta = delta + lax.ppermute(delta, "grp", OTHER_HALF)
+    gram = gathered(gram)
+    delta = gathered(delta)
     lower = jnp.linalg.cholesky(gram)
     inverse = lax.linalg.triangular_solve(
         lower, jnp.eye(rank, dtype=F32), left_side=True, lower=True

time: 306 us -> 274 us (0.90)
  the two profiles are of different devices: /device:TPU:192 before, /device:TPU:32 now
where the time goes in v2:
time: 274 us; the launch traced here: 273 us
  blocking collectives  103 us (38%)
  other arithmetic  61.8 us (23%)
  starting transfers between devices  57.9 us (21%)
  waiting for transfers between devices  21.8 us (8%)
  local copies, waits for them, and re-layouts  13.8 us (5%)
  matrix products  10.4 us (4%)
  between operations  3.31 us (1%)
    all_to_all x1, blocking collectives, per_device(): lax.all_to_all(jnp.concatenate([weighted.reshape(ZN, piece, ff), freq_sum...  35.1 us
    another operation x6, other arithmetic, per_device(): lower = jnp.linalg.cholesky(gram)  33.9 us
    all_to_all x1, blocking collectives, per_device(): lax.all_to_all(jnp.concatenate([own, tag], axis=2), 'exp', 0, 0, axis_ind...  27.5 us
    all_to_all x1, blocking collectives, per_device(): lax.all_to_all(jnp.broadcast_to(load, (ZN, piece, wide)), 'exp', 0, 0, ax...  22.9 us
    another operation x3, other arithmetic, per_device(): lax.linalg.triangular_solve(lower, jnp.eye(rank, dtype=F32), left_side=Tr...  20.5 us
    ppermute x6, starting transfers between devices, summed_along_x(): total = total + lax.ppermute(block, 'grp', along_x(k))  19.8 us
    ppermute x6, starting transfers between devices, gathered(): came = lax.ppermute(block, 'grp', along_x(k))  19.6 us
    all_to_all x1, blocking collectives, per_device(): lax.all_to_all(jnp.broadcast_to(load, (YN, ZN * piece, wide)), 'exp', 0,...  17.9 us
  transfers between devices with their start and end apart: 15, of which 3 were waited for; matrix products, arithmetic and copies ran while one was open for 25% of the time, Pallas kernels for 0%

profile of v2, /device:TPU:32, one launch (start us, length us, event | category | flops | bytes accessed | tf_op | source)
XLA Modules:
  0.0 272.6 jit_solution(12890027771349038575)
XLA Ops:
  3.2 27.5 %all_to_all.20 = bf16[8,64,1664]{2,1,0:T(8,128)(2,1)S(1)} all-to-all(bf16[8,64,1664]{2,1,0:T(8,128)(2,1)S(1)} %pad_maximum_fusion.1), channel_id=1, replica_groups={{0,1,16,17,32,33,48,49},{2,3,18,19,34,35,50,51},{4,5,20,21,36,37,52,53}..., dimensions={0} | all-to-all | bytes 3407872 | tf_op jit(solution)/shard_map/all_to_all | solution.py:41
  32.4 35.1 %all_to_all.21 = f32[8,8,1664]{2,1,0:T(8,128)S(1)} all-to-all(f32[8,8,1664]{2,1,0:T(8,128)S(1)} %concatenate.15), channel_id=1, replica_groups={{0,2,4,6,8,10,12,14},{1,3,5,7,9,11,13,15},{16,18,20,22,24,26,28,30},{17..., dimensions={0} | all-to-all | bytes 851968 | tf_op jit(solution)/shard_map/all_to_all | solution.py:48
  68.4 22.9 %all_to_all.22 = bf16[8,8,2304]{2,1,0:T(8,128)(2,1)S(1)} all-to-all(bf16[8,8,2304]{2,1,0:T(8,128)(2,1)S(1)} %broadcast_in_dim.55), channel_id=1, replica_groups={{0,2,4,6,8,10,12,14},{1,3,5,7,9,11,13,15},{16,18,20,22,24,26,28,30},{17..., dimensions={0} | all-to-all | bytes 589824 | tf_op jit(solution)/shard_map/all_to_all | solution.py:59
  91.3 17.9 %all_to_all.23 = bf16[4,64,2304]{2,1,0:T(8,128)(2,1)S(1)} all-to-all(bf16[4,64,2304]{2,1,0:T(8,128)(2,1)S(1)} %broadcast_in_dim.56), channel_id=1, replica_groups={{0,16,32,48},{1,17,33,49},{2,18,34,50},{3,19,35,51},{4,20,36,52},{5,21,..., dimensions={0} | all-to-all | bytes 2359296 | tf_op jit(solution)/shard_map/all_to_all | solution.py:62
  111.2 2.9 %collective-permute-done = bf16[4,64,2304]{2,1,0:T(8,128)(2,1)} collective-permute-done((bf16[4,64,2304]{2,1,0:T(8,128)(2,1)S(1)}, bf16[4,64,2304]{2,1,0:T(8,128)(2,1)}, u32[]{:S(2)}, u32[]{:S(2)}) %collective-permute-start) | collective-permute-done | bytes 1179680 | tf_op jit(solution)/shard_map/ppermute | solution.py:65
  121.4 3.4 %collective-permute-start.4 = (f32[64,256]{1,0:T(8,128)S(1)}, f32[64,256]{1,0:T(8,128)}, u32[]{:S(2)}, u32[]{:S(2)}) collective-permute-start(f32[64,256]{1,0:T(8,128)S(1)} %get-tuple-element.40), channel_id=1, source_target_pairs={{0,64},{64,0},{128,192},{192,128},{256,320},{320,256},{384,448},{4... | collective-permute-start | bytes 196616 | tf_op jit(solution)/shard_map/ppermute | solution.py:91
  124.8 4.0 %collective-permute-start.5 = (f32[64,256]{1,0:T(8,128)}, f32[64,256]{1,0:T(8,128)}, u32[]{:S(2)}, u32[]{:S(2)}) collective-permute-start(f32[64,256]{1,0:T(8,128)} %get-tuple-element.42), channel_id=1, source_target_pairs={{0,192},{64,128},{128,64},{192,0},{256,448},{320,384},{384,320},{4... | collective-permute-start | bytes 196616 | tf_op jit(solution)/shard_map/ppermute | solution.py:91
  135.9 3.2 %collective-permute-start.1 = (f32[64,1536]{1,0:T(8,128)}, f32[64,1536]{1,0:T(8,128)}, u32[]{:S(2)}, u32[]{:S(2)}) collective-permute-start(f32[64,1536]{1,0:T(8,128)} %get-tuple-element.34), channel_id=1, source_target_pairs={{0,64},{64,0},{128,192},{192,128},{256,320},{320,256},{384,448},{4... | collective-permute-start | bytes 1179656 | tf_op jit(solution)/shard_map/ppermute | solution.py:91
  139.1 4.0 %collective-permute-start.2 = (f32[64,1536]{1,0:T(8,128)}, f32[64,1536]{1,0:T(8,128)}, u32[]{:S(2)}, u32[]{:S(2)}) collective-permute-start(f32[64,1536]{1,0:T(8,128)} %get-tuple-element.36), channel_id=1, source_target_pairs={{0,192},{64,128},{128,64},{192,0},{256,448},{320,384},{384,320},{4... | collective-permute-start | bytes 1179656 | tf_op jit(solution)/shard_map/ppermute | solution.py:91
  147.3 8.2 %collective-permute-start.7 = (f32[64,256]{1,0:T(8,128)S(1)}, f32[64,256]{1,0:T(8,128)S(1)}, u32[]{:S(2)}, u32[]{:S(2)}) collective-permute-start(f32[64,256]{1,0:T(8,128)S(1)} %fusion.14), channel_id=1, source_target_pairs={{0,256},{64,320},{128,384},{192,448},{256,0},{320,64},{384,128},{4... | collective-permute-start | bytes 196616 | tf_op jit(solution)/shard_map/ppermute | solution.py:104
  155.5 6.7 %collective-permute-done.7 = f32[64,256]{1,0:T(8,128)S(1)} collective-permute-done((f32[64,256]{1,0:T(8,128)S(1)}, f32[64,256]{1,0:T(8,128)S(1)}, u32[]{:S(2)}, u32[]{:S(2)}) %collective-permute-start.7) | collective-permute-done | bytes 65568 | tf_op jit(solution)/shard_map/ppermute | solution.py:104
  163.6 3.2 %collective-permute-start.8 = (f32[64,256]{1,0:T(8,128)S(1)}, f32[64,256]{1,0:T(8,128)S(1)}, u32[]{:S(2)}, u32[]{:S(2)}) collective-permute-start(f32[64,256]{1,0:T(8,128)S(1)} %add.120), channel_id=1, source_target_pairs={{0,64},{64,0},{128,192},{192,128},{256,320},{320,256},{384,448},{4... | collective-permute-start | bytes 196616 | tf_op jit(solution)/shard_map/ppermute | solution.py:98
  166.8 4.0 %collective-permute-start.9 = (f32[64,256]{1,0:T(8,128)S(1)}, f32[64,256]{1,0:T(8,128)S(1)}, u32[]{:S(2)}, u32[]{:S(2)}) collective-permute-start(f32[64,256]{1,0:T(8,128)S(1)} %add.120), channel_id=1, source_target_pairs={{0,192},{64,128},{128,64},{192,0},{256,448},{320,384},{384,320},{4... | collective-permute-start | bytes 196616 | tf_op jit(solution)/shard_map/ppermute | solution.py:98
  170.8 2.6 collective-permute-start.10
  173.4 8.4 %collective-permute-start.11 = (f32[64,1536]{1,0:T(8,128)S(1)}, f32[64,1536]{1,0:T(8,128)}, u32[]{:S(2)}, u32[]{:S(2)}) collective-permute-start(f32[64,1536]{1,0:T(8,128)S(1)} %fusion.3), channel_id=1, source_target_pairs={{0,256},{64,320},{128,384},{192,448},{256,0},{320,64},{384,128},{4... | collective-permute-start | bytes 1179656 | tf_op jit(solution)/shard_map/ppermute | solution.py:106
  182.1 11.7 %cholesky.50 = f32[128,128]{1,0:T(8,128)S(1)} custom-call(f32[128,128]{1,0:T(8,128)S(1)} %cholesky.118), custom_call_target="Cholesky" | custom-call | tf_op jit(solution)/shard_map/jit(cholesky)/cholesky | solution.py:109
  193.9 9.8 %custom-call.14 = f32[1,128,128]{1,2,0:T(8,128)S(1)} custom-call(f32[1,128,128]{2,1,0:T(8,128)S(1)} %get-tuple-element.46), custom_call_target="InvertDiagBlocksLowerTriangular" | custom-call | tf_op jit(solution)/shard_map/jit(cholesky)/cholesky | solution.py:109
  204.2 11.7 %cholesky.105 = f32[128,128]{1,0:T(8,128)S(1)} custom-call(f32[128,128]{1,0:T(8,128)S(1)} %convolution_subtract_fusion.3), custom_call_target="Cholesky" | custom-call | tf_op jit(solution)/shard_map/jit(cholesky)/cholesky | solution.py:109
  218.0 5.4 %while.1 = (s32[]{:T(128)}, f32[256,256]{1,0:T(8,128)S(1)}, s32[2,2]{1,0:T(2,128)S(1)}, f32[2,128,128]{2,1,0:T(8,128)}, s32[]{:T(128)}) while((s32[]{:T(128)}, f32[256,256]{1,0:T(8,128)S(1)}, s32[2,2]{1,0:T(2,128)S(1)}, f32[2,128,128]{2,1,0:T(8,128)}, s32[]{:T(128)}) %tuple.43), condition=%wide.while_cond, body=%wide.while_body.sunk | while | flops 2 | bytes 132705 | solution.py:110
  223.4 20.5 %custom-call.15 = f32[2,128,128]{1,2,0:T(8,128)S(1)} custom-call(f32[2,128,128]{2,1,0:T(8,128)} %get-tuple-element.14), custom_call_target="InvertDiagBlocksLowerTriangular" | custom-call | tf_op jit(solution)/shard_map/triangular_solve | solution.py:110
  245.6 3.3 %collective-permute-start.12 = (f32[64,1536]{1,0:T(8,128)S(1)}, f32[64,1536]{1,0:T(8,128)S(1)}, u32[]{:S(2)}, u32[]{:S(2)}) collective-permute-start(f32[64,1536]{1,0:T(8,128)S(1)} %get-tuple-element.26), channel_id=1, source_target_pairs={{0,64},{64,0},{128,192},{192,128},{256,320},{320,256},{384,448},{4... | collective-permute-start | bytes 1179656 | tf_op jit(solution)/shard_map/ppermute | solution.py:98
  251.1 4.0 %collective-permute-start.13 = (f32[64,1536]{1,0:T(8,128)S(1)}, f32[64,1536]{1,0:T(8,128)S(1)}, u32[]{:S(2)}, u32[]{:S(2)}) collective-permute-start(f32[64,1536]{1,0:T(8,128)S(1)} %get-tuple-element.26), channel_id=1, source_target_pairs={{0,192},{64,128},{128,64},{192,0},{256,448},{320,384},{384,320},{4... | collective-permute-start | bytes 1179656 | tf_op jit(solution)/shard_map/ppermute | solution.py:98
  257.7 12.2 %collective-permute-done.13 = f32[64,1536]{1,0:T(8,128)S(1)} collective-permute-done((f32[64,1536]{1,0:T(8,128)S(1)}, f32[64,1536]{1,0:T(8,128)S(1)}, u32[]{:S(2)}, u32[]{:S(2)}) %collective-permute-start.13) | collective-permute-done | bytes 393248 | tf_op jit(solution)/shard_map/ppermute | solution.py:98
  270.0 2.6 convolution_bitcast_fusion
  (93 shorter events, 39.4 us)
Async XLA Ops:
  0.6 67.1 %copy-start = (bf16[1536,256]{1,0:T(8,128)(2,1)S(1)}, bf16[1536,256]{1,0:T(8,128)(2,1)}, u32[]{:S(2)}) copy-start(bf16[1536,256]{1,0:T(8,128)(2,1)} %param.5) | copy-start | bytes 2359300
  67.7 0.6 copy-start.4
  109.2 4.9 %collective-permute-start = (bf16[4,64,2304]{2,1,0:T(8,128)(2,1)S(1)}, bf16[4,64,2304]{2,1,0:T(8,128)(2,1)}, u32[]{:S(2)}, u32[]{:S(2)}) collective-permute-start(bf16[4,64,2304]{2,1,0:T(8,128)(2,1)S(1)} %all_to_all.23), channel_id=1, source_target_pairs={{0,1},{1,0},{2,3},{3,2},{4,5},{5,4},{6,7},{7,6},{8,9},{9,8},{10,11... | collective-permute-start | bytes 3538952 | tf_op jit(solution)/shard_map/ppermute | solution.py:65
  115.9 1.4 copy-start.1
  121.4 21.7 %collective-permute-start.4 = (f32[64,256]{1,0:T(8,128)S(1)}, f32[64,256]{1,0:T(8,128)}, u32[]{:S(2)}, u32[]{:S(2)}) collective-permute-start(f32[64,256]{1,0:T(8,128)S(1)} %get-tuple-element.40), channel_id=1, source_target_pairs={{0,64},{64,0},{128,192},{192,128},{256,320},{320,256},{384,448},{4... | collective-permute-start | bytes 196616 | tf_op jit(solution)/shard_map/ppermute | solution.py:91
  124.8 21.5 %collective-permute-start.5 = (f32[64,256]{1,0:T(8,128)}, f32[64,256]{1,0:T(8,128)}, u32[]{:S(2)}, u32[]{:S(2)}) collective-permute-start(f32[64,256]{1,0:T(8,128)} %get-tuple-element.42), channel_id=1, source_target_pairs={{0,192},{64,128},{128,64},{192,0},{256,448},{320,384},{384,320},{4... | collective-permute-start | bytes 196616 | tf_op jit(solution)/shard_map/ppermute | solution.py:91
  128.9 17.5 %collective-permute-start.6 = (f32[64,256]{1,0:T(8,128)}, f32[64,256]{1,0:T(8,128)}, u32[]{:S(2)}, u32[]{:S(2)}) collective-permute-start(f32[64,256]{1,0:T(8,128)} %get-tuple-element.41), channel_id=1, source_target_pairs={{0,128},{64,192},{128,0},{192,64},{256,384},{320,448},{384,256},{4... | collective-permute-start | bytes 196616 | tf_op jit(solution)/shard_map/ppermute | solution.py:91
  131.4 1.7 copy-start.2
  135.9 26.4 %collective-permute-start.1 = (f32[64,1536]{1,0:T(8,128)}, f32[64,1536]{1,0:T(8,128)}, u32[]{:S(2)}, u32[]{:S(2)}) collective-permute-start(f32[64,1536]{1,0:T(8,128)} %get-tuple-element.34), channel_id=1, source_target_pairs={{0,64},{64,0},{128,192},{192,128},{256,320},{320,256},{384,448},{4... | collective-permute-start | bytes 1179656 | tf_op jit(solution)/shard_map/ppermute | solution.py:91
  139.1 23.1 %collective-permute-start.2 = (f32[64,1536]{1,0:T(8,128)}, f32[64,1536]{1,0:T(8,128)}, u32[]{:S(2)}, u32[]{:S(2)}) collective-permute-start(f32[64,1536]{1,0:T(8,128)} %get-tuple-element.36), channel_id=1, source_target_pairs={{0,192},{64,128},{128,64},{192,0},{256,448},{320,384},{384,320},{4... | collective-permute-start | bytes 1179656 | tf_op jit(solution)/shard_map/ppermute | solution.py:91
  143.1 19.1 %collective-permute-start.3 = (f32[64,1536]{1,0:T(8,128)S(1)}, f32[64,1536]{1,0:T(8,128)}, u32[]{:S(2)}, u32[]{:S(2)}) collective-permute-start(f32[64,1536]{1,0:T(8,128)S(1)} %get-tuple-element.35), channel_id=1, source_target_pairs={{0,128},{64,192},{128,0},{192,64},{256,384},{320,448},{384,256},{4... | collective-permute-start | bytes 1179656 | tf_op jit(solution)/shard_map/ppermute | solution.py:91
  147.3 14.9 %collective-permute-start.7 = (f32[64,256]{1,0:T(8,128)S(1)}, f32[64,256]{1,0:T(8,128)S(1)}, u32[]{:S(2)}, u32[]{:S(2)}) collective-permute-start(f32[64,256]{1,0:T(8,128)S(1)} %fusion.14), channel_id=1, source_target_pairs={{0,256},{64,320},{128,384},{192,448},{256,0},{320,64},{384,128},{4... | collective-permute-start | bytes 196616 | tf_op jit(solution)/shard_map/ppermute | solution.py:104
  163.6 18.3 %collective-permute-start.8 = (f32[64,256]{1,0:T(8,128)S(1)}, f32[64,256]{1,0:T(8,128)S(1)}, u32[]{:S(2)}, u32[]{:S(2)}) collective-permute-start(f32[64,256]{1,0:T(8,128)S(1)} %add.120), channel_id=1, source_target_pairs={{0,64},{64,0},{128,192},{192,128},{256,320},{320,256},{384,448},{4... | collective-permute-start | bytes 196616 | tf_op jit(solution)/shard_map/ppermute | solution.py:98
  166.8 15.1 %collective-permute-start.9 = (f32[64,256]{1,0:T(8,128)S(1)}, f32[64,256]{1,0:T(8,128)S(1)}, u32[]{:S(2)}, u32[]{:S(2)}) collective-permute-start(f32[64,256]{1,0:T(8,128)S(1)} %add.120), channel_id=1, source_target_pairs={{0,192},{64,128},{128,64},{192,0},{256,448},{320,384},{384,320},{4... | collective-permute-start | bytes 196616 | tf_op jit(solution)/shard_map/ppermute | solution.py:98
  170.8 11.1 %collective-permute-start.10 = (f32[64,256]{1,0:T(8,128)S(1)}, f32[64,256]{1,0:T(8,128)S(1)}, u32[]{:S(2)}, u32[]{:S(2)}) collective-permute-start(f32[64,256]{1,0:T(8,128)S(1)} %add.120), channel_id=1, source_target_pairs={{0,128},{64,192},{128,0},{192,64},{256,384},{320,448},{384,256},{4... | collective-permute-start | bytes 196616 | tf_op jit(solution)/shard_map/ppermute | solution.py:98
  173.4 71.0 %collective-permute-start.11 = (f32[64,1536]{1,0:T(8,128)S(1)}, f32[64,1536]{1,0:T(8,128)}, u32[]{:S(2)}, u32[]{:S(2)}) collective-permute-start(f32[64,1536]{1,0:T(8,128)S(1)} %fusion.3), channel_id=1, source_target_pairs={{0,256},{64,320},{128,384},{192,448},{256,0},{320,64},{384,128},{4... | collective-permute-start | bytes 1179656 | tf_op jit(solution)/shard_map/ppermute | solution.py:106
  182.1 61.8 %copy-start.3 = (pred[256,256]{1,0:T(32,128)(4,1)S(1)}, pred[256,256]{1,0:T(32,128)(4,1)}, u32[]{:S(2)}) copy-start(pred[256,256]{1,0:T(32,128)(4,1)} %iota_compare_fusion) | copy-start | bytes 196612
  245.6 12.0 %collective-permute-start.12 = (f32[64,1536]{1,0:T(8,128)S(1)}, f32[64,1536]{1,0:T(8,128)S(1)}, u32[]{:S(2)}, u32[]{:S(2)}) collective-permute-start(f32[64,1536]{1,0:T(8,128)S(1)} %get-tuple-element.26), channel_id=1, source_target_pairs={{0,64},{64,0},{128,192},{192,128},{256,320},{320,256},{384,448},{4... | collective-permute-start | bytes 1179656 | tf_op jit(solution)/shard_map/ppermute | solution.py:98
  251.1 18.8 %collective-permute-start.13 = (f32[64,1536]{1,0:T(8,128)S(1)}, f32[64,1536]{1,0:T(8,128)S(1)}, u32[]{:S(2)}, u32[]{:S(2)}) collective-permute-start(f32[64,1536]{1,0:T(8,128)S(1)} %get-tuple-element.26), channel_id=1, source_target_pairs={{0,192},{64,128},{128,64},{192,0},{256,448},{320,384},{384,320},{4... | collective-permute-start | bytes 1179656 | tf_op jit(solution)/shard_map/ppermute | solution.py:98
  255.1 14.9 %collective-permute-start.14 = (f32[64,1536]{1,0:T(8,128)S(1)}, f32[64,1536]{1,0:T(8,128)S(1)}, u32[]{:S(2)}, u32[]{:S(2)}) collective-permute-start(f32[64,1536]{1,0:T(8,128)S(1)} %get-tuple-element.26), channel_id=1, source_target_pairs={{0,128},{64,192},{128,0},{192,64},{256,384},{320,448},{384,256},{4... | collective-permute-start | bytes 1179656 | tf_op jit(solution)/shard_map/ppermute | solution.py:98

commit v3 on v1

--- a/solution.py
+++ b/solution.py
@@ -3,6 +3,8 @@
 import jax
 import jax.numpy as jnp
 from jax import lax
+from jax.experimental import pallas as pl
+from jax.experimental.pallas import tpu as pltpu
 from jax.sharding import PartitionSpec as P
 
 F32, BF16 = jnp.float32, jnp.bfloat16
@@ -14,7 +16,6 @@
 Z_GROUPS = [[y * 16 + z * 2 + c for z in range(ZN)] for y in range(YN) for c in range(CN)]
 Y_GROUPS = [[y * 16 + z * 2 + c for y in range(YN)] for z in range(ZN) for c in range(CN)]
 OTHER_CORE = [(i, i ^ 1) for i in range(64)]
-X_GROUPS = [[h * 4 + x for x in range(XN)] for h in range(HN)]
 OTHER_HALF = [(i, i ^ 4) for i in range(8)]
 
 
@@ -27,6 +28,72 @@
     rest = value - first
     second = lax.reduce_precision(rest, 8, 7)
     return [first.astype(BF16), second.astype(BF16), (rest - second).astype(BF16)]
+
+
+PANEL = 64
+
+
+def eye(n):
+    row, col = (lax.broadcasted_iota(jnp.int32, (n, n), d) for d in (0, 1))
+    return jnp.where(row == col, 1.0, 0.0).astype(F32)
+
+
+def inverse_root(value):
+    guess = lax.rsqrt(value)
+    return guess * (1.5 - 0.5 * value * guess * guess)
+
+
+def inverse_factor_of_panel(square):
+    n = square.shape[0]
+    work = jnp.concatenate([square, eye(n)], axis=1)
+    row = lax.broadcasted_iota(jnp.int32, work.shape, 0)
+    for j in range(0, n, 2):
+        left = jnp.broadcast_to(work[:, j : j + 1], work.shape)
+        right = jnp.broadcast_to(work[:, j + 1 : j + 2], work.shape)
+        scale = inverse_root(left[j : j + 1])
+        cross = left[j + 1 : j + 2] * scale
+        scale_next = inverse_root(right[j + 1 : j + 2] - cross * cross)
+        top = work[j : j + 1] * scale
+        low = (work[j + 1 : j + 2] - cross * top) * scale_next
+        left = left * scale
+        right = (right - left * cross) * scale_next
+        rest = jnp.where(row > j + 1, work - left * top - right * low, work)
+        work = jnp.where(row == j, top, jnp.where(row == j + 1, low, rest))
+    return work[:, n:]
+
+
+def inverse_factor_kernel(gram_ref, inverse_ref, work_ref):
+    n = gram_ref.shape[0]
+    work_ref[:, :n] = gram_ref[...]
+    work_ref[:, n:] = eye(n)
+    for at in range(0, n, PANEL):
+        end = at + PANEL
+        own = inverse_factor_of_panel(work_ref[at:end, at:end])
+        done = jnp.dot(own, work_ref[at:end], precision=HIGHEST, preferred_element_type=F32)
+        inverse_ref[at:end] = done[:, n:]
+        if end < n:
+            below = lax.dot_general(
+                work_ref[end:, at:end], own, (((1,), (1,)), ((), ())),
+                precision=HIGHEST, preferred_element_type=F32,
+            )
+            work_ref[end:] = work_ref[end:] - jnp.dot(
+                below, done, precision=HIGHEST, preferred_element_type=F32
+            )
+
+
+def inverse_factor(gram):
+    n = gram.shape[0]
+    vmem = pl.BlockSpec(memory_space=pltpu.VMEM)
+    return pl.pallas_call(
+        inverse_factor_kernel,
+        out_shape=jax.ShapeDtypeStruct((n, n), F32),
+        in_specs=[vmem],
+        out_specs=vmem,
+        scratch_shapes=[pltpu.VMEM((n, 2 * n), F32)],
+        compiler_params=pltpu.CompilerParams(vmem_limit_bytes=16 * 2**20),
+        cost_estimate=pl.CostEstimate(flops=10**9, bytes_accessed=2**19, transcendentals=0),
+        name="inverse_factor",
+    )(gram)
 
 
 def per_device(counts, up_weights, sketch):
@@ -82,11 +149,19 @@
     delta = delta - lax.dot_general(three, base, contract_rows, preferred_element_type=F32)
     delta = delta[:rank] + delta[rank : 2 * rank] + delta[2 * rank :]
 
-    both = jnp.concatenate([gram, delta], axis=1).reshape(XN, rank // XN, rank + ff)
-    both = lax.all_to_all(both, "grp", 0, 0, axis_index_groups=X_GROUPS)
-    both = jnp.sum(both, axis=0)
-    both = both + lax.ppermute(both, "grp", OTHER_HALF)
     at_x = lax.axis_index("grp") % XN
+
+    def sent_along_x(whole):
+        blocks = whole.reshape(XN, rank // XN, whole.shape[1])
+        own = lax.dynamic_index_in_dim(blocks, at_x, 0, keepdims=False)
+        came = [
+            lax.ppermute(
+                lax.dynamic_index_in_dim(blocks, at_x ^ k, 0, keepdims=False),
+                "grp", along_x(k),
+            )
+            for k in (1, 3, 2)
+        ]
+        return [own] + came
 
     def gathered(block):
         whole = jnp.zeros((XN,) + block.shape, F32)
@@ -96,12 +171,16 @@
             whole = lax.dynamic_update_slice(whole, came[None], (at_x ^ k, 0, 0))
         return whole.reshape(XN * block.shape[0], block.shape[1])
 
-    gram = gathered(both[:, :rank])
-    delta = gathered(both[:, rank:])
-    lower = jnp.linalg.cholesky(gram)
-    inverse = lax.linalg.triangular_solve(
-        lower, jnp.eye(rank, dtype=F32), left_side=True, lower=True
-    )
+    gram = sent_along_x(gram)
+    gram, delta = lax.optimization_barrier((gram, delta))
+    delta = sum(sent_along_x(delta))
+    gram = sum(gram)
+    gram_came = lax.ppermute(gram, "grp", OTHER_HALF)
+    delta_came = lax.ppermute(delta, "grp", OTHER_HALF)
+    gram_came, delta = lax.optimization_barrier((gram_came, delta))
+    inverse = inverse_factor(gathered(gram + gram_came))
+    inverse, delta_came = lax.optimization_barrier((inverse, delta_came))
+    delta = gathered(delta + delta_came)
     ortho = lax.dot_general(
         range_rows, inverse, (((1,), (1,)), ((), ())), precision=HIGHEST
     )

time: 306 us -> 238 us (0.78)
  other arithmetic: 60.4 us -> 3.58 us
  starting transfers between devices: 28.2 us -> 57.3 us
  blocking collectives: 126 us -> 97.5 us
  Pallas kernels: 0 us -> 16.7 us
  waiting for transfers between devices: 58.4 us -> 45.4 us
  local copies, waits for them, and re-layouts: 16.5 us -> 6.17 us
  matrix products: 12.1 us -> 8.17 us
    another operation x9 -> x0, other arithmetic: 54.5 us -> none  [the longest x6 34 us: per_device(): lower = jnp.linalg.cholesky(gram)]
    all_to_all x1 -> x0, blocking collectives: 27.9 us -> none  [per_device(): both = lax.all_to_all(both, 'grp', 0, 0, axis_index_groups=X_GROUPS)]
    ppermute x1 -> x8, starting transfers between devices: 8.21 us -> 35.7 us  [the longest x6 19.8 us: sent_along_x(): lax.ppermute(lax.dynamic_index_in_dim(blocks, at_x ^ k, 0, keepdims=False...]
    pallas_call x0 -> x1, Pallas kernels: none -> 16.7 us  [inverse_factor(): pl.pallas_call(inverse_factor_kernel, out_shape=jax.ShapeDtypeStruct((n,...]
    ppermute x1 -> x8, waiting for transfers between devices: 43.2 us -> 29.5 us  [the longest x1 16.9 us: per_device(): delta_came = lax.ppermute(delta, 'grp', OTHER_HALF)]
    another operation x9 -> x0, local copies, waits for them, and re-layouts: 5.25 us -> none
  transfers between devices with their start and end apart: 8 -> 15, of which waited for: 5 -> 8; matrix products, arithmetic and copies ran while one was open for 22% -> 1% of each run, Pallas kernels for 0% -> 7%
where the time goes in v3:
time: 238 us; the launch traced here: 237 us
  blocking collectives  97.5 us (41%)
  starting transfers between devices  57.3 us (24%)
  waiting for transfers between devices  45.4 us (19%)
  Pallas kernels  16.7 us (7%)
  matrix products  8.17 us (3%)
  local copies, waits for them, and re-layouts  6.17 us (3%)
  other arithmetic  3.58 us (2%)
    all_to_all x1, blocking collectives, per_device(): lax.all_to_all(jnp.concatenate([weighted.reshape(ZN, piece, ff), freq_sum...  27.9 us
    all_to_all x1, blocking collectives, per_device(): lax.all_to_all(jnp.concatenate([own, tag], axis=2), 'exp', 0, 0, axis_ind...  27.5 us
    all_to_all x1, blocking collectives, per_device(): lax.all_to_all(jnp.broadcast_to(load, (ZN, piece, wide)), 'exp', 0, 0, ax...  23.3 us
    ppermute x6, starting transfers between devices, sent_along_x(): lax.ppermute(lax.dynamic_index_in_dim(blocks, at_x ^ k, 0, keepdims=False...  19.8 us
    ppermute x6, starting transfers between devices, gathered(): came = lax.ppermute(block, 'grp', along_x(k))  19.6 us
    all_to_all x1, blocking collectives, per_device(): lax.all_to_all(jnp.broadcast_to(load, (YN, ZN * piece, wide)), 'exp', 0,...  18.8 us
    ppermute x1, waiting for transfers between devices, per_device(): delta_came = lax.ppermute(delta, 'grp', OTHER_HALF)  16.9 us
    pallas_call x1, Pallas kernels, inverse_factor(): pl.pallas_call(inverse_factor_kernel, out_shape=jax.ShapeDtypeStruct((n,...  16.7 us
  transfers between devices with their start and end apart: 15, of which 8 were waited for; matrix products, arithmetic and copies ran while one was open for 1% of the time, Pallas kernels for 7%

profile of v3, /device:TPU:192, one launch (start us, length us, event | category | flops | bytes accessed | tf_op | source)
XLA Modules:
  0.0 236.8 jit_solution(10632971257732944822)
XLA Ops:
  3.2 27.5 %all_to_all.20 = bf16[8,64,1664]{2,1,0:T(8,128)(2,1)S(1)} all-to-all(bf16[8,64,1664]{2,1,0:T(8,128)(2,1)S(1)} %pad_maximum_fusion.1), channel_id=1, replica_groups={{0,1,16,17,32,33,48,49},{2,3,18,19,34,35,50,51},{4,5,20,21,36,37,52,53}..., dimensions={0} | all-to-all | bytes 3407872 | tf_op jit(solution)/shard_map/all_to_all | solution.py:109
  32.4 27.9 %all_to_all.21 = f32[8,8,1664]{2,1,0:T(8,128)S(1)} all-to-all(f32[8,8,1664]{2,1,0:T(8,128)S(1)} %concatenate.13), channel_id=1, replica_groups={{0,2,4,6,8,10,12,14},{1,3,5,7,9,11,13,15},{16,18,20,22,24,26,28,30},{17..., dimensions={0} | all-to-all | bytes 851968 | tf_op jit(solution)/shard_map/all_to_all | solution.py:116
  61.2 23.3 %all_to_all.22 = bf16[8,8,2304]{2,1,0:T(8,128)(2,1)S(1)} all-to-all(bf16[8,8,2304]{2,1,0:T(8,128)(2,1)S(1)} %broadcast_in_dim.53), channel_id=1, replica_groups={{0,2,4,6,8,10,12,14},{1,3,5,7,9,11,13,15},{16,18,20,22,24,26,28,30},{17..., dimensions={0} | all-to-all | bytes 589824 | tf_op jit(solution)/shard_map/all_to_all | solution.py:127
  84.6 18.8 %all_to_all.23 = bf16[4,64,2304]{2,1,0:T(8,128)(2,1)S(1)} all-to-all(bf16[4,64,2304]{2,1,0:T(8,128)(2,1)S(1)} %broadcast_in_dim.54), channel_id=1, replica_groups={{0,16,32,48},{1,17,33,49},{2,18,34,50},{3,19,35,51},{4,20,36,52},{5,21,..., dimensions={0} | all-to-all | bytes 2359296 | tf_op jit(solution)/shard_map/all_to_all | solution.py:130
  105.4 2.9 %collective-permute-done = bf16[4,64,2304]{2,1,0:T(8,128)(2,1)} collective-permute-done((bf16[4,64,2304]{2,1,0:T(8,128)(2,1)S(1)}, bf16[4,64,2304]{2,1,0:T(8,128)(2,1)}, u32[]{:S(2)}, u32[]{:S(2)}) %collective-permute-start) | collective-permute-done | bytes 1179680 | tf_op jit(solution)/shard_map/ppermute | solution.py:133
  116.4 3.4 %collective-permute-start.1 = (f32[64,256]{1,0:T(8,128)S(1)}, f32[64,256]{1,0:T(8,128)S(1)}, u32[]{:S(2)}, u32[]{:S(2)}) collective-permute-start(f32[64,256]{1,0:T(8,128)S(1)} %get-tuple-element.40), channel_id=1, source_target_pairs={{0,64},{64,0},{128,192},{192,128},{256,320},{320,256},{384,448},{4... | collective-permute-start | bytes 196616 | tf_op jit(solution)/shard_map/ppermute | solution.py:158
  119.9 4.0 %collective-permute-start.2 = (f32[64,256]{1,0:T(8,128)S(1)}, f32[64,256]{1,0:T(8,128)S(1)}, u32[]{:S(2)}, u32[]{:S(2)}) collective-permute-start(f32[64,256]{1,0:T(8,128)S(1)} %get-tuple-element.39), channel_id=1, source_target_pairs={{0,192},{64,128},{128,64},{192,0},{256,448},{320,384},{384,320},{4... | collective-permute-start | bytes 196616 | tf_op jit(solution)/shard_map/ppermute | solution.py:158
  123.9 2.6 %collective-permute-start.3 = (f32[64,256]{1,0:T(8,128)S(1)}, f32[64,256]{1,0:T(8,128)S(1)}, u32[]{:S(2)}, u32[]{:S(2)}) collective-permute-start(f32[64,256]{1,0:T(8,128)S(1)} %get-tuple-element.38), channel_id=1, source_target_pairs={{0,128},{64,192},{128,0},{192,64},{256,384},{320,448},{384,256},{4... | collective-permute-start | bytes 196616 | tf_op jit(solution)/shard_map/ppermute | solution.py:158
  127.2 4.3 %collective-permute-done.3 = f32[64,256]{1,0:T(8,128)S(1)} collective-permute-done((f32[64,256]{1,0:T(8,128)S(1)}, f32[64,256]{1,0:T(8,128)S(1)}, u32[]{:S(2)}, u32[]{:S(2)}) %collective-permute-start.3) | collective-permute-done | bytes 65568 | tf_op jit(solution)/shard_map/ppermute | solution.py:158
  131.6 2.5 %collective-permute-start.5 = (f32[64,1536]{1,0:T(8,128)S(1)}, f32[64,1536]{1,0:T(8,128)S(1)}, u32[]{:S(2)}, u32[]{:S(2)}) collective-permute-start(f32[64,1536]{1,0:T(8,128)S(1)} %get-tuple-element.32), channel_id=1, source_target_pairs={{0,64},{64,0},{128,192},{192,128},{256,320},{320,256},{384,448},{4... | collective-permute-start | bytes 1179656 | tf_op jit(solution)/shard_map/ppermute | solution.py:158
  134.1 2.5 %collective-permute-start.6 = (f32[64,1536]{1,0:T(8,128)S(1)}, f32[64,1536]{1,0:T(8,128)S(1)}, u32[]{:S(2)}, u32[]{:S(2)}) collective-permute-start(f32[64,1536]{1,0:T(8,128)S(1)} %get-tuple-element.34), channel_id=1, source_target_pairs={{0,192},{64,128},{128,64},{192,0},{256,448},{320,384},{384,320},{4... | collective-permute-start | bytes 1179656 | tf_op jit(solution)/shard_map/ppermute | solution.py:158
  136.7 4.8 %collective-permute-start.7 = (f32[64,1536]{1,0:T(8,128)S(1)}, f32[64,1536]{1,0:T(8,128)S(1)}, u32[]{:S(2)}, u32[]{:S(2)}) collective-permute-start(f32[64,1536]{1,0:T(8,128)S(1)} %get-tuple-element.33), channel_id=1, source_target_pairs={{0,128},{64,192},{128,0},{192,64},{256,384},{320,448},{384,256},{4... | collective-permute-start | bytes 1179656 | tf_op jit(solution)/shard_map/ppermute | solution.py:158
  141.5 8.2 %collective-permute-start.4 = (f32[64,256]{1,0:T(8,128)S(1)}, f32[64,256]{1,0:T(8,128)S(1)}, u32[]{:S(2)}, u32[]{:S(2)}) collective-permute-start(f32[64,256]{1,0:T(8,128)S(1)} %add_add_fusion), channel_id=1, source_target_pairs={{0,256},{64,320},{128,384},{192,448},{256,0},{320,64},{384,128},{4... | collective-permute-start | bytes 196616 | tf_op jit(solution)/shard_map/ppermute | solution.py:178
  149.7 5.1 %collective-permute-done.6 = f32[64,1536]{1,0:T(8,128)S(1)} collective-permute-done((f32[64,1536]{1,0:T(8,128)S(1)}, f32[64,1536]{1,0:T(8,128)S(1)}, u32[]{:S(2)}, u32[]{:S(2)}) %collective-permute-start.6) | collective-permute-done | bytes 393248 | tf_op jit(solution)/shard_map/ppermute | solution.py:158
  154.9 2.9 %collective-permute-done.4 = f32[64,256]{1,0:T(8,128)S(1)} collective-permute-done((f32[64,256]{1,0:T(8,128)S(1)}, f32[64,256]{1,0:T(8,128)S(1)}, u32[]{:S(2)}, u32[]{:S(2)}) %collective-permute-start.4) | collective-permute-done | bytes 65568 | tf_op jit(solution)/shard_map/ppermute | solution.py:178
  160.4 2.8 %collective-permute-start.9 = (f32[64,256]{1,0:T(8,128)S(1)}, f32[64,256]{1,0:T(8,128)S(1)}, u32[]{:S(2)}, u32[]{:S(2)}) collective-permute-start(f32[64,256]{1,0:T(8,128)S(1)} %get-tuple-element.26), channel_id=1, source_target_pairs={{0,192},{64,128},{128,64},{192,0},{256,448},{320,384},{384,320},{4... | collective-permute-start | bytes 196616 | tf_op jit(solution)/shard_map/ppermute | solution.py:170
  163.2 4.5 %collective-permute-start.10 = (f32[64,256]{1,0:T(8,128)S(1)}, f32[64,256]{1,0:T(8,128)S(1)}, u32[]{:S(2)}, u32[]{:S(2)}) collective-permute-start(f32[64,256]{1,0:T(8,128)S(1)} %get-tuple-element.26), channel_id=1, source_target_pairs={{0,128},{64,192},{128,0},{192,64},{256,384},{320,448},{384,256},{4... | collective-permute-start | bytes 196616 | tf_op jit(solution)/shard_map/ppermute | solution.py:170
  167.7 7.7 %collective-permute-start.11 = (f32[64,1536]{1,0:T(8,128)S(1)}, f32[64,1536]{1,0:T(8,128)S(1)}, u32[]{:S(2)}, u32[]{:S(2)}) collective-permute-start(f32[64,1536]{1,0:T(8,128)S(1)} %fusion.3), channel_id=1, source_target_pairs={{0,256},{64,320},{128,384},{192,448},{256,0},{320,64},{384,128},{4... | collective-permute-start | bytes 1179656 | tf_op jit(solution)/shard_map/ppermute | solution.py:179
  175.5 16.7 %inverse_factor.1 = f32[256,256]{1,0:T(8,128)S(1)} custom-call(f32[256,256]{1,0:T(8,128)S(1)} %bitcast.73), custom_call_target="tpu_custom_call" | custom-call | flops 1000000000 | bytes 524288 | tf_op jit(solution)/shard_map/inverse_factor/pallas_call | solution.py:87
  192.2 16.9 %collective-permute-done.11 = f32[64,1536]{1,0:T(8,128)S(1)} collective-permute-done((f32[64,1536]{1,0:T(8,128)S(1)}, f32[64,1536]{1,0:T(8,128)S(1)}, u32[]{:S(2)}, u32[]{:S(2)}) %collective-permute-start.11) | collective-permute-done | bytes 393248 | tf_op jit(solution)/shard_map/ppermute | solution.py:179
  211.9 2.9 %collective-permute-start.13 = (f32[64,1536]{1,0:T(8,128)S(1)}, f32[64,1536]{1,0:T(8,128)S(1)}, u32[]{:S(2)}, u32[]{:S(2)}) collective-permute-start(f32[64,1536]{1,0:T(8,128)S(1)} %get-tuple-element.24), channel_id=1, source_target_pairs={{0,192},{64,128},{128,64},{192,0},{256,448},{320,384},{384,320},{4... | collective-permute-start | bytes 1179656 | tf_op jit(solution)/shard_map/ppermute | solution.py:170
  214.8 4.4 %collective-permute-start.14 = (f32[64,1536]{1,0:T(8,128)S(1)}, f32[64,1536]{1,0:T(8,128)S(1)}, u32[]{:S(2)}, u32[]{:S(2)}) collective-permute-start(f32[64,1536]{1,0:T(8,128)S(1)} %get-tuple-element.24), channel_id=1, source_target_pairs={{0,128},{64,192},{128,0},{192,64},{256,384},{320,448},{384,256},{4... | collective-permute-start | bytes 1179656 | tf_op jit(solution)/shard_map/ppermute | solution.py:170
  223.3 10.8 %collective-permute-done.13 = f32[64,1536]{1,0:T(8,128)S(1)} collective-permute-done((f32[64,1536]{1,0:T(8,128)S(1)}, f32[64,1536]{1,0:T(8,128)S(1)}, u32[]{:S(2)}, u32[]{:S(2)}) %collective-permute-start.13) | collective-permute-done | bytes 393248 | tf_op jit(solution)/shard_map/ppermute | solution.py:170
  234.2 2.6 %convolution_bitcast_fusion = f32[1,256,1536]{2,1,0:T(8,128)} fusion(f32[256,256]{1,0:T(8,128)S(1)} %inverse_factor.1, f32[256,1536]{1,0:T(8,128)S(1)} %bitcast.79), kind=kOutput, calls=%fused_computation.2 | convolution fusion | flops 1207959552 | bytes 3407872 | tf_op jit(solution)/shard_map/dot_general | solution.py:187
  (63 shorter events, 24.8 us)
Async XLA Ops:
  0.6 59.9 %copy-start = (bf16[1536,256]{1,0:T(8,128)(2,1)S(1)}, bf16[1536,256]{1,0:T(8,128)(2,1)}, u32[]{:S(2)}) copy-start(bf16[1536,256]{1,0:T(8,128)(2,1)} %param.5) | copy-start | bytes 2359300
  60.6 0.6 copy-start.3
  103.4 4.9 %collective-permute-start = (bf16[4,64,2304]{2,1,0:T(8,128)(2,1)S(1)}, bf16[4,64,2304]{2,1,0:T(8,128)(2,1)}, u32[]{:S(2)}, u32[]{:S(2)}) collective-permute-start(bf16[4,64,2304]{2,1,0:T(8,128)(2,1)S(1)} %all_to_all.23), channel_id=1, source_target_pairs={{0,1},{1,0},{2,3},{3,2},{4,5},{5,4},{6,7},{7,6},{8,9},{9,8},{10,11... | collective-permute-start | bytes 3538952 | tf_op jit(solution)/shard_map/ppermute | solution.py:133
  110.1 1.4 copy-start.1
  112.7 1.7 copy-start.2
  116.4 10.4 %collective-permute-start.1 = (f32[64,256]{1,0:T(8,128)S(1)}, f32[64,256]{1,0:T(8,128)S(1)}, u32[]{:S(2)}, u32[]{:S(2)}) collective-permute-start(f32[64,256]{1,0:T(8,128)S(1)} %get-tuple-element.40), channel_id=1, source_target_pairs={{0,64},{64,0},{128,192},{192,128},{256,320},{320,256},{384,448},{4... | collective-permute-start | bytes 196616 | tf_op jit(solution)/shard_map/ppermute | solution.py:158
  119.9 7.4 %collective-permute-start.2 = (f32[64,256]{1,0:T(8,128)S(1)}, f32[64,256]{1,0:T(8,128)S(1)}, u32[]{:S(2)}, u32[]{:S(2)}) collective-permute-start(f32[64,256]{1,0:T(8,128)S(1)} %get-tuple-element.39), channel_id=1, source_target_pairs={{0,192},{64,128},{128,64},{192,0},{256,448},{320,384},{384,320},{4... | collective-permute-start | bytes 196616 | tf_op jit(solution)/shard_map/ppermute | solution.py:158
  123.9 7.7 %collective-permute-start.3 = (f32[64,256]{1,0:T(8,128)S(1)}, f32[64,256]{1,0:T(8,128)S(1)}, u32[]{:S(2)}, u32[]{:S(2)}) collective-permute-start(f32[64,256]{1,0:T(8,128)S(1)} %get-tuple-element.38), channel_id=1, source_target_pairs={{0,128},{64,192},{128,0},{192,64},{256,384},{320,448},{384,256},{4... | collective-permute-start | bytes 196616 | tf_op jit(solution)/shard_map/ppermute | solution.py:158
  131.6 18.1 %collective-permute-start.5 = (f32[64,1536]{1,0:T(8,128)S(1)}, f32[64,1536]{1,0:T(8,128)S(1)}, u32[]{:S(2)}, u32[]{:S(2)}) collective-permute-start(f32[64,1536]{1,0:T(8,128)S(1)} %get-tuple-element.32), channel_id=1, source_target_pairs={{0,64},{64,0},{128,192},{192,128},{256,320},{320,256},{384,448},{4... | collective-permute-start | bytes 1179656 | tf_op jit(solution)/shard_map/ppermute | solution.py:158
  134.1 20.7 %collective-permute-start.6 = (f32[64,1536]{1,0:T(8,128)S(1)}, f32[64,1536]{1,0:T(8,128)S(1)}, u32[]{:S(2)}, u32[]{:S(2)}) collective-permute-start(f32[64,1536]{1,0:T(8,128)S(1)} %get-tuple-element.34), channel_id=1, source_target_pairs={{0,192},{64,128},{128,64},{192,0},{256,448},{320,384},{384,320},{4... | collective-permute-start | bytes 1179656 | tf_op jit(solution)/shard_map/ppermute | solution.py:158
  136.7 18.2 %collective-permute-start.7 = (f32[64,1536]{1,0:T(8,128)S(1)}, f32[64,1536]{1,0:T(8,128)S(1)}, u32[]{:S(2)}, u32[]{:S(2)}) collective-permute-start(f32[64,1536]{1,0:T(8,128)S(1)} %get-tuple-element.33), channel_id=1, source_target_pairs={{0,128},{64,192},{128,0},{192,64},{256,384},{320,448},{384,256},{4... | collective-permute-start | bytes 1179656 | tf_op jit(solution)/shard_map/ppermute | solution.py:158
  141.5 16.3 %collective-permute-start.4 = (f32[64,256]{1,0:T(8,128)S(1)}, f32[64,256]{1,0:T(8,128)S(1)}, u32[]{:S(2)}, u32[]{:S(2)}) collective-permute-start(f32[64,256]{1,0:T(8,128)S(1)} %add_add_fusion), channel_id=1, source_target_pairs={{0,256},{64,320},{128,384},{192,448},{256,0},{320,64},{384,128},{4... | collective-permute-start | bytes 196616 | tf_op jit(solution)/shard_map/ppermute | solution.py:178
  157.8 17.6 %collective-permute-start.8 = (f32[64,256]{1,0:T(8,128)S(1)}, f32[64,256]{1,0:T(8,128)S(1)}, u32[]{:S(2)}, u32[]{:S(2)}) collective-permute-start(f32[64,256]{1,0:T(8,128)S(1)} %get-tuple-element.26), channel_id=1, source_target_pairs={{0,64},{64,0},{128,192},{192,128},{256,320},{320,256},{384,448},{4... | collective-permute-start | bytes 196616 | tf_op jit(solution)/shard_map/ppermute | solution.py:170
  160.4 15.1 %collective-permute-start.9 = (f32[64,256]{1,0:T(8,128)S(1)}, f32[64,256]{1,0:T(8,128)S(1)}, u32[]{:S(2)}, u32[]{:S(2)}) collective-permute-start(f32[64,256]{1,0:T(8,128)S(1)} %get-tuple-element.26), channel_id=1, source_target_pairs={{0,192},{64,128},{128,64},{192,0},{256,448},{320,384},{384,320},{4... | collective-permute-start | bytes 196616 | tf_op jit(solution)/shard_map/ppermute | solution.py:170
  163.2 12.3 %collective-permute-start.10 = (f32[64,256]{1,0:T(8,128)S(1)}, f32[64,256]{1,0:T(8,128)S(1)}, u32[]{:S(2)}, u32[]{:S(2)}) collective-permute-start(f32[64,256]{1,0:T(8,128)S(1)} %get-tuple-element.26), channel_id=1, source_target_pairs={{0,128},{64,192},{128,0},{192,64},{256,384},{320,448},{384,256},{4... | collective-permute-start | bytes 196616 | tf_op jit(solution)/shard_map/ppermute | solution.py:170
  167.7 41.4 %collective-permute-start.11 = (f32[64,1536]{1,0:T(8,128)S(1)}, f32[64,1536]{1,0:T(8,128)S(1)}, u32[]{:S(2)}, u32[]{:S(2)}) collective-permute-start(f32[64,1536]{1,0:T(8,128)S(1)} %fusion.3), channel_id=1, source_target_pairs={{0,256},{64,320},{128,384},{192,448},{256,0},{320,64},{384,128},{4... | collective-permute-start | bytes 1179656 | tf_op jit(solution)/shard_map/ppermute | solution.py:179
  209.3 13.9 %collective-permute-start.12 = (f32[64,1536]{1,0:T(8,128)S(1)}, f32[64,1536]{1,0:T(8,128)S(1)}, u32[]{:S(2)}, u32[]{:S(2)}) collective-permute-start(f32[64,1536]{1,0:T(8,128)S(1)} %get-tuple-element.24), channel_id=1, source_target_pairs={{0,64},{64,0},{128,192},{192,128},{256,320},{320,256},{384,448},{4... | collective-permute-start | bytes 1179656 | tf_op jit(solution)/shard_map/ppermute | solution.py:170
  211.9 22.2 %collective-permute-start.13 = (f32[64,1536]{1,0:T(8,128)S(1)}, f32[64,1536]{1,0:T(8,128)S(1)}, u32[]{:S(2)}, u32[]{:S(2)}) collective-permute-start(f32[64,1536]{1,0:T(8,128)S(1)} %get-tuple-element.24), channel_id=1, source_target_pairs={{0,192},{64,128},{128,64},{192,0},{256,448},{320,384},{384,320},{4... | collective-permute-start | bytes 1179656 | tf_op jit(solution)/shard_map/ppermute | solution.py:170
  214.8 19.3 %collective-permute-start.14 = (f32[64,1536]{1,0:T(8,128)S(1)}, f32[64,1536]{1,0:T(8,128)S(1)}, u32[]{:S(2)}, u32[]{:S(2)}) collective-permute-start(f32[64,1536]{1,0:T(8,128)S(1)} %get-tuple-element.24), channel_id=1, source_target_pairs={{0,128},{64,192},{128,0},{192,64},{256,384},{320,448},{384,256},{4... | collective-permute-start | bytes 1179656 | tf_op jit(solution)/shard_map/ppermute | solution.py:170

commit v4 on v3

v4 whole, which is shorter than its diff:
```python
import math

import jax
import jax.numpy as jnp
from jax import lax
from jax.experimental import pallas as pl
from jax.experimental.pallas import tpu as pltpu
from jax.sharding import PartitionSpec as P

F32, BF16 = jnp.float32, jnp.bfloat16
HIGHEST = lax.Precision.HIGHEST
MIB = 2**20

YN, FN, NN, CN, XN = 4, 4, 2, 2, 4


def at(y, far, near, core):
    return y * 16 + (2 * far + near) * 2 + core


CYN_GROUPS = [
    [at(y, f, n, c) for c in range(CN) for y in range(YN) for n in range(NN)] for f in range(FN)
]
YN_GROUPS = [
    [at(y, f, n, c) for y in range(YN) for n in range(NN)] for f in range(FN) for c in range(CN)
]
FAR_GROUPS = [
    [at(y, f, n, c) for f in range(FN)]
    for y in range(YN) for n in range(NN) for c in range(CN)
]
OTHER_CORE = [(i, i ^ 1) for i in range(64)]
OTHER_HALF = [(i, i ^ 4) for i in range(8)]
ALONG_X = [[(i, i ^ k) for i in range(8)] for k in range(XN)]

PANEL = 64


def parts_of(value):
    first = lax.reduce_precision(value, 8, 7)
    rest = value - first
    second = lax.reduce_precision(rest, 8, 7)
    return [first.astype(BF16), second.astype(BF16), (rest - second).astype(BF16)]


def eye(n):
    row, col = (lax.broadcasted_iota(jnp.int32, (n, n), d) for d in (0, 1))
    return jnp.where(row == col, 1.0, 0.0).astype(F32)


def inverse_root(value):
    guess = lax.rsqrt(value)
    return guess * (1.5 - 0.5 * value * guess * guess)


def inverse_factor_of_panel(square):
    n = square.shape[0]
    work = jnp.concatenate([square, eye(n)], axis=1)
    row = lax.broadcasted_iota(jnp.int32, work.shape, 0)
    for j in range(0, n, 2):
        left = jnp.broadcast_to(work[:, j : j + 1], work.shape)
        right = jnp.broadcast_to(work[:, j + 1 : j + 2], work.shape)
        scale = inverse_root(left[j : j + 1])
        cross = left[j + 1 : j + 2] * scale
        scale_next = inverse_root(right[j + 1 : j + 2] - cross * cross)
        top = work[j : j + 1] * scale
        low = (work[j + 1 : j + 2] - cross * top) * scale_next
        left = left * scale
        right = (right - left * cross) * scale_next
        rest = jnp.where(row > j + 1, work - left * top - right * low, work)
        work = jnp.where(row == j, top, jnp.where(row == j + 1, low, rest))
    return work[:, n:]


def inverse_factor_kernel(place_ref, own_ref, *refs):
    came_refs, inverse_ref, work_ref = refs[:-2], refs[-2], refs[-1]
    n = inverse_ref.shape[0]
    block = own_ref.shape[0]
    for k, ref in enumerate((own_ref,) + came_refs):
        start = pl.multiple_of((place_ref[0] ^ k) * block, block)
        work_ref[pl.ds(start, block), :n] = ref[...]
    work_ref[:, n:] = eye(n)
    for top in range(0, n, PANEL):
        end = top + PANEL
        own = inverse_factor_of_panel(work_ref[top:end, top:end])
        done = jnp.dot(own, work_ref[top:end], precision=HIGHEST, preferred_element_type=F32)
        inverse_ref[top:end] = done[:, n:]
        if end < n:
            below = lax.dot_general(
                work_ref[end:, top:end], own, (((1,), (1,)), ((), ())),
                precision=HIGHEST, preferred_element_type=F32,
            )
            work_ref[end:] = work_ref[end:] - jnp.dot(
                below, done, precision=HIGHEST, preferred_element_type=F32
            )


VMEM = pl.BlockSpec(memory_space=pltpu.VMEM)
SMEM = pl.BlockSpec(memory_space=pltpu.SMEM)


def inverse_factor(place, blocks):
    n = blocks[0].shape[1]
    return pl.pallas_call(
        inverse_factor_kernel,
        out_shape=jax.ShapeDtypeStruct((n, n), F32),
        in_specs=[SMEM] + [VMEM] * len(blocks),
        out_specs=VMEM,
        scratch_shapes=[pltpu.VMEM((n, 2 * n), F32)],
        compiler_params=pltpu.CompilerParams(vmem_limit_bytes=16 * MIB),
        cost_estimate=pl.CostEstimate(flops=2**20, bytes_accessed=2**19, transcendentals=0),
        name="inverse_factor",
    )(place, *blocks)


def products_kernel(place_ref, mine_ref, other_ref, own_ref, sketch_ref, both_ref, range_ref):
    half, wide = mine_ref.shape
    ff, rank = sketch_ref.shape
    block = rank // XN
    core, x = place_ref[0], place_ref[1]
    gram = jnp.zeros((rank, rank), F32)
    delta = jnp.zeros((rank, ff), F32)
    for load_ref, at_core in ((mine_ref, core), (other_ref, 1 - core)):
        rows = pl.ds(pl.multiple_of(at_core * half, half), half)
        own = own_ref[rows, :]
        base_sketch = (
            load_ref[:, ff : ff + rank].astype(F32)
            + load_ref[:, ff + rank : ff + 2 * rank].astype(F32)
            + load_ref[:, ff + 2 * rank :].astype(F32)
        )
        range_rows = jnp.dot(own, sketch_ref[...], preferred_element_type=F32) - base_sketch
        range_ref[rows, :] = range_rows
        turned = range_rows.T
        gram += jnp.dot(turned, range_rows, precision=HIGHEST, preferred_element_type=F32)
        base = load_ref[:, :ff]
        for step in range(3):
            part = turned.astype(BF16)
            turned = turned - part.astype(F32)
            delta += jnp.dot(part, own, preferred_element_type=F32)
            delta -= jnp.dot(part, base, preferred_element_type=F32)
    for b in range(XN):
        both_ref[b ^ x, :, :rank] = gram[b * block : (b + 1) * block]
        both_ref[b ^ x, :, rank:] = delta[b * block : (b + 1) * block]


def products(place, mine, other, own, sketch):
    rows, ff = own.shape
    rank = sketch.shape[1]
    return pl.pallas_call(
        products_kernel,
        out_shape=(
            jax.ShapeDtypeStruct((XN, rank // XN, rank + ff), F32),
            jax.ShapeDtypeStruct((rows, rank), F32),
        ),
        in_specs=[SMEM] + [VMEM] * 4,
        out_specs=(VMEM, VMEM),
        compiler_params=pltpu.CompilerParams(vmem_limit_bytes=40 * MIB),
        cost_estimate=pl.CostEstimate(flops=4 * 10**9, bytes_accessed=8 * MIB, transcendentals=0),
        name="products",
    )(place, mine, other, own, sketch)


def per_device(counts, up_weights, sketch):
    rows, ff = up_weights.shape[1:]
    rank = sketch.shape[1]
    piece = rows // 64
    own = up_weights[0].reshape(YN, FN, NN, CN, piece, ff).transpose(3, 0, 2, 1, 4, 5)
    members = CN * YN * NN
    own = own.reshape(members, FN * piece, ff)

    lane = lax.broadcasted_iota(jnp.int32, (members, FN * piece, 128), 2)
    count = counts[0]
    tag = jnp.where(lane == 0, count // 64, jnp.where(lane == 1, count % 64, 0)).astype(BF16)
    got = lax.all_to_all(
        jnp.concatenate([own, tag], axis=2), "exp", 0, 0, axis_index_groups=CYN_GROUPS
    )
    freq = got[:, 0, ff].astype(F32) * 64 + got[:, 0, ff + 1].astype(F32)
    weighted = jnp.sum(freq[:, None, None] * got[:, :, :ff].astype(F32), axis=0)
    freq_sum = jnp.broadcast_to(jnp.sum(freq), (FN, piece, 128))

    sums = lax.all_to_all(
        jnp.concatenate([weighted.reshape(FN, piece, ff), freq_sum], axis=2),
        "exp", 0, 0, axis_index_groups=FAR_GROUPS,
    )
    sums = jnp.sum(sums, axis=0)
    base_rows = sums[:, :ff] / sums[:, ff : ff + 1]
    base_piece = base_rows.astype(BF16)
    sketched = jnp.dot(base_rows, sketch.astype(F32), precision=HIGHEST)

    wide = ff + 3 * rank
    load = jnp.concatenate([base_piece] + parts_of(sketched), axis=1)
    load = lax.all_to_all(
        jnp.broadcast_to(load, (FN, piece, wide)), "exp", 0, 0, axis_index_groups=FAR_GROUPS
    ).reshape(FN * piece, wide)
    load = lax.all_to_all(
        jnp.broadcast_to(load, (YN * NN, FN * piece, wide)),
        "exp", 0, 0, axis_index_groups=YN_GROUPS,
    ).reshape(rows // CN, wide)
    other = lax.ppermute(load, "exp", OTHER_CORE)

    at_core, at_x = lax.axis_index("exp") % CN, lax.axis_index("grp") % XN
    both, range_rows = products(
        jnp.stack([at_core, at_x]), load, other, own.reshape(rows, ff), sketch
    )

    both = both[0] + sum(lax.ppermute(both[k], "grp", ALONG_X[k]) for k in (1, 2, 3))
    gram, delta = both[:, :rank], both[:, rank:]
    gram = gram + lax.ppermute(gram, "grp", OTHER_HALF)
    delta_came = lax.ppermute(delta, "grp", OTHER_HALF)
    inverse = inverse_factor(
        at_x.reshape(1), [gram] + [lax.ppermute(gram, "grp", ALONG_X[k]) for k in (1, 2, 3)]
    )
    inverse, delta_came = lax.optimization_barrier((inverse, delta_came))
    delta = delta + delta_came
    whole = jnp.zeros((XN,) + delta.shape, F32)
    whole = lax.dynamic_update_slice(whole, delta[None], (at_x, 0, 0))
    for k in (1, 2, 3):
        came = lax.ppermute(delta, "grp", ALONG_X[k])
        whole = lax.dynamic_update_slice(whole, came[None], (at_x ^ k, 0, 0))
    coeff = jnp.dot(inverse, whole.reshape(rank, ff), precision=HIGHEST)

    ortho = lax.dot_general(
        range_rows, inverse, (((1,), (1,)), ((), ())), precision=HIGHEST
    )
    basis = ortho * math.sqrt(rows * lax.axis_size("grp"))
    basis = basis.reshape(CN, YN, NN, FN, piece, rank).transpose(1, 3, 2, 0, 4, 5)
    return (base_piece, basis.reshape(1, rows, rank), coeff[None])


def solution(mesh):
    placed = (P("exp"), P("exp", "grp", None), P())
    return jax.shard_map(
        per_device,
        mesh=mesh,
        in_specs=placed,
        out_specs=(P(("grp", "exp"), None), P("exp", "grp", None), P("exp", None, None)),
        check_vma=False,
    )
```

time: 238 us -> 252 us (1.059)
  the two profiles are of different devices: /device:TPU:192 before, /device:TPU:32 now
where the time goes in v4:
time: 252 us; the launch traced here: 251 us
  blocking collectives  88.7 us (35%)
  waiting for transfers between devices  80.4 us (32%)
  starting transfers between devices  47.9 us (19%)
  Pallas kernels  22.4 us (9%)
  local copies, waits for them, and re-layouts  3.85 us (2%)
  matrix products  3.67 us (1%)
  other arithmetic  2.71 us (1%)
    ppermute x1, waiting for transfers between devices, per_device(): gram = gram + lax.ppermute(gram, 'grp', OTHER_HALF)  36.8 us
    all_to_all x1, blocking collectives, per_device(): lax.all_to_all(jnp.concatenate([own, tag], axis=2), 'exp', 0, 0, axis_ind...  30.3 us
    ppermute x3, waiting for transfers between devices, per_device(): lax.ppermute(both[k], 'grp', ALONG_X[k])  22.5 us
    all_to_all x1, blocking collectives, per_device(): lax.all_to_all(jnp.broadcast_to(load, (YN * NN, FN * piece, wide)), 'exp'...  20.4 us
    all_to_all x1, blocking collectives, per_device(): lax.all_to_all(jnp.concatenate([weighted.reshape(FN, piece, ff), freq_sum...  20 us
    all_to_all x1, blocking collectives, per_device(): lax.all_to_all(jnp.broadcast_to(load, (FN, piece, wide)), 'exp', 0, 0, ax...  18 us
    pallas_call x1, Pallas kernels, inverse_factor(): pl.pallas_call(inverse_factor_kernel, out_shape=jax.ShapeDtypeStruct((n,...  16.8 us
    ppermute x3, waiting for transfers between devices, per_device(): came = lax.ppermute(delta, 'grp', ALONG_X[k])  15.6 us
  transfers between devices with their start and end apart: 12, of which 9 were waited for; matrix products, arithmetic and copies ran while one was open for 1% of the time, Pallas kernels for 7%

profile of v4, /device:TPU:32, one launch (start us, length us, event | category | flops | bytes accessed | tf_op | source)
XLA Modules:
  0.0 251.4 jit_solution(2134373260514769456)
XLA Ops:
  3.1 30.3 %all_to_all.20 = bf16[16,32,1664]{2,1,0:T(8,128)(2,1)S(1)} all-to-all(bf16[16,32,1664]{2,1,0:T(8,128)(2,1)S(1)} %pad_maximum_fusion), channel_id=1, replica_groups={{0,2,16,18,32,34,48,50,1,3,17,19,33,35,49,51},{4,6,20,22,36,38,52,54,5,..., dimensions={0} | all-to-all | bytes 3407872 | tf_op jit(solution)/shard_map/all_to_all | solution.py:173
  35.3 20.0 %all_to_all.21 = f32[4,8,1664]{2,1,0:T(8,128)S(1)} all-to-all(f32[4,8,1664]{2,1,0:T(8,128)S(1)} %concatenate.10), channel_id=1, replica_groups={{0,4,8,12},{1,5,9,13},{2,6,10,14},{3,7,11,15},{16,20,24,28},{17,21,25,2..., dimensions={0} | all-to-all | bytes 425984 | tf_op jit(solution)/shard_map/all_to_all | solution.py:180
  56.1 18.0 %all_to_all.22 = bf16[4,8,2304]{2,1,0:T(8,128)(2,1)S(1)} all-to-all(bf16[4,8,2304]{2,1,0:T(8,128)(2,1)S(1)} %broadcast_in_dim.38), channel_id=1, replica_groups={{0,4,8,12},{1,5,9,13},{2,6,10,14},{3,7,11,15},{16,20,24,28},{17,21,25,2..., dimensions={0} | all-to-all | bytes 294912 | tf_op jit(solution)/shard_map/all_to_all | solution.py:191
  74.2 20.4 %all_to_all.23 = bf16[8,32,2304]{2,1,0:T(8,128)(2,1)S(1)} all-to-all(bf16[8,32,2304]{2,1,0:T(8,128)(2,1)S(1)} %broadcast_in_dim.39), channel_id=1, replica_groups={{0,2,16,18,32,34,48,50},{1,3,17,19,33,35,49,51},{4,6,20,22,36,38,52,54}..., dimensions={0} | all-to-all | bytes 2359296 | tf_op jit(solution)/shard_map/all_to_all | solution.py:194
  96.7 2.8 %collective-permute-done.other_ref = bf16[256,2304]{1,0:T(8,128)(2,1)} collective-permute-done((bf16[256,2304]{1,0:T(8,128)(2,1)S(1)}, bf16[256,2304]{1,0:T(8,128)(2,1)}, u32[]{:S(2)}, u32[]{:S(2)}) %collective-permute-start) | collective-permute-done | bytes 1179680 | tf_op jit(solution)/shard_map/ppermute | solution.py:198
  99.5 5.7 %products.1 = (f32[4,64,1792]{2,1,0:T(8,128)S(1)}, f32[512,256]{1,0:T(8,128)S(1)}) custom-call(s32[2]{0:T(128)S(1)} %pad_add_fusion.place_ref, bf16[256,2304]{1,0:T(8,128)(2,1)S(1)} %bitcast.46, bf16[256,2304]{1,0:T(8,128)(2,1)} %collective-permute-done.other_ref, bf16[512,1536]{1,0:T(8,128)(2,1)S(1)} %bitcast.44, bf16[1536,256]{1,0:T(8,128)(2,1)S(1)} %copy-done), custom_call_target="tpu_custom_call" | custom-call | flops 4000000000 | bytes 8388608 | tf_op jit(solution)/shard_map/products/pallas_call | solution.py:148
  105.3 3.4 %collective-permute-start.1 = (f32[64,1792]{1,0:T(8,128)S(1)}, f32[64,1792]{1,0:T(8,128)S(1)}, u32[]{:S(2)}, u32[]{:S(2)}) collective-permute-start(f32[64,1792]{1,0:T(8,128)S(1)} %get-tuple-element.17), channel_id=1, source_target_pairs={{0,64},{64,0},{128,192},{192,128},{256,320},{320,256},{384,448},{4... | collective-permute-start | bytes 1376264 | tf_op jit(solution)/shard_map/ppermute | solution.py:205
  108.7 4.6 %collective-permute-start.2 = (f32[64,1792]{1,0:T(8,128)S(1)}, f32[64,1792]{1,0:T(8,128)S(1)}, u32[]{:S(2)}, u32[]{:S(2)}) collective-permute-start(f32[64,1792]{1,0:T(8,128)S(1)} %get-tuple-element.15), channel_id=1, source_target_pairs={{0,128},{64,192},{128,0},{192,64},{256,384},{320,448},{384,256},{4... | collective-permute-start | bytes 1376264 | tf_op jit(solution)/shard_map/ppermute | solution.py:205
  113.4 2.4 collective-permute-start.3
  115.7 4.8 %collective-permute-done.1 = f32[64,1792]{1,0:T(8,128)S(1)} collective-permute-done((f32[64,1792]{1,0:T(8,128)S(1)}, f32[64,1792]{1,0:T(8,128)S(1)}, u32[]{:S(2)}, u32[]{:S(2)}) %collective-permute-start.1) | collective-permute-done | bytes 458784 | tf_op jit(solution)/shard_map/ppermute | solution.py:205
  120.6 11.3 %collective-permute-done.2 = f32[64,1792]{1,0:T(8,128)S(1)} collective-permute-done((f32[64,1792]{1,0:T(8,128)S(1)}, f32[64,1792]{1,0:T(8,128)S(1)}, u32[]{:S(2)}, u32[]{:S(2)}) %collective-permute-start.2) | collective-permute-done | bytes 458784 | tf_op jit(solution)/shard_map/ppermute | solution.py:205
  131.9 6.4 %collective-permute-done.3 = f32[64,1792]{1,0:T(8,128)S(1)} collective-permute-done((f32[64,1792]{1,0:T(8,128)S(1)}, f32[64,1792]{1,0:T(8,128)S(1)}, u32[]{:S(2)}, u32[]{:S(2)}) %collective-permute-start.3) | collective-permute-done | bytes 458784 | tf_op jit(solution)/shard_map/ppermute | solution.py:205
  138.4 8.2 %collective-permute-start.8 = (f32[64,1536]{1,0:T(8,128)S(1)}, f32[64,1536]{1,0:T(8,128)}, u32[]{:S(2)}, u32[]{:S(2)}) collective-permute-start(f32[64,1536]{1,0:T(8,128)S(1)} %slice.50), channel_id=1, source_target_pairs={{0,256},{64,320},{128,384},{192,448},{256,0},{320,64},{384,128},{4... | collective-permute-start | bytes 1179656 | tf_op jit(solution)/shard_map/ppermute | solution.py:208
  146.7 6.3 %collective-permute-start.4 = (f32[64,256]{1,0:T(8,128)S(1)}, f32[64,256]{1,0:T(8,128)S(1)}, u32[]{:S(2)}, u32[]{:S(2)}) collective-permute-start(f32[64,256]{1,0:T(8,128)S(1)} %slice.49), channel_id=1, source_target_pairs={{0,256},{64,320},{128,384},{192,448},{256,0},{320,64},{384,128},{4... | collective-permute-start | bytes 196616 | tf_op jit(solution)/shard_map/ppermute | solution.py:207
  153.0 36.8 %collective-permute-done.4 = f32[64,256]{1,0:T(8,128)S(1)} collective-permute-done((f32[64,256]{1,0:T(8,128)S(1)}, f32[64,256]{1,0:T(8,128)S(1)}, u32[]{:S(2)}, u32[]{:S(2)}) %collective-permute-start.4) | collective-permute-done | bytes 65568 | tf_op jit(solution)/shard_map/ppermute | solution.py:207
  191.8 3.8 %collective-permute-start.6 = (f32[64,256]{1,0:T(8,128)S(1)}, f32[64,256]{1,0:T(8,128)S(1)}, u32[]{:S(2)}, u32[]{:S(2)}) collective-permute-start(f32[64,256]{1,0:T(8,128)S(1)} %slice_add_fusion.own_ref), channel_id=1, source_target_pairs={{0,128},{64,192},{128,0},{192,64},{256,384},{320,448},{384,256},{4... | collective-permute-start | bytes 196616 | tf_op jit(solution)/shard_map/ppermute | solution.py:210
  195.6 4.8 %collective-permute-start.7 = (f32[64,256]{1,0:T(8,128)S(1)}, f32[64,256]{1,0:T(8,128)S(1)}, u32[]{:S(2)}, u32[]{:S(2)}) collective-permute-start(f32[64,256]{1,0:T(8,128)S(1)} %slice_add_fusion.own_ref), channel_id=1, source_target_pairs={{0,192},{64,128},{128,64},{192,0},{256,448},{320,384},{384,320},{4... | collective-permute-start | bytes 196616 | tf_op jit(solution)/shard_map/ppermute | solution.py:210
  200.5 2.5 collective-permute-done.7.refs_2_
  203.0 16.8 %inverse_factor.1 = f32[256,256]{1,0:T(8,128)S(1)} custom-call(s32[1]{0:T(128)} %bitcast.6.place_ref, f32[64,256]{1,0:T(8,128)S(1)} %slice_add_fusion.own_ref, f32[64,256]{1,0:T(8,128)S(1)} %collective-permute-done.5.refs_0_, f32[64,256]{1,0:T(8,128)S(1)} %collective-permute-done.6.refs_1_, f32[64,256]{1,0:T(8,128)S(1)} %collective-permute-done.7.refs_2_), custom_call_target="tpu_custom_call" | custom-call | flops 1048576 | bytes 524288 | tf_op jit(solution)/shard_map/inverse_factor/pallas_call | solution.py:103
  223.0 6.1 %collective-permute-start.10 = (f32[64,1536]{1,0:T(8,128)S(1)}, f32[64,1536]{1,0:T(8,128)S(1)}, u32[]{:S(2)}, u32[]{:S(2)}) collective-permute-start(f32[64,1536]{1,0:T(8,128)S(1)} %get-tuple-element.14), channel_id=1, source_target_pairs={{0,128},{64,192},{128,0},{192,64},{256,384},{320,448},{384,256},{4... | collective-permute-start | bytes 1179656 | tf_op jit(solution)/shard_map/ppermute | solution.py:217
  229.1 2.4 collective-permute-start.11
  235.0 7.8 %collective-permute-done.10 = f32[64,1536]{1,0:T(8,128)S(1)} collective-permute-done((f32[64,1536]{1,0:T(8,128)S(1)}, f32[64,1536]{1,0:T(8,128)S(1)}, u32[]{:S(2)}, u32[]{:S(2)}) %collective-permute-start.10) | collective-permute-done | bytes 393248 | tf_op jit(solution)/shard_map/ppermute | solution.py:217
  242.9 5.9 %collective-permute-done.11 = f32[64,1536]{1,0:T(8,128)S(1)} collective-permute-done((f32[64,1536]{1,0:T(8,128)S(1)}, f32[64,1536]{1,0:T(8,128)S(1)}, u32[]{:S(2)}, u32[]{:S(2)}) %collective-permute-start.11) | collective-permute-done | bytes 393248 | tf_op jit(solution)/shard_map/ppermute | solution.py:217
  248.8 2.6 %convolution_bitcast_fusion = f32[1,256,1536]{2,1,0:T(8,128)} fusion(f32[256,256]{1,0:T(8,128)S(1)} %inverse_factor.1, f32[256,1536]{1,0:T(8,128)S(1)} %bitcast.47), kind=kOutput, calls=%fused_computation.1 | convolution fusion | flops 1207959552 | bytes 3407872 | tf_op jit(solution)/shard_map/dot_general | solution.py:219
  (43 shorter events, 15.4 us)
Async XLA Ops:
  33.4 22.1 %copy-start = (bf16[1536,256]{1,0:T(8,128)(2,1)S(1)}, bf16[1536,256]{1,0:T(8,128)(2,1)}, u32[]{:S(2)}) copy-start(bf16[1536,256]{1,0:T(8,128)(2,1)} %sketch_ref.1) | copy-start | bytes 2359300
  55.5 0.6 copy-start.3
  94.6 4.9 %collective-permute-start = (bf16[256,2304]{1,0:T(8,128)(2,1)S(1)}, bf16[256,2304]{1,0:T(8,128)(2,1)}, u32[]{:S(2)}, u32[]{:S(2)}) collective-permute-start(bf16[256,2304]{1,0:T(8,128)(2,1)S(1)} %bitcast.45), channel_id=1, source_target_pairs={{0,1},{1,0},{2,3},{3,2},{4,5},{5,4},{6,7},{7,6},{8,9},{9,8},{10,11... | collective-permute-start | bytes 3538952 | tf_op jit(solution)/shard_map/ppermute | solution.py:198
  105.2 33.2 %copy-start.1 = (f32[512,256]{1,0:T(8,128)}, f32[512,256]{1,0:T(8,128)S(1)}, u32[]{:S(2)}) copy-start(f32[512,256]{1,0:T(8,128)S(1)} %get-tuple-element.7) | copy-start | bytes 1572868
  105.3 15.3 %collective-permute-start.1 = (f32[64,1792]{1,0:T(8,128)S(1)}, f32[64,1792]{1,0:T(8,128)S(1)}, u32[]{:S(2)}, u32[]{:S(2)}) collective-permute-start(f32[64,1792]{1,0:T(8,128)S(1)} %get-tuple-element.17), channel_id=1, source_target_pairs={{0,64},{64,0},{128,192},{192,128},{256,320},{320,256},{384,448},{4... | collective-permute-start | bytes 1376264 | tf_op jit(solution)/shard_map/ppermute | solution.py:205
  108.7 23.2 %collective-permute-start.2 = (f32[64,1792]{1,0:T(8,128)S(1)}, f32[64,1792]{1,0:T(8,128)S(1)}, u32[]{:S(2)}, u32[]{:S(2)}) collective-permute-start(f32[64,1792]{1,0:T(8,128)S(1)} %get-tuple-element.15), channel_id=1, source_target_pairs={{0,128},{64,192},{128,0},{192,64},{256,384},{320,448},{384,256},{4... | collective-permute-start | bytes 1376264 | tf_op jit(solution)/shard_map/ppermute | solution.py:205
  113.4 24.9 %collective-permute-start.3 = (f32[64,1792]{1,0:T(8,128)S(1)}, f32[64,1792]{1,0:T(8,128)S(1)}, u32[]{:S(2)}, u32[]{:S(2)}) collective-permute-start(f32[64,1792]{1,0:T(8,128)S(1)} %get-tuple-element.16), channel_id=1, source_target_pairs={{0,192},{64,128},{128,64},{192,0},{256,448},{320,384},{384,320},{4... | collective-permute-start | bytes 1376264 | tf_op jit(solution)/shard_map/ppermute | solution.py:205
  138.4 81.4 %collective-permute-start.8 = (f32[64,1536]{1,0:T(8,128)S(1)}, f32[64,1536]{1,0:T(8,128)}, u32[]{:S(2)}, u32[]{:S(2)}) collective-permute-start(f32[64,1536]{1,0:T(8,128)S(1)} %slice.50), channel_id=1, source_target_pairs={{0,256},{64,320},{128,384},{192,448},{256,0},{320,64},{384,128},{4... | collective-permute-start | bytes 1179656 | tf_op jit(solution)/shard_map/ppermute | solution.py:208
  146.7 43.2 %collective-permute-start.4 = (f32[64,256]{1,0:T(8,128)S(1)}, f32[64,256]{1,0:T(8,128)S(1)}, u32[]{:S(2)}, u32[]{:S(2)}) collective-permute-start(f32[64,256]{1,0:T(8,128)S(1)} %slice.49), channel_id=1, source_target_pairs={{0,256},{64,320},{128,384},{192,448},{256,0},{320,64},{384,128},{4... | collective-permute-start | bytes 196616 | tf_op jit(solution)/shard_map/ppermute | solution.py:207
  189.8 10.6 %collective-permute-start.5 = (f32[64,256]{1,0:T(8,128)S(1)}, f32[64,256]{1,0:T(8,128)S(1)}, u32[]{:S(2)}, u32[]{:S(2)}) collective-permute-start(f32[64,256]{1,0:T(8,128)S(1)} %slice_add_fusion.own_ref), channel_id=1, source_target_pairs={{0,64},{64,0},{128,192},{192,128},{256,320},{320,256},{384,448},{4... | collective-permute-start | bytes 196616 | tf_op jit(solution)/shard_map/ppermute | solution.py:210
  191.8 8.7 %collective-permute-start.6 = (f32[64,256]{1,0:T(8,128)S(1)}, f32[64,256]{1,0:T(8,128)S(1)}, u32[]{:S(2)}, u32[]{:S(2)}) collective-permute-start(f32[64,256]{1,0:T(8,128)S(1)} %slice_add_fusion.own_ref), channel_id=1, source_target_pairs={{0,128},{64,192},{128,0},{192,64},{256,384},{320,448},{384,256},{4... | collective-permute-start | bytes 196616 | tf_op jit(solution)/shard_map/ppermute | solution.py:210
  195.6 7.4 %collective-permute-start.7 = (f32[64,256]{1,0:T(8,128)S(1)}, f32[64,256]{1,0:T(8,128)S(1)}, u32[]{:S(2)}, u32[]{:S(2)}) collective-permute-start(f32[64,256]{1,0:T(8,128)S(1)} %slice_add_fusion.own_ref), channel_id=1, source_target_pairs={{0,192},{64,128},{128,64},{192,0},{256,448},{320,384},{384,320},{4... | collective-permute-start | bytes 196616 | tf_op jit(solution)/shard_map/ppermute | solution.py:210
  219.8 11.7 %copy-start.2 = (f32[512,256]{1,0:T(8,128)S(1)}, f32[512,256]{1,0:T(8,128)}, u32[]{:S(2)}) copy-start(f32[512,256]{1,0:T(8,128)} %copy-done.1) | copy-start | bytes 1572868
  221.1 13.9 %collective-permute-start.9 = (f32[64,1536]{1,0:T(8,128)S(1)}, f32[64,1536]{1,0:T(8,128)S(1)}, u32[]{:S(2)}, u32[]{:S(2)}) collective-permute-start(f32[64,1536]{1,0:T(8,128)S(1)} %get-tuple-element.14), channel_id=1, source_target_pairs={{0,64},{64,0},{128,192},{192,128},{256,320},{320,256},{384,448},{4... | collective-permute-start | bytes 1179656 | tf_op jit(solution)/shard_map/ppermute | solution.py:217
  223.0 19.8 %collective-permute-start.10 = (f32[64,1536]{1,0:T(8,128)S(1)}, f32[64,1536]{1,0:T(8,128)S(1)}, u32[]{:S(2)}, u32[]{:S(2)}) collective-permute-start(f32[64,1536]{1,0:T(8,128)S(1)} %get-tuple-element.14), channel_id=1, source_target_pairs={{0,128},{64,192},{128,0},{192,64},{256,384},{320,448},{384,256},{4... | collective-permute-start | bytes 1179656 | tf_op jit(solution)/shard_map/ppermute | solution.py:217
  229.1 19.6 %collective-permute-start.11 = (f32[64,1536]{1,0:T(8,128)S(1)}, f32[64,1536]{1,0:T(8,128)S(1)}, u32[]{:S(2)}, u32[]{:S(2)}) collective-permute-start(f32[64,1536]{1,0:T(8,128)S(1)} %get-tuple-element.14), channel_id=1, source_target_pairs={{0,192},{64,128},{128,64},{192,0},{256,448},{320,384},{384,320},{4... | collective-permute-start | bytes 1179656 | tf_op jit(solution)/shard_map/ppermute | solution.py:217

commit v5 on v4

--- a/solution.py
+++ b/solution.py
@@ -107,7 +107,7 @@
         out_specs=VMEM,
         scratch_shapes=[pltpu.VMEM((n, 2 * n), F32)],
         compiler_params=pltpu.CompilerParams(vmem_limit_bytes=16 * MIB),
-        cost_estimate=pl.CostEstimate(flops=2**20, bytes_accessed=2**19, transcendentals=0),
+        cost_estimate=pl.CostEstimate(flops=2**29, bytes_accessed=2**10, transcendentals=0),
         name="inverse_factor",
     )(place, *blocks)
 
@@ -202,7 +202,7 @@
         jnp.stack([at_core, at_x]), load, other, own.reshape(rows, ff), sketch
     )
 
-    both = both[0] + sum(lax.ppermute(both[k], "grp", ALONG_X[k]) for k in (1, 2, 3))
+    both = both[0] + sum(lax.ppermute(both[k], "grp", ALONG_X[k]) for k in (2, 3, 1))
     gram, delta = both[:, :rank], both[:, rank:]
     gram = gram + lax.ppermute(gram, "grp", OTHER_HALF)
     delta_came = lax.ppermute(delta, "grp", OTHER_HALF)
@@ -213,7 +213,7 @@
     delta = delta + delta_came
     whole = jnp.zeros((XN,) + delta.shape, F32)
     whole = lax.dynamic_update_slice(whole, delta[None], (at_x, 0, 0))
-    for k in (1, 2, 3):
+    for k in (2, 3, 1):
         came = lax.ppermute(delta, "grp", ALONG_X[k])
         whole = lax.dynamic_update_slice(whole, came[None], (at_x ^ k, 0, 0))
     coeff = jnp.dot(inverse, whole.reshape(rank, ff), precision=HIGHEST)

time: 252 us -> 212 us (0.84)
  the two profiles are of different devices: /device:TPU:32 before, /device:TPU:101 now
where the time goes in v5:
time: 212 us; the launch traced here: 211 us
  blocking collectives  84.2 us (40%)
  waiting for transfers between devices  46.4 us (22%)
  starting transfers between devices  46.3 us (22%)
  Pallas kernels  22.5 us (11%)
  local copies, waits for them, and re-layouts  3.86 us (2%)
  matrix products  3.66 us (2%)
  other arithmetic  2.71 us (1%)
    all_to_all x1, blocking collectives, per_device(): lax.all_to_all(jnp.concatenate([own, tag], axis=2), 'exp', 0, 0, axis_ind...  28 us
    all_to_all x1, blocking collectives, per_device(): lax.all_to_all(jnp.broadcast_to(load, (YN * NN, FN * piece, wide)), 'exp'...  20 us
    all_to_all x1, blocking collectives, per_device(): lax.all_to_all(jnp.concatenate([weighted.reshape(FN, piece, ff), freq_sum...  19.5 us
    pallas_call x1, Pallas kernels, inverse_factor(): pl.pallas_call(inverse_factor_kernel, out_shape=jax.ShapeDtypeStruct((n,...  16.8 us
    all_to_all x1, blocking collectives, per_device(): lax.all_to_all(jnp.broadcast_to(load, (FN, piece, wide)), 'exp', 0, 0, ax...  16.7 us
    ppermute x3, waiting for transfers between devices, per_device(): lax.ppermute(both[k], 'grp', ALONG_X[k])  16.1 us
    ppermute x1, waiting for transfers between devices, per_device(): delta_came = lax.ppermute(delta, 'grp', OTHER_HALF)  13.7 us
    ppermute x3, waiting for transfers between devices, per_device(): came = lax.ppermute(delta, 'grp', ALONG_X[k])  11.7 us
  transfers between devices with their start and end apart: 12, of which 9 were waited for; matrix products, arithmetic and copies ran while one was open for 1% of the time, Pallas kernels for 8%

profile of v5, /device:TPU:101, one launch (start us, length us, event | category | flops | bytes accessed | tf_op | source)
XLA Modules:
  0.0 211.2 jit_solution(15432115628526584571)
XLA Ops:
  3.1 28.0 %all_to_all.20 = bf16[16,32,1664]{2,1,0:T(8,128)(2,1)S(1)} all-to-all(bf16[16,32,1664]{2,1,0:T(8,128)(2,1)S(1)} %pad_maximum_fusion), channel_id=1, replica_groups={{0,2,16,18,32,34,48,50,1,3,17,19,33,35,49,51},{4,6,20,22,36,38,52,54,5,..., dimensions={0} | all-to-all | bytes 3407872 | tf_op jit(solution)/shard_map/all_to_all | solution.py:173
  32.9 19.5 %all_to_all.21 = f32[4,8,1664]{2,1,0:T(8,128)S(1)} all-to-all(f32[4,8,1664]{2,1,0:T(8,128)S(1)} %concatenate.10), channel_id=1, replica_groups={{0,4,8,12},{1,5,9,13},{2,6,10,14},{3,7,11,15},{16,20,24,28},{17,21,25,2..., dimensions={0} | all-to-all | bytes 425984 | tf_op jit(solution)/shard_map/all_to_all | solution.py:180
  53.3 16.7 %all_to_all.22 = bf16[4,8,2304]{2,1,0:T(8,128)(2,1)S(1)} all-to-all(bf16[4,8,2304]{2,1,0:T(8,128)(2,1)S(1)} %broadcast_in_dim.38), channel_id=1, replica_groups={{0,4,8,12},{1,5,9,13},{2,6,10,14},{3,7,11,15},{16,20,24,28},{17,21,25,2..., dimensions={0} | all-to-all | bytes 294912 | tf_op jit(solution)/shard_map/all_to_all | solution.py:191
  70.1 20.0 %all_to_all.23 = bf16[8,32,2304]{2,1,0:T(8,128)(2,1)S(1)} all-to-all(bf16[8,32,2304]{2,1,0:T(8,128)(2,1)S(1)} %broadcast_in_dim.39), channel_id=1, replica_groups={{0,2,16,18,32,34,48,50},{1,3,17,19,33,35,49,51},{4,6,20,22,36,38,52,54}..., dimensions={0} | all-to-all | bytes 2359296 | tf_op jit(solution)/shard_map/all_to_all | solution.py:194
  90.1 4.6 %collective-permute-start = (bf16[256,2304]{1,0:T(8,128)(2,1)S(1)}, bf16[256,2304]{1,0:T(8,128)(2,1)}, u32[]{:S(2)}, u32[]{:S(2)}) collective-permute-start(bf16[256,2304]{1,0:T(8,128)(2,1)S(1)} %bitcast.45), channel_id=1, source_target_pairs={{0,1},{1,0},{2,3},{3,2},{4,5},{5,4},{6,7},{7,6},{8,9},{9,8},{10,11... | collective-permute-start | bytes 3538952 | tf_op jit(solution)/shard_map/ppermute | solution.py:198
  94.8 2.5 %collective-permute-done.other_ref = bf16[256,2304]{1,0:T(8,128)(2,1)} collective-permute-done((bf16[256,2304]{1,0:T(8,128)(2,1)S(1)}, bf16[256,2304]{1,0:T(8,128)(2,1)}, u32[]{:S(2)}, u32[]{:S(2)}) %collective-permute-start) | collective-permute-done | bytes 1179680 | tf_op jit(solution)/shard_map/ppermute | solution.py:198
  97.2 5.7 %products.1 = (f32[4,64,1792]{2,1,0:T(8,128)S(1)}, f32[512,256]{1,0:T(8,128)S(1)}) custom-call(s32[2]{0:T(128)S(1)} %pad_add_fusion.place_ref, bf16[256,2304]{1,0:T(8,128)(2,1)S(1)} %bitcast.46, bf16[256,2304]{1,0:T(8,128)(2,1)} %collective-permute-done.other_ref, bf16[512,1536]{1,0:T(8,128)(2,1)S(1)} %bitcast.44, bf16[1536,256]{1,0:T(8,128)(2,1)S(1)} %copy-done), custom_call_target="tpu_custom_call" | custom-call | flops 4000000000 | bytes 8388608 | tf_op jit(solution)/shard_map/products/pallas_call | solution.py:148
  103.0 2.1 %collective-permute-start.1 = (f32[64,1792]{1,0:T(8,128)S(1)}, f32[64,1792]{1,0:T(8,128)S(1)}, u32[]{:S(2)}, u32[]{:S(2)}) collective-permute-start(f32[64,1792]{1,0:T(8,128)S(1)} %get-tuple-element.17), channel_id=1, source_target_pairs={{0,128},{64,192},{128,0},{192,64},{256,384},{320,448},{384,256},{4... | collective-permute-start | bytes 1376264 | tf_op jit(solution)/shard_map/ppermute | solution.py:205
  105.2 3.8 %collective-permute-start.2 = (f32[64,1792]{1,0:T(8,128)S(1)}, f32[64,1792]{1,0:T(8,128)S(1)}, u32[]{:S(2)}, u32[]{:S(2)}) collective-permute-start(f32[64,1792]{1,0:T(8,128)S(1)} %get-tuple-element.15), channel_id=1, source_target_pairs={{0,192},{64,128},{128,64},{192,0},{256,448},{320,384},{384,320},{4... | collective-permute-start | bytes 1376264 | tf_op jit(solution)/shard_map/ppermute | solution.py:205
  109.0 3.7 %collective-permute-start.3 = (f32[64,1792]{1,0:T(8,128)S(1)}, f32[64,1792]{1,0:T(8,128)S(1)}, u32[]{:S(2)}, u32[]{:S(2)}) collective-permute-start(f32[64,1792]{1,0:T(8,128)S(1)} %get-tuple-element.16), channel_id=1, source_target_pairs={{0,64},{64,0},{128,192},{192,128},{256,320},{320,256},{384,448},{4... | collective-permute-start | bytes 1376264 | tf_op jit(solution)/shard_map/ppermute | solution.py:205
  112.6 5.6 %collective-permute-done.1 = f32[64,1792]{1,0:T(8,128)S(1)} collective-permute-done((f32[64,1792]{1,0:T(8,128)S(1)}, f32[64,1792]{1,0:T(8,128)S(1)}, u32[]{:S(2)}, u32[]{:S(2)}) %collective-permute-start.1) | collective-permute-done | bytes 458784 | tf_op jit(solution)/shard_map/ppermute | solution.py:205
  118.2 10.5 %collective-permute-done.2 = f32[64,1792]{1,0:T(8,128)S(1)} collective-permute-done((f32[64,1792]{1,0:T(8,128)S(1)}, f32[64,1792]{1,0:T(8,128)S(1)}, u32[]{:S(2)}, u32[]{:S(2)}) %collective-permute-start.2) | collective-permute-done | bytes 458784 | tf_op jit(solution)/shard_map/ppermute | solution.py:205
  128.8 7.9 %collective-permute-start.4 = (f32[64,256]{1,0:T(8,128)S(1)}, f32[64,256]{1,0:T(8,128)S(1)}, u32[]{:S(2)}, u32[]{:S(2)}) collective-permute-start(f32[64,256]{1,0:T(8,128)S(1)} %slice.49), channel_id=1, source_target_pairs={{0,256},{64,320},{128,384},{192,448},{256,0},{320,64},{384,128},{4... | collective-permute-start | bytes 196616 | tf_op jit(solution)/shard_map/ppermute | solution.py:207
  136.8 6.1 %collective-permute-start.8 = (f32[64,1536]{1,0:T(8,128)S(1)}, f32[64,1536]{1,0:T(8,128)}, u32[]{:S(2)}, u32[]{:S(2)}) collective-permute-start(f32[64,1536]{1,0:T(8,128)S(1)} %slice.50), channel_id=1, source_target_pairs={{0,256},{64,320},{128,384},{192,448},{256,0},{320,64},{384,128},{4... | collective-permute-start | bytes 1179656 | tf_op jit(solution)/shard_map/ppermute | solution.py:208
  143.6 2.8 %collective-permute-start.5 = (f32[64,256]{1,0:T(8,128)S(1)}, f32[64,256]{1,0:T(8,128)S(1)}, u32[]{:S(2)}, u32[]{:S(2)}) collective-permute-start(f32[64,256]{1,0:T(8,128)S(1)} %slice_add_fusion.own_ref), channel_id=1, source_target_pairs={{0,64},{64,0},{128,192},{192,128},{256,320},{320,256},{384,448},{4... | collective-permute-start | bytes 196616 | tf_op jit(solution)/shard_map/ppermute | solution.py:210
  146.4 2.4 %collective-permute-start.6 = (f32[64,256]{1,0:T(8,128)S(1)}, f32[64,256]{1,0:T(8,128)S(1)}, u32[]{:S(2)}, u32[]{:S(2)}) collective-permute-start(f32[64,256]{1,0:T(8,128)S(1)} %slice_add_fusion.own_ref), channel_id=1, source_target_pairs={{0,128},{64,192},{128,0},{192,64},{256,384},{320,448},{384,256},{4... | collective-permute-start | bytes 196616 | tf_op jit(solution)/shard_map/ppermute | solution.py:210
  148.8 3.3 %collective-permute-start.7 = (f32[64,256]{1,0:T(8,128)S(1)}, f32[64,256]{1,0:T(8,128)S(1)}, u32[]{:S(2)}, u32[]{:S(2)}) collective-permute-start(f32[64,256]{1,0:T(8,128)S(1)} %slice_add_fusion.own_ref), channel_id=1, source_target_pairs={{0,192},{64,128},{128,64},{192,0},{256,448},{320,384},{384,320},{4... | collective-permute-start | bytes 196616 | tf_op jit(solution)/shard_map/ppermute | solution.py:210
  153.9 16.8 %inverse_factor.1 = f32[256,256]{1,0:T(8,128)S(1)} custom-call(s32[1]{0:T(128)} %bitcast.6.place_ref, f32[64,256]{1,0:T(8,128)S(1)} %slice_add_fusion.own_ref, f32[64,256]{1,0:T(8,128)S(1)} %collective-permute-done.5.refs_0_, f32[64,256]{1,0:T(8,128)S(1)} %collective-permute-done.6.refs_1_, f32[64,256]{1,0:T(8,128)S(1)} %collective-permute-done.7.refs_2_), custom_call_target="tpu_custom_call" | custom-call | flops 536870912 | bytes 1024 | tf_op jit(solution)/shard_map/inverse_factor/pallas_call | solution.py:103
  170.7 13.7 %collective-permute-done.8 = f32[64,1536]{1,0:T(8,128)} collective-permute-done((f32[64,1536]{1,0:T(8,128)S(1)}, f32[64,1536]{1,0:T(8,128)}, u32[]{:S(2)}, u32[]{:S(2)}) %collective-permute-start.8) | collective-permute-done | bytes 393248 | tf_op jit(solution)/shard_map/ppermute | solution.py:208
  185.7 2.1 collective-permute-start.9
  187.8 3.8 %collective-permute-start.10 = (f32[64,1536]{1,0:T(8,128)S(1)}, f32[64,1536]{1,0:T(8,128)S(1)}, u32[]{:S(2)}, u32[]{:S(2)}) collective-permute-start(f32[64,1536]{1,0:T(8,128)S(1)} %get-tuple-element.14), channel_id=1, source_target_pairs={{0,192},{64,128},{128,64},{192,0},{256,448},{320,384},{384,320},{4... | collective-permute-start | bytes 1179656 | tf_op jit(solution)/shard_map/ppermute | solution.py:217
  191.6 3.7 %collective-permute-start.11 = (f32[64,1536]{1,0:T(8,128)S(1)}, f32[64,1536]{1,0:T(8,128)S(1)}, u32[]{:S(2)}, u32[]{:S(2)}) collective-permute-start(f32[64,1536]{1,0:T(8,128)S(1)} %get-tuple-element.14), channel_id=1, source_target_pairs={{0,64},{64,0},{128,192},{192,128},{256,320},{320,256},{384,448},{4... | collective-permute-start | bytes 1179656 | tf_op jit(solution)/shard_map/ppermute | solution.py:217
  198.6 10.0 %collective-permute-done.10 = f32[64,1536]{1,0:T(8,128)S(1)} collective-permute-done((f32[64,1536]{1,0:T(8,128)S(1)}, f32[64,1536]{1,0:T(8,128)S(1)}, u32[]{:S(2)}, u32[]{:S(2)}) %collective-permute-start.10) | collective-permute-done | bytes 393248 | tf_op jit(solution)/shard_map/ppermute | solution.py:217
  208.6 2.6 %convolution_bitcast_fusion = f32[1,256,1536]{2,1,0:T(8,128)} fusion(f32[256,256]{1,0:T(8,128)S(1)} %inverse_factor.1, f32[256,1536]{1,0:T(8,128)S(1)} %bitcast.47), kind=kOutput, calls=%fused_computation.1 | convolution fusion | flops 1207959552 | bytes 3407872 | tf_op jit(solution)/shard_map/dot_general | solution.py:219
  (43 shorter events, 11.7 us)
Async XLA Ops:
  31.1 21.6 %copy-start = (bf16[1536,256]{1,0:T(8,128)(2,1)S(1)}, bf16[1536,256]{1,0:T(8,128)(2,1)}, u32[]{:S(2)}) copy-start(bf16[1536,256]{1,0:T(8,128)(2,1)} %sketch_ref.1) | copy-start | bytes 2359300
  52.7 0.6 copy-start.3
  90.1 7.2 %collective-permute-start = (bf16[256,2304]{1,0:T(8,128)(2,1)S(1)}, bf16[256,2304]{1,0:T(8,128)(2,1)}, u32[]{:S(2)}, u32[]{:S(2)}) collective-permute-start(bf16[256,2304]{1,0:T(8,128)(2,1)S(1)} %bitcast.45), channel_id=1, source_target_pairs={{0,1},{1,0},{2,3},{3,2},{4,5},{5,4},{6,7},{7,6},{8,9},{9,8},{10,11... | collective-permute-start | bytes 3538952 | tf_op jit(solution)/shard_map/ppermute | solution.py:198
  102.9 25.9 %copy-start.1 = (f32[512,256]{1,0:T(8,128)}, f32[512,256]{1,0:T(8,128)S(1)}, u32[]{:S(2)}) copy-start(f32[512,256]{1,0:T(8,128)S(1)} %get-tuple-element.7) | copy-start | bytes 1572868
  103.0 15.2 %collective-permute-start.1 = (f32[64,1792]{1,0:T(8,128)S(1)}, f32[64,1792]{1,0:T(8,128)S(1)}, u32[]{:S(2)}, u32[]{:S(2)}) collective-permute-start(f32[64,1792]{1,0:T(8,128)S(1)} %get-tuple-element.17), channel_id=1, source_target_pairs={{0,128},{64,192},{128,0},{192,64},{256,384},{320,448},{384,256},{4... | collective-permute-start | bytes 1376264 | tf_op jit(solution)/shard_map/ppermute | solution.py:205
  105.2 23.5 %collective-permute-start.2 = (f32[64,1792]{1,0:T(8,128)S(1)}, f32[64,1792]{1,0:T(8,128)S(1)}, u32[]{:S(2)}, u32[]{:S(2)}) collective-permute-start(f32[64,1792]{1,0:T(8,128)S(1)} %get-tuple-element.15), channel_id=1, source_target_pairs={{0,192},{64,128},{128,64},{192,0},{256,448},{320,384},{384,320},{4... | collective-permute-start | bytes 1376264 | tf_op jit(solution)/shard_map/ppermute | solution.py:205
  109.0 19.8 %collective-permute-start.3 = (f32[64,1792]{1,0:T(8,128)S(1)}, f32[64,1792]{1,0:T(8,128)S(1)}, u32[]{:S(2)}, u32[]{:S(2)}) collective-permute-start(f32[64,1792]{1,0:T(8,128)S(1)} %get-tuple-element.16), channel_id=1, source_target_pairs={{0,64},{64,0},{128,192},{192,128},{256,320},{320,256},{384,448},{4... | collective-permute-start | bytes 1376264 | tf_op jit(solution)/shard_map/ppermute | solution.py:205
  128.8 14.7 %collective-permute-start.4 = (f32[64,256]{1,0:T(8,128)S(1)}, f32[64,256]{1,0:T(8,128)S(1)}, u32[]{:S(2)}, u32[]{:S(2)}) collective-permute-start(f32[64,256]{1,0:T(8,128)S(1)} %slice.49), channel_id=1, source_target_pairs={{0,256},{64,320},{128,384},{192,448},{256,0},{320,64},{384,128},{4... | collective-permute-start | bytes 196616 | tf_op jit(solution)/shard_map/ppermute | solution.py:207
  136.8 47.6 %collective-permute-start.8 = (f32[64,1536]{1,0:T(8,128)S(1)}, f32[64,1536]{1,0:T(8,128)}, u32[]{:S(2)}, u32[]{:S(2)}) collective-permute-start(f32[64,1536]{1,0:T(8,128)S(1)} %slice.50), channel_id=1, source_target_pairs={{0,256},{64,320},{128,384},{192,448},{256,0},{320,64},{384,128},{4... | collective-permute-start | bytes 1179656 | tf_op jit(solution)/shard_map/ppermute | solution.py:208
  143.6 8.6 %collective-permute-start.5 = (f32[64,256]{1,0:T(8,128)S(1)}, f32[64,256]{1,0:T(8,128)S(1)}, u32[]{:S(2)}, u32[]{:S(2)}) collective-permute-start(f32[64,256]{1,0:T(8,128)S(1)} %slice_add_fusion.own_ref), channel_id=1, source_target_pairs={{0,64},{64,0},{128,192},{192,128},{256,320},{320,256},{384,448},{4... | collective-permute-start | bytes 196616 | tf_op jit(solution)/shard_map/ppermute | solution.py:210
  146.4 6.5 %collective-permute-start.6 = (f32[64,256]{1,0:T(8,128)S(1)}, f32[64,256]{1,0:T(8,128)S(1)}, u32[]{:S(2)}, u32[]{:S(2)}) collective-permute-start(f32[64,256]{1,0:T(8,128)S(1)} %slice_add_fusion.own_ref), channel_id=1, source_target_pairs={{0,128},{64,192},{128,0},{192,64},{256,384},{320,448},{384,256},{4... | collective-permute-start | bytes 196616 | tf_op jit(solution)/shard_map/ppermute | solution.py:210
  148.8 5.0 %collective-permute-start.7 = (f32[64,256]{1,0:T(8,128)S(1)}, f32[64,256]{1,0:T(8,128)S(1)}, u32[]{:S(2)}, u32[]{:S(2)}) collective-permute-start(f32[64,256]{1,0:T(8,128)S(1)} %slice_add_fusion.own_ref), channel_id=1, source_target_pairs={{0,192},{64,128},{128,64},{192,0},{256,448},{320,384},{384,320},{4... | collective-permute-start | bytes 196616 | tf_op jit(solution)/shard_map/ppermute | solution.py:210
  170.7 24.6 %copy-start.2 = (f32[512,256]{1,0:T(8,128)S(1)}, f32[512,256]{1,0:T(8,128)}, u32[]{:S(2)}) copy-start(f32[512,256]{1,0:T(8,128)} %copy-done.1) | copy-start | bytes 1572868
  185.7 12.8 %collective-permute-start.9 = (f32[64,1536]{1,0:T(8,128)S(1)}, f32[64,1536]{1,0:T(8,128)S(1)}, u32[]{:S(2)}, u32[]{:S(2)}) collective-permute-start(f32[64,1536]{1,0:T(8,128)S(1)} %get-tuple-element.14), channel_id=1, source_target_pairs={{0,128},{64,192},{128,0},{192,64},{256,384},{320,448},{384,256},{4... | collective-permute-start | bytes 1179656 | tf_op jit(solution)/shard_map/ppermute | solution.py:217
  187.8 20.8 %collective-permute-start.10 = (f32[64,1536]{1,0:T(8,128)S(1)}, f32[64,1536]{1,0:T(8,128)S(1)}, u32[]{:S(2)}, u32[]{:S(2)}) collective-permute-start(f32[64,1536]{1,0:T(8,128)S(1)} %get-tuple-element.14), channel_id=1, source_target_pairs={{0,192},{64,128},{128,64},{192,0},{256,448},{320,384},{384,320},{4... | collective-permute-start | bytes 1179656 | tf_op jit(solution)/shard_map/ppermute | solution.py:217
  191.6 17.0 %collective-permute-start.11 = (f32[64,1536]{1,0:T(8,128)S(1)}, f32[64,1536]{1,0:T(8,128)S(1)}, u32[]{:S(2)}, u32[]{:S(2)}) collective-permute-start(f32[64,1536]{1,0:T(8,128)S(1)} %get-tuple-element.14), channel_id=1, source_target_pairs={{0,64},{64,0},{128,192},{192,128},{256,320},{320,256},{384,448},{4... | collective-permute-start | bytes 1179656 | tf_op jit(solution)/shard_map/ppermute | solution.py:217

commit v6 on v5

--- a/solution.py
+++ b/solution.py
@@ -33,6 +33,7 @@
 ALONG_X = [[(i, i ^ k) for i in range(8)] for k in range(XN)]
 
 PANEL = 64
+TOP_POWER = 13
 
 
 def parts_of(value):
@@ -115,7 +116,7 @@
 def products_kernel(place_ref, mine_ref, other_ref, own_ref, sketch_ref, both_ref, range_ref):
     half, wide = mine_ref.shape
     ff, rank = sketch_ref.shape
-    block = rank // XN
+    block, slab = rank // XN, ff // XN
     core, x = place_ref[0], place_ref[1]
     gram = jnp.zeros((rank, rank), F32)
     delta = jnp.zeros((rank, ff), F32)
@@ -137,9 +138,10 @@
             turned = turned - part.astype(F32)
             delta += jnp.dot(part, own, preferred_element_type=F32)
             delta -= jnp.dot(part, base, preferred_element_type=F32)
+    both_ref[:, rank:, rank:] = jnp.zeros((XN, block, slab - rank), F32)
     for b in range(XN):
-        both_ref[b ^ x, :, :rank] = gram[b * block : (b + 1) * block]
-        both_ref[b ^ x, :, rank:] = delta[b * block : (b + 1) * block]
+        both_ref[b ^ x, :rank, :] = delta[:, b * slab : (b + 1) * slab]
+        both_ref[b ^ x, rank:, :rank] = gram[b * block : (b + 1) * block]
 
 
 def products(place, mine, other, own, sketch):
@@ -148,7 +150,7 @@
     return pl.pallas_call(
         products_kernel,
         out_shape=(
-            jax.ShapeDtypeStruct((XN, rank // XN, rank + ff), F32),
+            jax.ShapeDtypeStruct((XN, rank + rank // XN, ff // XN), F32),
             jax.ShapeDtypeStruct((rows, rank), F32),
         ),
         in_specs=[SMEM] + [VMEM] * 4,
@@ -157,6 +159,56 @@
         cost_estimate=pl.CostEstimate(flops=4 * 10**9, bytes_accessed=8 * MIB, transcendentals=0),
         name="products",
     )(place, mine, other, own, sketch)
+
+
+def finished_kernel(inverse_ref, own_ref, came_ref, out_ref):
+    rank = inverse_ref.shape[0]
+    values = jnp.dot(
+        inverse_ref[...], own_ref[...] + came_ref[...],
+        precision=HIGHEST, preferred_element_type=F32,
+    )
+    top = jnp.max(jnp.max(jnp.abs(values), axis=0, keepdims=True), axis=1, keepdims=True)
+    power = jnp.floor(jnp.log(jnp.maximum(top, 1e-30)) * (1 / math.log(2)))
+    out_ref[:rank] = values * jnp.exp2(TOP_POWER - power)
+    out_ref[rank:] = jnp.broadcast_to(power, (out_ref.shape[0] - rank, out_ref.shape[1]))
+
+
+def finished(inverse, own, came):
+    rank, slab = own.shape
+    return pl.pallas_call(
+        finished_kernel,
+        out_shape=jax.ShapeDtypeStruct((rank + 16, slab), F32),
+        in_specs=[VMEM] * 3,
+        out_specs=VMEM,
+        compiler_params=pltpu.CompilerParams(vmem_limit_bytes=16 * MIB),
+        name="finished",
+    )(inverse, own, came)
+
+
+def assembled_kernel(place_ref, *refs):
+    blocks, out_ref, sems = refs[:XN], refs[XN], refs[XN + 1]
+    slab = blocks[0].shape[1]
+    copies = []
+    for k, ref in enumerate(blocks):
+        start = pl.multiple_of((place_ref[0] ^ k) * slab, slab)
+        copies.append(pltpu.make_async_copy(ref, out_ref.at[:, pl.ds(start, slab)], sems.at[k]))
+    for copy in copies:
+        copy.start()
+    for copy in copies:
+        copy.wait()
+
+
+def assembled(place, blocks):
+    rank, slab = blocks[0].shape
+    return pl.pallas_call(
+        assembled_kernel,
+        out_shape=jax.ShapeDtypeStruct((rank, XN * slab), F32),
+        in_specs=[SMEM] + [VMEM] * XN,
+        out_specs=pl.BlockSpec(memory_space=pl.ANY),
+        scratch_shapes=[pltpu.SemaphoreType.DMA((XN,))],
+        compiler_params=pltpu.CompilerParams(vmem_limit_bytes=16 * MIB),
+        name="assembled",
+    )(place, *blocks)
 
 
 def per_device(counts, up_weights, sketch):
@@ -203,20 +255,23 @@
     )
 
     both = both[0] + sum(lax.ppermute(both[k], "grp", ALONG_X[k]) for k in (2, 3, 1))
-    gram, delta = both[:, :rank], both[:, rank:]
+    gram, delta = both[rank:, :rank], both[:rank]
     gram = gram + lax.ppermute(gram, "grp", OTHER_HALF)
     delta_came = lax.ppermute(delta, "grp", OTHER_HALF)
+    place = at_x.reshape(1)
     inverse = inverse_factor(
-        at_x.reshape(1), [gram] + [lax.ppermute(gram, "grp", ALONG_X[k]) for k in (1, 2, 3)]
+        place, [gram] + [lax.ppermute(gram, "grp", ALONG_X[k]) for k in (1, 2, 3)]
     )
     inverse, delta_came = lax.optimization_barrier((inverse, delta_came))
-    delta = delta + delta_came
-    whole = jnp.zeros((XN,) + delta.shape, F32)
-    whole = lax.dynamic_update_slice(whole, delta[None], (at_x, 0, 0))
+    block = lax.optimization_barrier(finished(inverse, delta, delta_came).astype(jnp.float16))
+    blocks = {0: block}
     for k in (2, 3, 1):
-        came = lax.ppermute(delta, "grp", ALONG_X[k])
-        whole = lax.dynamic_update_slice(whole, came[None], (at_x ^ k, 0, 0))
-    coeff = jnp.dot(inverse, whole.reshape(rank, ff), precision=HIGHEST)
+        blocks[k] = lax.ppermute(block, "grp", ALONG_X[k])
+    blocks = {k: block.astype(F32) for k, block in blocks.items()}
+    coeff = assembled(
+        place,
+        [blocks[k][:rank] * jnp.exp2(blocks[k][rank : rank + 1, :1] - TOP_POWER) for k in range(XN)],
+    )
 
     ortho = lax.dot_general(
         range_rows, inverse, (((1,), (1,)), ((), ())), precision=HIGHEST

time: 212 us -> 211 us (level)
  the two profiles are of different devices: /device:TPU:101 before, /device:TPU:32 now
where the time goes in v6:
time: 211 us; the launch traced here: 210 us
  blocking collectives  88.7 us (42%)
  starting transfers between devices  46.7 us (22%)
  waiting for transfers between devices  37.2 us (18%)
  Pallas kernels  24.3 us (12%)
  local copies, waits for them, and re-layouts  5.63 us (3%)
  between operations  4.6 us (2%)
    all_to_all x1, blocking collectives, per_device(): lax.all_to_all(jnp.concatenate([own, tag], axis=2), 'exp', 0, 0, axis_ind...  30.3 us
    all_to_all x1, blocking collectives, per_device(): lax.all_to_all(jnp.broadcast_to(load, (YN * NN, FN * piece, wide)), 'exp'...  20.4 us
    all_to_all x1, blocking collectives, per_device(): lax.all_to_all(jnp.concatenate([weighted.reshape(FN, piece, ff), freq_sum...  20 us
    ppermute x3, waiting for transfers between devices, per_device(): lax.ppermute(both[k], 'grp', ALONG_X[k])  19.5 us
    all_to_all x1, blocking collectives, per_device(): lax.all_to_all(jnp.broadcast_to(load, (FN, piece, wide)), 'exp', 0, 0, ax...  18 us
    pallas_call x1, Pallas kernels, inverse_factor(): pl.pallas_call(inverse_factor_kernel, out_shape=jax.ShapeDtypeStruct((n,...  16.8 us
    ppermute x3, starting transfers between devices, per_device(): lax.ppermute(both[k], 'grp', ALONG_X[k])  10.4 us
    ppermute x3, starting transfers between devices, per_device(): lax.ppermute(gram, 'grp', ALONG_X[k])  10 us
  transfers between devices with their start and end apart: 12, of which 10 were waited for; matrix products, arithmetic and copies ran while one was open for 2% of the time, Pallas kernels for 8%

profile of v6, /device:TPU:32, one launch (start us, length us, event | category | flops | bytes accessed | tf_op | source)
XLA Modules:
  0.0 210.2 jit_solution(1785821645001560795)
XLA Ops:
  3.1 30.3 %all_to_all.20 = bf16[16,32,1664]{2,1,0:T(8,128)(2,1)S(1)} all-to-all(bf16[16,32,1664]{2,1,0:T(8,128)(2,1)S(1)} %pad_maximum_fusion), channel_id=1, replica_groups={{0,2,16,18,32,34,48,50,1,3,17,19,33,35,49,51},{4,6,20,22,36,38,52,54,5,..., dimensions={0} | all-to-all | bytes 3407872 | tf_op jit(solution)/shard_map/all_to_all | solution.py:225
  35.3 20.0 %all_to_all.21 = f32[4,8,1664]{2,1,0:T(8,128)S(1)} all-to-all(f32[4,8,1664]{2,1,0:T(8,128)S(1)} %concatenate.10), channel_id=1, replica_groups={{0,4,8,12},{1,5,9,13},{2,6,10,14},{3,7,11,15},{16,20,24,28},{17,21,25,2..., dimensions={0} | all-to-all | bytes 425984 | tf_op jit(solution)/shard_map/all_to_all | solution.py:232
  56.1 18.0 %all_to_all.22 = bf16[4,8,2304]{2,1,0:T(8,128)(2,1)S(1)} all-to-all(bf16[4,8,2304]{2,1,0:T(8,128)(2,1)S(1)} %broadcast_in_dim.23), channel_id=1, replica_groups={{0,4,8,12},{1,5,9,13},{2,6,10,14},{3,7,11,15},{16,20,24,28},{17,21,25,2..., dimensions={0} | all-to-all | bytes 294912 | tf_op jit(solution)/shard_map/all_to_all | solution.py:243
  74.2 20.4 %all_to_all.23 = bf16[8,32,2304]{2,1,0:T(8,128)(2,1)S(1)} all-to-all(bf16[8,32,2304]{2,1,0:T(8,128)(2,1)S(1)} %broadcast_in_dim.24), channel_id=1, replica_groups={{0,2,16,18,32,34,48,50},{1,3,17,19,33,35,49,51},{4,6,20,22,36,38,52,54}..., dimensions={0} | all-to-all | bytes 2359296 | tf_op jit(solution)/shard_map/all_to_all | solution.py:246
  96.7 2.8 %collective-permute-done.other_ref = bf16[256,2304]{1,0:T(8,128)(2,1)} collective-permute-done((bf16[256,2304]{1,0:T(8,128)(2,1)S(1)}, bf16[256,2304]{1,0:T(8,128)(2,1)}, u32[]{:S(2)}, u32[]{:S(2)}) %collective-permute-start) | collective-permute-done | bytes 1179680 | tf_op jit(solution)/shard_map/ppermute | solution.py:250
  99.5 5.6 %products.1 = (f32[4,320,384]{2,1,0:T(8,128)S(1)}, f32[512,256]{1,0:T(8,128)S(1)}) custom-call(s32[2]{0:T(128)S(1)} %pad_add_fusion.place_ref, bf16[256,2304]{1,0:T(8,128)(2,1)S(1)} %bitcast.38, bf16[256,2304]{1,0:T(8,128)(2,1)} %collective-permute-done.other_ref, bf16[512,1536]{1,0:T(8,128)(2,1)S(1)} %bitcast.36, bf16[1536,256]{1,0:T(8,128)(2,1)S(1)} %copy-done), custom_call_target="tpu_custom_call" | custom-call | flops 4000000000 | bytes 8388608 | tf_op jit(solution)/shard_map/products/pallas_call | solution.py:150
  105.3 4.7 %collective-permute-start.2 = (f32[320,384]{1,0:T(8,128)S(1)}, f32[320,384]{1,0:T(8,128)S(1)}, u32[]{:S(2)}, u32[]{:S(2)}) collective-permute-start(f32[320,384]{1,0:T(8,128)S(1)} %get-tuple-element.13), channel_id=1, source_target_pairs={{0,192},{64,128},{128,64},{192,0},{256,448},{320,384},{384,320},{4... | collective-permute-start | bytes 1474568 | tf_op jit(solution)/shard_map/ppermute | solution.py:257
  109.9 2.1 %collective-permute-start.3 = (f32[320,384]{1,0:T(8,128)S(1)}, f32[320,384]{1,0:T(8,128)S(1)}, u32[]{:S(2)}, u32[]{:S(2)}) collective-permute-start(f32[320,384]{1,0:T(8,128)S(1)} %get-tuple-element.14), channel_id=1, source_target_pairs={{0,64},{64,0},{128,192},{192,128},{256,320},{320,256},{384,448},{4... | collective-permute-start | bytes 1474568 | tf_op jit(solution)/shard_map/ppermute | solution.py:257
  112.1 3.6 %collective-permute-start.1 = (f32[320,384]{1,0:T(8,128)S(1)}, f32[320,384]{1,0:T(8,128)S(1)}, u32[]{:S(2)}, u32[]{:S(2)}) collective-permute-start(f32[320,384]{1,0:T(8,128)S(1)} %get-tuple-element.15), channel_id=1, source_target_pairs={{0,128},{64,192},{128,0},{192,64},{256,384},{320,448},{384,256},{4... | collective-permute-start | bytes 1474568 | tf_op jit(solution)/shard_map/ppermute | solution.py:257
  115.7 5.9 %collective-permute-done.2 = f32[320,384]{1,0:T(8,128)S(1)} collective-permute-done((f32[320,384]{1,0:T(8,128)S(1)}, f32[320,384]{1,0:T(8,128)S(1)}, u32[]{:S(2)}, u32[]{:S(2)}) %collective-permute-start.2) | collective-permute-done | bytes 491552 | tf_op jit(solution)/shard_map/ppermute | solution.py:257
  121.6 4.3 %collective-permute-done.3 = f32[320,384]{1,0:T(8,128)S(1)} collective-permute-done((f32[320,384]{1,0:T(8,128)S(1)}, f32[320,384]{1,0:T(8,128)S(1)}, u32[]{:S(2)}, u32[]{:S(2)}) %collective-permute-start.3) | collective-permute-done | bytes 491552 | tf_op jit(solution)/shard_map/ppermute | solution.py:257
  125.9 9.3 %collective-permute-done.1 = f32[320,384]{1,0:T(8,128)S(1)} collective-permute-done((f32[320,384]{1,0:T(8,128)S(1)}, f32[320,384]{1,0:T(8,128)S(1)}, u32[]{:S(2)}, u32[]{:S(2)}) %collective-permute-start.1) | collective-permute-done | bytes 491552 | tf_op jit(solution)/shard_map/ppermute | solution.py:257
  135.4 8.2 %collective-permute-start.4 = (f32[64,256]{1,0:T(8,128)S(1)}, f32[64,256]{1,0:T(8,128)S(1)}, u32[]{:S(2)}, u32[]{:S(2)}) collective-permute-start(f32[64,256]{1,0:T(8,128)S(1)} %slice.81), channel_id=1, source_target_pairs={{0,256},{64,320},{128,384},{192,448},{256,0},{320,64},{384,128},{4... | collective-permute-start | bytes 196616 | tf_op jit(solution)/shard_map/ppermute | solution.py:259
  143.6 6.3 %collective-permute-start.8 = (f32[256,384]{1,0:T(8,128)S(1)}, f32[256,384]{1,0:T(8,128)S(1)}, u32[]{:S(2)}, u32[]{:S(2)}) collective-permute-start(f32[256,384]{1,0:T(8,128)S(1)} %slice.82.own_ref), channel_id=1, source_target_pairs={{0,256},{64,320},{128,384},{192,448},{256,0},{320,64},{384,128},{4... | collective-permute-start | bytes 1179656 | tf_op jit(solution)/shard_map/ppermute | solution.py:260
  150.0 2.6 %collective-permute-done.4 = f32[64,256]{1,0:T(8,128)S(1)} collective-permute-done((f32[64,256]{1,0:T(8,128)S(1)}, f32[64,256]{1,0:T(8,128)S(1)}, u32[]{:S(2)}, u32[]{:S(2)}) %collective-permute-start.4) | collective-permute-done | bytes 65568 | tf_op jit(solution)/shard_map/ppermute | solution.py:259
  152.6 4.7 %collective-permute-start.7 = (f32[64,256]{1,0:T(8,128)S(1)}, f32[64,256]{1,0:T(8,128)S(1)}, u32[]{:S(2)}, u32[]{:S(2)}) collective-permute-start(f32[64,256]{1,0:T(8,128)S(1)} %slice_add_fusion.own_ref), channel_id=1, source_target_pairs={{0,192},{64,128},{128,64},{192,0},{256,448},{320,384},{384,320},{4... | collective-permute-start | bytes 196616 | tf_op jit(solution)/shard_map/ppermute | solution.py:263
  157.3 1.9 collective-permute-start.6
  159.2 3.4 %collective-permute-start.5 = (f32[64,256]{1,0:T(8,128)S(1)}, f32[64,256]{1,0:T(8,128)S(1)}, u32[]{:S(2)}, u32[]{:S(2)}) collective-permute-start(f32[64,256]{1,0:T(8,128)S(1)} %slice_add_fusion.own_ref), channel_id=1, source_target_pairs={{0,64},{64,0},{128,192},{192,128},{256,320},{320,256},{384,448},{4... | collective-permute-start | bytes 196616 | tf_op jit(solution)/shard_map/ppermute | solution.py:263
  162.7 2.6 %collective-permute-done.6.refs_1_ = f32[64,256]{1,0:T(8,128)S(1)} collective-permute-done((f32[64,256]{1,0:T(8,128)S(1)}, f32[64,256]{1,0:T(8,128)S(1)}, u32[]{:S(2)}, u32[]{:S(2)}) %collective-permute-start.6) | collective-permute-done | bytes 65568 | tf_op jit(solution)/shard_map/ppermute | solution.py:263
  165.4 16.8 %inverse_factor.1.inverse_ref = f32[256,256]{1,0:T(8,128)S(1)} custom-call(s32[1]{0:T(128)} %bitcast.6.place_ref, f32[64,256]{1,0:T(8,128)S(1)} %slice_add_fusion.own_ref, f32[64,256]{1,0:T(8,128)S(1)} %collective-permute-done.5.refs_0_, f32[64,256]{1,0:T(8,128)S(1)} %collective-permute-done.6.refs_1_, f32[64,256]{1,0:T(8,128)S(1)} %collective-permute-done.7.refs_2_), custom_call_target="tpu_custom_call" | custom-call | flops 536870912 | bytes 1024 | tf_op jit(solution)/shard_map/inverse_factor/pallas_call | solution.py:104
  182.2 7.1 %collective-permute-done.8.came_ref = f32[256,384]{1,0:T(8,128)S(1)} collective-permute-done((f32[256,384]{1,0:T(8,128)S(1)}, f32[256,384]{1,0:T(8,128)S(1)}, u32[]{:S(2)}, u32[]{:S(2)}) %collective-permute-start.8) | collective-permute-done | bytes 393248 | tf_op jit(solution)/shard_map/ppermute | solution.py:260
  190.1 4.7 %collective-permute-start.11 = (f16[272,384]{1,0:T(8,128)(2,1)S(1)}, f16[272,384]{1,0:T(8,128)(2,1)S(1)}, u32[]{:S(2)}, u32[]{:S(2)}) collective-permute-start(f16[272,384]{1,0:T(8,128)(2,1)S(1)} %convert_element_type.52), channel_id=1, source_target_pairs={{0,192},{64,128},{128,64},{192,0},{256,448},{320,384},{384,320},{4... | collective-permute-start | bytes 626696 | tf_op jit(solution)/shard_map/ppermute | solution.py:269
  194.8 1.9 collective-permute-start.10
  196.7 3.2 %collective-permute-start.9 = (f16[272,384]{1,0:T(8,128)(2,1)S(1)}, f16[272,384]{1,0:T(8,128)(2,1)S(1)}, u32[]{:S(2)}, u32[]{:S(2)}) collective-permute-start(f16[272,384]{1,0:T(8,128)(2,1)S(1)} %convert_element_type.52), channel_id=1, source_target_pairs={{0,64},{64,0},{128,192},{192,128},{256,320},{320,256},{384,448},{4... | collective-permute-start | bytes 626696 | tf_op jit(solution)/shard_map/ppermute | solution.py:269
  (48 shorter events, 14.9 us)
Async XLA Ops:
  33.4 22.1 %copy-start = (bf16[1536,256]{1,0:T(8,128)(2,1)S(1)}, bf16[1536,256]{1,0:T(8,128)(2,1)}, u32[]{:S(2)}) copy-start(bf16[1536,256]{1,0:T(8,128)(2,1)} %sketch_ref.1) | copy-start | bytes 2359300
  55.5 0.6 copy-start.1
  94.6 4.9 %collective-permute-start = (bf16[256,2304]{1,0:T(8,128)(2,1)S(1)}, bf16[256,2304]{1,0:T(8,128)(2,1)}, u32[]{:S(2)}, u32[]{:S(2)}) collective-permute-start(bf16[256,2304]{1,0:T(8,128)(2,1)S(1)} %bitcast.37), channel_id=1, source_target_pairs={{0,1},{1,0},{2,3},{3,2},{4,5},{5,4},{6,7},{7,6},{8,9},{9,8},{10,11... | collective-permute-start | bytes 3538952 | tf_op jit(solution)/shard_map/ppermute | solution.py:250
  105.3 16.4 %collective-permute-start.2 = (f32[320,384]{1,0:T(8,128)S(1)}, f32[320,384]{1,0:T(8,128)S(1)}, u32[]{:S(2)}, u32[]{:S(2)}) collective-permute-start(f32[320,384]{1,0:T(8,128)S(1)} %get-tuple-element.13), channel_id=1, source_target_pairs={{0,192},{64,128},{128,64},{192,0},{256,448},{320,384},{384,320},{4... | collective-permute-start | bytes 1474568 | tf_op jit(solution)/shard_map/ppermute | solution.py:257
  109.9 16.0 %collective-permute-start.3 = (f32[320,384]{1,0:T(8,128)S(1)}, f32[320,384]{1,0:T(8,128)S(1)}, u32[]{:S(2)}, u32[]{:S(2)}) collective-permute-start(f32[320,384]{1,0:T(8,128)S(1)} %get-tuple-element.14), channel_id=1, source_target_pairs={{0,64},{64,0},{128,192},{192,128},{256,320},{320,256},{384,448},{4... | collective-permute-start | bytes 1474568 | tf_op jit(solution)/shard_map/ppermute | solution.py:257
  112.1 23.2 %collective-permute-start.1 = (f32[320,384]{1,0:T(8,128)S(1)}, f32[320,384]{1,0:T(8,128)S(1)}, u32[]{:S(2)}, u32[]{:S(2)}) collective-permute-start(f32[320,384]{1,0:T(8,128)S(1)} %get-tuple-element.15), channel_id=1, source_target_pairs={{0,128},{64,192},{128,0},{192,64},{256,384},{320,448},{384,256},{4... | collective-permute-start | bytes 1474568 | tf_op jit(solution)/shard_map/ppermute | solution.py:257
  135.4 17.2 %collective-permute-start.4 = (f32[64,256]{1,0:T(8,128)S(1)}, f32[64,256]{1,0:T(8,128)S(1)}, u32[]{:S(2)}, u32[]{:S(2)}) collective-permute-start(f32[64,256]{1,0:T(8,128)S(1)} %slice.81), channel_id=1, source_target_pairs={{0,256},{64,320},{128,384},{192,448},{256,0},{320,64},{384,128},{4... | collective-permute-start | bytes 196616 | tf_op jit(solution)/shard_map/ppermute | solution.py:259
  143.6 45.7 %collective-permute-start.8 = (f32[256,384]{1,0:T(8,128)S(1)}, f32[256,384]{1,0:T(8,128)S(1)}, u32[]{:S(2)}, u32[]{:S(2)}) collective-permute-start(f32[256,384]{1,0:T(8,128)S(1)} %slice.82.own_ref), channel_id=1, source_target_pairs={{0,256},{64,320},{128,384},{192,448},{256,0},{320,64},{384,128},{4... | collective-permute-start | bytes 1179656 | tf_op jit(solution)/shard_map/ppermute | solution.py:260
  152.6 10.0 %collective-permute-start.7 = (f32[64,256]{1,0:T(8,128)S(1)}, f32[64,256]{1,0:T(8,128)S(1)}, u32[]{:S(2)}, u32[]{:S(2)}) collective-permute-start(f32[64,256]{1,0:T(8,128)S(1)} %slice_add_fusion.own_ref), channel_id=1, source_target_pairs={{0,192},{64,128},{128,64},{192,0},{256,448},{320,384},{384,320},{4... | collective-permute-start | bytes 196616 | tf_op jit(solution)/shard_map/ppermute | solution.py:263
  157.3 7.9 %collective-permute-start.6 = (f32[64,256]{1,0:T(8,128)S(1)}, f32[64,256]{1,0:T(8,128)S(1)}, u32[]{:S(2)}, u32[]{:S(2)}) collective-permute-start(f32[64,256]{1,0:T(8,128)S(1)} %slice_add_fusion.own_ref), channel_id=1, source_target_pairs={{0,128},{64,192},{128,0},{192,64},{256,384},{320,448},{384,256},{4... | collective-permute-start | bytes 196616 | tf_op jit(solution)/shard_map/ppermute | solution.py:263
  159.2 6.2 %collective-permute-start.5 = (f32[64,256]{1,0:T(8,128)S(1)}, f32[64,256]{1,0:T(8,128)S(1)}, u32[]{:S(2)}, u32[]{:S(2)}) collective-permute-start(f32[64,256]{1,0:T(8,128)S(1)} %slice_add_fusion.own_ref), channel_id=1, source_target_pairs={{0,64},{64,0},{128,192},{192,128},{256,320},{320,256},{384,448},{4... | collective-permute-start | bytes 196616 | tf_op jit(solution)/shard_map/ppermute | solution.py:263
  190.1 13.4 %collective-permute-start.11 = (f16[272,384]{1,0:T(8,128)(2,1)S(1)}, f16[272,384]{1,0:T(8,128)(2,1)S(1)}, u32[]{:S(2)}, u32[]{:S(2)}) collective-permute-start(f16[272,384]{1,0:T(8,128)(2,1)S(1)} %convert_element_type.52), channel_id=1, source_target_pairs={{0,192},{64,128},{128,64},{192,0},{256,448},{320,384},{384,320},{4... | collective-permute-start | bytes 626696 | tf_op jit(solution)/shard_map/ppermute | solution.py:269
  194.8 11.5 %collective-permute-start.10 = (f16[272,384]{1,0:T(8,128)(2,1)S(1)}, f16[272,384]{1,0:T(8,128)(2,1)S(1)}, u32[]{:S(2)}, u32[]{:S(2)}) collective-permute-start(f16[272,384]{1,0:T(8,128)(2,1)S(1)} %convert_element_type.52), channel_id=1, source_target_pairs={{0,128},{64,192},{128,0},{192,64},{256,384},{320,448},{384,256},{4... | collective-permute-start | bytes 626696 | tf_op jit(solution)/shard_map/ppermute | solution.py:269
  196.7 10.8 %collective-permute-start.9 = (f16[272,384]{1,0:T(8,128)(2,1)S(1)}, f16[272,384]{1,0:T(8,128)(2,1)S(1)}, u32[]{:S(2)}, u32[]{:S(2)}) collective-permute-start(f16[272,384]{1,0:T(8,128)(2,1)S(1)} %convert_element_type.52), channel_id=1, source_target_pairs={{0,64},{64,0},{128,192},{192,128},{256,320},{320,256},{384,448},{4... | collective-permute-start | bytes 626696 | tf_op jit(solution)/shard_map/ppermute | solution.py:269

commit v7 on v6

--- a/solution.py
+++ b/solution.py
@@ -34,6 +34,7 @@
 
 PANEL = 64
 TOP_POWER = 13
+FACTOR_COST = 2**29
 
 
 def parts_of(value):
@@ -75,10 +76,25 @@
 def inverse_factor_kernel(place_ref, own_ref, *refs):
     came_refs, inverse_ref, work_ref = refs[:-2], refs[-2], refs[-1]
     n = inverse_ref.shape[0]
-    block = own_ref.shape[0]
-    for k, ref in enumerate((own_ref,) + came_refs):
-        start = pl.multiple_of((place_ref[0] ^ k) * block, block)
-        work_ref[pl.ds(start, block), :n] = ref[...]
+    block = n // XN
+    held = []
+    for ref in (own_ref,) + came_refs:
+        packed = ref[...]
+        width = packed.shape[1] // 2
+        held.append(jnp.concatenate([packed[:, :width], packed[:, width:]], axis=0))
+    for x in range(XN):
+
+        @pl.when(place_ref[0] == x)
+        def _():
+            for b in range(XN):
+                rows = pl.ds(b * block, block)
+                for j in range(XN - 1):
+                    c = (b + j) % XN
+                    part = held[b ^ x][:, j * block : (j + 1) * block]
+                    work_ref[rows, c * block : (c + 1) * block] = part
+                c = (b + XN - 1) % XN
+                work_ref[rows, c * block : (c + 1) * block] = held[c ^ x][:, block : 2 * block].T
+
     work_ref[:, n:] = eye(n)
     for top in range(0, n, PANEL):
         end = top + PANEL
@@ -99,8 +115,7 @@
 SMEM = pl.BlockSpec(memory_space=pltpu.SMEM)
 
 
-def inverse_factor(place, blocks):
-    n = blocks[0].shape[1]
+def inverse_factor(place, blocks, n):
     return pl.pallas_call(
         inverse_factor_kernel,
         out_shape=jax.ShapeDtypeStruct((n, n), F32),
@@ -108,18 +123,29 @@
         out_specs=VMEM,
         scratch_shapes=[pltpu.VMEM((n, 2 * n), F32)],
         compiler_params=pltpu.CompilerParams(vmem_limit_bytes=16 * MIB),
-        cost_estimate=pl.CostEstimate(flops=2**29, bytes_accessed=2**10, transcendentals=0),
+        cost_estimate=pl.CostEstimate(flops=FACTOR_COST, bytes_accessed=2**10, transcendentals=0),
         name="inverse_factor",
     )(place, *blocks)
 
 
-def products_kernel(place_ref, mine_ref, other_ref, own_ref, sketch_ref, both_ref, range_ref):
-    half, wide = mine_ref.shape
+def range_product(turned, own, base):
+    total = None
+    for step in range(3):
+        part = turned.astype(BF16)
+        turned = turned - part.astype(F32)
+        term = jnp.dot(part, own, preferred_element_type=F32)
+        term -= jnp.dot(part, base, preferred_element_type=F32)
+        total = term if total is None else total + term
+    return total
+
+
+def first_products_kernel(place_ref, mine_ref, other_ref, own_ref, sketch_ref, out_ref, range_ref):
+    half = mine_ref.shape[0]
     ff, rank = sketch_ref.shape
-    block, slab = rank // XN, ff // XN
+    block, slab, chunk = rank // XN, ff // XN, rank // 2
     core, x = place_ref[0], place_ref[1]
     gram = jnp.zeros((rank, rank), F32)
-    delta = jnp.zeros((rank, ff), F32)
+    delta = jnp.zeros((chunk, ff), F32)
     for load_ref, at_core in ((mine_ref, core), (other_ref, 1 - core)):
         rows = pl.ds(pl.multiple_of(at_core * half, half), half)
         own = own_ref[rows, :]
@@ -132,40 +158,70 @@
         range_ref[rows, :] = range_rows
         turned = range_rows.T
         gram += jnp.dot(turned, range_rows, precision=HIGHEST, preferred_element_type=F32)
-        base = load_ref[:, :ff]
-        for step in range(3):
-            part = turned.astype(BF16)
-            turned = turned - part.astype(F32)
-            delta += jnp.dot(part, own, preferred_element_type=F32)
-            delta -= jnp.dot(part, base, preferred_element_type=F32)
-    both_ref[:, rank:, rank:] = jnp.zeros((XN, block, slab - rank), F32)
+        delta += range_product(turned[:chunk], own, load_ref[:, :ff])
     for b in range(XN):
-        both_ref[b ^ x, :rank, :] = delta[:, b * slab : (b + 1) * slab]
-        both_ref[b ^ x, rank:, :rank] = gram[b * block : (b + 1) * block]
-
-
-def products(place, mine, other, own, sketch):
+        mine = gram[b * block : (b + 1) * block]
+        kept = jnp.concatenate(
+            [mine[:, (b + j) % XN * block :][:, :block] for j in range(XN - 1)], axis=1
+        )
+        packed = jnp.concatenate([kept[: block // 2], kept[block // 2 :]], axis=1)
+        out_ref[b ^ x, : block // 2, :] = packed
+        out_ref[b ^ x, block // 2 :, :] = delta[:, b * slab : (b + 1) * slab]
+
+
+def first_products(place, mine, other, own, sketch):
     rows, ff = own.shape
     rank = sketch.shape[1]
     return pl.pallas_call(
-        products_kernel,
+        first_products_kernel,
         out_shape=(
-            jax.ShapeDtypeStruct((XN, rank + rank // XN, ff // XN), F32),
+            jax.ShapeDtypeStruct((XN, rank // XN // 2 + rank // 2, ff // XN), F32),
             jax.ShapeDtypeStruct((rows, rank), F32),
         ),
         in_specs=[SMEM] + [VMEM] * 4,
         out_specs=(VMEM, VMEM),
         compiler_params=pltpu.CompilerParams(vmem_limit_bytes=40 * MIB),
-        cost_estimate=pl.CostEstimate(flops=4 * 10**9, bytes_accessed=8 * MIB, transcendentals=0),
-        name="products",
+        cost_estimate=pl.CostEstimate(flops=3 * 10**9, bytes_accessed=2**10, transcendentals=0),
+        name="first_products",
     )(place, mine, other, own, sketch)
 
 
-def finished_kernel(inverse_ref, own_ref, came_ref, out_ref):
+def second_products_kernel(place_ref, mine_ref, other_ref, own_ref, range_ref, out_ref):
+    half = mine_ref.shape[0]
+    ff, rank = own_ref.shape[1], range_ref.shape[1]
+    slab, chunk = ff // XN, rank // 2
+    core, x = place_ref[0], place_ref[1]
+    delta = jnp.zeros((chunk, ff), F32)
+    for load_ref, at_core in ((mine_ref, core), (other_ref, 1 - core)):
+        rows = pl.ds(pl.multiple_of(at_core * half, half), half)
+        delta += range_product(range_ref[rows, chunk:].T, own_ref[rows, :], load_ref[:, :ff])
+    for b in range(XN):
+        out_ref[b ^ x] = delta[:, b * slab : (b + 1) * slab]
+
+
+def second_products(place, mine, other, own, range_rows):
+    ff, rank = own.shape[1], range_rows.shape[1]
+    return pl.pallas_call(
+        second_products_kernel,
+        out_shape=jax.ShapeDtypeStruct((XN, rank // 2, ff // XN), F32),
+        in_specs=[SMEM] + [VMEM] * 4,
+        out_specs=VMEM,
+        compiler_params=pltpu.CompilerParams(vmem_limit_bytes=40 * MIB),
+        cost_estimate=pl.CostEstimate(flops=2 * 10**9, bytes_accessed=2**10, transcendentals=0),
+        name="second_products",
+    )(place, mine, other, own, range_rows)
+
+
+def finished_kernel(inverse_ref, *refs):
+    out_ref = refs[-1]
     rank = inverse_ref.shape[0]
-    values = jnp.dot(
-        inverse_ref[...], own_ref[...] + came_ref[...],
-        precision=HIGHEST, preferred_element_type=F32,
+    chunk = rank // 2
+    values = sum(
+        jnp.dot(
+            inverse_ref[:, i * chunk : (i + 1) * chunk], refs[2 * i][...] + refs[2 * i + 1][...],
+            precision=HIGHEST, preferred_element_type=F32,
+        )
+        for i in range(2)
     )
     top = jnp.max(jnp.max(jnp.abs(values), axis=0, keepdims=True), axis=1, keepdims=True)
     power = jnp.floor(jnp.log(jnp.maximum(top, 1e-30)) * (1 / math.log(2)))
@@ -173,39 +229,42 @@
     out_ref[rank:] = jnp.broadcast_to(power, (out_ref.shape[0] - rank, out_ref.shape[1]))
 
 
-def finished(inverse, own, came):
-    rank, slab = own.shape
+def finished(inverse, chunks):
+    rank, slab = inverse.shape[0], chunks[0].shape[1]
     return pl.pallas_call(
         finished_kernel,
         out_shape=jax.ShapeDtypeStruct((rank + 16, slab), F32),
-        in_specs=[VMEM] * 3,
+        in_specs=[VMEM] * (1 + len(chunks)),
         out_specs=VMEM,
         compiler_params=pltpu.CompilerParams(vmem_limit_bytes=16 * MIB),
         name="finished",
-    )(inverse, own, came)
+    )(inverse, *chunks)
 
 
 def assembled_kernel(place_ref, *refs):
-    blocks, out_ref, sems = refs[:XN], refs[XN], refs[XN + 1]
-    slab = blocks[0].shape[1]
+    blocks, (out_ref, held_ref, sems) = refs[:XN], refs[XN:]
+    rank, slab = held_ref.shape[1:]
     copies = []
     for k, ref in enumerate(blocks):
+        held_ref[k] = ref[:rank] * jnp.exp2(ref[rank : rank + 1] - TOP_POWER)
         start = pl.multiple_of((place_ref[0] ^ k) * slab, slab)
-        copies.append(pltpu.make_async_copy(ref, out_ref.at[:, pl.ds(start, slab)], sems.at[k]))
-    for copy in copies:
+        copy = pltpu.make_async_copy(
+            held_ref.at[k], out_ref.at[:, pl.ds(start, slab)], sems.at[k]
+        )
         copy.start()
+        copies.append(copy)
     for copy in copies:
         copy.wait()
 
 
 def assembled(place, blocks):
-    rank, slab = blocks[0].shape
+    rank, slab = blocks[0].shape[0] - 16, blocks[0].shape[1]
     return pl.pallas_call(
         assembled_kernel,
         out_shape=jax.ShapeDtypeStruct((rank, XN * slab), F32),
         in_specs=[SMEM] + [VMEM] * XN,
         out_specs=pl.BlockSpec(memory_space=pl.ANY),
-        scratch_shapes=[pltpu.SemaphoreType.DMA((XN,))],
+        scratch_shapes=[pltpu.VMEM((XN, rank, slab), F32), pltpu.SemaphoreType.DMA((XN,))],
         compiler_params=pltpu.CompilerParams(vmem_limit_bytes=16 * MIB),
         name="assembled",
     )(place, *blocks)
@@ -250,28 +309,33 @@
     other = lax.ppermute(load, "exp", OTHER_CORE)
 
     at_core, at_x = lax.axis_index("exp") % CN, lax.axis_index("grp") % XN
-    both, range_rows = products(
-        jnp.stack([at_core, at_x]), load, other, own.reshape(rows, ff), sketch
-    )
-
-    both = both[0] + sum(lax.ppermute(both[k], "grp", ALONG_X[k]) for k in (2, 3, 1))
-    gram, delta = both[rank:, :rank], both[:rank]
-    gram = gram + lax.ppermute(gram, "grp", OTHER_HALF)
-    delta_came = lax.ppermute(delta, "grp", OTHER_HALF)
-    place = at_x.reshape(1)
+    place, own = jnp.stack([at_core, at_x]), own.reshape(rows, ff)
+
+    def along_x(blocks):
+        return [blocks[0]] + [lax.ppermute(blocks[k], "grp", ALONG_X[k]) for k in (2, 3, 1)]
+
+    first, range_rows = first_products(place, load, other, own, sketch)
+    first = along_x(first)
+    second = along_x(second_products(place, load, other, own, range_rows))
+    first = sum(first)
+    packed = rank // XN // 2
+    gram, first = first[:packed], first[packed:]
+    gram_came = lax.ppermute(gram, "grp", OTHER_HALF)
+    _, second = lax.optimization_barrier((gram_came, second))
+    gram, second = gram + gram_came, sum(second)
+    chunks = [first, lax.ppermute(first, "grp", OTHER_HALF)]
+    chunks += [second, lax.ppermute(second, "grp", OTHER_HALF)]
     inverse = inverse_factor(
-        place, [gram] + [lax.ppermute(gram, "grp", ALONG_X[k]) for k in (1, 2, 3)]
-    )
-    inverse, delta_came = lax.optimization_barrier((inverse, delta_came))
-    block = lax.optimization_barrier(finished(inverse, delta, delta_came).astype(jnp.float16))
+        at_x.reshape(1),
+        [gram] + [lax.ppermute(gram, "grp", ALONG_X[k]) for k in (1, 2, 3)],
+        rank,
+    )
+    inverse, chunks = lax.optimization_barrier((inverse, chunks))
+    block = lax.optimization_barrier(finished(inverse, chunks).astype(jnp.float16))
     blocks = {0: block}
     for k in (2, 3, 1):
         blocks[k] = lax.ppermute(block, "grp", ALONG_X[k])
-    blocks = {k: block.astype(F32) for k, block in blocks.items()}
-    coeff = assembled(
-        place,
-        [blocks[k][:rank] * jnp.exp2(blocks[k][rank : rank + 1, :1] - TOP_POWER) for k in range(XN)],
-    )
+    coeff = assembled(at_x.reshape(1), [blocks[k].astype(F32) for k in range(XN)])
 
     ortho = lax.dot_general(
         range_rows, inverse, (((1,), (1,)), ((), ())), precision=HIGHEST

time: 211 us -> 201 us (0.953)
  the two profiles are of different devices: /device:TPU:32 before, /device:TPU:4 now
where the time goes in v7:
time: 201 us
  blocking collectives  89.9 us (45%)
  starting transfers between devices  65 us (32%)
  Pallas kernels  26.7 us (13%)
  waiting for transfers between devices  10.6 us (5%)
  local copies, waits for them, and re-layouts  3.57 us (2%)
    all_to_all x1, blocking collectives, per_device(): lax.all_to_all(jnp.concatenate([own, tag], axis=2), 'exp', 0, 0, axis_ind...  29.4 us
    all_to_all x1, blocking collectives, per_device(): lax.all_to_all(jnp.concatenate([weighted.reshape(FN, piece, ff), freq_sum...  26 us
    ppermute x6, starting transfers between devices, along_x(): lax.ppermute(blocks[k], 'grp', ALONG_X[k])  19.6 us
    all_to_all x1, blocking collectives, per_device(): lax.all_to_all(jnp.broadcast_to(load, (YN * NN, FN * piece, wide)), 'exp'...  19.4 us
    pallas_call x1, Pallas kernels, inverse_factor(): pl.pallas_call(inverse_factor_kernel, out_shape=jax.ShapeDtypeStruct((n,...  17.3 us
    all_to_all x1, blocking collectives, per_device(): lax.all_to_all(jnp.broadcast_to(load, (FN, piece, wide)), 'exp', 0, 0, ax...  15.2 us
    ppermute x3, starting transfers between devices, per_device(): lax.ppermute(gram, 'grp', ALONG_X[k])  9.82 us
    ppermute x3, starting transfers between devices, per_device(): blocks[k] = lax.ppermute(block, 'grp', ALONG_X[k])  9.82 us
  transfers between devices with their start and end apart: 16, of which 6 were waited for; matrix products, arithmetic and copies ran while one was open for 1% of the time, Pallas kernels for 10%

profile of v7, /device:TPU:4, one launch (start us, length us, event | category | flops | bytes accessed | tf_op | source)
XLA Modules:
  0.0 200.6 jit_solution(14770643384218018388)
XLA Ops:
  3.1 29.4 %all_to_all.20 = bf16[16,32,1664]{2,1,0:T(8,128)(2,1)S(1)} all-to-all(bf16[16,32,1664]{2,1,0:T(8,128)(2,1)S(1)} %pad_maximum_fusion), channel_id=1, replica_groups={{0,2,16,18,32,34,48,50,1,3,17,19,33,35,49,51},{4,6,20,22,36,38,52,54,5,..., dimensions={0} | all-to-all | bytes 3407872 | tf_op jit(solution)/shard_map/all_to_all | solution.py:284
  34.3 26.0 %all_to_all.21 = f32[4,8,1664]{2,1,0:T(8,128)S(1)} all-to-all(f32[4,8,1664]{2,1,0:T(8,128)S(1)} %concatenate.10), channel_id=1, replica_groups={{0,4,8,12},{1,5,9,13},{2,6,10,14},{3,7,11,15},{16,20,24,28},{17,21,25,2..., dimensions={0} | all-to-all | bytes 425984 | tf_op jit(solution)/shard_map/all_to_all | solution.py:291
  61.2 15.2 %all_to_all.22 = bf16[4,8,2304]{2,1,0:T(8,128)(2,1)S(1)} all-to-all(bf16[4,8,2304]{2,1,0:T(8,128)(2,1)S(1)} %broadcast_in_dim.23), channel_id=1, replica_groups={{0,4,8,12},{1,5,9,13},{2,6,10,14},{3,7,11,15},{16,20,24,28},{17,21,25,2..., dimensions={0} | all-to-all | bytes 294912 | tf_op jit(solution)/shard_map/all_to_all | solution.py:302
  76.4 19.4 %all_to_all.23 = bf16[8,32,2304]{2,1,0:T(8,128)(2,1)S(1)} all-to-all(bf16[8,32,2304]{2,1,0:T(8,128)(2,1)S(1)} %broadcast_in_dim.24), channel_id=1, replica_groups={{0,2,16,18,32,34,48,50},{1,3,17,19,33,35,49,51},{4,6,20,22,36,38,52,54}..., dimensions={0} | all-to-all | bytes 2359296 | tf_op jit(solution)/shard_map/all_to_all | solution.py:305
  97.8 2.8 %collective-permute-done.other_ref = bf16[256,2304]{1,0:T(8,128)(2,1)} collective-permute-done((bf16[256,2304]{1,0:T(8,128)(2,1)S(1)}, bf16[256,2304]{1,0:T(8,128)(2,1)}, u32[]{:S(2)}, u32[]{:S(2)}) %collective-permute-start) | collective-permute-done | bytes 1179680 | tf_op jit(solution)/shard_map/ppermute | solution.py:309
  100.7 4.3 %first_products.1 = (f32[4,160,384]{2,1,0:T(8,128)S(1)}, f32[512,256]{1,0:T(8,128)S(1)}) custom-call(s32[2]{0:T(128)S(1)} %pad_add_fusion.place_ref, bf16[256,2304]{1,0:T(8,128)(2,1)S(1)} %bitcast.47, bf16[256,2304]{1,0:T(8,128)(2,1)} %collective-permute-done.other_ref, bf16[512,1536]{1,0:T(8,128)(2,1)S(1)} %bitcast.44, bf16[1536,256]{1,0:T(8,128)(2,1)S(1)} %copy-done), custom_call_target="tpu_custom_call" | custom-call | flops 3000000000 | bytes 1024 | tf_op jit(solution)/shard_map/first_products/pallas_call | solution.py:175
  105.0 2.4 %collective-permute-start.1 = (f32[160,384]{1,0:T(8,128)S(1)}, f32[160,384]{1,0:T(8,128)S(1)}, u32[]{:S(2)}, u32[]{:S(2)}) collective-permute-start(f32[160,384]{1,0:T(8,128)S(1)} %get-tuple-element.27), channel_id=1, source_target_pairs={{0,128},{64,192},{128,0},{192,64},{256,384},{320,448},{384,256},{4... | collective-permute-start | bytes 737288 | tf_op jit(solution)/shard_map/ppermute | solution.py:315
  107.5 4.0 %collective-permute-start.3 = (f32[160,384]{1,0:T(8,128)S(1)}, f32[160,384]{1,0:T(8,128)S(1)}, u32[]{:S(2)}, u32[]{:S(2)}) collective-permute-start(f32[160,384]{1,0:T(8,128)S(1)} %get-tuple-element.28), channel_id=1, source_target_pairs={{0,64},{64,0},{128,192},{192,128},{256,320},{320,256},{384,448},{4... | collective-permute-start | bytes 737288 | tf_op jit(solution)/shard_map/ppermute | solution.py:315
  111.5 3.4 %collective-permute-start.2 = (f32[160,384]{1,0:T(8,128)S(1)}, f32[160,384]{1,0:T(8,128)S(1)}, u32[]{:S(2)}, u32[]{:S(2)}) collective-permute-start(f32[160,384]{1,0:T(8,128)S(1)} %get-tuple-element.29), channel_id=1, source_target_pairs={{0,192},{64,128},{128,64},{192,0},{256,448},{320,384},{384,320},{4... | collective-permute-start | bytes 737288 | tf_op jit(solution)/shard_map/ppermute | solution.py:315
  114.9 3.0 %second_products.1 = f32[4,128,384]{2,1,0:T(8,128)S(1)} custom-call(s32[2]{0:T(128)S(1)} %pad_add_fusion.place_ref, bf16[256,2304]{1,0:T(8,128)(2,1)S(1)} %bitcast.48, bf16[256,2304]{1,0:T(8,128)(2,1)} %collective-permute-done.other_ref, bf16[512,1536]{1,0:T(8,128)(2,1)S(1)} %bitcast.45, f32[512,256]{1,0:T(8,128)S(1)} %get-tuple-element.14.range_ref), custom_call_target="tpu_custom_call" | custom-call | flops 2000000000 | bytes 1024 | tf_op jit(solution)/shard_map/second_products/pallas_call | solution.py:204
  117.9 3.1 %collective-permute-start.11 = (f32[128,384]{1,0:T(8,128)S(1)}, f32[128,384]{1,0:T(8,128)S(1)}, u32[]{:S(2)}, u32[]{:S(2)}) collective-permute-start(f32[128,384]{1,0:T(8,128)S(1)} %get-tuple-element.30), channel_id=1, source_target_pairs={{0,64},{64,0},{128,192},{192,128},{256,320},{320,256},{384,448},{4... | collective-permute-start | bytes 589832 | tf_op jit(solution)/shard_map/ppermute | solution.py:315
  123.0 4.8 %collective-permute-start.9 = (f32[128,384]{1,0:T(8,128)S(1)}, f32[128,384]{1,0:T(8,128)S(1)}, u32[]{:S(2)}, u32[]{:S(2)}) collective-permute-start(f32[128,384]{1,0:T(8,128)S(1)} %get-tuple-element.32), channel_id=1, source_target_pairs={{0,128},{64,192},{128,0},{192,64},{256,384},{320,448},{384,256},{4... | collective-permute-start | bytes 589832 | tf_op jit(solution)/shard_map/ppermute | solution.py:315
  127.9 8.2 %collective-permute-start.4 = (f32[32,384]{1,0:T(8,128)S(1)}, f32[32,384]{1,0:T(8,128)S(1)}, u32[]{:S(2)}, u32[]{:S(2)}) collective-permute-start(f32[32,384]{1,0:T(8,128)S(1)} %slice.65), channel_id=1, source_target_pairs={{0,256},{64,320},{128,384},{192,448},{256,0},{320,64},{384,128},{4... | collective-permute-start | bytes 147464 | tf_op jit(solution)/shard_map/ppermute | solution.py:323
  136.1 6.3 %collective-permute-start.8 = (f32[128,384]{1,0:T(8,128)S(1)}, f32[128,384]{1,0:T(8,128)S(1)}, u32[]{:S(2)}, u32[]{:S(2)}) collective-permute-start(f32[128,384]{1,0:T(8,128)S(1)} %slice.66.refs_0_), channel_id=1, source_target_pairs={{0,256},{64,320},{128,384},{192,448},{256,0},{320,64},{384,128},{4... | collective-permute-start | bytes 589832 | tf_op jit(solution)/shard_map/ppermute | solution.py:326
  142.8 9.3 %collective-permute-start.12 = (f32[128,384]{1,0:T(8,128)S(1)}, f32[128,384]{1,0:T(8,128)S(1)}, u32[]{:S(2)}, u32[]{:S(2)}) collective-permute-start(f32[128,384]{1,0:T(8,128)S(1)} %add_add_fusion.refs_2_), channel_id=1, source_target_pairs={{0,256},{64,320},{128,384},{192,448},{256,0},{320,64},{384,128},{4... | collective-permute-start | bytes 589832 | tf_op jit(solution)/shard_map/ppermute | solution.py:327
  152.1 2.4 %collective-permute-start.7 = (f32[32,384]{1,0:T(8,128)S(1)}, f32[32,384]{1,0:T(8,128)S(1)}, u32[]{:S(2)}, u32[]{:S(2)}) collective-permute-start(f32[32,384]{1,0:T(8,128)S(1)} %slice_add_fusion.own_ref), channel_id=1, source_target_pairs={{0,192},{64,128},{128,64},{192,0},{256,448},{320,384},{384,320},{4... | collective-permute-start | bytes 147464 | tf_op jit(solution)/shard_map/ppermute | solution.py:330
  154.6 4.6 %collective-permute-start.6 = (f32[32,384]{1,0:T(8,128)S(1)}, f32[32,384]{1,0:T(8,128)S(1)}, u32[]{:S(2)}, u32[]{:S(2)}) collective-permute-start(f32[32,384]{1,0:T(8,128)S(1)} %slice_add_fusion.own_ref), channel_id=1, source_target_pairs={{0,128},{64,192},{128,0},{192,64},{256,384},{320,448},{384,256},{4... | collective-permute-start | bytes 147464 | tf_op jit(solution)/shard_map/ppermute | solution.py:330
  159.2 2.7 %collective-permute-start.5 = (f32[32,384]{1,0:T(8,128)S(1)}, f32[32,384]{1,0:T(8,128)S(1)}, u32[]{:S(2)}, u32[]{:S(2)}) collective-permute-start(f32[32,384]{1,0:T(8,128)S(1)} %slice_add_fusion.own_ref), channel_id=1, source_target_pairs={{0,64},{64,0},{128,192},{192,128},{256,320},{320,256},{384,448},{4... | collective-permute-start | bytes 147464 | tf_op jit(solution)/shard_map/ppermute | solution.py:330
  162.1 3.1 %collective-permute-done.5.refs_0_ = f32[32,384]{1,0:T(8,128)S(1)} collective-permute-done((f32[32,384]{1,0:T(8,128)S(1)}, f32[32,384]{1,0:T(8,128)S(1)}, u32[]{:S(2)}, u32[]{:S(2)}) %collective-permute-start.5) | collective-permute-done | bytes 49184 | tf_op jit(solution)/shard_map/ppermute | solution.py:330
  165.2 17.3 %inverse_factor.1.inverse_ref = f32[256,256]{1,0:T(8,128)S(1)} custom-call(s32[1]{0:T(128)} %bitcast.6.place_ref, f32[32,384]{1,0:T(8,128)S(1)} %slice_add_fusion.own_ref, f32[32,384]{1,0:T(8,128)S(1)} %collective-permute-done.5.refs_0_, f32[32,384]{1,0:T(8,128)S(1)} %collective-permute-done.6.refs_1_, f32[32,384]{1,0:T(8,128)S(1)} %collective-permute-done.7.refs_2_), custom_call_target="tpu_custom_call" | custom-call | flops 536870912 | bytes 1024 | tf_op jit(solution)/shard_map/inverse_factor/pallas_call | solution.py:119
  183.5 2.1 %collective-permute-start.15 = (f16[272,384]{1,0:T(8,128)(2,1)S(1)}, f16[272,384]{1,0:T(8,128)(2,1)S(1)}, u32[]{:S(2)}, u32[]{:S(2)}) collective-permute-start(f16[272,384]{1,0:T(8,128)(2,1)S(1)} %convert_element_type.52), channel_id=1, source_target_pairs={{0,192},{64,128},{128,64},{192,0},{256,448},{320,384},{384,320},{4... | collective-permute-start | bytes 626696 | tf_op jit(solution)/shard_map/ppermute | solution.py:337
  185.7 4.6 %collective-permute-start.14 = (f16[272,384]{1,0:T(8,128)(2,1)S(1)}, f16[272,384]{1,0:T(8,128)(2,1)S(1)}, u32[]{:S(2)}, u32[]{:S(2)}) collective-permute-start(f16[272,384]{1,0:T(8,128)(2,1)S(1)} %convert_element_type.52), channel_id=1, source_target_pairs={{0,128},{64,192},{128,0},{192,64},{256,384},{320,448},{384,256},{4... | collective-permute-start | bytes 626696 | tf_op jit(solution)/shard_map/ppermute | solution.py:337
  190.3 3.1 %collective-permute-start.13 = (f16[272,384]{1,0:T(8,128)(2,1)S(1)}, f16[272,384]{1,0:T(8,128)(2,1)S(1)}, u32[]{:S(2)}, u32[]{:S(2)}) collective-permute-start(f16[272,384]{1,0:T(8,128)(2,1)S(1)} %convert_element_type.52), channel_id=1, source_target_pairs={{0,64},{64,0},{128,192},{192,128},{256,320},{320,256},{384,448},{4... | collective-permute-start | bytes 626696 | tf_op jit(solution)/shard_map/ppermute | solution.py:337
  196.7 2.5 %collective-permute-done.13 = f16[272,384]{1,0:T(8,128)(2,1)S(1)} collective-permute-done((f16[272,384]{1,0:T(8,128)(2,1)S(1)}, f16[272,384]{1,0:T(8,128)(2,1)S(1)}, u32[]{:S(2)}, u32[]{:S(2)}) %collective-permute-start.13) | collective-permute-done | bytes 208928 | tf_op jit(solution)/shard_map/ppermute | solution.py:337
  (51 shorter events, 14.5 us)
Async XLA Ops:
  32.5 28.0 %copy-start = (bf16[1536,256]{1,0:T(8,128)(2,1)S(1)}, bf16[1536,256]{1,0:T(8,128)(2,1)}, u32[]{:S(2)}) copy-start(bf16[1536,256]{1,0:T(8,128)(2,1)} %sketch_ref.1) | copy-start | bytes 2359300
  60.5 0.6 copy-start.1
  95.8 4.9 %collective-permute-start = (bf16[256,2304]{1,0:T(8,128)(2,1)S(1)}, bf16[256,2304]{1,0:T(8,128)(2,1)}, u32[]{:S(2)}, u32[]{:S(2)}) collective-permute-start(bf16[256,2304]{1,0:T(8,128)(2,1)S(1)} %bitcast.46), channel_id=1, source_target_pairs={{0,1},{1,0},{2,3},{3,2},{4,5},{5,4},{6,7},{7,6},{8,9},{9,8},{10,11... | collective-permute-start | bytes 3538952 | tf_op jit(solution)/shard_map/ppermute | solution.py:309
  105.0 17.9 %collective-permute-start.1 = (f32[160,384]{1,0:T(8,128)S(1)}, f32[160,384]{1,0:T(8,128)S(1)}, u32[]{:S(2)}, u32[]{:S(2)}) collective-permute-start(f32[160,384]{1,0:T(8,128)S(1)} %get-tuple-element.27), channel_id=1, source_target_pairs={{0,128},{64,192},{128,0},{192,64},{256,384},{320,448},{384,256},{4... | collective-permute-start | bytes 737288 | tf_op jit(solution)/shard_map/ppermute | solution.py:315
  107.5 20.3 %collective-permute-start.3 = (f32[160,384]{1,0:T(8,128)S(1)}, f32[160,384]{1,0:T(8,128)S(1)}, u32[]{:S(2)}, u32[]{:S(2)}) collective-permute-start(f32[160,384]{1,0:T(8,128)S(1)} %get-tuple-element.28), channel_id=1, source_target_pairs={{0,64},{64,0},{128,192},{192,128},{256,320},{320,256},{384,448},{4... | collective-permute-start | bytes 737288 | tf_op jit(solution)/shard_map/ppermute | solution.py:315
  111.5 16.3 %collective-permute-start.2 = (f32[160,384]{1,0:T(8,128)S(1)}, f32[160,384]{1,0:T(8,128)S(1)}, u32[]{:S(2)}, u32[]{:S(2)}) collective-permute-start(f32[160,384]{1,0:T(8,128)S(1)} %get-tuple-element.29), channel_id=1, source_target_pairs={{0,192},{64,128},{128,64},{192,0},{256,448},{320,384},{384,320},{4... | collective-permute-start | bytes 737288 | tf_op jit(solution)/shard_map/ppermute | solution.py:315
  117.9 24.5 %collective-permute-start.11 = (f32[128,384]{1,0:T(8,128)S(1)}, f32[128,384]{1,0:T(8,128)S(1)}, u32[]{:S(2)}, u32[]{:S(2)}) collective-permute-start(f32[128,384]{1,0:T(8,128)S(1)} %get-tuple-element.30), channel_id=1, source_target_pairs={{0,64},{64,0},{128,192},{192,128},{256,320},{320,256},{384,448},{4... | collective-permute-start | bytes 589832 | tf_op jit(solution)/shard_map/ppermute | solution.py:315
  121.0 21.4 %collective-permute-start.10 = (f32[128,384]{1,0:T(8,128)S(1)}, f32[128,384]{1,0:T(8,128)S(1)}, u32[]{:S(2)}, u32[]{:S(2)}) collective-permute-start(f32[128,384]{1,0:T(8,128)S(1)} %get-tuple-element.31), channel_id=1, source_target_pairs={{0,192},{64,128},{128,64},{192,0},{256,448},{320,384},{384,320},{4... | collective-permute-start | bytes 589832 | tf_op jit(solution)/shard_map/ppermute | solution.py:315
  123.0 19.5 %collective-permute-start.9 = (f32[128,384]{1,0:T(8,128)S(1)}, f32[128,384]{1,0:T(8,128)S(1)}, u32[]{:S(2)}, u32[]{:S(2)}) collective-permute-start(f32[128,384]{1,0:T(8,128)S(1)} %get-tuple-element.32), channel_id=1, source_target_pairs={{0,128},{64,192},{128,0},{192,64},{256,384},{320,448},{384,256},{4... | collective-permute-start | bytes 589832 | tf_op jit(solution)/shard_map/ppermute | solution.py:315
  127.9 14.9 %collective-permute-start.4 = (f32[32,384]{1,0:T(8,128)S(1)}, f32[32,384]{1,0:T(8,128)S(1)}, u32[]{:S(2)}, u32[]{:S(2)}) collective-permute-start(f32[32,384]{1,0:T(8,128)S(1)} %slice.65), channel_id=1, source_target_pairs={{0,256},{64,320},{128,384},{192,448},{256,0},{320,64},{384,128},{4... | collective-permute-start | bytes 147464 | tf_op jit(solution)/shard_map/ppermute | solution.py:323
  136.1 46.4 %collective-permute-start.8 = (f32[128,384]{1,0:T(8,128)S(1)}, f32[128,384]{1,0:T(8,128)S(1)}, u32[]{:S(2)}, u32[]{:S(2)}) collective-permute-start(f32[128,384]{1,0:T(8,128)S(1)} %slice.66.refs_0_), channel_id=1, source_target_pairs={{0,256},{64,320},{128,384},{192,448},{256,0},{320,64},{384,128},{4... | collective-permute-start | bytes 589832 | tf_op jit(solution)/shard_map/ppermute | solution.py:326
  142.8 39.7 %collective-permute-start.12 = (f32[128,384]{1,0:T(8,128)S(1)}, f32[128,384]{1,0:T(8,128)S(1)}, u32[]{:S(2)}, u32[]{:S(2)}) collective-permute-start(f32[128,384]{1,0:T(8,128)S(1)} %add_add_fusion.refs_2_), channel_id=1, source_target_pairs={{0,256},{64,320},{128,384},{192,448},{256,0},{320,64},{384,128},{4... | collective-permute-start | bytes 589832 | tf_op jit(solution)/shard_map/ppermute | solution.py:327
  152.1 9.8 %collective-permute-start.7 = (f32[32,384]{1,0:T(8,128)S(1)}, f32[32,384]{1,0:T(8,128)S(1)}, u32[]{:S(2)}, u32[]{:S(2)}) collective-permute-start(f32[32,384]{1,0:T(8,128)S(1)} %slice_add_fusion.own_ref), channel_id=1, source_target_pairs={{0,192},{64,128},{128,64},{192,0},{256,448},{320,384},{384,320},{4... | collective-permute-start | bytes 147464 | tf_op jit(solution)/shard_map/ppermute | solution.py:330
  154.6 7.5 %collective-permute-start.6 = (f32[32,384]{1,0:T(8,128)S(1)}, f32[32,384]{1,0:T(8,128)S(1)}, u32[]{:S(2)}, u32[]{:S(2)}) collective-permute-start(f32[32,384]{1,0:T(8,128)S(1)} %slice_add_fusion.own_ref), channel_id=1, source_target_pairs={{0,128},{64,192},{128,0},{192,64},{256,384},{320,448},{384,256},{4... | collective-permute-start | bytes 147464 | tf_op jit(solution)/shard_map/ppermute | solution.py:330
  159.2 6.0 %collective-permute-start.5 = (f32[32,384]{1,0:T(8,128)S(1)}, f32[32,384]{1,0:T(8,128)S(1)}, u32[]{:S(2)}, u32[]{:S(2)}) collective-permute-start(f32[32,384]{1,0:T(8,128)S(1)} %slice_add_fusion.own_ref), channel_id=1, source_target_pairs={{0,64},{64,0},{128,192},{192,128},{256,320},{320,256},{384,448},{4... | collective-permute-start | bytes 147464 | tf_op jit(solution)/shard_map/ppermute | solution.py:330
  183.5 11.4 %collective-permute-start.15 = (f16[272,384]{1,0:T(8,128)(2,1)S(1)}, f16[272,384]{1,0:T(8,128)(2,1)S(1)}, u32[]{:S(2)}, u32[]{:S(2)}) collective-permute-start(f16[272,384]{1,0:T(8,128)(2,1)S(1)} %convert_element_type.52), channel_id=1, source_target_pairs={{0,192},{64,128},{128,64},{192,0},{256,448},{320,384},{384,320},{4... | collective-permute-start | bytes 626696 | tf_op jit(solution)/shard_map/ppermute | solution.py:337
  185.7 11.0 %collective-permute-start.14 = (f16[272,384]{1,0:T(8,128)(2,1)S(1)}, f16[272,384]{1,0:T(8,128)(2,1)S(1)}, u32[]{:S(2)}, u32[]{:S(2)}) collective-permute-start(f16[272,384]{1,0:T(8,128)(2,1)S(1)} %convert_element_type.52), channel_id=1, source_target_pairs={{0,128},{64,192},{128,0},{192,64},{256,384},{320,448},{384,256},{4... | collective-permute-start | bytes 626696 | tf_op jit(solution)/shard_map/ppermute | solution.py:337
  190.3 9.0 %collective-permute-start.13 = (f16[272,384]{1,0:T(8,128)(2,1)S(1)}, f16[272,384]{1,0:T(8,128)(2,1)S(1)}, u32[]{:S(2)}, u32[]{:S(2)}) collective-permute-start(f16[272,384]{1,0:T(8,128)(2,1)S(1)} %convert_element_type.52), channel_id=1, source_target_pairs={{0,64},{64,0},{128,192},{192,128},{256,320},{320,256},{384,448},{4... | collective-permute-start | bytes 626696 | tf_op jit(solution)/shard_map/ppermute | solution.py:337

commit v8 on v7

--- a/solution.py
+++ b/solution.py
@@ -32,9 +32,10 @@
 OTHER_HALF = [(i, i ^ 4) for i in range(8)]
 ALONG_X = [[(i, i ^ k) for i in range(8)] for k in range(XN)]
 
-PANEL = 64
+PANEL, STEP = 64, 8
 TOP_POWER = 13
 FACTOR_COST = 2**29
+FIRST = 64
 
 
 def parts_of(value):
@@ -49,28 +50,45 @@
     return jnp.where(row == col, 1.0, 0.0).astype(F32)
 
 
-def inverse_root(value):
-    guess = lax.rsqrt(value)
-    return guess * (1.5 - 0.5 * value * guess * guess)
-
-
 def inverse_factor_of_panel(square):
     n = square.shape[0]
     work = jnp.concatenate([square, eye(n)], axis=1)
-    row = lax.broadcasted_iota(jnp.int32, work.shape, 0)
-    for j in range(0, n, 2):
-        left = jnp.broadcast_to(work[:, j : j + 1], work.shape)
-        right = jnp.broadcast_to(work[:, j + 1 : j + 2], work.shape)
-        scale = inverse_root(left[j : j + 1])
-        cross = left[j + 1 : j + 2] * scale
-        scale_next = inverse_root(right[j + 1 : j + 2] - cross * cross)
-        top = work[j : j + 1] * scale
-        low = (work[j + 1 : j + 2] - cross * top) * scale_next
-        left = left * scale
-        right = (right - left * cross) * scale_next
-        rest = jnp.where(row > j + 1, work - left * top - right * low, work)
-        work = jnp.where(row == j, top, jnp.where(row == j + 1, low, rest))
-    return work[:, n:]
+    tiles = [work[t : t + STEP] for t in range(0, n, STEP)]
+    row = lax.broadcasted_iota(jnp.int32, tiles[0].shape, 0)
+    for t in range(n // STEP):
+        columns = {
+            u: [
+                jnp.broadcast_to(tiles[u][:, t * STEP + s :][:, :1], tiles[u].shape)
+                for s in range(STEP)
+            ]
+            for u in range(t, n // STEP)
+        }
+        lower, scale, done = {}, [], []
+        for s in range(STEP):
+            pivot = columns[t][s][s : s + 1]
+            for m in range(s):
+                pivot = pivot - lower[s, m] * lower[s, m]
+            scale.append(lax.rsqrt(pivot))
+            for q in range(s + 1, STEP):
+                entry = columns[t][s][q : q + 1]
+                for m in range(s):
+                    entry = entry - lower[q, m] * lower[s, m]
+                lower[q, s] = entry * scale[s]
+            line = tiles[t][s : s + 1]
+            for m in range(s):
+                line = line - lower[s, m] * done[m]
+            done.append(line * scale[s])
+        for u in range(t + 1, n // STEP):
+            factors = []
+            for s in range(STEP):
+                factor = columns[u][s]
+                for m in range(s):
+                    factor = factor - factors[m] * lower[s, m]
+                factors.append(factor * scale[s])
+                tiles[u] = tiles[u] - factors[s] * done[s]
+        for s in range(STEP):
+            tiles[t] = jnp.where(row == s, done[s], tiles[t])
+    return jnp.concatenate(tiles, axis=0)[:, n:]
 
 
 def inverse_factor_kernel(place_ref, own_ref, *refs):
@@ -139,13 +157,13 @@
     return total
 
 
-def first_products_kernel(place_ref, mine_ref, other_ref, own_ref, sketch_ref, out_ref, range_ref):
+def products_kernel(place_ref, mine_ref, other_ref, own_ref, sketch_ref, out_ref, range_ref):
     half = mine_ref.shape[0]
     ff, rank = sketch_ref.shape
-    block, slab, chunk = rank // XN, ff // XN, rank // 2
+    block, slab = rank // XN, ff // XN
     core, x = place_ref[0], place_ref[1]
     gram = jnp.zeros((rank, rank), F32)
-    delta = jnp.zeros((chunk, ff), F32)
+    delta = jnp.zeros((rank, ff), F32)
     for load_ref, at_core in ((mine_ref, core), (other_ref, 1 - core)):
         rows = pl.ds(pl.multiple_of(at_core * half, half), half)
         own = own_ref[rows, :]
@@ -158,7 +176,7 @@
         range_ref[rows, :] = range_rows
         turned = range_rows.T
         gram += jnp.dot(turned, range_rows, precision=HIGHEST, preferred_element_type=F32)
-        delta += range_product(turned[:chunk], own, load_ref[:, :ff])
+        delta += range_product(turned, own, load_ref[:, :ff])
     for b in range(XN):
         mine = gram[b * block : (b + 1) * block]
         kept = jnp.concatenate(
@@ -169,76 +187,51 @@
         out_ref[b ^ x, block // 2 :, :] = delta[:, b * slab : (b + 1) * slab]
 
 
-def first_products(place, mine, other, own, sketch):
+def products(place, mine, other, own, sketch):
     rows, ff = own.shape
     rank = sketch.shape[1]
     return pl.pallas_call(
-        first_products_kernel,
+        products_kernel,
         out_shape=(
-            jax.ShapeDtypeStruct((XN, rank // XN // 2 + rank // 2, ff // XN), F32),
+            jax.ShapeDtypeStruct((XN, rank // XN // 2 + rank, ff // XN), F32),
             jax.ShapeDtypeStruct((rows, rank), F32),
         ),
         in_specs=[SMEM] + [VMEM] * 4,
         out_specs=(VMEM, VMEM),
         compiler_params=pltpu.CompilerParams(vmem_limit_bytes=40 * MIB),
-        cost_estimate=pl.CostEstimate(flops=3 * 10**9, bytes_accessed=2**10, transcendentals=0),
-        name="first_products",
+        cost_estimate=pl.CostEstimate(flops=5 * 10**9, bytes_accessed=2**10, transcendentals=0),
+        name="products",
     )(place, mine, other, own, sketch)
 
 
-def second_products_kernel(place_ref, mine_ref, other_ref, own_ref, range_ref, out_ref):
-    half = mine_ref.shape[0]
-    ff, rank = own_ref.shape[1], range_ref.shape[1]
-    slab, chunk = ff // XN, rank // 2
-    core, x = place_ref[0], place_ref[1]
-    delta = jnp.zeros((chunk, ff), F32)
-    for load_ref, at_core in ((mine_ref, core), (other_ref, 1 - core)):
-        rows = pl.ds(pl.multiple_of(at_core * half, half), half)
-        delta += range_product(range_ref[rows, chunk:].T, own_ref[rows, :], load_ref[:, :ff])
-    for b in range(XN):
-        out_ref[b ^ x] = delta[:, b * slab : (b + 1) * slab]
-
-
-def second_products(place, mine, other, own, range_rows):
-    ff, rank = own.shape[1], range_rows.shape[1]
-    return pl.pallas_call(
-        second_products_kernel,
-        out_shape=jax.ShapeDtypeStruct((XN, rank // 2, ff // XN), F32),
-        in_specs=[SMEM] + [VMEM] * 4,
-        out_specs=VMEM,
-        compiler_params=pltpu.CompilerParams(vmem_limit_bytes=40 * MIB),
-        cost_estimate=pl.CostEstimate(flops=2 * 10**9, bytes_accessed=2**10, transcendentals=0),
-        name="second_products",
-    )(place, mine, other, own, range_rows)
-
-
 def finished_kernel(inverse_ref, *refs):
-    out_ref = refs[-1]
+    pairs, (out_ref, sums_ref) = refs[:-2], refs[-2:]
     rank = inverse_ref.shape[0]
-    chunk = rank // 2
-    values = sum(
-        jnp.dot(
-            inverse_ref[:, i * chunk : (i + 1) * chunk], refs[2 * i][...] + refs[2 * i + 1][...],
-            precision=HIGHEST, preferred_element_type=F32,
-        )
-        for i in range(2)
-    )
-    top = jnp.max(jnp.max(jnp.abs(values), axis=0, keepdims=True), axis=1, keepdims=True)
-    power = jnp.floor(jnp.log(jnp.maximum(top, 1e-30)) * (1 / math.log(2)))
+    top = 0
+    for i in range(0, len(pairs), 2):
+        end = top + pairs[i].shape[0]
+        sums_ref[top:end] = pairs[i][...] + pairs[i + 1][...]
+        top = end
+    values = jnp.dot(
+        inverse_ref[...], sums_ref[...], precision=HIGHEST, preferred_element_type=F32
+    )
+    most = jnp.max(jnp.max(jnp.abs(values), axis=0, keepdims=True), axis=1, keepdims=True)
+    power = jnp.floor(jnp.log(jnp.maximum(most, 1e-30)) * (1 / math.log(2)))
     out_ref[:rank] = values * jnp.exp2(TOP_POWER - power)
     out_ref[rank:] = jnp.broadcast_to(power, (out_ref.shape[0] - rank, out_ref.shape[1]))
 
 
-def finished(inverse, chunks):
-    rank, slab = inverse.shape[0], chunks[0].shape[1]
+def finished(inverse, pairs):
+    rank, slab = inverse.shape[0], pairs[0].shape[1]
     return pl.pallas_call(
         finished_kernel,
         out_shape=jax.ShapeDtypeStruct((rank + 16, slab), F32),
-        in_specs=[VMEM] * (1 + len(chunks)),
+        in_specs=[VMEM] * (1 + len(pairs)),
         out_specs=VMEM,
+        scratch_shapes=[pltpu.VMEM((rank, slab), F32)],
         compiler_params=pltpu.CompilerParams(vmem_limit_bytes=16 * MIB),
         name="finished",
-    )(inverse, *chunks)
+    )(inverse, *pairs)
 
 
 def assembled_kernel(place_ref, *refs):
@@ -311,27 +304,21 @@
     at_core, at_x = lax.axis_index("exp") % CN, lax.axis_index("grp") % XN
     place, own = jnp.stack([at_core, at_x]), own.reshape(rows, ff)
 
-    def along_x(blocks):
-        return [blocks[0]] + [lax.ppermute(blocks[k], "grp", ALONG_X[k]) for k in (2, 3, 1)]
-
-    first, range_rows = first_products(place, load, other, own, sketch)
-    first = along_x(first)
-    second = along_x(second_products(place, load, other, own, range_rows))
-    first = sum(first)
+    blocks, range_rows = products(place, load, other, own, sketch)
+    total = blocks[0] + sum(lax.ppermute(blocks[k], "grp", ALONG_X[k]) for k in (2, 3, 1))
     packed = rank // XN // 2
-    gram, first = first[:packed], first[packed:]
-    gram_came = lax.ppermute(gram, "grp", OTHER_HALF)
-    _, second = lax.optimization_barrier((gram_came, second))
-    gram, second = gram + gram_came, sum(second)
-    chunks = [first, lax.ppermute(first, "grp", OTHER_HALF)]
-    chunks += [second, lax.ppermute(second, "grp", OTHER_HALF)]
+    first, second = total[: packed + FIRST], total[packed + FIRST :]
+    first_came = lax.ppermute(first, "grp", OTHER_HALF)
+    second_came = lax.ppermute(second, "grp", OTHER_HALF)
+    gram = first[:packed] + first_came[:packed]
     inverse = inverse_factor(
         at_x.reshape(1),
         [gram] + [lax.ppermute(gram, "grp", ALONG_X[k]) for k in (1, 2, 3)],
         rank,
     )
-    inverse, chunks = lax.optimization_barrier((inverse, chunks))
-    block = lax.optimization_barrier(finished(inverse, chunks).astype(jnp.float16))
+    pairs = [first[packed:], first_came[packed:], second, second_came]
+    inverse, pairs = lax.optimization_barrier((inverse, pairs))
+    block = lax.optimization_barrier(finished(inverse, pairs).astype(jnp.float16))
     blocks = {0: block}
     for k in (2, 3, 1):
         blocks[k] = lax.ppermute(block, "grp", ALONG_X[k])

time: 201 us -> 218 us (1.085)
  the two profiles are of different devices: /device:TPU:4 before, /device:TPU:32 now
where the time goes in v8:
time: 218 us; the launch traced here: 217 us
  blocking collectives  88.7 us (41%)
  waiting for transfers between devices  57.2 us (26%)
  starting transfers between devices  46.5 us (21%)
  Pallas kernels  16.7 us (8%)
  local copies, waits for them, and re-layouts  3.58 us (2%)
    all_to_all x1, blocking collectives, per_device(): lax.all_to_all(jnp.concatenate([own, tag], axis=2), 'exp', 0, 0, axis_ind...  30.3 us
    ppermute x1, waiting for transfers between devices, per_device(): first_came = lax.ppermute(first, 'grp', OTHER_HALF)  29.5 us
    all_to_all x1, blocking collectives, per_device(): lax.all_to_all(jnp.broadcast_to(load, (YN * NN, FN * piece, wide)), 'exp'...  20.4 us
    all_to_all x1, blocking collectives, per_device(): lax.all_to_all(jnp.concatenate([weighted.reshape(FN, piece, ff), freq_sum...  20 us
    all_to_all x1, blocking collectives, per_device(): lax.all_to_all(jnp.broadcast_to(load, (FN, piece, wide)), 'exp', 0, 0, ax...  18 us
    ppermute x3, waiting for transfers between devices, per_device(): lax.ppermute(blocks[k], 'grp', ALONG_X[k])  17.5 us
    ppermute x3, starting transfers between devices, per_device(): lax.ppermute(blocks[k], 'grp', ALONG_X[k])  10.4 us
    ppermute x3, starting transfers between devices, per_device(): lax.ppermute(gram, 'grp', ALONG_X[k])  9.82 us
  transfers between devices with their start and end apart: 12, of which 10 were waited for; matrix products, arithmetic and copies ran while one was open for 1% of the time, Pallas kernels for 4%

profile of v8, /device:TPU:32, one launch (start us, length us, event | category | flops | bytes accessed | tf_op | source)
XLA Modules:
  0.0 217.5 jit_solution(10895144972813075513)
XLA Ops:
  3.1 30.3 %all_to_all.20 = bf16[16,32,1664]{2,1,0:T(8,128)(2,1)S(1)} all-to-all(bf16[16,32,1664]{2,1,0:T(8,128)(2,1)S(1)} %pad_maximum_fusion), channel_id=1, replica_groups={{0,2,16,18,32,34,48,50,1,3,17,19,33,35,49,51},{4,6,20,22,36,38,52,54,5,..., dimensions={0} | all-to-all | bytes 3407872 | tf_op jit(solution)/shard_map/all_to_all | solution.py:277
  35.3 20.0 %all_to_all.21 = f32[4,8,1664]{2,1,0:T(8,128)S(1)} all-to-all(f32[4,8,1664]{2,1,0:T(8,128)S(1)} %concatenate.10), channel_id=1, replica_groups={{0,4,8,12},{1,5,9,13},{2,6,10,14},{3,7,11,15},{16,20,24,28},{17,21,25,2..., dimensions={0} | all-to-all | bytes 425984 | tf_op jit(solution)/shard_map/all_to_all | solution.py:284
  56.1 18.0 %all_to_all.22 = bf16[4,8,2304]{2,1,0:T(8,128)(2,1)S(1)} all-to-all(bf16[4,8,2304]{2,1,0:T(8,128)(2,1)S(1)} %broadcast_in_dim.23), channel_id=1, replica_groups={{0,4,8,12},{1,5,9,13},{2,6,10,14},{3,7,11,15},{16,20,24,28},{17,21,25,2..., dimensions={0} | all-to-all | bytes 294912 | tf_op jit(solution)/shard_map/all_to_all | solution.py:295
  74.2 20.4 %all_to_all.23 = bf16[8,32,2304]{2,1,0:T(8,128)(2,1)S(1)} all-to-all(bf16[8,32,2304]{2,1,0:T(8,128)(2,1)S(1)} %broadcast_in_dim.24), channel_id=1, replica_groups={{0,2,16,18,32,34,48,50},{1,3,17,19,33,35,49,51},{4,6,20,22,36,38,52,54}..., dimensions={0} | all-to-all | bytes 2359296 | tf_op jit(solution)/shard_map/all_to_all | solution.py:298
  96.7 2.8 %collective-permute-done.other_ref = bf16[256,2304]{1,0:T(8,128)(2,1)} collective-permute-done((bf16[256,2304]{1,0:T(8,128)(2,1)S(1)}, bf16[256,2304]{1,0:T(8,128)(2,1)}, u32[]{:S(2)}, u32[]{:S(2)}) %collective-permute-start) | collective-permute-done | bytes 1179680 | tf_op jit(solution)/shard_map/ppermute | solution.py:302
  99.5 5.6 %products.1 = (f32[4,288,384]{2,1,0:T(8,128)S(1)}, f32[512,256]{1,0:T(8,128)S(1)}) custom-call(s32[2]{0:T(128)S(1)} %pad_add_fusion.place_ref, bf16[256,2304]{1,0:T(8,128)(2,1)S(1)} %bitcast.34, bf16[256,2304]{1,0:T(8,128)(2,1)} %collective-permute-done.other_ref, bf16[512,1536]{1,0:T(8,128)(2,1)S(1)} %bitcast.32, bf16[1536,256]{1,0:T(8,128)(2,1)S(1)} %copy-done), custom_call_target="tpu_custom_call" | custom-call | flops 5000000000 | bytes 1024 | tf_op jit(solution)/shard_map/products/pallas_call | solution.py:193
  105.2 4.7 %collective-permute-start.2 = (f32[288,384]{1,0:T(8,128)S(1)}, f32[288,384]{1,0:T(8,128)S(1)}, u32[]{:S(2)}, u32[]{:S(2)}) collective-permute-start(f32[288,384]{1,0:T(8,128)S(1)} %get-tuple-element.19), channel_id=1, source_target_pairs={{0,192},{64,128},{128,64},{192,0},{256,448},{320,384},{384,320},{4... | collective-permute-start | bytes 1327112 | tf_op jit(solution)/shard_map/ppermute | solution.py:308
  109.9 2.1 collective-permute-start.3
  112.1 3.6 %collective-permute-start.1 = (f32[288,384]{1,0:T(8,128)S(1)}, f32[288,384]{1,0:T(8,128)S(1)}, u32[]{:S(2)}, u32[]{:S(2)}) collective-permute-start(f32[288,384]{1,0:T(8,128)S(1)} %get-tuple-element.21), channel_id=1, source_target_pairs={{0,128},{64,192},{128,0},{192,64},{256,384},{320,448},{384,256},{4... | collective-permute-start | bytes 1327112 | tf_op jit(solution)/shard_map/ppermute | solution.py:308
  115.7 4.9 %collective-permute-done.2 = f32[288,384]{1,0:T(8,128)S(1)} collective-permute-done((f32[288,384]{1,0:T(8,128)S(1)}, f32[288,384]{1,0:T(8,128)S(1)}, u32[]{:S(2)}, u32[]{:S(2)}) %collective-permute-start.2) | collective-permute-done | bytes 442400 | tf_op jit(solution)/shard_map/ppermute | solution.py:308
  120.6 4.3 %collective-permute-done.3 = f32[288,384]{1,0:T(8,128)S(1)} collective-permute-done((f32[288,384]{1,0:T(8,128)S(1)}, f32[288,384]{1,0:T(8,128)S(1)}, u32[]{:S(2)}, u32[]{:S(2)}) %collective-permute-start.3) | collective-permute-done | bytes 442400 | tf_op jit(solution)/shard_map/ppermute | solution.py:308
  124.9 8.3 %collective-permute-done.1 = f32[288,384]{1,0:T(8,128)S(1)} collective-permute-done((f32[288,384]{1,0:T(8,128)S(1)}, f32[288,384]{1,0:T(8,128)S(1)}, u32[]{:S(2)}, u32[]{:S(2)}) %collective-permute-start.1) | collective-permute-done | bytes 442400 | tf_op jit(solution)/shard_map/ppermute | solution.py:308
  133.3 8.2 %collective-permute-start.4 = (f32[96,384]{1,0:T(8,128)S(1)}, f32[96,384]{1,0:T(8,128)S(1)}, u32[]{:S(2)}, u32[]{:S(2)}) collective-permute-start(f32[96,384]{1,0:T(8,128)S(1)} %slice.68), channel_id=1, source_target_pairs={{0,256},{64,320},{128,384},{192,448},{256,0},{320,64},{384,128},{4... | collective-permute-start | bytes 442376 | tf_op jit(solution)/shard_map/ppermute | solution.py:311
  141.5 6.3 %collective-permute-start.8 = (f32[192,384]{1,0:T(8,128)S(1)}, f32[192,384]{1,0:T(8,128)S(1)}, u32[]{:S(2)}, u32[]{:S(2)}) collective-permute-start(f32[192,384]{1,0:T(8,128)S(1)} %slice.72.refs_2_), channel_id=1, source_target_pairs={{0,256},{64,320},{128,384},{192,448},{256,0},{320,64},{384,128},{4... | collective-permute-start | bytes 884744 | tf_op jit(solution)/shard_map/ppermute | solution.py:312
  147.9 29.5 %collective-permute-done.4 = f32[96,384]{1,0:T(8,128)S(1)} collective-permute-done((f32[96,384]{1,0:T(8,128)S(1)}, f32[96,384]{1,0:T(8,128)S(1)}, u32[]{:S(2)}, u32[]{:S(2)}) %collective-permute-start.4) | collective-permute-done | bytes 147488 | tf_op jit(solution)/shard_map/ppermute | solution.py:311
  177.4 4.6 %collective-permute-start.7 = (f32[32,384]{1,0:T(8,128)S(1)}, f32[32,384]{1,0:T(8,128)S(1)}, u32[]{:S(2)}, u32[]{:S(2)}) collective-permute-start(f32[32,384]{1,0:T(8,128)S(1)} %slice_add_fusion.own_ref), channel_id=1, source_target_pairs={{0,192},{64,128},{128,64},{192,0},{256,448},{320,384},{384,320},{4... | collective-permute-start | bytes 147464 | tf_op jit(solution)/shard_map/ppermute | solution.py:316
  182.0 1.9 collective-permute-start.6
  184.0 3.3 %collective-permute-start.5 = (f32[32,384]{1,0:T(8,128)S(1)}, f32[32,384]{1,0:T(8,128)S(1)}, u32[]{:S(2)}, u32[]{:S(2)}) collective-permute-start(f32[32,384]{1,0:T(8,128)S(1)} %slice_add_fusion.own_ref), channel_id=1, source_target_pairs={{0,64},{64,0},{128,192},{192,128},{256,320},{320,256},{384,448},{4... | collective-permute-start | bytes 147464 | tf_op jit(solution)/shard_map/ppermute | solution.py:316
  187.3 2.4 %collective-permute-done.6.refs_1_ = f32[32,384]{1,0:T(8,128)S(1)} collective-permute-done((f32[32,384]{1,0:T(8,128)S(1)}, f32[32,384]{1,0:T(8,128)S(1)}, u32[]{:S(2)}, u32[]{:S(2)}) %collective-permute-start.6) | collective-permute-done | bytes 49184 | tf_op jit(solution)/shard_map/ppermute | solution.py:316
  189.9 9.2 %inverse_factor.1.inverse_ref = f32[256,256]{1,0:T(8,128)S(1)} custom-call(s32[1]{0:T(128)} %bitcast.6.place_ref, f32[32,384]{1,0:T(8,128)S(1)} %slice_add_fusion.own_ref, f32[32,384]{1,0:T(8,128)S(1)} %collective-permute-done.5.refs_0_, f32[32,384]{1,0:T(8,128)S(1)} %collective-permute-done.6.refs_1_, f32[32,384]{1,0:T(8,128)S(1)} %collective-permute-done.7.refs_2_), custom_call_target="tpu_custom_call" | custom-call | flops 536870912 | bytes 1024 | tf_op jit(solution)/shard_map/inverse_factor/pallas_call | solution.py:137
  199.9 4.0 %collective-permute-start.11 = (f16[272,384]{1,0:T(8,128)(2,1)S(1)}, f16[272,384]{1,0:T(8,128)(2,1)S(1)}, u32[]{:S(2)}, u32[]{:S(2)}) collective-permute-start(f16[272,384]{1,0:T(8,128)(2,1)S(1)} %convert_element_type.52), channel_id=1, source_target_pairs={{0,192},{64,128},{128,64},{192,0},{256,448},{320,384},{384,320},{4... | collective-permute-start | bytes 626696 | tf_op jit(solution)/shard_map/ppermute | solution.py:324
  203.9 3.4 %collective-permute-start.10 = (f16[272,384]{1,0:T(8,128)(2,1)S(1)}, f16[272,384]{1,0:T(8,128)(2,1)S(1)}, u32[]{:S(2)}, u32[]{:S(2)}) collective-permute-start(f16[272,384]{1,0:T(8,128)(2,1)S(1)} %convert_element_type.52), channel_id=1, source_target_pairs={{0,128},{64,192},{128,0},{192,64},{256,384},{320,448},{384,256},{4... | collective-permute-start | bytes 626696 | tf_op jit(solution)/shard_map/ppermute | solution.py:324
  207.3 2.5 %collective-permute-start.9 = (f16[272,384]{1,0:T(8,128)(2,1)S(1)}, f16[272,384]{1,0:T(8,128)(2,1)S(1)}, u32[]{:S(2)}, u32[]{:S(2)}) collective-permute-start(f16[272,384]{1,0:T(8,128)(2,1)S(1)} %convert_element_type.52), channel_id=1, source_target_pairs={{0,64},{64,0},{128,192},{192,128},{256,320},{320,256},{384,448},{4... | collective-permute-start | bytes 626696 | tf_op jit(solution)/shard_map/ppermute | solution.py:324
  211.6 3.4 %collective-permute-done.10 = f16[272,384]{1,0:T(8,128)(2,1)S(1)} collective-permute-done((f16[272,384]{1,0:T(8,128)(2,1)S(1)}, f16[272,384]{1,0:T(8,128)(2,1)S(1)}, u32[]{:S(2)}, u32[]{:S(2)}) %collective-permute-start.10) | collective-permute-done | bytes 208928 | tf_op jit(solution)/shard_map/ppermute | solution.py:324
  (42 shorter events, 11.9 us)
Async XLA Ops:
  33.4 22.1 %copy-start = (bf16[1536,256]{1,0:T(8,128)(2,1)S(1)}, bf16[1536,256]{1,0:T(8,128)(2,1)}, u32[]{:S(2)}) copy-start(bf16[1536,256]{1,0:T(8,128)(2,1)} %sketch_ref.1) | copy-start | bytes 2359300
  55.5 0.6 copy-start.1
  94.6 4.9 %collective-permute-start = (bf16[256,2304]{1,0:T(8,128)(2,1)S(1)}, bf16[256,2304]{1,0:T(8,128)(2,1)}, u32[]{:S(2)}, u32[]{:S(2)}) collective-permute-start(bf16[256,2304]{1,0:T(8,128)(2,1)S(1)} %bitcast.33), channel_id=1, source_target_pairs={{0,1},{1,0},{2,3},{3,2},{4,5},{5,4},{6,7},{7,6},{8,9},{9,8},{10,11... | collective-permute-start | bytes 3538952 | tf_op jit(solution)/shard_map/ppermute | solution.py:302
  105.2 15.3 %collective-permute-start.2 = (f32[288,384]{1,0:T(8,128)S(1)}, f32[288,384]{1,0:T(8,128)S(1)}, u32[]{:S(2)}, u32[]{:S(2)}) collective-permute-start(f32[288,384]{1,0:T(8,128)S(1)} %get-tuple-element.19), channel_id=1, source_target_pairs={{0,192},{64,128},{128,64},{192,0},{256,448},{320,384},{384,320},{4... | collective-permute-start | bytes 1327112 | tf_op jit(solution)/shard_map/ppermute | solution.py:308
  109.9 14.9 %collective-permute-start.3 = (f32[288,384]{1,0:T(8,128)S(1)}, f32[288,384]{1,0:T(8,128)S(1)}, u32[]{:S(2)}, u32[]{:S(2)}) collective-permute-start(f32[288,384]{1,0:T(8,128)S(1)} %get-tuple-element.20), channel_id=1, source_target_pairs={{0,64},{64,0},{128,192},{192,128},{256,320},{320,256},{384,448},{4... | collective-permute-start | bytes 1327112 | tf_op jit(solution)/shard_map/ppermute | solution.py:308
  112.1 21.1 %collective-permute-start.1 = (f32[288,384]{1,0:T(8,128)S(1)}, f32[288,384]{1,0:T(8,128)S(1)}, u32[]{:S(2)}, u32[]{:S(2)}) collective-permute-start(f32[288,384]{1,0:T(8,128)S(1)} %get-tuple-element.21), channel_id=1, source_target_pairs={{0,128},{64,192},{128,0},{192,64},{256,384},{320,448},{384,256},{4... | collective-permute-start | bytes 1327112 | tf_op jit(solution)/shard_map/ppermute | solution.py:308
  133.3 44.1 %collective-permute-start.4 = (f32[96,384]{1,0:T(8,128)S(1)}, f32[96,384]{1,0:T(8,128)S(1)}, u32[]{:S(2)}, u32[]{:S(2)}) collective-permute-start(f32[96,384]{1,0:T(8,128)S(1)} %slice.68), channel_id=1, source_target_pairs={{0,256},{64,320},{128,384},{192,448},{256,0},{320,64},{384,128},{4... | collective-permute-start | bytes 442376 | tf_op jit(solution)/shard_map/ppermute | solution.py:311
  141.5 57.6 %collective-permute-start.8 = (f32[192,384]{1,0:T(8,128)S(1)}, f32[192,384]{1,0:T(8,128)S(1)}, u32[]{:S(2)}, u32[]{:S(2)}) collective-permute-start(f32[192,384]{1,0:T(8,128)S(1)} %slice.72.refs_2_), channel_id=1, source_target_pairs={{0,256},{64,320},{128,384},{192,448},{256,0},{320,64},{384,128},{4... | collective-permute-start | bytes 884744 | tf_op jit(solution)/shard_map/ppermute | solution.py:312
  177.4 9.9 %collective-permute-start.7 = (f32[32,384]{1,0:T(8,128)S(1)}, f32[32,384]{1,0:T(8,128)S(1)}, u32[]{:S(2)}, u32[]{:S(2)}) collective-permute-start(f32[32,384]{1,0:T(8,128)S(1)} %slice_add_fusion.own_ref), channel_id=1, source_target_pairs={{0,192},{64,128},{128,64},{192,0},{256,448},{320,384},{384,320},{4... | collective-permute-start | bytes 147464 | tf_op jit(solution)/shard_map/ppermute | solution.py:316
  182.0 7.7 %collective-permute-start.6 = (f32[32,384]{1,0:T(8,128)S(1)}, f32[32,384]{1,0:T(8,128)S(1)}, u32[]{:S(2)}, u32[]{:S(2)}) collective-permute-start(f32[32,384]{1,0:T(8,128)S(1)} %slice_add_fusion.own_ref), channel_id=1, source_target_pairs={{0,128},{64,192},{128,0},{192,64},{256,384},{320,448},{384,256},{4... | collective-permute-start | bytes 147464 | tf_op jit(solution)/shard_map/ppermute | solution.py:316
  184.0 6.0 %collective-permute-start.5 = (f32[32,384]{1,0:T(8,128)S(1)}, f32[32,384]{1,0:T(8,128)S(1)}, u32[]{:S(2)}, u32[]{:S(2)}) collective-permute-start(f32[32,384]{1,0:T(8,128)S(1)} %slice_add_fusion.own_ref), channel_id=1, source_target_pairs={{0,64},{64,0},{128,192},{192,128},{256,320},{320,256},{384,448},{4... | collective-permute-start | bytes 147464 | tf_op jit(solution)/shard_map/ppermute | solution.py:316
  199.9 11.7 %collective-permute-start.11 = (f16[272,384]{1,0:T(8,128)(2,1)S(1)}, f16[272,384]{1,0:T(8,128)(2,1)S(1)}, u32[]{:S(2)}, u32[]{:S(2)}) collective-permute-start(f16[272,384]{1,0:T(8,128)(2,1)S(1)} %convert_element_type.52), channel_id=1, source_target_pairs={{0,192},{64,128},{128,64},{192,0},{256,448},{320,384},{384,320},{4... | collective-permute-start | bytes 626696 | tf_op jit(solution)/shard_map/ppermute | solution.py:324
  203.9 11.1 %collective-permute-start.10 = (f16[272,384]{1,0:T(8,128)(2,1)S(1)}, f16[272,384]{1,0:T(8,128)(2,1)S(1)}, u32[]{:S(2)}, u32[]{:S(2)}) collective-permute-start(f16[272,384]{1,0:T(8,128)(2,1)S(1)} %convert_element_type.52), channel_id=1, source_target_pairs={{0,128},{64,192},{128,0},{192,64},{256,384},{320,448},{384,256},{4... | collective-permute-start | bytes 626696 | tf_op jit(solution)/shard_map/ppermute | solution.py:324
  207.3 8.8 %collective-permute-start.9 = (f16[272,384]{1,0:T(8,128)(2,1)S(1)}, f16[272,384]{1,0:T(8,128)(2,1)S(1)}, u32[]{:S(2)}, u32[]{:S(2)}) collective-permute-start(f16[272,384]{1,0:T(8,128)(2,1)S(1)} %convert_element_type.52), channel_id=1, source_target_pairs={{0,64},{64,0},{128,192},{192,128},{256,320},{320,256},{384,448},{4... | collective-permute-start | bytes 626696 | tf_op jit(solution)/shard_map/ppermute | solution.py:324

commit v9 on v7

--- a/solution.py
+++ b/solution.py
@@ -30,9 +30,10 @@
 ]
 OTHER_CORE = [(i, i ^ 1) for i in range(64)]
 OTHER_HALF = [(i, i ^ 4) for i in range(8)]
+X_GROUPS = [[h * XN + x for x in range(XN)] for h in range(2)]
 ALONG_X = [[(i, i ^ k) for i in range(8)] for k in range(XN)]
 
-PANEL = 64
+PANEL, STEP = 64, 8
 TOP_POWER = 13
 FACTOR_COST = 2**29
 
@@ -49,52 +50,58 @@
     return jnp.where(row == col, 1.0, 0.0).astype(F32)
 
 
-def inverse_root(value):
-    guess = lax.rsqrt(value)
-    return guess * (1.5 - 0.5 * value * guess * guess)
-
-
 def inverse_factor_of_panel(square):
     n = square.shape[0]
     work = jnp.concatenate([square, eye(n)], axis=1)
-    row = lax.broadcasted_iota(jnp.int32, work.shape, 0)
-    for j in range(0, n, 2):
-        left = jnp.broadcast_to(work[:, j : j + 1], work.shape)
-        right = jnp.broadcast_to(work[:, j + 1 : j + 2], work.shape)
-        scale = inverse_root(left[j : j + 1])
-        cross = left[j + 1 : j + 2] * scale
-        scale_next = inverse_root(right[j + 1 : j + 2] - cross * cross)
-        top = work[j : j + 1] * scale
-        low = (work[j + 1 : j + 2] - cross * top) * scale_next
-        left = left * scale
-        right = (right - left * cross) * scale_next
-        rest = jnp.where(row > j + 1, work - left * top - right * low, work)
-        work = jnp.where(row == j, top, jnp.where(row == j + 1, low, rest))
-    return work[:, n:]
-
-
-def inverse_factor_kernel(place_ref, own_ref, *refs):
-    came_refs, inverse_ref, work_ref = refs[:-2], refs[-2], refs[-1]
+    tiles = [work[t : t + STEP] for t in range(0, n, STEP)]
+    row = lax.broadcasted_iota(jnp.int32, tiles[0].shape, 0)
+    for t in range(n // STEP):
+        columns = {
+            u: [
+                jnp.broadcast_to(tiles[u][:, t * STEP + s :][:, :1], tiles[u].shape)
+                for s in range(STEP)
+            ]
+            for u in range(t, n // STEP)
+        }
+        lower, scale, done = {}, [], []
+        for s in range(STEP):
+            pivot = columns[t][s][s : s + 1]
+            for m in range(s):
+                pivot = pivot - lower[s, m] * lower[s, m]
+            scale.append(lax.rsqrt(pivot))
+            for q in range(s + 1, STEP):
+                entry = columns[t][s][q : q + 1]
+                for m in range(s):
+                    entry = entry - lower[q, m] * lower[s, m]
+                lower[q, s] = entry * scale[s]
+            line = tiles[t][s : s + 1]
+            for m in range(s):
+                line = line - lower[s, m] * done[m]
+            done.append(line * scale[s])
+        for u in range(t + 1, n // STEP):
+            factors = []
+            for s in range(STEP):
+                factor = columns[u][s]
+                for m in range(s):
+                    factor = factor - factors[m] * lower[s, m]
+                factors.append(factor * scale[s])
+                tiles[u] = tiles[u] - factors[s] * done[s]
+        for s in range(STEP):
+            tiles[t] = jnp.where(row == s, done[s], tiles[t])
+    return jnp.concatenate(tiles, axis=0)[:, n:]
+
+
+def inverse_factor_kernel(packed_ref, inverse_ref, work_ref):
     n = inverse_ref.shape[0]
-    block = n // XN
-    held = []
-    for ref in (own_ref,) + came_refs:
-        packed = ref[...]
-        width = packed.shape[1] // 2
-        held.append(jnp.concatenate([packed[:, :width], packed[:, width:]], axis=0))
-    for x in range(XN):
-
-        @pl.when(place_ref[0] == x)
-        def _():
-            for b in range(XN):
-                rows = pl.ds(b * block, block)
-                for j in range(XN - 1):
-                    c = (b + j) % XN
-                    part = held[b ^ x][:, j * block : (j + 1) * block]
-                    work_ref[rows, c * block : (c + 1) * block] = part
-                c = (b + XN - 1) % XN
-                work_ref[rows, c * block : (c + 1) * block] = held[c ^ x][:, block : 2 * block].T
-
+    block, width = n // XN, packed_ref.shape[2] // 2
+    for b in range(XN):
+        rows = jnp.concatenate([packed_ref[b, :, :width], packed_ref[b, :, width:]], axis=0)
+        here = pl.ds(b * block, block)
+        for j in range(XN - 1):
+            c = (b + j) % XN * block
+            work_ref[here, c : c + block] = rows[:, j * block : (j + 1) * block]
+        below = (b + 1) % XN * block
+        work_ref[below : below + block, b * block : (b + 1) * block] = rows[:, block : 2 * block].T
     work_ref[:, n:] = eye(n)
     for top in range(0, n, PANEL):
         end = top + PANEL
@@ -115,17 +122,17 @@
 SMEM = pl.BlockSpec(memory_space=pltpu.SMEM)
 
 
-def inverse_factor(place, blocks, n):
+def inverse_factor(packed, n):
     return pl.pallas_call(
         inverse_factor_kernel,
         out_shape=jax.ShapeDtypeStruct((n, n), F32),
-        in_specs=[SMEM] + [VMEM] * len(blocks),
+        in_specs=[VMEM],
         out_specs=VMEM,
         scratch_shapes=[pltpu.VMEM((n, 2 * n), F32)],
         compiler_params=pltpu.CompilerParams(vmem_limit_bytes=16 * MIB),
         cost_estimate=pl.CostEstimate(flops=FACTOR_COST, bytes_accessed=2**10, transcendentals=0),
         name="inverse_factor",
-    )(place, *blocks)
+    )(packed)
 
 
 def range_product(turned, own, base):
@@ -325,11 +332,10 @@
     gram, second = gram + gram_came, sum(second)
     chunks = [first, lax.ppermute(first, "grp", OTHER_HALF)]
     chunks += [second, lax.ppermute(second, "grp", OTHER_HALF)]
-    inverse = inverse_factor(
-        at_x.reshape(1),
-        [gram] + [lax.ppermute(gram, "grp", ALONG_X[k]) for k in (1, 2, 3)],
-        rank,
-    )
+    gram = lax.all_to_all(
+        jnp.broadcast_to(gram, (XN,) + gram.shape), "grp", 0, 0, axis_index_groups=X_GROUPS
+    )
+    inverse = inverse_factor(gram, rank)
     inverse, chunks = lax.optimization_barrier((inverse, chunks))
     block = lax.optimization_barrier(finished(inverse, chunks).astype(jnp.float16))
     blocks = {0: block}

time: 201 us -> 201 us (level)
  the two profiles are of different devices: /device:TPU:4 before, /device:TPU:6 now
where the time goes in v9:
time: 201 us; the launch traced here: 200 us
  blocking collectives  89.9 us (45%)
  starting transfers between devices  60.1 us (30%)
  waiting for transfers between devices  22.8 us (11%)
  Pallas kernels  18.2 us (9%)
  local copies, waits for them, and re-layouts  4.27 us (2%)
    all_to_all x1, blocking collectives, per_device(): lax.all_to_all(jnp.concatenate([own, tag], axis=2), 'exp', 0, 0, axis_ind...  29.4 us
    all_to_all x1, blocking collectives, per_device(): lax.all_to_all(jnp.concatenate([weighted.reshape(FN, piece, ff), freq_sum...  26 us
    ppermute x6, starting transfers between devices, along_x(): lax.ppermute(blocks[k], 'grp', ALONG_X[k])  19.6 us
    all_to_all x1, blocking collectives, per_device(): lax.all_to_all(jnp.broadcast_to(load, (YN * NN, FN * piece, wide)), 'exp'...  19.4 us
    all_to_all x1, blocking collectives, per_device(): lax.all_to_all(jnp.broadcast_to(load, (FN, piece, wide)), 'exp', 0, 0, ax...  15.2 us
    ppermute x1, waiting for transfers between devices, per_device(): chunks += [second, lax.ppermute(second, 'grp', OTHER_HALF)]  11.5 us
    ppermute x3, starting transfers between devices, per_device(): blocks[k] = lax.ppermute(block, 'grp', ALONG_X[k])  9.82 us
    ppermute x1, starting transfers between devices, per_device(): chunks += [second, lax.ppermute(second, 'grp', OTHER_HALF)]  9.46 us
  transfers between devices with their start and end apart: 14, of which 7 were waited for; matrix products, arithmetic and copies ran while one was open for 1% of the time, Pallas kernels for 6%

profile of v9, /device:TPU:6, one launch (start us, length us, event | category | flops | bytes accessed | tf_op | source)
XLA Modules:
  0.0 200.1 jit_solution(6728588554450842503)
XLA Ops:
  3.1 29.4 %all_to_all.25 = bf16[16,32,1664]{2,1,0:T(8,128)(2,1)S(1)} all-to-all(bf16[16,32,1664]{2,1,0:T(8,128)(2,1)S(1)} %pad_maximum_fusion), channel_id=1, replica_groups={{0,2,16,18,32,34,48,50,1,3,17,19,33,35,49,51},{4,6,20,22,36,38,52,54,5,..., dimensions={0} | all-to-all | bytes 3407872 | tf_op jit(solution)/shard_map/all_to_all | solution.py:291
  34.3 26.0 %all_to_all.26 = f32[4,8,1664]{2,1,0:T(8,128)S(1)} all-to-all(f32[4,8,1664]{2,1,0:T(8,128)S(1)} %concatenate.10), channel_id=1, replica_groups={{0,4,8,12},{1,5,9,13},{2,6,10,14},{3,7,11,15},{16,20,24,28},{17,21,25,2..., dimensions={0} | all-to-all | bytes 425984 | tf_op jit(solution)/shard_map/all_to_all | solution.py:298
  61.2 15.2 %all_to_all.27 = bf16[4,8,2304]{2,1,0:T(8,128)(2,1)S(1)} all-to-all(bf16[4,8,2304]{2,1,0:T(8,128)(2,1)S(1)} %broadcast_in_dim.26), channel_id=1, replica_groups={{0,4,8,12},{1,5,9,13},{2,6,10,14},{3,7,11,15},{16,20,24,28},{17,21,25,2..., dimensions={0} | all-to-all | bytes 294912 | tf_op jit(solution)/shard_map/all_to_all | solution.py:309
  76.4 19.4 %all_to_all.28 = bf16[8,32,2304]{2,1,0:T(8,128)(2,1)S(1)} all-to-all(bf16[8,32,2304]{2,1,0:T(8,128)(2,1)S(1)} %broadcast_in_dim.27), channel_id=1, replica_groups={{0,2,16,18,32,34,48,50},{1,3,17,19,33,35,49,51},{4,6,20,22,36,38,52,54}..., dimensions={0} | all-to-all | bytes 2359296 | tf_op jit(solution)/shard_map/all_to_all | solution.py:312
  97.8 2.8 %collective-permute-done.other_ref = bf16[256,2304]{1,0:T(8,128)(2,1)} collective-permute-done((bf16[256,2304]{1,0:T(8,128)(2,1)S(1)}, bf16[256,2304]{1,0:T(8,128)(2,1)}, u32[]{:S(2)}, u32[]{:S(2)}) %collective-permute-start) | collective-permute-done | bytes 1179680 | tf_op jit(solution)/shard_map/ppermute | solution.py:316
  100.7 4.3 %first_products.1 = (f32[4,160,384]{2,1,0:T(8,128)S(1)}, f32[512,256]{1,0:T(8,128)S(1)}) custom-call(s32[2]{0:T(128)S(1)} %pad_add_fusion.place_ref, bf16[256,2304]{1,0:T(8,128)(2,1)S(1)} %bitcast.47, bf16[256,2304]{1,0:T(8,128)(2,1)} %collective-permute-done.other_ref, bf16[512,1536]{1,0:T(8,128)(2,1)S(1)} %bitcast.44, bf16[1536,256]{1,0:T(8,128)(2,1)S(1)} %copy-done), custom_call_target="tpu_custom_call" | custom-call | flops 3000000000 | bytes 1024 | tf_op jit(solution)/shard_map/first_products/pallas_call | solution.py:182
  105.0 3.3 %collective-permute-start.1 = (f32[160,384]{1,0:T(8,128)S(1)}, f32[160,384]{1,0:T(8,128)S(1)}, u32[]{:S(2)}, u32[]{:S(2)}) collective-permute-start(f32[160,384]{1,0:T(8,128)S(1)} %get-tuple-element.27), channel_id=1, source_target_pairs={{0,128},{64,192},{128,0},{192,64},{256,384},{320,448},{384,256},{4... | collective-permute-start | bytes 737288 | tf_op jit(solution)/shard_map/ppermute | solution.py:322
  110.3 4.6 %collective-permute-start.2 = (f32[160,384]{1,0:T(8,128)S(1)}, f32[160,384]{1,0:T(8,128)S(1)}, u32[]{:S(2)}, u32[]{:S(2)}) collective-permute-start(f32[160,384]{1,0:T(8,128)S(1)} %get-tuple-element.29), channel_id=1, source_target_pairs={{0,192},{64,128},{128,64},{192,0},{256,448},{320,384},{384,320},{4... | collective-permute-start | bytes 737288 | tf_op jit(solution)/shard_map/ppermute | solution.py:322
  114.9 3.0 %second_products.1 = f32[4,128,384]{2,1,0:T(8,128)S(1)} custom-call(s32[2]{0:T(128)S(1)} %pad_add_fusion.place_ref, bf16[256,2304]{1,0:T(8,128)(2,1)S(1)} %bitcast.48, bf16[256,2304]{1,0:T(8,128)(2,1)} %collective-permute-done.other_ref, bf16[512,1536]{1,0:T(8,128)(2,1)S(1)} %bitcast.45, f32[512,256]{1,0:T(8,128)S(1)} %get-tuple-element.14.range_ref), custom_call_target="tpu_custom_call" | custom-call | flops 2000000000 | bytes 1024 | tf_op jit(solution)/shard_map/second_products/pallas_call | solution.py:211
  118.0 2.7 %collective-permute-start.8 = (f32[128,384]{1,0:T(8,128)S(1)}, f32[128,384]{1,0:T(8,128)S(1)}, u32[]{:S(2)}, u32[]{:S(2)}) collective-permute-start(f32[128,384]{1,0:T(8,128)S(1)} %get-tuple-element.30), channel_id=1, source_target_pairs={{0,64},{64,0},{128,192},{192,128},{256,320},{320,256},{384,448},{4... | collective-permute-start | bytes 589832 | tf_op jit(solution)/shard_map/ppermute | solution.py:322
  120.7 3.0 %collective-permute-start.7 = (f32[128,384]{1,0:T(8,128)S(1)}, f32[128,384]{1,0:T(8,128)S(1)}, u32[]{:S(2)}, u32[]{:S(2)}) collective-permute-start(f32[128,384]{1,0:T(8,128)S(1)} %get-tuple-element.31), channel_id=1, source_target_pairs={{0,192},{64,128},{128,64},{192,0},{256,448},{320,384},{384,320},{4... | collective-permute-start | bytes 589832 | tf_op jit(solution)/shard_map/ppermute | solution.py:322
  123.8 4.0 %collective-permute-start.6 = (f32[128,384]{1,0:T(8,128)S(1)}, f32[128,384]{1,0:T(8,128)S(1)}, u32[]{:S(2)}, u32[]{:S(2)}) collective-permute-start(f32[128,384]{1,0:T(8,128)S(1)} %get-tuple-element.32), channel_id=1, source_target_pairs={{0,128},{64,192},{128,0},{192,64},{256,384},{320,448},{384,256},{4... | collective-permute-start | bytes 589832 | tf_op jit(solution)/shard_map/ppermute | solution.py:322
  127.9 8.2 %collective-permute-start.4 = (f32[32,384]{1,0:T(8,128)S(1)}, f32[32,384]{1,0:T(8,128)S(1)}, u32[]{:S(2)}, u32[]{:S(2)}) collective-permute-start(f32[32,384]{1,0:T(8,128)S(1)} %slice.65), channel_id=1, source_target_pairs={{0,256},{64,320},{128,384},{192,448},{256,0},{320,64},{384,128},{4... | collective-permute-start | bytes 147464 | tf_op jit(solution)/shard_map/ppermute | solution.py:330
  136.1 6.3 %collective-permute-start.5 = (f32[128,384]{1,0:T(8,128)S(1)}, f32[128,384]{1,0:T(8,128)S(1)}, u32[]{:S(2)}, u32[]{:S(2)}) collective-permute-start(f32[128,384]{1,0:T(8,128)S(1)} %slice.66.refs_0_), channel_id=1, source_target_pairs={{0,256},{64,320},{128,384},{192,448},{256,0},{320,64},{384,128},{4... | collective-permute-start | bytes 589832 | tf_op jit(solution)/shard_map/ppermute | solution.py:333
  143.5 4.8 %all-to-all-start.4 = ((f32[4,32,384]{2,1,0:T(8,128)}), f32[4,32,384]{2,1,0:T(8,128)S(1)}, u32[]{:S(2)}, u32[]{:S(2)}) async-start(f32[4,32,384]{2,1,0:T(8,128)} %broadcast_in_dim.28), calls=%async_computation.4 | async-start | bytes 393216 | tf_op jit(solution)/shard_map/all_to_all | solution.py:335
  148.3 9.5 %collective-permute-start.9 = (f32[128,384]{1,0:T(8,128)S(1)}, f32[128,384]{1,0:T(8,128)S(1)}, u32[]{:S(2)}, u32[]{:S(2)}) collective-permute-start(f32[128,384]{1,0:T(8,128)S(1)} %add_add_fusion.refs_2_), channel_id=1, source_target_pairs={{0,256},{64,320},{128,384},{192,448},{256,0},{320,64},{384,128},{4... | collective-permute-start | bytes 589832 | tf_op jit(solution)/shard_map/ppermute | solution.py:334
  157.8 8.9 %inverse_factor.1.inverse_ref = f32[256,256]{1,0:T(8,128)S(1)} custom-call(f32[4,32,384]{2,1,0:T(8,128)S(1)} %all-to-all-done.4.packed_ref), custom_call_target="tpu_custom_call" | custom-call | flops 536870912 | bytes 1024 | tf_op jit(solution)/shard_map/inverse_factor/pallas_call | solution.py:126
  166.7 2.9 %collective-permute-done.5.refs_1_ = f32[128,384]{1,0:T(8,128)S(1)} collective-permute-done((f32[128,384]{1,0:T(8,128)S(1)}, f32[128,384]{1,0:T(8,128)S(1)}, u32[]{:S(2)}, u32[]{:S(2)}) %collective-permute-start.5) | collective-permute-done | bytes 196640 | tf_op jit(solution)/shard_map/ppermute | solution.py:333
  169.6 11.5 %collective-permute-done.9.refs_3_ = f32[128,384]{1,0:T(8,128)S(1)} collective-permute-done((f32[128,384]{1,0:T(8,128)S(1)}, f32[128,384]{1,0:T(8,128)S(1)}, u32[]{:S(2)}, u32[]{:S(2)}) %collective-permute-start.9) | collective-permute-done | bytes 196640 | tf_op jit(solution)/shard_map/ppermute | solution.py:334
  182.1 2.8 %collective-permute-start.12 = (f16[272,384]{1,0:T(8,128)(2,1)S(1)}, f16[272,384]{1,0:T(8,128)(2,1)S(1)}, u32[]{:S(2)}, u32[]{:S(2)}) collective-permute-start(f16[272,384]{1,0:T(8,128)(2,1)S(1)} %convert_element_type.52), channel_id=1, source_target_pairs={{0,192},{64,128},{128,64},{192,0},{256,448},{320,384},{384,320},{4... | collective-permute-start | bytes 626696 | tf_op jit(solution)/shard_map/ppermute | solution.py:343
  184.9 3.9 %collective-permute-start.11 = (f16[272,384]{1,0:T(8,128)(2,1)S(1)}, f16[272,384]{1,0:T(8,128)(2,1)S(1)}, u32[]{:S(2)}, u32[]{:S(2)}) collective-permute-start(f16[272,384]{1,0:T(8,128)(2,1)S(1)} %convert_element_type.52), channel_id=1, source_target_pairs={{0,128},{64,192},{128,0},{192,64},{256,384},{320,448},{384,256},{4... | collective-permute-start | bytes 626696 | tf_op jit(solution)/shard_map/ppermute | solution.py:343
  188.8 3.1 %collective-permute-start.10 = (f16[272,384]{1,0:T(8,128)(2,1)S(1)}, f16[272,384]{1,0:T(8,128)(2,1)S(1)}, u32[]{:S(2)}, u32[]{:S(2)}) collective-permute-start(f16[272,384]{1,0:T(8,128)(2,1)S(1)} %convert_element_type.52), channel_id=1, source_target_pairs={{0,64},{64,0},{128,192},{192,128},{256,320},{320,256},{384,448},{4... | collective-permute-start | bytes 626696 | tf_op jit(solution)/shard_map/ppermute | solution.py:343
  193.4 2.6 %collective-permute-done.12 = f16[272,384]{1,0:T(8,128)(2,1)S(1)} collective-permute-done((f16[272,384]{1,0:T(8,128)(2,1)S(1)}, f16[272,384]{1,0:T(8,128)(2,1)S(1)}, u32[]{:S(2)}, u32[]{:S(2)}) %collective-permute-start.12) | collective-permute-done | bytes 208928 | tf_op jit(solution)/shard_map/ppermute | solution.py:343
  196.4 2.3 %collective-permute-done.10 = f16[272,384]{1,0:T(8,128)(2,1)S(1)} collective-permute-done((f16[272,384]{1,0:T(8,128)(2,1)S(1)}, f16[272,384]{1,0:T(8,128)(2,1)S(1)}, u32[]{:S(2)}, u32[]{:S(2)}) %collective-permute-start.10) | collective-permute-done | bytes 208928 | tf_op jit(solution)/shard_map/ppermute | solution.py:343
  (52 shorter events, 13.7 us)
Async XLA Ops:
  32.5 28.0 %copy-start = (bf16[1536,256]{1,0:T(8,128)(2,1)S(1)}, bf16[1536,256]{1,0:T(8,128)(2,1)}, u32[]{:S(2)}) copy-start(bf16[1536,256]{1,0:T(8,128)(2,1)} %sketch_ref.1) | copy-start | bytes 2359300
  60.5 0.6 copy-start.3
  95.8 4.9 %collective-permute-start = (bf16[256,2304]{1,0:T(8,128)(2,1)S(1)}, bf16[256,2304]{1,0:T(8,128)(2,1)}, u32[]{:S(2)}, u32[]{:S(2)}) collective-permute-start(bf16[256,2304]{1,0:T(8,128)(2,1)S(1)} %bitcast.46), channel_id=1, source_target_pairs={{0,1},{1,0},{2,3},{3,2},{4,5},{5,4},{6,7},{7,6},{8,9},{9,8},{10,11... | collective-permute-start | bytes 3538952 | tf_op jit(solution)/shard_map/ppermute | solution.py:316
  105.0 12.9 %copy-start.1 = (f32[512,256]{1,0:T(8,128)}, f32[512,256]{1,0:T(8,128)S(1)}, u32[]{:S(2)}) copy-start(f32[512,256]{1,0:T(8,128)S(1)} %get-tuple-element.14.range_ref) | copy-start | bytes 1572868
  105.0 18.7 %collective-permute-start.1 = (f32[160,384]{1,0:T(8,128)S(1)}, f32[160,384]{1,0:T(8,128)S(1)}, u32[]{:S(2)}, u32[]{:S(2)}) collective-permute-start(f32[160,384]{1,0:T(8,128)S(1)} %get-tuple-element.27), channel_id=1, source_target_pairs={{0,128},{64,192},{128,0},{192,64},{256,384},{320,448},{384,256},{4... | collective-permute-start | bytes 737288 | tf_op jit(solution)/shard_map/ppermute | solution.py:322
  108.4 19.4 %collective-permute-start.3 = (f32[160,384]{1,0:T(8,128)S(1)}, f32[160,384]{1,0:T(8,128)S(1)}, u32[]{:S(2)}, u32[]{:S(2)}) collective-permute-start(f32[160,384]{1,0:T(8,128)S(1)} %get-tuple-element.28), channel_id=1, source_target_pairs={{0,64},{64,0},{128,192},{192,128},{256,320},{320,256},{384,448},{4... | collective-permute-start | bytes 737288 | tf_op jit(solution)/shard_map/ppermute | solution.py:322
  110.3 17.5 %collective-permute-start.2 = (f32[160,384]{1,0:T(8,128)S(1)}, f32[160,384]{1,0:T(8,128)S(1)}, u32[]{:S(2)}, u32[]{:S(2)}) collective-permute-start(f32[160,384]{1,0:T(8,128)S(1)} %get-tuple-element.29), channel_id=1, source_target_pairs={{0,192},{64,128},{128,64},{192,0},{256,448},{320,384},{384,320},{4... | collective-permute-start | bytes 737288 | tf_op jit(solution)/shard_map/ppermute | solution.py:322
  118.0 24.5 %collective-permute-start.8 = (f32[128,384]{1,0:T(8,128)S(1)}, f32[128,384]{1,0:T(8,128)S(1)}, u32[]{:S(2)}, u32[]{:S(2)}) collective-permute-start(f32[128,384]{1,0:T(8,128)S(1)} %get-tuple-element.30), channel_id=1, source_target_pairs={{0,64},{64,0},{128,192},{192,128},{256,320},{320,256},{384,448},{4... | collective-permute-start | bytes 589832 | tf_op jit(solution)/shard_map/ppermute | solution.py:322
  120.7 21.8 %collective-permute-start.7 = (f32[128,384]{1,0:T(8,128)S(1)}, f32[128,384]{1,0:T(8,128)S(1)}, u32[]{:S(2)}, u32[]{:S(2)}) collective-permute-start(f32[128,384]{1,0:T(8,128)S(1)} %get-tuple-element.31), channel_id=1, source_target_pairs={{0,192},{64,128},{128,64},{192,0},{256,448},{320,384},{384,320},{4... | collective-permute-start | bytes 589832 | tf_op jit(solution)/shard_map/ppermute | solution.py:322
  123.8 18.8 %collective-permute-start.6 = (f32[128,384]{1,0:T(8,128)S(1)}, f32[128,384]{1,0:T(8,128)S(1)}, u32[]{:S(2)}, u32[]{:S(2)}) collective-permute-start(f32[128,384]{1,0:T(8,128)S(1)} %get-tuple-element.32), channel_id=1, source_target_pairs={{0,128},{64,192},{128,0},{192,64},{256,384},{320,448},{384,256},{4... | collective-permute-start | bytes 589832 | tf_op jit(solution)/shard_map/ppermute | solution.py:322
  127.9 14.9 %collective-permute-start.4 = (f32[32,384]{1,0:T(8,128)S(1)}, f32[32,384]{1,0:T(8,128)S(1)}, u32[]{:S(2)}, u32[]{:S(2)}) collective-permute-start(f32[32,384]{1,0:T(8,128)S(1)} %slice.65), channel_id=1, source_target_pairs={{0,256},{64,320},{128,384},{192,448},{256,0},{320,64},{384,128},{4... | collective-permute-start | bytes 147464 | tf_op jit(solution)/shard_map/ppermute | solution.py:330
  136.1 33.5 %collective-permute-start.5 = (f32[128,384]{1,0:T(8,128)S(1)}, f32[128,384]{1,0:T(8,128)S(1)}, u32[]{:S(2)}, u32[]{:S(2)}) collective-permute-start(f32[128,384]{1,0:T(8,128)S(1)} %slice.66.refs_0_), channel_id=1, source_target_pairs={{0,256},{64,320},{128,384},{192,448},{256,0},{320,64},{384,128},{4... | collective-permute-start | bytes 589832 | tf_op jit(solution)/shard_map/ppermute | solution.py:333
  143.5 14.3 %all-to-all-start.4 = ((f32[4,32,384]{2,1,0:T(8,128)}), f32[4,32,384]{2,1,0:T(8,128)S(1)}, u32[]{:S(2)}, u32[]{:S(2)}) async-start(f32[4,32,384]{2,1,0:T(8,128)} %broadcast_in_dim.28), calls=%async_computation.4 | async-start | bytes 393216 | tf_op jit(solution)/shard_map/all_to_all | solution.py:335
  148.3 32.8 %collective-permute-start.9 = (f32[128,384]{1,0:T(8,128)S(1)}, f32[128,384]{1,0:T(8,128)S(1)}, u32[]{:S(2)}, u32[]{:S(2)}) collective-permute-start(f32[128,384]{1,0:T(8,128)S(1)} %add_add_fusion.refs_2_), channel_id=1, source_target_pairs={{0,256},{64,320},{128,384},{192,448},{256,0},{320,64},{384,128},{4... | collective-permute-start | bytes 589832 | tf_op jit(solution)/shard_map/ppermute | solution.py:334
  166.7 25.3 %copy-start.2 = (f32[512,256]{1,0:T(8,128)S(1)}, f32[512,256]{1,0:T(8,128)}, u32[]{:S(2)}) copy-start(f32[512,256]{1,0:T(8,128)} %copy-done.1) | copy-start | bytes 1572868
  182.1 13.9 %collective-permute-start.12 = (f16[272,384]{1,0:T(8,128)(2,1)S(1)}, f16[272,384]{1,0:T(8,128)(2,1)S(1)}, u32[]{:S(2)}, u32[]{:S(2)}) collective-permute-start(f16[272,384]{1,0:T(8,128)(2,1)S(1)} %convert_element_type.52), channel_id=1, source_target_pairs={{0,192},{64,128},{128,64},{192,0},{256,448},{320,384},{384,320},{4... | collective-permute-start | bytes 626696 | tf_op jit(solution)/shard_map/ppermute | solution.py:343
  184.9 11.5 %collective-permute-start.11 = (f16[272,384]{1,0:T(8,128)(2,1)S(1)}, f16[272,384]{1,0:T(8,128)(2,1)S(1)}, u32[]{:S(2)}, u32[]{:S(2)}) collective-permute-start(f16[272,384]{1,0:T(8,128)(2,1)S(1)} %convert_element_type.52), channel_id=1, source_target_pairs={{0,128},{64,192},{128,0},{192,64},{256,384},{320,448},{384,256},{4... | collective-permute-start | bytes 626696 | tf_op jit(solution)/shard_map/ppermute | solution.py:343
  188.8 9.9 %collective-permute-start.10 = (f16[272,384]{1,0:T(8,128)(2,1)S(1)}, f16[272,384]{1,0:T(8,128)(2,1)S(1)}, u32[]{:S(2)}, u32[]{:S(2)}) collective-permute-start(f16[272,384]{1,0:T(8,128)(2,1)S(1)} %convert_element_type.52), channel_id=1, source_target_pairs={{0,64},{64,0},{128,192},{192,128},{256,320},{320,256},{384,448},{4... | collective-permute-start | bytes 626696 | tf_op jit(solution)/shard_map/ppermute | solution.py:343

commit v10 on v9

--- a/solution.py
+++ b/solution.py
@@ -35,6 +35,7 @@
 
 PANEL, STEP = 64, 8
 TOP_POWER = 13
+FIRST = 64
 FACTOR_COST = 2**29
 
 
@@ -149,8 +150,8 @@
 def first_products_kernel(place_ref, mine_ref, other_ref, own_ref, sketch_ref, out_ref, range_ref):
     half = mine_ref.shape[0]
     ff, rank = sketch_ref.shape
-    block, slab, chunk = rank // XN, ff // XN, rank // 2
-    core, x = place_ref[0], place_ref[1]
+    block, slab, chunk = rank // XN, ff // XN, FIRST
+    core = place_ref[0]
     gram = jnp.zeros((rank, rank), F32)
     delta = jnp.zeros((chunk, ff), F32)
     for load_ref, at_core in ((mine_ref, core), (other_ref, 1 - core)):
@@ -172,8 +173,8 @@
             [mine[:, (b + j) % XN * block :][:, :block] for j in range(XN - 1)], axis=1
         )
         packed = jnp.concatenate([kept[: block // 2], kept[block // 2 :]], axis=1)
-        out_ref[b ^ x, : block // 2, :] = packed
-        out_ref[b ^ x, block // 2 :, :] = delta[:, b * slab : (b + 1) * slab]
+        out_ref[b, : block // 2, :] = packed
+        out_ref[b, block // 2 :, :] = delta[:, b * slab : (b + 1) * slab]
 
 
 def first_products(place, mine, other, own, sketch):
@@ -182,7 +183,7 @@
     return pl.pallas_call(
         first_products_kernel,
         out_shape=(
-            jax.ShapeDtypeStruct((XN, rank // XN // 2 + rank // 2, ff // XN), F32),
+            jax.ShapeDtypeStruct((XN, rank // XN // 2 + FIRST, ff // XN), F32),
             jax.ShapeDtypeStruct((rows, rank), F32),
         ),
         in_specs=[SMEM] + [VMEM] * 4,
@@ -196,21 +197,22 @@
 def second_products_kernel(place_ref, mine_ref, other_ref, own_ref, range_ref, out_ref):
     half = mine_ref.shape[0]
     ff, rank = own_ref.shape[1], range_ref.shape[1]
-    slab, chunk = ff // XN, rank // 2
-    core, x = place_ref[0], place_ref[1]
-    delta = jnp.zeros((chunk, ff), F32)
+    slab, chunk = ff // XN, FIRST
+    core = place_ref[0]
+    delta = jnp.zeros((rank - chunk, ff), F32)
     for load_ref, at_core in ((mine_ref, core), (other_ref, 1 - core)):
         rows = pl.ds(pl.multiple_of(at_core * half, half), half)
-        delta += range_product(range_ref[rows, chunk:].T, own_ref[rows, :], load_ref[:, :ff])
+        turned = range_ref[rows, :].T
+        delta += range_product(turned[chunk:], own_ref[rows, :], load_ref[:, :ff])
     for b in range(XN):
-        out_ref[b ^ x] = delta[:, b * slab : (b + 1) * slab]
+        out_ref[b] = delta[:, b * slab : (b + 1) * slab]
 
 
 def second_products(place, mine, other, own, range_rows):
     ff, rank = own.shape[1], range_rows.shape[1]
     return pl.pallas_call(
         second_products_kernel,
-        out_shape=jax.ShapeDtypeStruct((XN, rank // 2, ff // XN), F32),
+        out_shape=jax.ShapeDtypeStruct((XN, rank - FIRST, ff // XN), F32),
         in_specs=[SMEM] + [VMEM] * 4,
         out_specs=VMEM,
         compiler_params=pltpu.CompilerParams(vmem_limit_bytes=40 * MIB),
@@ -220,32 +222,33 @@
 
 
 def finished_kernel(inverse_ref, *refs):
-    out_ref = refs[-1]
+    pairs, (out_ref, sums_ref) = refs[:-2], refs[-2:]
     rank = inverse_ref.shape[0]
-    chunk = rank // 2
-    values = sum(
-        jnp.dot(
-            inverse_ref[:, i * chunk : (i + 1) * chunk], refs[2 * i][...] + refs[2 * i + 1][...],
-            precision=HIGHEST, preferred_element_type=F32,
-        )
-        for i in range(2)
-    )
-    top = jnp.max(jnp.max(jnp.abs(values), axis=0, keepdims=True), axis=1, keepdims=True)
-    power = jnp.floor(jnp.log(jnp.maximum(top, 1e-30)) * (1 / math.log(2)))
+    top = 0
+    for i in range(0, len(pairs), 2):
+        end = top + pairs[i].shape[0]
+        sums_ref[top:end] = pairs[i][...] + pairs[i + 1][...]
+        top = end
+    values = jnp.dot(
+        inverse_ref[...], sums_ref[...], precision=HIGHEST, preferred_element_type=F32
+    )
+    most = jnp.max(jnp.max(jnp.abs(values), axis=0, keepdims=True), axis=1, keepdims=True)
+    power = jnp.floor(jnp.log(jnp.maximum(most, 1e-30)) * (1 / math.log(2)))
     out_ref[:rank] = values * jnp.exp2(TOP_POWER - power)
     out_ref[rank:] = jnp.broadcast_to(power, (out_ref.shape[0] - rank, out_ref.shape[1]))
 
 
-def finished(inverse, chunks):
-    rank, slab = inverse.shape[0], chunks[0].shape[1]
+def finished(inverse, pairs):
+    rank, slab = inverse.shape[0], pairs[0].shape[1]
     return pl.pallas_call(
         finished_kernel,
         out_shape=jax.ShapeDtypeStruct((rank + 16, slab), F32),
-        in_specs=[VMEM] * (1 + len(chunks)),
+        in_specs=[VMEM] * (1 + len(pairs)),
         out_specs=VMEM,
+        scratch_shapes=[pltpu.VMEM((rank, slab), F32)],
         compiler_params=pltpu.CompilerParams(vmem_limit_bytes=16 * MIB),
         name="finished",
-    )(inverse, *chunks)
+    )(inverse, *pairs)
 
 
 def assembled_kernel(place_ref, *refs):
@@ -316,26 +319,22 @@
     other = lax.ppermute(load, "exp", OTHER_CORE)
 
     at_core, at_x = lax.axis_index("exp") % CN, lax.axis_index("grp") % XN
-    place, own = jnp.stack([at_core, at_x]), own.reshape(rows, ff)
-
-    def along_x(blocks):
-        return [blocks[0]] + [lax.ppermute(blocks[k], "grp", ALONG_X[k]) for k in (2, 3, 1)]
+    place, own = at_core.reshape(1), own.reshape(rows, ff)
+
+    def to_owners(blocks):
+        return lax.all_to_all(blocks, "grp", 0, 0, axis_index_groups=X_GROUPS)
 
     first, range_rows = first_products(place, load, other, own, sketch)
-    first = along_x(first)
-    second = along_x(second_products(place, load, other, own, range_rows))
-    first = sum(first)
+    first = to_owners(first)
+    second = to_owners(second_products(place, load, other, own, range_rows))
+    first = jnp.sum(first, axis=0)
+    first_came = lax.ppermute(first, "grp", OTHER_HALF)
+    second = jnp.sum(second, axis=0)
+    second_came = lax.ppermute(second, "grp", OTHER_HALF)
     packed = rank // XN // 2
-    gram, first = first[:packed], first[packed:]
-    gram_came = lax.ppermute(gram, "grp", OTHER_HALF)
-    _, second = lax.optimization_barrier((gram_came, second))
-    gram, second = gram + gram_came, sum(second)
-    chunks = [first, lax.ppermute(first, "grp", OTHER_HALF)]
-    chunks += [second, lax.ppermute(second, "grp", OTHER_HALF)]
-    gram = lax.all_to_all(
-        jnp.broadcast_to(gram, (XN,) + gram.shape), "grp", 0, 0, axis_index_groups=X_GROUPS
-    )
-    inverse = inverse_factor(gram, rank)
+    gram = first[:packed] + first_came[:packed]
+    inverse = inverse_factor(to_owners(jnp.broadcast_to(gram, (XN,) + gram.shape)), rank)
+    chunks = [first[packed:], first_came[packed:], second, second_came]
     inverse, chunks = lax.optimization_barrier((inverse, chunks))
     block = lax.optimization_barrier(finished(inverse, chunks).astype(jnp.float16))
     blocks = {0: block}

time: 201 us -> 199 us (0.990)
  the two profiles are of different devices: /device:TPU:6 before, /device:TPU:65 now
where the time goes in v10:
time: 199 us
  blocking collectives  85.4 us (43%)
  starting transfers between devices  51.7 us (26%)
  waiting for transfers between devices  29.1 us (15%)
  Pallas kernels  18.8 us (9%)
  local copies, waits for them, and re-layouts  7.83 us (4%)
  other arithmetic  2.8 us (1%)
    all_to_all x1, blocking collectives, per_device(): lax.all_to_all(jnp.concatenate([own, tag], axis=2), 'exp', 0, 0, axis_ind...  29 us
    all_to_all x1, blocking collectives, per_device(): lax.all_to_all(jnp.concatenate([weighted.reshape(FN, piece, ff), freq_sum...  22.6 us
    all_to_all x1, blocking collectives, per_device(): lax.all_to_all(jnp.broadcast_to(load, (YN * NN, FN * piece, wide)), 'exp'...  21.9 us
    ppermute x3, starting transfers between devices, per_device(): blocks[k] = lax.ppermute(block, 'grp', ALONG_X[k])  20.1 us
    all_to_all x3, waiting for transfers between devices, to_owners(): return lax.all_to_all(blocks, 'grp', 0, 0, axis_index_groups=X_GROUPS)  15.2 us
    all_to_all x1, blocking collectives, per_device(): lax.all_to_all(jnp.broadcast_to(load, (FN, piece, wide)), 'exp', 0, 0, ax...  11.8 us
    all_to_all x3, starting transfers between devices, to_owners(): return lax.all_to_all(blocks, 'grp', 0, 0, axis_index_groups=X_GROUPS)  11.2 us
    ppermute x3, waiting for transfers between devices, per_device(): blocks[k] = lax.ppermute(block, 'grp', ALONG_X[k])  9.16 us
  transfers between devices with their start and end apart: 9, of which 7 were waited for; matrix products, arithmetic and copies ran while one was open for 2% of the time, Pallas kernels for 6%

profile of v10, /device:TPU:65, one launch (start us, length us, event | category | flops | bytes accessed | tf_op | source)
XLA Modules:
  0.0 198.5 jit_solution(14094963307308288509)
XLA Ops:
  1.3 1.6 copy.16
  3.1 29.0 %all_to_all.35 = bf16[16,32,1664]{2,1,0:T(8,128)(2,1)S(1)} all-to-all(bf16[16,32,1664]{2,1,0:T(8,128)(2,1)S(1)} %pad_maximum_fusion), channel_id=1, replica_groups={{0,2,16,18,32,34,48,50,1,3,17,19,33,35,49,51},{4,6,20,22,36,38,52,54,5,..., dimensions={0} | all-to-all | bytes 3407872 | tf_op jit(solution)/shard_map/all_to_all | solution.py:294
  33.9 22.6 %all_to_all.36 = f32[4,8,1664]{2,1,0:T(8,128)S(1)} all-to-all(f32[4,8,1664]{2,1,0:T(8,128)S(1)} %concatenate.10), channel_id=1, replica_groups={{0,4,8,12},{1,5,9,13},{2,6,10,14},{3,7,11,15},{16,20,24,28},{17,21,25,2..., dimensions={0} | all-to-all | bytes 425984 | tf_op jit(solution)/shard_map/all_to_all | solution.py:301
  57.4 11.8 %all_to_all.37 = bf16[4,8,2304]{2,1,0:T(8,128)(2,1)S(1)} all-to-all(bf16[4,8,2304]{2,1,0:T(8,128)(2,1)S(1)} %broadcast_in_dim.26), channel_id=1, replica_groups={{0,4,8,12},{1,5,9,13},{2,6,10,14},{3,7,11,15},{16,20,24,28},{17,21,25,2..., dimensions={0} | all-to-all | bytes 294912 | tf_op jit(solution)/shard_map/all_to_all | solution.py:312
  69.4 21.9 %all_to_all.38 = bf16[8,32,2304]{2,1,0:T(8,128)(2,1)S(1)} all-to-all(bf16[8,32,2304]{2,1,0:T(8,128)(2,1)S(1)} %broadcast_in_dim.27), channel_id=1, replica_groups={{0,2,16,18,32,34,48,50},{1,3,17,19,33,35,49,51},{4,6,20,22,36,38,52,54}..., dimensions={0} | all-to-all | bytes 2359296 | tf_op jit(solution)/shard_map/all_to_all | solution.py:315
  91.3 4.5 %collective-permute-start = (bf16[256,2304]{1,0:T(8,128)(2,1)S(1)}, bf16[256,2304]{1,0:T(8,128)(2,1)}, u32[]{:S(2)}, u32[]{:S(2)}) collective-permute-start(bf16[256,2304]{1,0:T(8,128)(2,1)S(1)} %bitcast.26), channel_id=1, source_target_pairs={{0,1},{1,0},{2,3},{3,2},{4,5},{5,4},{6,7},{7,6},{8,9},{9,8},{10,11... | collective-permute-start | bytes 3538952 | tf_op jit(solution)/shard_map/ppermute | solution.py:319
  95.8 2.6 %collective-permute-done.other_ref = bf16[256,2304]{1,0:T(8,128)(2,1)} collective-permute-done((bf16[256,2304]{1,0:T(8,128)(2,1)S(1)}, bf16[256,2304]{1,0:T(8,128)(2,1)}, u32[]{:S(2)}, u32[]{:S(2)}) %collective-permute-start) | collective-permute-done | bytes 1179680 | tf_op jit(solution)/shard_map/ppermute | solution.py:319
  98.4 4.5 %first_products.1 = (f32[4,96,384]{2,1,0:T(8,128)S(1)}, f32[512,256]{1,0:T(8,128)S(1)}) custom-call(s32[1]{0:T(128)} %bitcast.5.place_ref, bf16[256,2304]{1,0:T(8,128)(2,1)S(1)} %bitcast.27, bf16[256,2304]{1,0:T(8,128)(2,1)} %collective-permute-done.other_ref, bf16[512,1536]{1,0:T(8,128)(2,1)S(1)} %bitcast.24, bf16[1536,256]{1,0:T(8,128)(2,1)S(1)} %copy-done.1), custom_call_target="tpu_custom_call" | custom-call | flops 3000000000 | bytes 1024 | tf_op jit(solution)/shard_map/first_products/pallas_call | solution.py:183
  104.6 4.2 %all-to-all-start.4 = ((f32[4,96,384]{2,1,0:T(8,128)}), f32[4,96,384]{2,1,0:T(8,128)}, u32[]{:S(2)}, u32[]{:S(2)}) async-start(f32[4,96,384]{2,1,0:T(8,128)} %copy-done.2), calls=%async_computation.4 | async-start | bytes 1179648 | tf_op jit(solution)/shard_map/all_to_all | solution.py:325
  109.8 3.5 %second_products.1 = f32[4,192,384]{2,1,0:T(8,128)S(1)} custom-call(s32[1]{0:T(128)} %bitcast.5.place_ref, bf16[256,2304]{1,0:T(8,128)(2,1)S(1)} %bitcast.28, bf16[256,2304]{1,0:T(8,128)(2,1)} %collective-permute-done.other_ref, bf16[512,1536]{1,0:T(8,128)(2,1)S(1)} %bitcast.25, f32[512,256]{1,0:T(8,128)S(1)} %copy-done.4), custom_call_target="tpu_custom_call" | custom-call | flops 2000000000 | bytes 1024 | tf_op jit(solution)/shard_map/second_products/pallas_call | solution.py:213
  114.3 4.3 %all-to-all-done.4 = f32[4,96,384]{2,1,0:T(8,128)} async-done(((f32[4,96,384]{2,1,0:T(8,128)}), f32[4,96,384]{2,1,0:T(8,128)}, u32[]{:S(2)}, u32[]{:S(2)}) %all-to-all-start.4) | async-done | bytes 589856 | tf_op jit(solution)/shard_map/all_to_all | solution.py:325
  118.5 3.5 %all-to-all-start.6 = ((f32[4,192,384]{2,1,0:T(8,128)}), f32[4,192,384]{2,1,0:T(8,128)S(1)}, u32[]{:S(2)}, u32[]{:S(2)}) async-start(f32[4,192,384]{2,1,0:T(8,128)} %copy-done), calls=%async_computation.6 | async-start | bytes 2359296 | tf_op jit(solution)/shard_map/all_to_all | solution.py:325
  123.2 7.9 %collective-permute-start.1 = (f32[96,384]{1,0:T(8,128)S(1)}, f32[96,384]{1,0:T(8,128)S(1)}, u32[]{:S(2)}, u32[]{:S(2)}) collective-permute-start(f32[96,384]{1,0:T(8,128)S(1)} %reduce_sum.48), channel_id=1, source_target_pairs={{0,256},{64,320},{128,384},{192,448},{256,0},{320,64},{384,128},{4... | collective-permute-start | bytes 442376 | tf_op jit(solution)/shard_map/ppermute | solution.py:331
  131.1 6.0 %all-to-all-done.6 = f32[4,192,384]{2,1,0:T(8,128)S(1)} async-done(((f32[4,192,384]{2,1,0:T(8,128)}), f32[4,192,384]{2,1,0:T(8,128)S(1)}, u32[]{:S(2)}, u32[]{:S(2)}) %all-to-all-start.6) | async-done | bytes 1179680 | tf_op jit(solution)/shard_map/all_to_all | solution.py:325
  137.3 7.9 %collective-permute-start.2 = (f32[192,384]{1,0:T(8,128)S(1)}, f32[192,384]{1,0:T(8,128)S(1)}, u32[]{:S(2)}, u32[]{:S(2)}) collective-permute-start(f32[192,384]{1,0:T(8,128)S(1)} %reduce_sum.49.refs_2_), channel_id=1, source_target_pairs={{0,256},{64,320},{128,384},{192,448},{256,0},{320,64},{384,128},{4... | collective-permute-start | bytes 884744 | tf_op jit(solution)/shard_map/ppermute | solution.py:333
  145.9 3.5 %all-to-all-start.5 = ((f32[4,32,384]{2,1,0:T(8,128)}), f32[4,32,384]{2,1,0:T(8,128)S(1)}, u32[]{:S(2)}, u32[]{:S(2)}) async-start(f32[4,32,384]{2,1,0:T(8,128)} %broadcast_in_dim.28), calls=%async_computation.5 | async-start | bytes 393216 | tf_op jit(solution)/shard_map/all_to_all | solution.py:325
  149.5 4.9 %all-to-all-done.5.packed_ref = f32[4,32,384]{2,1,0:T(8,128)S(1)} async-done(((f32[4,32,384]{2,1,0:T(8,128)}), f32[4,32,384]{2,1,0:T(8,128)S(1)}, u32[]{:S(2)}, u32[]{:S(2)}) %all-to-all-start.5) | async-done | bytes 196640 | tf_op jit(solution)/shard_map/all_to_all | solution.py:325
  154.4 8.9 %inverse_factor.1.inverse_ref = f32[256,256]{1,0:T(8,128)S(1)} custom-call(f32[4,32,384]{2,1,0:T(8,128)S(1)} %all-to-all-done.5.packed_ref), custom_call_target="tpu_custom_call" | custom-call | flops 536870912 | bytes 1024 | tf_op jit(solution)/shard_map/inverse_factor/pallas_call | solution.py:127
  163.3 2.2 %collective-permute-done.2.refs_3_ = f32[192,384]{1,0:T(8,128)S(1)} collective-permute-done((f32[192,384]{1,0:T(8,128)S(1)}, f32[192,384]{1,0:T(8,128)S(1)}, u32[]{:S(2)}, u32[]{:S(2)}) %collective-permute-start.2) | collective-permute-done | bytes 294944 | tf_op jit(solution)/shard_map/ppermute | solution.py:333
  166.3 13.4 %collective-permute-start.3 = (f16[272,384]{1,0:T(8,128)(2,1)S(1)}, f16[272,384]{1,0:T(8,128)(2,1)S(1)}, u32[]{:S(2)}, u32[]{:S(2)}) collective-permute-start(f16[272,384]{1,0:T(8,128)(2,1)S(1)} %convert_element_type.52), channel_id=1, source_target_pairs={{0,64},{64,0},{128,192},{192,128},{256,320},{320,256},{384,448},{4... | collective-permute-start | bytes 626696 | tf_op jit(solution)/shard_map/ppermute | solution.py:342
  179.7 4.7 %collective-permute-start.4 = (f16[272,384]{1,0:T(8,128)(2,1)S(1)}, f16[272,384]{1,0:T(8,128)(2,1)S(1)}, u32[]{:S(2)}, u32[]{:S(2)}) collective-permute-start(f16[272,384]{1,0:T(8,128)(2,1)S(1)} %convert_element_type.52), channel_id=1, source_target_pairs={{0,128},{64,192},{128,0},{192,64},{256,384},{320,448},{384,256},{4... | collective-permute-start | bytes 626696 | tf_op jit(solution)/shard_map/ppermute | solution.py:342
  184.5 1.9 collective-permute-start.5
  187.9 3.8 %collective-permute-done.4 = f16[272,384]{1,0:T(8,128)(2,1)S(1)} collective-permute-done((f16[272,384]{1,0:T(8,128)(2,1)S(1)}, f16[272,384]{1,0:T(8,128)(2,1)S(1)}, u32[]{:S(2)}, u32[]{:S(2)}) %collective-permute-start.4) | collective-permute-done | bytes 208928 | tf_op jit(solution)/shard_map/ppermute | solution.py:342
  191.7 5.4 %collective-permute-done.5 = f16[272,384]{1,0:T(8,128)(2,1)S(1)} collective-permute-done((f16[272,384]{1,0:T(8,128)(2,1)S(1)}, f16[272,384]{1,0:T(8,128)(2,1)S(1)}, u32[]{:S(2)}, u32[]{:S(2)}) %collective-permute-start.5) | collective-permute-done | bytes 208928 | tf_op jit(solution)/shard_map/ppermute | solution.py:342
  (43 shorter events, 12.1 us)
Async XLA Ops:
  32.1 24.7 %copy-start.1 = (bf16[1536,256]{1,0:T(8,128)(2,1)S(1)}, bf16[1536,256]{1,0:T(8,128)(2,1)}, u32[]{:S(2)}) copy-start(bf16[1536,256]{1,0:T(8,128)(2,1)} %sketch_ref.1) | copy-start | bytes 2359300
  56.8 0.6 copy-start.5
  91.3 7.1 %collective-permute-start = (bf16[256,2304]{1,0:T(8,128)(2,1)S(1)}, bf16[256,2304]{1,0:T(8,128)(2,1)}, u32[]{:S(2)}, u32[]{:S(2)}) collective-permute-start(bf16[256,2304]{1,0:T(8,128)(2,1)S(1)} %bitcast.26), channel_id=1, source_target_pairs={{0,1},{1,0},{2,3},{3,2},{4,5},{5,4},{6,7},{7,6},{8,9},{9,8},{10,11... | collective-permute-start | bytes 3538952 | tf_op jit(solution)/shard_map/ppermute | solution.py:319
  102.9 0.8 copy-start.2
  103.8 0.8 copy-start.3
  104.6 14.0 %all-to-all-start.4 = ((f32[4,96,384]{2,1,0:T(8,128)}), f32[4,96,384]{2,1,0:T(8,128)}, u32[]{:S(2)}, u32[]{:S(2)}) async-start(f32[4,96,384]{2,1,0:T(8,128)} %copy-done.2), calls=%async_computation.4 | async-start | bytes 1179648 | tf_op jit(solution)/shard_map/all_to_all | solution.py:325
  108.8 1.0 copy-start.4
  113.3 1.0 copy-start
  118.5 18.6 %all-to-all-start.6 = ((f32[4,192,384]{2,1,0:T(8,128)}), f32[4,192,384]{2,1,0:T(8,128)S(1)}, u32[]{:S(2)}, u32[]{:S(2)}) async-start(f32[4,192,384]{2,1,0:T(8,128)} %copy-done), calls=%async_computation.6 | async-start | bytes 2359296 | tf_op jit(solution)/shard_map/all_to_all | solution.py:325
  123.2 22.0 %collective-permute-start.1 = (f32[96,384]{1,0:T(8,128)S(1)}, f32[96,384]{1,0:T(8,128)S(1)}, u32[]{:S(2)}, u32[]{:S(2)}) collective-permute-start(f32[96,384]{1,0:T(8,128)S(1)} %reduce_sum.48), channel_id=1, source_target_pairs={{0,256},{64,320},{128,384},{192,448},{256,0},{320,64},{384,128},{4... | collective-permute-start | bytes 442376 | tf_op jit(solution)/shard_map/ppermute | solution.py:331
  137.3 28.3 %collective-permute-start.2 = (f32[192,384]{1,0:T(8,128)S(1)}, f32[192,384]{1,0:T(8,128)S(1)}, u32[]{:S(2)}, u32[]{:S(2)}) collective-permute-start(f32[192,384]{1,0:T(8,128)S(1)} %reduce_sum.49.refs_2_), channel_id=1, source_target_pairs={{0,256},{64,320},{128,384},{192,448},{256,0},{320,64},{384,128},{4... | collective-permute-start | bytes 884744 | tf_op jit(solution)/shard_map/ppermute | solution.py:333
  145.9 8.5 %all-to-all-start.5 = ((f32[4,32,384]{2,1,0:T(8,128)}), f32[4,32,384]{2,1,0:T(8,128)S(1)}, u32[]{:S(2)}, u32[]{:S(2)}) async-start(f32[4,32,384]{2,1,0:T(8,128)} %broadcast_in_dim.28), calls=%async_computation.5 | async-start | bytes 393216 | tf_op jit(solution)/shard_map/all_to_all | solution.py:325
  166.3 21.6 %collective-permute-start.3 = (f16[272,384]{1,0:T(8,128)(2,1)S(1)}, f16[272,384]{1,0:T(8,128)(2,1)S(1)}, u32[]{:S(2)}, u32[]{:S(2)}) collective-permute-start(f16[272,384]{1,0:T(8,128)(2,1)S(1)} %convert_element_type.52), channel_id=1, source_target_pairs={{0,64},{64,0},{128,192},{192,128},{256,320},{320,256},{384,448},{4... | collective-permute-start | bytes 626696 | tf_op jit(solution)/shard_map/ppermute | solution.py:342
  179.7 12.0 %collective-permute-start.4 = (f16[272,384]{1,0:T(8,128)(2,1)S(1)}, f16[272,384]{1,0:T(8,128)(2,1)S(1)}, u32[]{:S(2)}, u32[]{:S(2)}) collective-permute-start(f16[272,384]{1,0:T(8,128)(2,1)S(1)} %convert_element_type.52), channel_id=1, source_target_pairs={{0,128},{64,192},{128,0},{192,64},{256,384},{320,448},{384,256},{4... | collective-permute-start | bytes 626696 | tf_op jit(solution)/shard_map/ppermute | solution.py:342
  184.5 12.6 %collective-permute-start.5 = (f16[272,384]{1,0:T(8,128)(2,1)S(1)}, f16[272,384]{1,0:T(8,128)(2,1)S(1)}, u32[]{:S(2)}, u32[]{:S(2)}) collective-permute-start(f16[272,384]{1,0:T(8,128)(2,1)S(1)} %convert_element_type.52), channel_id=1, source_target_pairs={{0,192},{64,128},{128,64},{192,0},{256,448},{320,384},{384,320},{4... | collective-permute-start | bytes 626696 | tf_op jit(solution)/shard_map/ppermute | solution.py:342

commit v11 on v10

--- a/solution.py
+++ b/solution.py
@@ -31,7 +31,6 @@
 OTHER_CORE = [(i, i ^ 1) for i in range(64)]
 OTHER_HALF = [(i, i ^ 4) for i in range(8)]
 X_GROUPS = [[h * XN + x for x in range(XN)] for h in range(2)]
-ALONG_X = [[(i, i ^ k) for i in range(8)] for k in range(XN)]
 
 PANEL, STEP = 64, 8
 TOP_POWER = 13
@@ -147,15 +146,18 @@
     return total
 
 
-def first_products_kernel(place_ref, mine_ref, other_ref, own_ref, sketch_ref, out_ref, range_ref):
+def products_kernel(
+    core_ref, mine_ref, other_ref, own_ref, sketch_ref,
+    first_ref, second_ref, range_ref, held_first, held_second, held_range, sems,
+):
     half = mine_ref.shape[0]
     ff, rank = sketch_ref.shape
-    block, slab, chunk = rank // XN, ff // XN, FIRST
-    core = place_ref[0]
+    block, slab = rank // XN, ff // XN
     gram = jnp.zeros((rank, rank), F32)
-    delta = jnp.zeros((chunk, ff), F32)
-    for load_ref, at_core in ((mine_ref, core), (other_ref, 1 - core)):
-        rows = pl.ds(pl.multiple_of(at_core * half, half), half)
+    delta = jnp.zeros((rank, ff), F32)
+    copies = []
+    for i, load_ref in enumerate((mine_ref, other_ref)):
+        rows = pl.ds(pl.multiple_of((core_ref[0] ^ i) * half, half), half)
         own = own_ref[rows, :]
         base_sketch = (
             load_ref[:, ff : ff + rank].astype(F32)
@@ -163,62 +165,50 @@
             + load_ref[:, ff + 2 * rank :].astype(F32)
         )
         range_rows = jnp.dot(own, sketch_ref[...], preferred_element_type=F32) - base_sketch
-        range_ref[rows, :] = range_rows
+        held_range[i] = range_rows
+        copies.append(pltpu.make_async_copy(held_range.at[i], range_ref.at[rows], sems.at[i]))
+        copies[i].start()
         turned = range_rows.T
         gram += jnp.dot(turned, range_rows, precision=HIGHEST, preferred_element_type=F32)
-        delta += range_product(turned[:chunk], own, load_ref[:, :ff])
+        delta += range_product(turned, own, load_ref[:, :ff])
     for b in range(XN):
         mine = gram[b * block : (b + 1) * block]
         kept = jnp.concatenate(
             [mine[:, (b + j) % XN * block :][:, :block] for j in range(XN - 1)], axis=1
         )
         packed = jnp.concatenate([kept[: block // 2], kept[block // 2 :]], axis=1)
-        out_ref[b, : block // 2, :] = packed
-        out_ref[b, block // 2 :, :] = delta[:, b * slab : (b + 1) * slab]
-
-
-def first_products(place, mine, other, own, sketch):
+        held_first[b, : block // 2, :] = packed
+        held_first[b, block // 2 :, :] = delta[:FIRST, b * slab : (b + 1) * slab]
+    copies.append(pltpu.make_async_copy(held_first, first_ref, sems.at[2]))
+    copies[2].start()
+    for b in range(XN):
+        held_second[b] = delta[FIRST:, b * slab : (b + 1) * slab]
+    copies.append(pltpu.make_async_copy(held_second, second_ref, sems.at[3]))
+    copies[3].start()
+    for copy in copies:
+        copy.wait()
+
+
+def products(core, mine, other, own, sketch):
     rows, ff = own.shape
     rank = sketch.shape[1]
+    first = (XN, rank // XN // 2 + FIRST, ff // XN)
+    second = (XN, rank - FIRST, ff // XN)
     return pl.pallas_call(
-        first_products_kernel,
-        out_shape=(
-            jax.ShapeDtypeStruct((XN, rank // XN // 2 + FIRST, ff // XN), F32),
-            jax.ShapeDtypeStruct((rows, rank), F32),
-        ),
+        products_kernel,
+        out_shape=[jax.ShapeDtypeStruct(shape, F32) for shape in (first, second, (rows, rank))],
         in_specs=[SMEM] + [VMEM] * 4,
-        out_specs=(VMEM, VMEM),
-        compiler_params=pltpu.CompilerParams(vmem_limit_bytes=40 * MIB),
-        cost_estimate=pl.CostEstimate(flops=3 * 10**9, bytes_accessed=2**10, transcendentals=0),
-        name="first_products",
-    )(place, mine, other, own, sketch)
-
-
-def second_products_kernel(place_ref, mine_ref, other_ref, own_ref, range_ref, out_ref):
-    half = mine_ref.shape[0]
-    ff, rank = own_ref.shape[1], range_ref.shape[1]
-    slab, chunk = ff // XN, FIRST
-    core = place_ref[0]
-    delta = jnp.zeros((rank - chunk, ff), F32)
-    for load_ref, at_core in ((mine_ref, core), (other_ref, 1 - core)):
-        rows = pl.ds(pl.multiple_of(at_core * half, half), half)
-        turned = range_ref[rows, :].T
-        delta += range_product(turned[chunk:], own_ref[rows, :], load_ref[:, :ff])
-    for b in range(XN):
-        out_ref[b] = delta[:, b * slab : (b + 1) * slab]
-
-
-def second_products(place, mine, other, own, range_rows):
-    ff, rank = own.shape[1], range_rows.shape[1]
-    return pl.pallas_call(
-        second_products_kernel,
-        out_shape=jax.ShapeDtypeStruct((XN, rank - FIRST, ff // XN), F32),
-        in_specs=[SMEM] + [VMEM] * 4,
-        out_specs=VMEM,
-        compiler_params=pltpu.CompilerParams(vmem_limit_bytes=40 * MIB),
-        cost_estimate=pl.CostEstimate(flops=2 * 10**9, bytes_accessed=2**10, transcendentals=0),
-        name="second_products",
-    )(place, mine, other, own, range_rows)
+        out_specs=[pl.BlockSpec(memory_space=pltpu.HBM)] * 3,
+        scratch_shapes=[
+            pltpu.VMEM(first, F32),
+            pltpu.VMEM(second, F32),
+            pltpu.VMEM((CN, rows // CN, rank), F32),
+            pltpu.SemaphoreType.DMA((4,)),
+        ],
+        compiler_params=pltpu.CompilerParams(vmem_limit_bytes=32 * MIB),
+        cost_estimate=pl.CostEstimate(flops=5 * 10**9, bytes_accessed=2**10, transcendentals=0),
+        name="products",
+    )(core, mine, other, own, sketch)
 
 
 def finished_kernel(inverse_ref, *refs):
@@ -251,15 +241,14 @@
     )(inverse, *pairs)
 
 
-def assembled_kernel(place_ref, *refs):
-    blocks, (out_ref, held_ref, sems) = refs[:XN], refs[XN:]
+def assembled_kernel(blocks_ref, out_ref, held_ref, sems):
     rank, slab = held_ref.shape[1:]
     copies = []
-    for k, ref in enumerate(blocks):
-        held_ref[k] = ref[:rank] * jnp.exp2(ref[rank : rank + 1] - TOP_POWER)
-        start = pl.multiple_of((place_ref[0] ^ k) * slab, slab)
+    for b in range(XN):
+        scale = jnp.exp2(blocks_ref[b, rank : rank + 1] - TOP_POWER)
+        held_ref[b] = blocks_ref[b, :rank] * scale
         copy = pltpu.make_async_copy(
-            held_ref.at[k], out_ref.at[:, pl.ds(start, slab)], sems.at[k]
+            held_ref.at[b], out_ref.at[:, pl.ds(b * slab, slab)], sems.at[b]
         )
         copy.start()
         copies.append(copy)
@@ -267,17 +256,17 @@
         copy.wait()
 
 
-def assembled(place, blocks):
-    rank, slab = blocks[0].shape[0] - 16, blocks[0].shape[1]
+def assembled(blocks):
+    rank, slab = blocks.shape[1] - 16, blocks.shape[2]
     return pl.pallas_call(
         assembled_kernel,
         out_shape=jax.ShapeDtypeStruct((rank, XN * slab), F32),
-        in_specs=[SMEM] + [VMEM] * XN,
+        in_specs=[VMEM],
         out_specs=pl.BlockSpec(memory_space=pl.ANY),
         scratch_shapes=[pltpu.VMEM((XN, rank, slab), F32), pltpu.SemaphoreType.DMA((XN,))],
         compiler_params=pltpu.CompilerParams(vmem_limit_bytes=16 * MIB),
         name="assembled",
-    )(place, *blocks)
+    )(blocks)
 
 
 def per_device(counts, up_weights, sketch):
@@ -318,15 +307,13 @@
     ).reshape(rows // CN, wide)
     other = lax.ppermute(load, "exp", OTHER_CORE)
 
-    at_core, at_x = lax.axis_index("exp") % CN, lax.axis_index("grp") % XN
-    place, own = at_core.reshape(1), own.reshape(rows, ff)
+    core, own = (lax.axis_index("exp") % CN).reshape(1), own.reshape(rows, ff)
 
     def to_owners(blocks):
         return lax.all_to_all(blocks, "grp", 0, 0, axis_index_groups=X_GROUPS)
 
-    first, range_rows = first_products(place, load, other, own, sketch)
-    first = to_owners(first)
-    second = to_owners(second_products(place, load, other, own, range_rows))
+    first, second, range_rows = products(core, load, other, own, sketch)
+    first, second = to_owners(first), to_owners(second)
     first = jnp.sum(first, axis=0)
     first_came = lax.ppermute(first, "grp", OTHER_HALF)
     second = jnp.sum(second, axis=0)
@@ -336,11 +323,9 @@
     inverse = inverse_factor(to_owners(jnp.broadcast_to(gram, (XN,) + gram.shape)), rank)
     chunks = [first[packed:], first_came[packed:], second, second_came]
     inverse, chunks = lax.optimization_barrier((inverse, chunks))
-    block = lax.optimization_barrier(finished(inverse, chunks).astype(jnp.float16))
-    blocks = {0: block}
-    for k in (2, 3, 1):
-        blocks[k] = lax.ppermute(block, "grp", ALONG_X[k])
-    coeff = assembled(at_x.reshape(1), [blocks[k].astype(F32) for k in range(XN)])
+    block = finished(inverse, chunks).astype(jnp.float16)
+    blocks = to_owners(jnp.broadcast_to(block, (XN,) + block.shape))
+    coeff = assembled(blocks.astype(F32))
 
     ortho = lax.dot_general(
         range_rows, inverse, (((1,), (1,)), ((), ())), precision=HIGHEST

time: 199 us -> 197 us (0.990)
  the two profiles are of different devices: /device:TPU:65 before, /device:TPU:96 now
where the time goes in v11:
time: 197 us
  blocking collectives  101 us (51%)
  waiting for transfers between devices  39.6 us (20%)
  starting transfers between devices  28.9 us (15%)
  Pallas kernels  17 us (9%)
  local copies, waits for them, and re-layouts  5.93 us (3%)
    all_to_all x1, blocking collectives, per_device(): lax.all_to_all(jnp.concatenate([own, tag], axis=2), 'exp', 0, 0, axis_ind...  28.1 us
    all_to_all x3, waiting for transfers between devices, to_owners(): return lax.all_to_all(blocks, 'grp', 0, 0, axis_index_groups=X_GROUPS)  24.8 us
    all_to_all x1, blocking collectives, per_device(): lax.all_to_all(jnp.broadcast_to(load, (YN * NN, FN * piece, wide)), 'exp'...  20.5 us
    all_to_all x1, blocking collectives, per_device(): lax.all_to_all(jnp.concatenate([weighted.reshape(FN, piece, ff), freq_sum...  19.7 us
    all_to_all x1, blocking collectives, per_device(): lax.all_to_all(jnp.broadcast_to(load, (FN, piece, wide)), 'exp', 0, 0, ax...  17.9 us
    all_to_all x1, blocking collectives, to_owners(): return lax.all_to_all(blocks, 'grp', 0, 0, axis_index_groups=X_GROUPS)  14.6 us
    ppermute x1, waiting for transfers between devices, per_device(): second_came = lax.ppermute(second, 'grp', OTHER_HALF)  11.9 us
    all_to_all x3, starting transfers between devices, to_owners(): return lax.all_to_all(blocks, 'grp', 0, 0, axis_index_groups=X_GROUPS)  10.6 us
  transfers between devices with their start and end apart: 6, of which 5 were waited for; matrix products, arithmetic and copies ran while one was open for 1% of the time, Pallas kernels for 5%

profile of v11, /device:TPU:96, one launch (start us, length us, event | category | flops | bytes accessed | tf_op | source)
XLA Modules:
  0.0 196.7 jit_solution(1873877209097691001)
XLA Ops:
  1.3 1.6 copy.16
  3.1 28.1 %all_to_all.40 = bf16[16,32,1664]{2,1,0:T(8,128)(2,1)S(1)} all-to-all(bf16[16,32,1664]{2,1,0:T(8,128)(2,1)S(1)} %pad_maximum_fusion), channel_id=1, replica_groups={{0,2,16,18,32,34,48,50,1,3,17,19,33,35,49,51},{4,6,20,22,36,38,52,54,5,..., dimensions={0} | all-to-all | bytes 3407872 | tf_op jit(solution)/shard_map/all_to_all | solution.py:283
  31.2 0.8 fusion.5
  33.1 19.7 %all_to_all.41 = f32[4,8,1664]{2,1,0:T(8,128)S(1)} all-to-all(f32[4,8,1664]{2,1,0:T(8,128)S(1)} %concatenate.10), channel_id=1, replica_groups={{0,4,8,12},{1,5,9,13},{2,6,10,14},{3,7,11,15},{16,20,24,28},{17,21,25,2..., dimensions={0} | all-to-all | bytes 425984 | tf_op jit(solution)/shard_map/all_to_all | solution.py:290
  53.6 17.9 %all_to_all.42 = bf16[4,8,2304]{2,1,0:T(8,128)(2,1)S(1)} all-to-all(bf16[4,8,2304]{2,1,0:T(8,128)(2,1)S(1)} %broadcast_in_dim.29), channel_id=1, replica_groups={{0,4,8,12},{1,5,9,13},{2,6,10,14},{3,7,11,15},{16,20,24,28},{17,21,25,2..., dimensions={0} | all-to-all | bytes 294912 | tf_op jit(solution)/shard_map/all_to_all | solution.py:301
  71.6 20.5 %all_to_all.43 = bf16[8,32,2304]{2,1,0:T(8,128)(2,1)S(1)} all-to-all(bf16[8,32,2304]{2,1,0:T(8,128)(2,1)S(1)} %broadcast_in_dim.30), channel_id=1, replica_groups={{0,2,16,18,32,34,48,50},{1,3,17,19,33,35,49,51},{4,6,20,22,36,38,52,54}..., dimensions={0} | all-to-all | bytes 2359296 | tf_op jit(solution)/shard_map/all_to_all | solution.py:304
  92.1 1.9 collective-permute-start
  94.0 2.9 %collective-permute-done.other_ref = bf16[256,2304]{1,0:T(8,128)(2,1)} collective-permute-done((bf16[256,2304]{1,0:T(8,128)(2,1)S(1)}, bf16[256,2304]{1,0:T(8,128)(2,1)}, u32[]{:S(2)}, u32[]{:S(2)}) %collective-permute-start) | collective-permute-done | bytes 1179680 | tf_op jit(solution)/shard_map/ppermute | solution.py:308
  96.9 6.2 %products.1 = (f32[4,96,384]{2,1,0:T(8,128)S(1)}, f32[4,192,384]{2,1,0:T(8,128)S(1)}, f32[512,256]{1,0:T(8,128)S(1)}) custom-call(s32[1]{0:T(128)} %bitcast.5.core_ref, bf16[256,2304]{1,0:T(8,128)(2,1)S(1)} %bitcast.25, bf16[256,2304]{1,0:T(8,128)(2,1)} %collective-permute-done.other_ref, bf16[512,1536]{1,0:T(8,128)(2,1)S(1)} %bitcast.23, ...), custom_call_target="tpu_custom_call" | custom-call | flops 5000000000 | bytes 1024 | tf_op jit(solution)/shard_map/products/pallas_call | solution.py:197
  103.1 0.8 copy-done.2
  103.9 14.6 %all_to_all.44 = f32[4,96,384]{2,1,0:T(8,128)S(1)} all-to-all(f32[4,96,384]{2,1,0:T(8,128)S(1)} %get-tuple-element.12), channel_id=1, replica_groups={{0,64,128,192},{256,320,384,448},{1,65,129,193},{257,321,385,449},{2,66..., dimensions={0} | all-to-all | bytes 1179648 | tf_op jit(solution)/shard_map/all_to_all | solution.py:313
  118.5 3.5 %all-to-all-start.6 = ((f32[4,192,384]{2,1,0:T(8,128)}), f32[4,192,384]{2,1,0:T(8,128)S(1)}, u32[]{:S(2)}, u32[]{:S(2)}) async-start(f32[4,192,384]{2,1,0:T(8,128)} %copy-done), calls=%async_computation.6 | async-start | bytes 2359296 | tf_op jit(solution)/shard_map/all_to_all | solution.py:313
  122.0 8.2 %collective-permute-start.1 = (f32[96,384]{1,0:T(8,128)S(1)}, f32[96,384]{1,0:T(8,128)S(1)}, u32[]{:S(2)}, u32[]{:S(2)}) collective-permute-start(f32[96,384]{1,0:T(8,128)S(1)} %reduce_sum.48), channel_id=1, source_target_pairs={{0,256},{64,320},{128,384},{192,448},{256,0},{320,64},{384,128},{4... | collective-permute-start | bytes 442376 | tf_op jit(solution)/shard_map/ppermute | solution.py:318
  130.3 7.6 %all-to-all-done.6 = f32[4,192,384]{2,1,0:T(8,128)S(1)} async-done(((f32[4,192,384]{2,1,0:T(8,128)}), f32[4,192,384]{2,1,0:T(8,128)S(1)}, u32[]{:S(2)}, u32[]{:S(2)}) %all-to-all-start.6) | async-done | bytes 1179680 | tf_op jit(solution)/shard_map/all_to_all | solution.py:313
  138.0 8.2 %collective-permute-start.2 = (f32[192,384]{1,0:T(8,128)S(1)}, f32[192,384]{1,0:T(8,128)S(1)}, u32[]{:S(2)}, u32[]{:S(2)}) collective-permute-start(f32[192,384]{1,0:T(8,128)S(1)} %reduce_sum.49.refs_2_), channel_id=1, source_target_pairs={{0,256},{64,320},{128,384},{192,448},{256,0},{320,64},{384,128},{4... | collective-permute-start | bytes 884744 | tf_op jit(solution)/shard_map/ppermute | solution.py:320
  146.9 3.5 %all-to-all-start.5 = ((f32[4,32,384]{2,1,0:T(8,128)}), f32[4,32,384]{2,1,0:T(8,128)S(1)}, u32[]{:S(2)}, u32[]{:S(2)}) async-start(f32[4,32,384]{2,1,0:T(8,128)} %broadcast_in_dim.31), calls=%async_computation.5 | async-start | bytes 393216 | tf_op jit(solution)/shard_map/all_to_all | solution.py:313
  150.5 6.1 %all-to-all-done.5.packed_ref = f32[4,32,384]{2,1,0:T(8,128)S(1)} async-done(((f32[4,32,384]{2,1,0:T(8,128)}), f32[4,32,384]{2,1,0:T(8,128)S(1)}, u32[]{:S(2)}, u32[]{:S(2)}) %all-to-all-start.5) | async-done | bytes 196640 | tf_op jit(solution)/shard_map/all_to_all | solution.py:313
  156.6 8.9 %inverse_factor.1.inverse_ref = f32[256,256]{1,0:T(8,128)S(1)} custom-call(f32[4,32,384]{2,1,0:T(8,128)S(1)} %all-to-all-done.5.packed_ref), custom_call_target="tpu_custom_call" | custom-call | flops 536870912 | bytes 1024 | tf_op jit(solution)/shard_map/inverse_factor/pallas_call | solution.py:126
  165.5 11.9 %collective-permute-done.2.refs_3_ = f32[192,384]{1,0:T(8,128)S(1)} collective-permute-done((f32[192,384]{1,0:T(8,128)S(1)}, f32[192,384]{1,0:T(8,128)S(1)}, u32[]{:S(2)}, u32[]{:S(2)}) %collective-permute-start.2) | collective-permute-done | bytes 294944 | tf_op jit(solution)/shard_map/ppermute | solution.py:320
  178.1 1.0 broadcast_in_dim.32
  179.1 3.5 %all-to-all-start.7 = ((f16[4,272,384]{2,1,0:T(8,128)(2,1)}), f16[4,272,384]{2,1,0:T(8,128)(2,1)S(1)}, u32[]{:S(2)}, u32[]{:S(2)}) async-start(f16[4,272,384]{2,1,0:T(8,128)(2,1)} %broadcast_in_dim.32), calls=%async_computation.7 | async-start | bytes 1671168 | tf_op jit(solution)/shard_map/all_to_all | solution.py:313
  183.2 0.9 copy.18
  184.1 11.1 %all-to-all-done.7 = f16[4,272,384]{2,1,0:T(8,128)(2,1)S(1)} async-done(((f16[4,272,384]{2,1,0:T(8,128)(2,1)}), f16[4,272,384]{2,1,0:T(8,128)(2,1)S(1)}, u32[]{:S(2)}, u32[]{:S(2)}) %all-to-all-start.7) | async-done | bytes 835616 | tf_op jit(solution)/shard_map/all_to_all | solution.py:313
  195.3 1.2 assembled.1
  (33 shorter events, 4.5 us)
Async XLA Ops:
  31.2 21.8 %copy-start.1 = (bf16[1536,256]{1,0:T(8,128)(2,1)S(1)}, bf16[1536,256]{1,0:T(8,128)(2,1)}, u32[]{:S(2)}) copy-start(bf16[1536,256]{1,0:T(8,128)(2,1)} %sketch_ref.1) | copy-start | bytes 2359300
  53.0 0.6 copy-start.4
  92.1 4.9 %collective-permute-start = (bf16[256,2304]{1,0:T(8,128)(2,1)S(1)}, bf16[256,2304]{1,0:T(8,128)(2,1)}, u32[]{:S(2)}, u32[]{:S(2)}) collective-permute-start(bf16[256,2304]{1,0:T(8,128)(2,1)S(1)} %bitcast.24), channel_id=1, source_target_pairs={{0,1},{1,0},{2,3},{3,2},{4,5},{5,4},{6,7},{7,6},{8,9},{9,8},{10,11... | collective-permute-start | bytes 3538952 | tf_op jit(solution)/shard_map/ppermute | solution.py:308
  103.1 0.8 copy-start.2
  103.9 14.6 %copy-start = (f32[4,192,384]{2,1,0:T(8,128)}, f32[4,192,384]{2,1,0:T(8,128)S(1)}, u32[]{:S(2)}) copy-start(f32[4,192,384]{2,1,0:T(8,128)S(1)} %get-tuple-element.13) | copy-start | bytes 3538948
  118.5 19.4 %all-to-all-start.6 = ((f32[4,192,384]{2,1,0:T(8,128)}), f32[4,192,384]{2,1,0:T(8,128)S(1)}, u32[]{:S(2)}, u32[]{:S(2)}) async-start(f32[4,192,384]{2,1,0:T(8,128)} %copy-done), calls=%async_computation.6 | async-start | bytes 2359296 | tf_op jit(solution)/shard_map/all_to_all | solution.py:313
  122.0 24.2 %collective-permute-start.1 = (f32[96,384]{1,0:T(8,128)S(1)}, f32[96,384]{1,0:T(8,128)S(1)}, u32[]{:S(2)}, u32[]{:S(2)}) collective-permute-start(f32[96,384]{1,0:T(8,128)S(1)} %reduce_sum.48), channel_id=1, source_target_pairs={{0,256},{64,320},{128,384},{192,448},{256,0},{320,64},{384,128},{4... | collective-permute-start | bytes 442376 | tf_op jit(solution)/shard_map/ppermute | solution.py:318
  138.0 39.3 %collective-permute-start.2 = (f32[192,384]{1,0:T(8,128)S(1)}, f32[192,384]{1,0:T(8,128)S(1)}, u32[]{:S(2)}, u32[]{:S(2)}) collective-permute-start(f32[192,384]{1,0:T(8,128)S(1)} %reduce_sum.49.refs_2_), channel_id=1, source_target_pairs={{0,256},{64,320},{128,384},{192,448},{256,0},{320,64},{384,128},{4... | collective-permute-start | bytes 884744 | tf_op jit(solution)/shard_map/ppermute | solution.py:320
  146.9 9.7 %all-to-all-start.5 = ((f32[4,32,384]{2,1,0:T(8,128)}), f32[4,32,384]{2,1,0:T(8,128)S(1)}, u32[]{:S(2)}, u32[]{:S(2)}) async-start(f32[4,32,384]{2,1,0:T(8,128)} %broadcast_in_dim.31), calls=%async_computation.5 | async-start | bytes 393216 | tf_op jit(solution)/shard_map/all_to_all | solution.py:313
  178.0 4.5 %copy-start.3 = (f32[512,256]{1,0:T(8,128)S(1)}, f32[512,256]{1,0:T(8,128)}, u32[]{:S(2)}) copy-start(f32[512,256]{1,0:T(8,128)} %copy-done.2) | copy-start | bytes 1572868
  179.1 16.1 %all-to-all-start.7 = ((f16[4,272,384]{2,1,0:T(8,128)(2,1)}), f16[4,272,384]{2,1,0:T(8,128)(2,1)S(1)}, u32[]{:S(2)}, u32[]{:S(2)}) async-start(f16[4,272,384]{2,1,0:T(8,128)(2,1)} %broadcast_in_dim.32), calls=%async_computation.7 | async-start | bytes 1671168 | tf_op jit(solution)/shard_map/all_to_all | solution.py:313

commit v12 on v11

--- a/solution.py
+++ b/solution.py
@@ -146,69 +146,102 @@
     return total
 
 
+def weighted_kernel(got_ref, out_ref):
+    members, rows, wide = got_ref.shape
+    ff = wide - 128
+    piece = rows // FN
+    total, freq_sum = jnp.zeros((rows, ff), F32), jnp.zeros((1, 1), F32)
+    for j in range(members):
+        tag = got_ref[j, :16, ff:].astype(F32)
+        freq = tag[:1, :1] * 64 + tag[:1, 1:2]
+        freq_sum += freq
+        total += freq * got_ref[j, :, :ff].astype(F32)
+    for f in range(FN):
+        out_ref[f, :, :ff] = total[f * piece : (f + 1) * piece]
+        out_ref[f, :, ff:] = jnp.broadcast_to(freq_sum, (piece, 128))
+
+
+def weighted(got):
+    members, rows, wide = got.shape
+    return pl.pallas_call(
+        weighted_kernel,
+        out_shape=jax.ShapeDtypeStruct((FN, rows // FN, wide), F32),
+        in_specs=[VMEM],
+        out_specs=VMEM,
+        compiler_params=pltpu.CompilerParams(vmem_limit_bytes=16 * MIB),
+        cost_estimate=pl.CostEstimate(flops=2**20, bytes_accessed=2**21, transcendentals=0),
+        name="weighted",
+    )(got)
+
+
+def half_products(core, load_ref, own_ref, sketch_ref, range_ref):
+    half = load_ref.shape[0]
+    ff, rank = sketch_ref.shape
+    own = own_ref[pl.ds(pl.multiple_of(core * half, half), half), :]
+    base_sketch = (
+        load_ref[:, ff : ff + rank].astype(F32)
+        + load_ref[:, ff + rank : ff + 2 * rank].astype(F32)
+        + load_ref[:, ff + 2 * rank :].astype(F32)
+    )
+    range_rows = jnp.dot(own, sketch_ref[...], preferred_element_type=F32) - base_sketch
+    range_ref[...] = range_rows
+    turned = range_rows.T
+    gram = jnp.dot(turned, range_rows, precision=HIGHEST, preferred_element_type=F32)
+    return gram, range_product(turned, own, load_ref[:, :ff])
+
+
+def own_products_kernel(core_ref, load_ref, own_ref, sketch_ref, gram_ref, delta_ref, range_ref):
+    gram_ref[...], delta_ref[...] = half_products(
+        core_ref[0], load_ref, own_ref, sketch_ref, range_ref
+    )
+
+
 def products_kernel(
-    core_ref, mine_ref, other_ref, own_ref, sketch_ref,
-    first_ref, second_ref, range_ref, held_first, held_second, held_range, sems,
+    core_ref, load_ref, own_ref, sketch_ref, own_gram_ref, own_delta_ref,
+    first_ref, second_ref, range_ref,
 ):
-    half = mine_ref.shape[0]
     ff, rank = sketch_ref.shape
     block, slab = rank // XN, ff // XN
-    gram = jnp.zeros((rank, rank), F32)
-    delta = jnp.zeros((rank, ff), F32)
-    copies = []
-    for i, load_ref in enumerate((mine_ref, other_ref)):
-        rows = pl.ds(pl.multiple_of((core_ref[0] ^ i) * half, half), half)
-        own = own_ref[rows, :]
-        base_sketch = (
-            load_ref[:, ff : ff + rank].astype(F32)
-            + load_ref[:, ff + rank : ff + 2 * rank].astype(F32)
-            + load_ref[:, ff + 2 * rank :].astype(F32)
-        )
-        range_rows = jnp.dot(own, sketch_ref[...], preferred_element_type=F32) - base_sketch
-        held_range[i] = range_rows
-        copies.append(pltpu.make_async_copy(held_range.at[i], range_ref.at[rows], sems.at[i]))
-        copies[i].start()
-        turned = range_rows.T
-        gram += jnp.dot(turned, range_rows, precision=HIGHEST, preferred_element_type=F32)
-        delta += range_product(turned, own, load_ref[:, :ff])
+    gram, delta = half_products(1 - core_ref[0], load_ref, own_ref, sketch_ref, range_ref)
+    gram += own_gram_ref[...]
+    delta += own_delta_ref[...]
     for b in range(XN):
         mine = gram[b * block : (b + 1) * block]
         kept = jnp.concatenate(
             [mine[:, (b + j) % XN * block :][:, :block] for j in range(XN - 1)], axis=1
         )
         packed = jnp.concatenate([kept[: block // 2], kept[block // 2 :]], axis=1)
-        held_first[b, : block // 2, :] = packed
-        held_first[b, block // 2 :, :] = delta[:FIRST, b * slab : (b + 1) * slab]
-    copies.append(pltpu.make_async_copy(held_first, first_ref, sems.at[2]))
-    copies[2].start()
-    for b in range(XN):
-        held_second[b] = delta[FIRST:, b * slab : (b + 1) * slab]
-    copies.append(pltpu.make_async_copy(held_second, second_ref, sems.at[3]))
-    copies[3].start()
-    for copy in copies:
-        copy.wait()
-
-
-def products(core, mine, other, own, sketch):
-    rows, ff = own.shape
-    rank = sketch.shape[1]
+        first_ref[b, : block // 2, :] = packed
+        first_ref[b, block // 2 :, :] = delta[:FIRST, b * slab : (b + 1) * slab]
+        second_ref[b] = delta[FIRST:, b * slab : (b + 1) * slab]
+
+
+def own_products(core, load, own, sketch):
+    half, (ff, rank) = load.shape[0], sketch.shape
+    return pl.pallas_call(
+        own_products_kernel,
+        out_shape=[jax.ShapeDtypeStruct(shape, F32) for shape in ((rank, rank), (rank, ff), (half, rank))],
+        in_specs=[SMEM] + [VMEM] * 3,
+        out_specs=[VMEM] * 3,
+        compiler_params=pltpu.CompilerParams(vmem_limit_bytes=32 * MIB),
+        cost_estimate=pl.CostEstimate(flops=2 * 10**9, bytes_accessed=2**10, transcendentals=0),
+        name="own_products",
+    )(core, load, own, sketch)
+
+
+def products(core, load, own, sketch, own_gram, own_delta):
+    half, (ff, rank) = load.shape[0], sketch.shape
     first = (XN, rank // XN // 2 + FIRST, ff // XN)
     second = (XN, rank - FIRST, ff // XN)
     return pl.pallas_call(
         products_kernel,
-        out_shape=[jax.ShapeDtypeStruct(shape, F32) for shape in (first, second, (rows, rank))],
-        in_specs=[SMEM] + [VMEM] * 4,
-        out_specs=[pl.BlockSpec(memory_space=pltpu.HBM)] * 3,
-        scratch_shapes=[
-            pltpu.VMEM(first, F32),
-            pltpu.VMEM(second, F32),
-            pltpu.VMEM((CN, rows // CN, rank), F32),
-            pltpu.SemaphoreType.DMA((4,)),
-        ],
+        out_shape=[jax.ShapeDtypeStruct(shape, F32) for shape in (first, second, (half, rank))],
+        in_specs=[SMEM] + [VMEM] * 5,
+        out_specs=[VMEM] * 3,
         compiler_params=pltpu.CompilerParams(vmem_limit_bytes=32 * MIB),
-        cost_estimate=pl.CostEstimate(flops=5 * 10**9, bytes_accessed=2**10, transcendentals=0),
+        cost_estimate=pl.CostEstimate(flops=3 * 10**9, bytes_accessed=2**10, transcendentals=0),
         name="products",
-    )(core, mine, other, own, sketch)
+    )(core, load, own, sketch, own_gram, own_delta)
 
 
 def finished_kernel(inverse_ref, *refs):
@@ -283,14 +316,8 @@
     got = lax.all_to_all(
         jnp.concatenate([own, tag], axis=2), "exp", 0, 0, axis_index_groups=CYN_GROUPS
     )
-    freq = got[:, 0, ff].astype(F32) * 64 + got[:, 0, ff + 1].astype(F32)
-    weighted = jnp.sum(freq[:, None, None] * got[:, :, :ff].astype(F32), axis=0)
-    freq_sum = jnp.broadcast_to(jnp.sum(freq), (FN, piece, 128))
-
-    sums = lax.all_to_all(
-        jnp.concatenate([weighted.reshape(FN, piece, ff), freq_sum], axis=2),
-        "exp", 0, 0, axis_index_groups=FAR_GROUPS,
-    )
+
+    sums = lax.all_to_all(weighted(got), "exp", 0, 0, axis_index_groups=FAR_GROUPS)
     sums = jnp.sum(sums, axis=0)
     base_rows = sums[:, :ff] / sums[:, ff : ff + 1]
     base_piece = base_rows.astype(BF16)
@@ -312,7 +339,8 @@
     def to_owners(blocks):
         return lax.all_to_all(blocks, "grp", 0, 0, axis_index_groups=X_GROUPS)
 
-    first, second, range_rows = products(core, load, other, own, sketch)
+    own_gram, own_delta, own_range = own_products(core, load, own, sketch)
+    first, second, other_range = products(core, other, own, sketch, own_gram, own_delta)
     first, second = to_owners(first), to_owners(second)
     first = jnp.sum(first, axis=0)
     first_came = lax.ppermute(first, "grp", OTHER_HALF)
@@ -327,10 +355,15 @@
     blocks = to_owners(jnp.broadcast_to(block, (XN,) + block.shape))
     coeff = assembled(blocks.astype(F32))
 
-    ortho = lax.dot_general(
-        range_rows, inverse, (((1,), (1,)), ((), ())), precision=HIGHEST
-    )
-    basis = ortho * math.sqrt(rows * lax.axis_size("grp"))
+    scale = math.sqrt(rows * lax.axis_size("grp"))
+    halves = [
+        scale * lax.dot_general(half, inverse, (((1,), (1,)), ((), ())), precision=HIGHEST)
+        for half in (own_range, other_range)
+    ]
+    on_first = core[0] == 0
+    basis = jnp.stack(
+        [jnp.where(on_first, halves[i], halves[1 - i]) for i in range(CN)]
+    )
     basis = basis.reshape(CN, YN, NN, FN, piece, rank).transpose(1, 3, 2, 0, 4, 5)
     return (base_piece, basis.reshape(1, rows, rank), coeff[None])
 

time: 197 us -> 194 us (0.985)
  waiting for transfers between devices: 39.6 us -> 36.9 us
    pallas_call x0 -> x2, Pallas kernels: none -> 2.88 us  [the longest x1 2.4 us: own_products(): pl.pallas_call(own_products_kernel, out_shape=[jax.ShapeDtypeStruct(shape...]
    ppermute x1, waiting for transfers between devices: 2.93 us -> 0.52 us  [per_device(): other = lax.ppermute(load, 'exp', OTHER_CORE)]
  transfers between devices with their start and end apart: 6 -> 6, of which waited for: 5 -> 5; matrix products, arithmetic and copies ran while one was open for 1% -> 1% of each run, Pallas kernels for 5% -> 6%
where the time goes in v12:
time: 194 us; the launch traced here: 193 us
  blocking collectives  101 us (52%)
  waiting for transfers between devices  36.9 us (19%)
  starting transfers between devices  28.9 us (15%)
  Pallas kernels  18.2 us (9%)
  local copies, waits for them, and re-layouts  4.47 us (2%)
    all_to_all x1, blocking collectives, per_device(): lax.all_to_all(jnp.concatenate([own, tag], axis=2), 'exp', 0, 0, axis_ind...  28.1 us
    all_to_all x3, waiting for transfers between devices, to_owners(): return lax.all_to_all(blocks, 'grp', 0, 0, axis_index_groups=X_GROUPS)  24.5 us
    all_to_all x1, blocking collectives, per_device(): lax.all_to_all(jnp.broadcast_to(load, (YN * NN, FN * piece, wide)), 'exp'...  20.5 us
    all_to_all x1, blocking collectives, per_device(): lax.all_to_all(weighted(got), 'exp', 0, 0, axis_index_groups=FAR_GROUPS)  19.7 us
    all_to_all x1, blocking collectives, per_device(): lax.all_to_all(jnp.broadcast_to(load, (FN, piece, wide)), 'exp', 0, 0, ax...  17.9 us
    all_to_all x1, blocking collectives, to_owners(): return lax.all_to_all(blocks, 'grp', 0, 0, axis_index_groups=X_GROUPS)  14.6 us
    ppermute x1, waiting for transfers between devices, per_device(): second_came = lax.ppermute(second, 'grp', OTHER_HALF)  11.8 us
    all_to_all x3, starting transfers between devices, to_owners(): return lax.all_to_all(blocks, 'grp', 0, 0, axis_index_groups=X_GROUPS)  10.6 us
  transfers between devices with their start and end apart: 6, of which 5 were waited for; matrix products, arithmetic and copies ran while one was open for 1% of the time, Pallas kernels for 6%

profile of v12, /device:TPU:96, one launch (start us, length us, event | category | flops | bytes accessed | tf_op | source)
XLA Modules:
  0.0 192.9 jit_solution(8927597886351510042)
XLA Ops:
  1.3 1.6 copy.6
  3.1 28.1 %all_to_all.40.got_ref = bf16[16,32,1664]{2,1,0:T(8,128)(2,1)S(1)} all-to-all(bf16[16,32,1664]{2,1,0:T(8,128)(2,1)S(1)} %pad_maximum_fusion), channel_id=1, replica_groups={{0,2,16,18,32,34,48,50,1,3,17,19,33,35,49,51},{4,6,20,22,36,38,52,54,5,..., dimensions={0} | all-to-all | bytes 3407872 | tf_op jit(solution)/shard_map/all_to_all | solution.py:316
  31.7 19.7 %all_to_all.41 = f32[4,8,1664]{2,1,0:T(8,128)S(1)} all-to-all(f32[4,8,1664]{2,1,0:T(8,128)S(1)} %weighted.1), channel_id=1, replica_groups={{0,4,8,12},{1,5,9,13},{2,6,10,14},{3,7,11,15},{16,20,24,28},{17,21,25,2..., dimensions={0} | all-to-all | bytes 425984 | tf_op jit(solution)/shard_map/all_to_all | solution.py:320
  52.3 17.9 %all_to_all.42 = bf16[4,8,2304]{2,1,0:T(8,128)(2,1)S(1)} all-to-all(bf16[4,8,2304]{2,1,0:T(8,128)(2,1)S(1)} %broadcast_in_dim.27), channel_id=1, replica_groups={{0,4,8,12},{1,5,9,13},{2,6,10,14},{3,7,11,15},{16,20,24,28},{17,21,25,2..., dimensions={0} | all-to-all | bytes 294912 | tf_op jit(solution)/shard_map/all_to_all | solution.py:328
  70.3 20.5 %all_to_all.43 = bf16[8,32,2304]{2,1,0:T(8,128)(2,1)S(1)} all-to-all(bf16[8,32,2304]{2,1,0:T(8,128)(2,1)S(1)} %broadcast_in_dim.28), channel_id=1, replica_groups={{0,2,16,18,32,34,48,50},{1,3,17,19,33,35,49,51},{4,6,20,22,36,38,52,54}..., dimensions={0} | all-to-all | bytes 2359296 | tf_op jit(solution)/shard_map/all_to_all | solution.py:331
  90.7 1.9 collective-permute-start
  92.6 2.4 %own_products.1 = (f32[256,256]{1,0:T(8,128)S(1)}, f32[256,1536]{1,0:T(8,128)S(1)}, f32[256,256]{1,0:T(8,128)S(1)}) custom-call(s32[1]{0:T(128)} %bitcast.4.core_ref, bf16[256,2304]{1,0:T(8,128)(2,1)S(1)} %bitcast.29, bf16[512,1536]{1,0:T(8,128)(2,1)S(1)} %bitcast.26, bf16[1536,256]{1,0:T(8,128)(2,1)S(1)} %copy-done), custom_call_target="tpu_custom_call" | custom-call | flops 2000000000 | bytes 1024 | tf_op jit(solution)/shard_map/own_products/pallas_call | solution.py:221
  95.6 4.5 %products.1 = (f32[4,96,384]{2,1,0:T(8,128)S(1)}, f32[4,192,384]{2,1,0:T(8,128)}, f32[256,256]{1,0:T(8,128)S(1)}) custom-call(s32[1]{0:T(128)} %bitcast.4.core_ref, bf16[256,2304]{1,0:T(8,128)(2,1)} %collective-permute-done.load_ref, bf16[512,1536]{1,0:T(8,128)(2,1)S(1)} %bitcast.27, bf16[1536,256]{1,0:T(8,128)(2,1)S(1)} %copy-done, ...), custom_call_target="tpu_custom_call" | custom-call | flops 3000000000 | bytes 1024 | tf_op jit(solution)/shard_map/products/pallas_call | solution.py:236
  100.1 14.6 %all_to_all.44 = f32[4,96,384]{2,1,0:T(8,128)S(1)} all-to-all(f32[4,96,384]{2,1,0:T(8,128)S(1)} %get-tuple-element.17), channel_id=1, replica_groups={{0,64,128,192},{256,320,384,448},{1,65,129,193},{257,321,385,449},{2,66..., dimensions={0} | all-to-all | bytes 1179648 | tf_op jit(solution)/shard_map/all_to_all | solution.py:340
  114.7 3.5 %all-to-all-start.6 = ((f32[4,192,384]{2,1,0:T(8,128)}), f32[4,192,384]{2,1,0:T(8,128)S(1)}, u32[]{:S(2)}, u32[]{:S(2)}) async-start(f32[4,192,384]{2,1,0:T(8,128)} %get-tuple-element.18), calls=%async_computation.6 | async-start | bytes 2359296 | tf_op jit(solution)/shard_map/all_to_all | solution.py:340
  118.3 8.2 %collective-permute-start.1 = (f32[96,384]{1,0:T(8,128)S(1)}, f32[96,384]{1,0:T(8,128)S(1)}, u32[]{:S(2)}, u32[]{:S(2)}) collective-permute-start(f32[96,384]{1,0:T(8,128)S(1)} %reduce_sum.28), channel_id=1, source_target_pairs={{0,256},{64,320},{128,384},{192,448},{256,0},{320,64},{384,128},{4... | collective-permute-start | bytes 442376 | tf_op jit(solution)/shard_map/ppermute | solution.py:346
  126.5 7.6 %all-to-all-done.6 = f32[4,192,384]{2,1,0:T(8,128)S(1)} async-done(((f32[4,192,384]{2,1,0:T(8,128)}), f32[4,192,384]{2,1,0:T(8,128)S(1)}, u32[]{:S(2)}, u32[]{:S(2)}) %all-to-all-start.6) | async-done | bytes 1179680 | tf_op jit(solution)/shard_map/all_to_all | solution.py:340
  134.2 8.2 %collective-permute-start.2 = (f32[192,384]{1,0:T(8,128)S(1)}, f32[192,384]{1,0:T(8,128)S(1)}, u32[]{:S(2)}, u32[]{:S(2)}) collective-permute-start(f32[192,384]{1,0:T(8,128)S(1)} %reduce_sum.29.refs_2_), channel_id=1, source_target_pairs={{0,256},{64,320},{128,384},{192,448},{256,0},{320,64},{384,128},{4... | collective-permute-start | bytes 884744 | tf_op jit(solution)/shard_map/ppermute | solution.py:348
  142.4 0.7 broadcast_in_dim.29
  143.1 3.5 %all-to-all-start.5 = ((f32[4,32,384]{2,1,0:T(8,128)}), f32[4,32,384]{2,1,0:T(8,128)S(1)}, u32[]{:S(2)}, u32[]{:S(2)}) async-start(f32[4,32,384]{2,1,0:T(8,128)} %broadcast_in_dim.29), calls=%async_computation.5 | async-start | bytes 393216 | tf_op jit(solution)/shard_map/all_to_all | solution.py:340
  146.7 6.1 %all-to-all-done.5.packed_ref = f32[4,32,384]{2,1,0:T(8,128)S(1)} async-done(((f32[4,32,384]{2,1,0:T(8,128)}), f32[4,32,384]{2,1,0:T(8,128)S(1)}, u32[]{:S(2)}, u32[]{:S(2)}) %all-to-all-start.5) | async-done | bytes 196640 | tf_op jit(solution)/shard_map/all_to_all | solution.py:340
  152.8 8.9 %inverse_factor.1.inverse_ref = f32[256,256]{1,0:T(8,128)S(1)} custom-call(f32[4,32,384]{2,1,0:T(8,128)S(1)} %all-to-all-done.5.packed_ref), custom_call_target="tpu_custom_call" | custom-call | flops 536870912 | bytes 1024 | tf_op jit(solution)/shard_map/inverse_factor/pallas_call | solution.py:126
  161.7 11.8 %collective-permute-done.2.refs_3_ = f32[192,384]{1,0:T(8,128)S(1)} collective-permute-done((f32[192,384]{1,0:T(8,128)S(1)}, f32[192,384]{1,0:T(8,128)S(1)}, u32[]{:S(2)}, u32[]{:S(2)}) %collective-permute-start.2) | collective-permute-done | bytes 294944 | tf_op jit(solution)/shard_map/ppermute | solution.py:348
  173.5 0.7 finished.1
  174.3 1.0 broadcast_in_dim.30
  175.3 3.5 %all-to-all-start.7 = ((f16[4,272,384]{2,1,0:T(8,128)(2,1)}), f16[4,272,384]{2,1,0:T(8,128)(2,1)S(1)}, u32[]{:S(2)}, u32[]{:S(2)}) async-start(f16[4,272,384]{2,1,0:T(8,128)(2,1)} %broadcast_in_dim.30), calls=%async_computation.7 | async-start | bytes 1671168 | tf_op jit(solution)/shard_map/all_to_all | solution.py:340
  179.7 0.9 copy.7
  180.6 10.8 %all-to-all-done.7 = f16[4,272,384]{2,1,0:T(8,128)(2,1)S(1)} async-done(((f16[4,272,384]{2,1,0:T(8,128)(2,1)}), f16[4,272,384]{2,1,0:T(8,128)(2,1)S(1)}, u32[]{:S(2)}, u32[]{:S(2)}) %all-to-all-start.7) | async-done | bytes 835616 | tf_op jit(solution)/shard_map/all_to_all | solution.py:340
  191.5 1.2 assembled.1
  (32 shorter events, 3.2 us)
Async XLA Ops:
  31.2 20.4 %copy-start = (bf16[1536,256]{1,0:T(8,128)(2,1)S(1)}, bf16[1536,256]{1,0:T(8,128)(2,1)}, u32[]{:S(2)}) copy-start(bf16[1536,256]{1,0:T(8,128)(2,1)} %sketch_ref.3) | copy-start | bytes 2359300
  51.6 0.6 copy-start.3
  90.7 4.9 %collective-permute-start = (bf16[256,2304]{1,0:T(8,128)(2,1)S(1)}, bf16[256,2304]{1,0:T(8,128)(2,1)}, u32[]{:S(2)}, u32[]{:S(2)}) collective-permute-start(bf16[256,2304]{1,0:T(8,128)(2,1)S(1)} %bitcast.28), channel_id=1, source_target_pairs={{0,1},{1,0},{2,3},{3,2},{4,5},{5,4},{6,7},{7,6},{8,9},{9,8},{10,11... | collective-permute-start | bytes 3538952 | tf_op jit(solution)/shard_map/ppermute | solution.py:335
  95.0 5.1 %copy-start.1 = (f32[256,256]{1,0:T(8,128)}, f32[256,256]{1,0:T(8,128)S(1)}, u32[]{:S(2)}) copy-start(f32[256,256]{1,0:T(8,128)S(1)} %get-tuple-element.14) | copy-start | bytes 786436
  114.7 19.4 %all-to-all-start.6 = ((f32[4,192,384]{2,1,0:T(8,128)}), f32[4,192,384]{2,1,0:T(8,128)S(1)}, u32[]{:S(2)}, u32[]{:S(2)}) async-start(f32[4,192,384]{2,1,0:T(8,128)} %get-tuple-element.18), calls=%async_computation.6 | async-start | bytes 2359296 | tf_op jit(solution)/shard_map/all_to_all | solution.py:340
  118.3 24.2 %collective-permute-start.1 = (f32[96,384]{1,0:T(8,128)S(1)}, f32[96,384]{1,0:T(8,128)S(1)}, u32[]{:S(2)}, u32[]{:S(2)}) collective-permute-start(f32[96,384]{1,0:T(8,128)S(1)} %reduce_sum.28), channel_id=1, source_target_pairs={{0,256},{64,320},{128,384},{192,448},{256,0},{320,64},{384,128},{4... | collective-permute-start | bytes 442376 | tf_op jit(solution)/shard_map/ppermute | solution.py:346
  134.2 39.3 %collective-permute-start.2 = (f32[192,384]{1,0:T(8,128)S(1)}, f32[192,384]{1,0:T(8,128)S(1)}, u32[]{:S(2)}, u32[]{:S(2)}) collective-permute-start(f32[192,384]{1,0:T(8,128)S(1)} %reduce_sum.29.refs_2_), channel_id=1, source_target_pairs={{0,256},{64,320},{128,384},{192,448},{256,0},{320,64},{384,128},{4... | collective-permute-start | bytes 884744 | tf_op jit(solution)/shard_map/ppermute | solution.py:348
  143.1 9.7 %all-to-all-start.5 = ((f32[4,32,384]{2,1,0:T(8,128)}), f32[4,32,384]{2,1,0:T(8,128)S(1)}, u32[]{:S(2)}, u32[]{:S(2)}) async-start(f32[4,32,384]{2,1,0:T(8,128)} %broadcast_in_dim.29), calls=%async_computation.5 | async-start | bytes 393216 | tf_op jit(solution)/shard_map/all_to_all | solution.py:340
  174.3 4.9 %copy-start.2 = (f32[256,256]{1,0:T(8,128)S(1)}, f32[256,256]{1,0:T(8,128)}, u32[]{:S(2)}) copy-start(f32[256,256]{1,0:T(8,128)} %copy-done.1) | copy-start | bytes 786436
  175.3 16.1 %all-to-all-start.7 = ((f16[4,272,384]{2,1,0:T(8,128)(2,1)}), f16[4,272,384]{2,1,0:T(8,128)(2,1)S(1)}, u32[]{:S(2)}, u32[]{:S(2)}) async-start(f16[4,272,384]{2,1,0:T(8,128)(2,1)} %broadcast_in_dim.30), calls=%async_computation.7 | async-start | bytes 1671168 | tf_op jit(solution)/shard_map/all_to_all | solution.py:340

commit v13 on v12

--- a/solution.py
+++ b/solution.py
@@ -29,6 +29,7 @@
     for y in range(YN) for n in range(NN) for c in range(CN)
 ]
 OTHER_CORE = [(i, i ^ 1) for i in range(64)]
+ALONG_X = [[(i, i ^ k) for i in range(8)] for k in range(XN)]
 OTHER_HALF = [(i, i ^ 4) for i in range(8)]
 X_GROUPS = [[h * XN + x for x in range(XN)] for h in range(2)]
 
@@ -197,12 +198,13 @@
 
 
 def products_kernel(
-    core_ref, load_ref, own_ref, sketch_ref, own_gram_ref, own_delta_ref,
+    place_ref, load_ref, own_ref, sketch_ref, own_gram_ref, own_delta_ref,
     first_ref, second_ref, range_ref,
 ):
     ff, rank = sketch_ref.shape
     block, slab = rank // XN, ff // XN
-    gram, delta = half_products(1 - core_ref[0], load_ref, own_ref, sketch_ref, range_ref)
+    core, x = place_ref[0], place_ref[1]
+    gram, delta = half_products(1 - core, load_ref, own_ref, sketch_ref, range_ref)
     gram += own_gram_ref[...]
     delta += own_delta_ref[...]
     for b in range(XN):
@@ -211,8 +213,8 @@
             [mine[:, (b + j) % XN * block :][:, :block] for j in range(XN - 1)], axis=1
         )
         packed = jnp.concatenate([kept[: block // 2], kept[block // 2 :]], axis=1)
-        first_ref[b, : block // 2, :] = packed
-        first_ref[b, block // 2 :, :] = delta[:FIRST, b * slab : (b + 1) * slab]
+        first_ref[b ^ x, : block // 2, :] = packed
+        first_ref[b ^ x, block // 2 :, :] = delta[:FIRST, b * slab : (b + 1) * slab]
         second_ref[b] = delta[FIRST:, b * slab : (b + 1) * slab]
 
 
@@ -229,7 +231,7 @@
     )(core, load, own, sketch)
 
 
-def products(core, load, own, sketch, own_gram, own_delta):
+def products(place, load, own, sketch, own_gram, own_delta):
     half, (ff, rank) = load.shape[0], sketch.shape
     first = (XN, rank // XN // 2 + FIRST, ff // XN)
     second = (XN, rank - FIRST, ff // XN)
@@ -241,7 +243,7 @@
         compiler_params=pltpu.CompilerParams(vmem_limit_bytes=32 * MIB),
         cost_estimate=pl.CostEstimate(flops=3 * 10**9, bytes_accessed=2**10, transcendentals=0),
         name="products",
-    )(core, load, own, sketch, own_gram, own_delta)
+    )(place, load, own, sketch, own_gram, own_delta)
 
 
 def finished_kernel(inverse_ref, *refs):
@@ -340,11 +342,11 @@
         return lax.all_to_all(blocks, "grp", 0, 0, axis_index_groups=X_GROUPS)
 
     own_gram, own_delta, own_range = own_products(core, load, own, sketch)
-    first, second, other_range = products(core, other, own, sketch, own_gram, own_delta)
-    first, second = to_owners(first), to_owners(second)
-    first = jnp.sum(first, axis=0)
+    place = jnp.concatenate([core, (lax.axis_index("grp") % XN).reshape(1)])
+    first, second, other_range = products(place, other, own, sketch, own_gram, own_delta)
+    first = first[0] + sum(lax.ppermute(first[k], "grp", ALONG_X[k]) for k in (2, 3, 1))
     first_came = lax.ppermute(first, "grp", OTHER_HALF)
-    second = jnp.sum(second, axis=0)
+    second = jnp.sum(to_owners(second), axis=0)
     second_came = lax.ppermute(second, "grp", OTHER_HALF)
     packed = rank // XN // 2
     gram = first[:packed] + first_came[:packed]

time: 194 us -> 211 us (1.088)
  the two profiles are of different devices: /device:TPU:96 before, /device:TPU:32 now
where the time goes in v13:
time: 211 us; the launch traced here: 210 us
  blocking collectives  88.7 us (42%)
  waiting for transfers between devices  55.5 us (26%)
  starting transfers between devices  38.2 us (18%)
  Pallas kernels  18.2 us (9%)
  local copies, waits for them, and re-layouts  4.5 us (2%)
    all_to_all x1, blocking collectives, per_device(): lax.all_to_all(jnp.concatenate([own, tag], axis=2), 'exp', 0, 0, axis_ind...  30.3 us
    ppermute x1, waiting for transfers between devices, per_device(): first_came = lax.ppermute(first, 'grp', OTHER_HALF)  26.2 us
    all_to_all x1, blocking collectives, per_device(): lax.all_to_all(jnp.broadcast_to(load, (YN * NN, FN * piece, wide)), 'exp'...  20.4 us
    all_to_all x1, blocking collectives, per_device(): lax.all_to_all(weighted(got), 'exp', 0, 0, axis_index_groups=FAR_GROUPS)  20 us
    all_to_all x1, blocking collectives, per_device(): lax.all_to_all(jnp.broadcast_to(load, (FN, piece, wide)), 'exp', 0, 0, ax...  18 us
    all_to_all x3, waiting for transfers between devices, to_owners(): return lax.all_to_all(blocks, 'grp', 0, 0, axis_index_groups=X_GROUPS)  15.9 us
    ppermute x3, waiting for transfers between devices, per_device(): lax.ppermute(first[k], 'grp', ALONG_X[k])  12.9 us
    all_to_all x3, starting transfers between devices, to_owners(): return lax.all_to_all(blocks, 'grp', 0, 0, axis_index_groups=X_GROUPS)  11.3 us
  transfers between devices with their start and end apart: 9, of which 6 were waited for; matrix products, arithmetic and copies ran while one was open for 2% of the time, Pallas kernels for 5%

profile of v13, /device:TPU:32, one launch (start us, length us, event | category | flops | bytes accessed | tf_op | source)
XLA Modules:
  0.0 210.2 jit_solution(8863704113124793207)
XLA Ops:
  1.3 1.6 copy.6
  3.1 30.3 %all_to_all.35.got_ref = bf16[16,32,1664]{2,1,0:T(8,128)(2,1)S(1)} all-to-all(bf16[16,32,1664]{2,1,0:T(8,128)(2,1)S(1)} %pad_maximum_fusion), channel_id=1, replica_groups={{0,2,16,18,32,34,48,50,1,3,17,19,33,35,49,51},{4,6,20,22,36,38,52,54,5,..., dimensions={0} | all-to-all | bytes 3407872 | tf_op jit(solution)/shard_map/all_to_all | solution.py:318
  33.9 20.0 %all_to_all.36 = f32[4,8,1664]{2,1,0:T(8,128)S(1)} all-to-all(f32[4,8,1664]{2,1,0:T(8,128)S(1)} %weighted.1), channel_id=1, replica_groups={{0,4,8,12},{1,5,9,13},{2,6,10,14},{3,7,11,15},{16,20,24,28},{17,21,25,2..., dimensions={0} | all-to-all | bytes 425984 | tf_op jit(solution)/shard_map/all_to_all | solution.py:322
  54.8 18.0 %all_to_all.37 = bf16[4,8,2304]{2,1,0:T(8,128)(2,1)S(1)} all-to-all(bf16[4,8,2304]{2,1,0:T(8,128)(2,1)S(1)} %broadcast_in_dim.27), channel_id=1, replica_groups={{0,4,8,12},{1,5,9,13},{2,6,10,14},{3,7,11,15},{16,20,24,28},{17,21,25,2..., dimensions={0} | all-to-all | bytes 294912 | tf_op jit(solution)/shard_map/all_to_all | solution.py:330
  72.9 20.4 %all_to_all.38 = bf16[8,32,2304]{2,1,0:T(8,128)(2,1)S(1)} all-to-all(bf16[8,32,2304]{2,1,0:T(8,128)(2,1)S(1)} %broadcast_in_dim.28), channel_id=1, replica_groups={{0,2,16,18,32,34,48,50},{1,3,17,19,33,35,49,51},{4,6,20,22,36,38,52,54}..., dimensions={0} | all-to-all | bytes 2359296 | tf_op jit(solution)/shard_map/all_to_all | solution.py:333
  93.3 1.9 collective-permute-start
  95.3 2.4 %own_products.1 = (f32[256,256]{1,0:T(8,128)S(1)}, f32[256,1536]{1,0:T(8,128)S(1)}, f32[256,256]{1,0:T(8,128)S(1)}) custom-call(s32[1]{0:T(128)} %bitcast.4.core_ref, bf16[256,2304]{1,0:T(8,128)(2,1)S(1)} %bitcast.38, bf16[512,1536]{1,0:T(8,128)(2,1)S(1)} %bitcast.35, bf16[1536,256]{1,0:T(8,128)(2,1)S(1)} %copy-done), custom_call_target="tpu_custom_call" | custom-call | flops 2000000000 | bytes 1024 | tf_op jit(solution)/shard_map/own_products/pallas_call | solution.py:223
  98.1 4.5 %products.1 = (f32[4,96,384]{2,1,0:T(8,128)S(1)}, f32[4,192,384]{2,1,0:T(8,128)}, f32[256,256]{1,0:T(8,128)S(1)}) custom-call(s32[2]{0:T(128)S(1)} %pad_add_fusion.place_ref, bf16[256,2304]{1,0:T(8,128)(2,1)} %collective-permute-done.load_ref, bf16[512,1536]{1,0:T(8,128)(2,1)S(1)} %bitcast.36, bf16[1536,256]{1,0:T(8,128)(2,1)S(1)} %copy-done, ...), custom_call_target="tpu_custom_call" | custom-call | flops 3000000000 | bytes 1024 | tf_op jit(solution)/shard_map/products/pallas_call | solution.py:238
  102.7 4.3 %all-to-all-start.5 = ((f32[4,192,384]{2,1,0:T(8,128)}), f32[4,192,384]{2,1,0:T(8,128)}, u32[]{:S(2)}, u32[]{:S(2)}) async-start(f32[4,192,384]{2,1,0:T(8,128)} %get-tuple-element.18), calls=%async_computation.5 | async-start | bytes 2359296 | tf_op jit(solution)/shard_map/all_to_all | solution.py:342
  107.0 5.1 %collective-permute-start.2 = (f32[96,384]{1,0:T(8,128)S(1)}, f32[96,384]{1,0:T(8,128)S(1)}, u32[]{:S(2)}, u32[]{:S(2)}) collective-permute-start(f32[96,384]{1,0:T(8,128)S(1)} %get-tuple-element.25), channel_id=1, source_target_pairs={{0,192},{64,128},{128,64},{192,0},{256,448},{320,384},{384,320},{4... | collective-permute-start | bytes 442376 | tf_op jit(solution)/shard_map/ppermute | solution.py:347
  112.2 2.2 %collective-permute-start.3 = (f32[96,384]{1,0:T(8,128)S(1)}, f32[96,384]{1,0:T(8,128)S(1)}, u32[]{:S(2)}, u32[]{:S(2)}) collective-permute-start(f32[96,384]{1,0:T(8,128)S(1)} %get-tuple-element.26), channel_id=1, source_target_pairs={{0,64},{64,0},{128,192},{192,128},{256,320},{320,256},{384,448},{4... | collective-permute-start | bytes 442376 | tf_op jit(solution)/shard_map/ppermute | solution.py:347
  114.3 3.1 %collective-permute-start.1 = (f32[96,384]{1,0:T(8,128)S(1)}, f32[96,384]{1,0:T(8,128)S(1)}, u32[]{:S(2)}, u32[]{:S(2)}) collective-permute-start(f32[96,384]{1,0:T(8,128)S(1)} %get-tuple-element.27), channel_id=1, source_target_pairs={{0,128},{64,192},{128,0},{192,64},{256,384},{320,448},{384,256},{4... | collective-permute-start | bytes 442376 | tf_op jit(solution)/shard_map/ppermute | solution.py:347
  117.5 9.9 %collective-permute-done.2 = f32[96,384]{1,0:T(8,128)S(1)} collective-permute-done((f32[96,384]{1,0:T(8,128)S(1)}, f32[96,384]{1,0:T(8,128)S(1)}, u32[]{:S(2)}, u32[]{:S(2)}) %collective-permute-start.2) | collective-permute-done | bytes 147488 | tf_op jit(solution)/shard_map/ppermute | solution.py:347
  127.4 3.0 %collective-permute-done.1 = f32[96,384]{1,0:T(8,128)S(1)} collective-permute-done((f32[96,384]{1,0:T(8,128)S(1)}, f32[96,384]{1,0:T(8,128)S(1)}, u32[]{:S(2)}, u32[]{:S(2)}) %collective-permute-start.1) | collective-permute-done | bytes 147488 | tf_op jit(solution)/shard_map/ppermute | solution.py:347
  130.4 8.2 %collective-permute-start.4 = (f32[96,384]{1,0:T(8,128)S(1)}, f32[96,384]{1,0:T(8,128)S(1)}, u32[]{:S(2)}, u32[]{:S(2)}) collective-permute-start(f32[96,384]{1,0:T(8,128)S(1)} %bitcast_add_fusion), channel_id=1, source_target_pairs={{0,256},{64,320},{128,384},{192,448},{256,0},{320,64},{384,128},{4... | collective-permute-start | bytes 442376 | tf_op jit(solution)/shard_map/ppermute | solution.py:348
  138.7 1.4 reduce_sum.19.refs_2_
  140.0 6.3 %collective-permute-start.5 = (f32[192,384]{1,0:T(8,128)S(1)}, f32[192,384]{1,0:T(8,128)S(1)}, u32[]{:S(2)}, u32[]{:S(2)}) collective-permute-start(f32[192,384]{1,0:T(8,128)S(1)} %reduce_sum.19.refs_2_), channel_id=1, source_target_pairs={{0,256},{64,320},{128,384},{192,448},{256,0},{320,64},{384,128},{4... | collective-permute-start | bytes 884744 | tf_op jit(solution)/shard_map/ppermute | solution.py:350
  146.4 26.2 %collective-permute-done.4 = f32[96,384]{1,0:T(8,128)S(1)} collective-permute-done((f32[96,384]{1,0:T(8,128)S(1)}, f32[96,384]{1,0:T(8,128)S(1)}, u32[]{:S(2)}, u32[]{:S(2)}) %collective-permute-start.4) | collective-permute-done | bytes 147488 | tf_op jit(solution)/shard_map/ppermute | solution.py:348
  173.3 3.5 %all-to-all-start.4 = ((f32[4,32,384]{2,1,0:T(8,128)}), f32[4,32,384]{2,1,0:T(8,128)S(1)}, u32[]{:S(2)}, u32[]{:S(2)}) async-start(f32[4,32,384]{2,1,0:T(8,128)} %broadcast_in_dim.29), calls=%async_computation.4 | async-start | bytes 393216 | tf_op jit(solution)/shard_map/all_to_all | solution.py:342
  176.9 6.1 %all-to-all-done.4.packed_ref = f32[4,32,384]{2,1,0:T(8,128)S(1)} async-done(((f32[4,32,384]{2,1,0:T(8,128)}), f32[4,32,384]{2,1,0:T(8,128)S(1)}, u32[]{:S(2)}, u32[]{:S(2)}) %all-to-all-start.4) | async-done | bytes 196640 | tf_op jit(solution)/shard_map/all_to_all | solution.py:342
  182.9 8.9 %inverse_factor.1.inverse_ref = f32[256,256]{1,0:T(8,128)S(1)} custom-call(f32[4,32,384]{2,1,0:T(8,128)S(1)} %all-to-all-done.4.packed_ref), custom_call_target="tpu_custom_call" | custom-call | flops 536870912 | bytes 1024 | tf_op jit(solution)/shard_map/inverse_factor/pallas_call | solution.py:127
  193.6 3.5 %all-to-all-start.6 = ((f16[4,272,384]{2,1,0:T(8,128)(2,1)}), f16[4,272,384]{2,1,0:T(8,128)(2,1)S(1)}, u32[]{:S(2)}, u32[]{:S(2)}) async-start(f16[4,272,384]{2,1,0:T(8,128)(2,1)} %broadcast_in_dim.30), calls=%async_computation.6 | async-start | bytes 1671168 | tf_op jit(solution)/shard_map/all_to_all | solution.py:342
  198.9 9.8 %all-to-all-done.6 = f16[4,272,384]{2,1,0:T(8,128)(2,1)S(1)} async-done(((f16[4,272,384]{2,1,0:T(8,128)(2,1)}), f16[4,272,384]{2,1,0:T(8,128)(2,1)S(1)}, u32[]{:S(2)}, u32[]{:S(2)}) %all-to-all-start.6) | async-done | bytes 835616 | tf_op jit(solution)/shard_map/all_to_all | solution.py:342
  208.8 1.2 assembled.1
  (39 shorter events, 6.4 us)
Async XLA Ops:
  33.4 20.7 %copy-start = (bf16[1536,256]{1,0:T(8,128)(2,1)S(1)}, bf16[1536,256]{1,0:T(8,128)(2,1)}, u32[]{:S(2)}) copy-start(bf16[1536,256]{1,0:T(8,128)(2,1)} %sketch_ref.3) | copy-start | bytes 2359300
  54.1 0.6 copy-start.3
  93.3 4.9 %collective-permute-start = (bf16[256,2304]{1,0:T(8,128)(2,1)S(1)}, bf16[256,2304]{1,0:T(8,128)(2,1)}, u32[]{:S(2)}, u32[]{:S(2)}) collective-permute-start(bf16[256,2304]{1,0:T(8,128)(2,1)S(1)} %bitcast.37), channel_id=1, source_target_pairs={{0,1},{1,0},{2,3},{3,2},{4,5},{5,4},{6,7},{7,6},{8,9},{9,8},{10,11... | collective-permute-start | bytes 3538952 | tf_op jit(solution)/shard_map/ppermute | solution.py:337
  97.7 5.0 %copy-start.1 = (f32[256,256]{1,0:T(8,128)}, f32[256,256]{1,0:T(8,128)S(1)}, u32[]{:S(2)}) copy-start(f32[256,256]{1,0:T(8,128)S(1)} %get-tuple-element.14) | copy-start | bytes 786436
  102.7 36.0 %all-to-all-start.5 = ((f32[4,192,384]{2,1,0:T(8,128)}), f32[4,192,384]{2,1,0:T(8,128)}, u32[]{:S(2)}, u32[]{:S(2)}) async-start(f32[4,192,384]{2,1,0:T(8,128)} %get-tuple-element.18), calls=%async_computation.5 | async-start | bytes 2359296 | tf_op jit(solution)/shard_map/all_to_all | solution.py:342
  107.0 20.4 %collective-permute-start.2 = (f32[96,384]{1,0:T(8,128)S(1)}, f32[96,384]{1,0:T(8,128)S(1)}, u32[]{:S(2)}, u32[]{:S(2)}) collective-permute-start(f32[96,384]{1,0:T(8,128)S(1)} %get-tuple-element.25), channel_id=1, source_target_pairs={{0,192},{64,128},{128,64},{192,0},{256,448},{320,384},{384,320},{4... | collective-permute-start | bytes 442376 | tf_op jit(solution)/shard_map/ppermute | solution.py:347
  112.2 15.2 %collective-permute-start.3 = (f32[96,384]{1,0:T(8,128)S(1)}, f32[96,384]{1,0:T(8,128)S(1)}, u32[]{:S(2)}, u32[]{:S(2)}) collective-permute-start(f32[96,384]{1,0:T(8,128)S(1)} %get-tuple-element.26), channel_id=1, source_target_pairs={{0,64},{64,0},{128,192},{192,128},{256,320},{320,256},{384,448},{4... | collective-permute-start | bytes 442376 | tf_op jit(solution)/shard_map/ppermute | solution.py:347
  114.3 16.1 %collective-permute-start.1 = (f32[96,384]{1,0:T(8,128)S(1)}, f32[96,384]{1,0:T(8,128)S(1)}, u32[]{:S(2)}, u32[]{:S(2)}) collective-permute-start(f32[96,384]{1,0:T(8,128)S(1)} %get-tuple-element.27), channel_id=1, source_target_pairs={{0,128},{64,192},{128,0},{192,64},{256,384},{320,448},{384,256},{4... | collective-permute-start | bytes 442376 | tf_op jit(solution)/shard_map/ppermute | solution.py:347
  130.4 42.1 %collective-permute-start.4 = (f32[96,384]{1,0:T(8,128)S(1)}, f32[96,384]{1,0:T(8,128)S(1)}, u32[]{:S(2)}, u32[]{:S(2)}) collective-permute-start(f32[96,384]{1,0:T(8,128)S(1)} %bitcast_add_fusion), channel_id=1, source_target_pairs={{0,256},{64,320},{128,384},{192,448},{256,0},{320,64},{384,128},{4... | collective-permute-start | bytes 442376 | tf_op jit(solution)/shard_map/ppermute | solution.py:348
  140.0 51.8 %collective-permute-start.5 = (f32[192,384]{1,0:T(8,128)S(1)}, f32[192,384]{1,0:T(8,128)S(1)}, u32[]{:S(2)}, u32[]{:S(2)}) collective-permute-start(f32[192,384]{1,0:T(8,128)S(1)} %reduce_sum.19.refs_2_), channel_id=1, source_target_pairs={{0,256},{64,320},{128,384},{192,448},{256,0},{320,64},{384,128},{4... | collective-permute-start | bytes 884744 | tf_op jit(solution)/shard_map/ppermute | solution.py:350
  173.3 9.7 %all-to-all-start.4 = ((f32[4,32,384]{2,1,0:T(8,128)}), f32[4,32,384]{2,1,0:T(8,128)S(1)}, u32[]{:S(2)}, u32[]{:S(2)}) async-start(f32[4,32,384]{2,1,0:T(8,128)} %broadcast_in_dim.29), calls=%async_computation.4 | async-start | bytes 393216 | tf_op jit(solution)/shard_map/all_to_all | solution.py:342
  192.6 4.9 %copy-start.2 = (f32[256,256]{1,0:T(8,128)S(1)}, f32[256,256]{1,0:T(8,128)}, u32[]{:S(2)}) copy-start(f32[256,256]{1,0:T(8,128)} %copy-done.1) | copy-start | bytes 786436
  193.6 15.1 %all-to-all-start.6 = ((f16[4,272,384]{2,1,0:T(8,128)(2,1)}), f16[4,272,384]{2,1,0:T(8,128)(2,1)S(1)}, u32[]{:S(2)}, u32[]{:S(2)}) async-start(f16[4,272,384]{2,1,0:T(8,128)(2,1)} %broadcast_in_dim.30), calls=%async_computation.6 | async-start | bytes 1671168 | tf_op jit(solution)/shard_map/all_to_all | solution.py:342

commit v14 on v12

--- a/solution.py
+++ b/solution.py
@@ -34,7 +34,7 @@
 
 PANEL, STEP = 64, 8
 TOP_POWER = 13
-FIRST = 64
+FIRST = 96
 FACTOR_COST = 2**29
 
 

time: 194 us -> 207 us (1.067)
  the two profiles are of different devices: /device:TPU:96 before, /device:TPU:32 now
where the time goes in v14:
time: 207 us; the launch traced here: 206 us
  blocking collectives  105 us (51%)
  waiting for transfers between devices  40.8 us (20%)
  starting transfers between devices  33.8 us (16%)
  Pallas kernels  18.1 us (9%)
  local copies, waits for them, and re-layouts  4.47 us (2%)
    all_to_all x1, blocking collectives, per_device(): lax.all_to_all(jnp.concatenate([own, tag], axis=2), 'exp', 0, 0, axis_ind...  30.3 us
    all_to_all x3, waiting for transfers between devices, to_owners(): return lax.all_to_all(blocks, 'grp', 0, 0, axis_index_groups=X_GROUPS)  21.1 us
    all_to_all x1, blocking collectives, per_device(): lax.all_to_all(jnp.broadcast_to(load, (YN * NN, FN * piece, wide)), 'exp'...  20.4 us
    all_to_all x1, blocking collectives, per_device(): lax.all_to_all(weighted(got), 'exp', 0, 0, axis_index_groups=FAR_GROUPS)  20 us
    ppermute x1, waiting for transfers between devices, per_device(): first_came = lax.ppermute(first, 'grp', OTHER_HALF)  19.1 us
    all_to_all x1, blocking collectives, per_device(): lax.all_to_all(jnp.broadcast_to(load, (FN, piece, wide)), 'exp', 0, 0, ax...  18 us
    all_to_all x1, blocking collectives, to_owners(): return lax.all_to_all(blocks, 'grp', 0, 0, axis_index_groups=X_GROUPS)  16.7 us
    all_to_all x3, starting transfers between devices, to_owners(): return lax.all_to_all(blocks, 'grp', 0, 0, axis_index_groups=X_GROUPS)  15.5 us
  transfers between devices with their start and end apart: 6, of which 5 were waited for; matrix products, arithmetic and copies ran while one was open for 1% of the time, Pallas kernels for 5%

profile of v14, /device:TPU:32, one launch (start us, length us, event | category | flops | bytes accessed | tf_op | source)
XLA Modules:
  0.0 206.2 jit_solution(2547864710197669727)
XLA Ops:
  1.3 1.6 copy.6
  3.1 30.3 %all_to_all.40.got_ref = bf16[16,32,1664]{2,1,0:T(8,128)(2,1)S(1)} all-to-all(bf16[16,32,1664]{2,1,0:T(8,128)(2,1)S(1)} %pad_maximum_fusion), channel_id=1, replica_groups={{0,2,16,18,32,34,48,50,1,3,17,19,33,35,49,51},{4,6,20,22,36,38,52,54,5,..., dimensions={0} | all-to-all | bytes 3407872 | tf_op jit(solution)/shard_map/all_to_all | solution.py:316
  33.9 20.0 %all_to_all.41 = f32[4,8,1664]{2,1,0:T(8,128)S(1)} all-to-all(f32[4,8,1664]{2,1,0:T(8,128)S(1)} %weighted.1), channel_id=1, replica_groups={{0,4,8,12},{1,5,9,13},{2,6,10,14},{3,7,11,15},{16,20,24,28},{17,21,25,2..., dimensions={0} | all-to-all | bytes 425984 | tf_op jit(solution)/shard_map/all_to_all | solution.py:320
  54.8 18.0 %all_to_all.42 = bf16[4,8,2304]{2,1,0:T(8,128)(2,1)S(1)} all-to-all(bf16[4,8,2304]{2,1,0:T(8,128)(2,1)S(1)} %broadcast_in_dim.27), channel_id=1, replica_groups={{0,4,8,12},{1,5,9,13},{2,6,10,14},{3,7,11,15},{16,20,24,28},{17,21,25,2..., dimensions={0} | all-to-all | bytes 294912 | tf_op jit(solution)/shard_map/all_to_all | solution.py:328
  72.9 20.4 %all_to_all.43 = bf16[8,32,2304]{2,1,0:T(8,128)(2,1)S(1)} all-to-all(bf16[8,32,2304]{2,1,0:T(8,128)(2,1)S(1)} %broadcast_in_dim.28), channel_id=1, replica_groups={{0,2,16,18,32,34,48,50},{1,3,17,19,33,35,49,51},{4,6,20,22,36,38,52,54}..., dimensions={0} | all-to-all | bytes 2359296 | tf_op jit(solution)/shard_map/all_to_all | solution.py:331
  93.3 1.9 collective-permute-start
  95.2 2.4 %own_products.1 = (f32[256,256]{1,0:T(8,128)S(1)}, f32[256,1536]{1,0:T(8,128)S(1)}, f32[256,256]{1,0:T(8,128)S(1)}) custom-call(s32[1]{0:T(128)} %bitcast.4.core_ref, bf16[256,2304]{1,0:T(8,128)(2,1)S(1)} %bitcast.29, bf16[512,1536]{1,0:T(8,128)(2,1)S(1)} %bitcast.26, bf16[1536,256]{1,0:T(8,128)(2,1)S(1)} %copy-done), custom_call_target="tpu_custom_call" | custom-call | flops 2000000000 | bytes 1024 | tf_op jit(solution)/shard_map/own_products/pallas_call | solution.py:221
  98.1 4.5 %products.1 = (f32[4,128,384]{2,1,0:T(8,128)S(1)}, f32[4,160,384]{2,1,0:T(8,128)}, f32[256,256]{1,0:T(8,128)S(1)}) custom-call(s32[1]{0:T(128)} %bitcast.4.core_ref, bf16[256,2304]{1,0:T(8,128)(2,1)} %collective-permute-done.load_ref, bf16[512,1536]{1,0:T(8,128)(2,1)S(1)} %bitcast.27, bf16[1536,256]{1,0:T(8,128)(2,1)S(1)} %copy-done, ...), custom_call_target="tpu_custom_call" | custom-call | flops 3000000000 | bytes 1024 | tf_op jit(solution)/shard_map/products/pallas_call | solution.py:236
  102.6 16.7 %all_to_all.44 = f32[4,128,384]{2,1,0:T(8,128)S(1)} all-to-all(f32[4,128,384]{2,1,0:T(8,128)S(1)} %get-tuple-element.17), channel_id=1, replica_groups={{0,64,128,192},{256,320,384,448},{1,65,129,193},{257,321,385,449},{2,66..., dimensions={0} | all-to-all | bytes 1572864 | tf_op jit(solution)/shard_map/all_to_all | solution.py:340
  119.3 3.5 %all-to-all-start.6 = ((f32[4,160,384]{2,1,0:T(8,128)}), f32[4,160,384]{2,1,0:T(8,128)S(1)}, u32[]{:S(2)}, u32[]{:S(2)}) async-start(f32[4,160,384]{2,1,0:T(8,128)} %get-tuple-element.18), calls=%async_computation.6 | async-start | bytes 1966080 | tf_op jit(solution)/shard_map/all_to_all | solution.py:340
  122.8 8.2 %collective-permute-start.1 = (f32[128,384]{1,0:T(8,128)S(1)}, f32[128,384]{1,0:T(8,128)S(1)}, u32[]{:S(2)}, u32[]{:S(2)}) collective-permute-start(f32[128,384]{1,0:T(8,128)S(1)} %reduce_sum.28), channel_id=1, source_target_pairs={{0,256},{64,320},{128,384},{192,448},{256,0},{320,64},{384,128},{4... | collective-permute-start | bytes 589832 | tf_op jit(solution)/shard_map/ppermute | solution.py:346
  131.1 5.2 %all-to-all-done.6 = f32[4,160,384]{2,1,0:T(8,128)S(1)} async-done(((f32[4,160,384]{2,1,0:T(8,128)}), f32[4,160,384]{2,1,0:T(8,128)S(1)}, u32[]{:S(2)}, u32[]{:S(2)}) %all-to-all-start.6) | async-done | bytes 983072 | tf_op jit(solution)/shard_map/all_to_all | solution.py:340
  136.4 8.2 %collective-permute-start.2 = (f32[160,384]{1,0:T(8,128)S(1)}, f32[160,384]{1,0:T(8,128)S(1)}, u32[]{:S(2)}, u32[]{:S(2)}) collective-permute-start(f32[160,384]{1,0:T(8,128)S(1)} %reduce_sum.29.refs_2_), channel_id=1, source_target_pairs={{0,256},{64,320},{128,384},{192,448},{256,0},{320,64},{384,128},{4... | collective-permute-start | bytes 737288 | tf_op jit(solution)/shard_map/ppermute | solution.py:348
  144.6 19.1 %collective-permute-done.1 = f32[128,384]{1,0:T(8,128)S(1)} collective-permute-done((f32[128,384]{1,0:T(8,128)S(1)}, f32[128,384]{1,0:T(8,128)S(1)}, u32[]{:S(2)}, u32[]{:S(2)}) %collective-permute-start.1) | collective-permute-done | bytes 196640 | tf_op jit(solution)/shard_map/ppermute | solution.py:346
  163.7 0.7 broadcast_in_dim.29
  164.4 8.4 %all-to-all-start.5 = ((f32[4,32,384]{2,1,0:T(8,128)}), f32[4,32,384]{2,1,0:T(8,128)S(1)}, u32[]{:S(2)}, u32[]{:S(2)}) async-start(f32[4,32,384]{2,1,0:T(8,128)} %broadcast_in_dim.29), calls=%async_computation.5 | async-start | bytes 393216 | tf_op jit(solution)/shard_map/all_to_all | solution.py:340
  172.9 6.3 %all-to-all-done.5.packed_ref = f32[4,32,384]{2,1,0:T(8,128)S(1)} async-done(((f32[4,32,384]{2,1,0:T(8,128)}), f32[4,32,384]{2,1,0:T(8,128)S(1)}, u32[]{:S(2)}, u32[]{:S(2)}) %all-to-all-start.5) | async-done | bytes 196640 | tf_op jit(solution)/shard_map/all_to_all | solution.py:340
  179.2 8.9 %inverse_factor.1.inverse_ref = f32[256,256]{1,0:T(8,128)S(1)} custom-call(f32[4,32,384]{2,1,0:T(8,128)S(1)} %all-to-all-done.5.packed_ref), custom_call_target="tpu_custom_call" | custom-call | flops 536870912 | bytes 1024 | tf_op jit(solution)/shard_map/inverse_factor/pallas_call | solution.py:126
  188.1 0.7 finished.1
  188.9 1.0 broadcast_in_dim.30
  189.8 3.5 %all-to-all-start.7 = ((f16[4,272,384]{2,1,0:T(8,128)(2,1)}), f16[4,272,384]{2,1,0:T(8,128)(2,1)S(1)}, u32[]{:S(2)}, u32[]{:S(2)}) async-start(f16[4,272,384]{2,1,0:T(8,128)(2,1)} %broadcast_in_dim.30), calls=%async_computation.7 | async-start | bytes 1671168 | tf_op jit(solution)/shard_map/all_to_all | solution.py:340
  194.2 0.9 copy.7
  195.1 9.6 %all-to-all-done.7 = f16[4,272,384]{2,1,0:T(8,128)(2,1)S(1)} async-done(((f16[4,272,384]{2,1,0:T(8,128)(2,1)}), f16[4,272,384]{2,1,0:T(8,128)(2,1)S(1)}, u32[]{:S(2)}, u32[]{:S(2)}) %all-to-all-start.7) | async-done | bytes 835616 | tf_op jit(solution)/shard_map/all_to_all | solution.py:340
  204.8 1.2 assembled.1
  (32 shorter events, 3.2 us)
Async XLA Ops:
  33.4 20.7 %copy-start = (bf16[1536,256]{1,0:T(8,128)(2,1)S(1)}, bf16[1536,256]{1,0:T(8,128)(2,1)}, u32[]{:S(2)}) copy-start(bf16[1536,256]{1,0:T(8,128)(2,1)} %sketch_ref.3) | copy-start | bytes 2359300
  54.1 0.6 copy-start.3
  93.3 4.9 %collective-permute-start = (bf16[256,2304]{1,0:T(8,128)(2,1)S(1)}, bf16[256,2304]{1,0:T(8,128)(2,1)}, u32[]{:S(2)}, u32[]{:S(2)}) collective-permute-start(bf16[256,2304]{1,0:T(8,128)(2,1)S(1)} %bitcast.28), channel_id=1, source_target_pairs={{0,1},{1,0},{2,3},{3,2},{4,5},{5,4},{6,7},{7,6},{8,9},{9,8},{10,11... | collective-permute-start | bytes 3538952 | tf_op jit(solution)/shard_map/ppermute | solution.py:335
  97.6 5.0 %copy-start.1 = (f32[256,256]{1,0:T(8,128)}, f32[256,256]{1,0:T(8,128)S(1)}, u32[]{:S(2)}) copy-start(f32[256,256]{1,0:T(8,128)S(1)} %get-tuple-element.14) | copy-start | bytes 786436
  119.3 17.0 %all-to-all-start.6 = ((f32[4,160,384]{2,1,0:T(8,128)}), f32[4,160,384]{2,1,0:T(8,128)S(1)}, u32[]{:S(2)}, u32[]{:S(2)}) async-start(f32[4,160,384]{2,1,0:T(8,128)} %get-tuple-element.18), calls=%async_computation.6 | async-start | bytes 1966080 | tf_op jit(solution)/shard_map/all_to_all | solution.py:340
  122.8 40.9 %collective-permute-start.1 = (f32[128,384]{1,0:T(8,128)S(1)}, f32[128,384]{1,0:T(8,128)S(1)}, u32[]{:S(2)}, u32[]{:S(2)}) collective-permute-start(f32[128,384]{1,0:T(8,128)S(1)} %reduce_sum.28), channel_id=1, source_target_pairs={{0,256},{64,320},{128,384},{192,448},{256,0},{320,64},{384,128},{4... | collective-permute-start | bytes 589832 | tf_op jit(solution)/shard_map/ppermute | solution.py:346
  136.4 51.7 %collective-permute-start.2 = (f32[160,384]{1,0:T(8,128)S(1)}, f32[160,384]{1,0:T(8,128)S(1)}, u32[]{:S(2)}, u32[]{:S(2)}) collective-permute-start(f32[160,384]{1,0:T(8,128)S(1)} %reduce_sum.29.refs_2_), channel_id=1, source_target_pairs={{0,256},{64,320},{128,384},{192,448},{256,0},{320,64},{384,128},{4... | collective-permute-start | bytes 737288 | tf_op jit(solution)/shard_map/ppermute | solution.py:348
  164.4 14.8 %all-to-all-start.5 = ((f32[4,32,384]{2,1,0:T(8,128)}), f32[4,32,384]{2,1,0:T(8,128)S(1)}, u32[]{:S(2)}, u32[]{:S(2)}) async-start(f32[4,32,384]{2,1,0:T(8,128)} %broadcast_in_dim.29), calls=%async_computation.5 | async-start | bytes 393216 | tf_op jit(solution)/shard_map/all_to_all | solution.py:340
  188.8 4.9 %copy-start.2 = (f32[256,256]{1,0:T(8,128)S(1)}, f32[256,256]{1,0:T(8,128)}, u32[]{:S(2)}) copy-start(f32[256,256]{1,0:T(8,128)} %copy-done.1) | copy-start | bytes 786436
  189.8 14.9 %all-to-all-start.7 = ((f16[4,272,384]{2,1,0:T(8,128)(2,1)}), f16[4,272,384]{2,1,0:T(8,128)(2,1)S(1)}, u32[]{:S(2)}, u32[]{:S(2)}) async-start(f16[4,272,384]{2,1,0:T(8,128)(2,1)} %broadcast_in_dim.30), calls=%async_computation.7 | async-start | bytes 1671168 | tf_op jit(solution)/shard_map/all_to_all | solution.py:340

commit v15 on v12

--- a/solution.py
+++ b/solution.py
@@ -40,9 +40,7 @@
 
 def parts_of(value):
     first = lax.reduce_precision(value, 8, 7)
-    rest = value - first
-    second = lax.reduce_precision(rest, 8, 7)
-    return [first.astype(BF16), second.astype(BF16), (rest - second).astype(BF16)]
+    return [first.astype(BF16), (value - first).astype(BF16)]
 
 
 def eye(n):
@@ -178,11 +176,7 @@
     half = load_ref.shape[0]
     ff, rank = sketch_ref.shape
     own = own_ref[pl.ds(pl.multiple_of(core * half, half), half), :]
-    base_sketch = (
-        load_ref[:, ff : ff + rank].astype(F32)
-        + load_ref[:, ff + rank : ff + 2 * rank].astype(F32)
-        + load_ref[:, ff + 2 * rank :].astype(F32)
-    )
+    base_sketch = load_ref[:, ff : ff + rank].astype(F32) + load_ref[:, ff + rank :].astype(F32)
     range_rows = jnp.dot(own, sketch_ref[...], preferred_element_type=F32) - base_sketch
     range_ref[...] = range_rows
     turned = range_rows.T
@@ -323,7 +317,7 @@
     base_piece = base_rows.astype(BF16)
     sketched = jnp.dot(base_rows, sketch.astype(F32), precision=HIGHEST)
 
-    wide = ff + 3 * rank
+    wide = ff + 2 * rank
     load = jnp.concatenate([base_piece] + parts_of(sketched), axis=1)
     load = lax.all_to_all(
         jnp.broadcast_to(load, (FN, piece, wide)), "exp", 0, 0, axis_index_groups=FAR_GROUPS

time: 194 us -> 192 us (0.990)
  the two profiles are of different devices: /device:TPU:96 before, /device:TPU:32 now
where the time goes in v15:
time: 192 us; the launch traced here: 191 us
  blocking collectives  99.1 us (52%)
  waiting for transfers between devices  36.7 us (19%)
  starting transfers between devices  28.9 us (15%)
  Pallas kernels  18.1 us (9%)
  local copies, waits for them, and re-layouts  4.38 us (2%)
    all_to_all x1, blocking collectives, per_device(): lax.all_to_all(jnp.concatenate([own, tag], axis=2), 'exp', 0, 0, axis_ind...  30.3 us
    all_to_all x3, waiting for transfers between devices, to_owners(): return lax.all_to_all(blocks, 'grp', 0, 0, axis_index_groups=X_GROUPS)  24.8 us
    all_to_all x1, blocking collectives, per_device(): lax.all_to_all(weighted(got), 'exp', 0, 0, axis_index_groups=FAR_GROUPS)  20 us
    all_to_all x1, blocking collectives, per_device(): lax.all_to_all(jnp.broadcast_to(load, (FN, piece, wide)), 'exp', 0, 0, ax...  17.6 us
    all_to_all x1, blocking collectives, per_device(): lax.all_to_all(jnp.broadcast_to(load, (YN * NN, FN * piece, wide)), 'exp'...  16.5 us
    all_to_all x1, blocking collectives, to_owners(): return lax.all_to_all(blocks, 'grp', 0, 0, axis_index_groups=X_GROUPS)  14.7 us
    ppermute x1, waiting for transfers between devices, per_device(): second_came = lax.ppermute(second, 'grp', OTHER_HALF)  11.6 us
    all_to_all x3, starting transfers between devices, to_owners(): return lax.all_to_all(blocks, 'grp', 0, 0, axis_index_groups=X_GROUPS)  10.6 us
  transfers between devices with their start and end apart: 6, of which 5 were waited for; matrix products, arithmetic and copies ran while one was open for 1% of the time, Pallas kernels for 6%

profile of v15, /device:TPU:32, one launch (start us, length us, event | category | flops | bytes accessed | tf_op | source)
XLA Modules:
  0.0 190.8 jit_solution(3331944362042974278)
XLA Ops:
  1.3 1.6 copy.6
  3.1 30.3 %all_to_all.40.got_ref = bf16[16,32,1664]{2,1,0:T(8,128)(2,1)S(1)} all-to-all(bf16[16,32,1664]{2,1,0:T(8,128)(2,1)S(1)} %pad_maximum_fusion), channel_id=1, replica_groups={{0,2,16,18,32,34,48,50,1,3,17,19,33,35,49,51},{4,6,20,22,36,38,52,54,5,..., dimensions={0} | all-to-all | bytes 3407872 | tf_op jit(solution)/shard_map/all_to_all | solution.py:310
  33.9 20.0 %all_to_all.41 = f32[4,8,1664]{2,1,0:T(8,128)S(1)} all-to-all(f32[4,8,1664]{2,1,0:T(8,128)S(1)} %weighted.1), channel_id=1, replica_groups={{0,4,8,12},{1,5,9,13},{2,6,10,14},{3,7,11,15},{16,20,24,28},{17,21,25,2..., dimensions={0} | all-to-all | bytes 425984 | tf_op jit(solution)/shard_map/all_to_all | solution.py:314
  54.6 17.6 %all_to_all.42 = bf16[4,8,2048]{2,1,0:T(8,128)(2,1)S(1)} all-to-all(bf16[4,8,2048]{2,1,0:T(8,128)(2,1)S(1)} %broadcast_in_dim.27), channel_id=1, replica_groups={{0,4,8,12},{1,5,9,13},{2,6,10,14},{3,7,11,15},{16,20,24,28},{17,21,25,2..., dimensions={0} | all-to-all | bytes 262144 | tf_op jit(solution)/shard_map/all_to_all | solution.py:322
  72.4 16.5 %all_to_all.43 = bf16[8,32,2048]{2,1,0:T(8,128)(2,1)S(1)} all-to-all(bf16[8,32,2048]{2,1,0:T(8,128)(2,1)S(1)} %broadcast_in_dim.28), channel_id=1, replica_groups={{0,2,16,18,32,34,48,50},{1,3,17,19,33,35,49,51},{4,6,20,22,36,38,52,54}..., dimensions={0} | all-to-all | bytes 2097152 | tf_op jit(solution)/shard_map/all_to_all | solution.py:325
  88.8 1.9 %collective-permute-start = (bf16[256,2048]{1,0:T(8,128)(2,1)S(1)}, bf16[256,2048]{1,0:T(8,128)(2,1)}, u32[]{:S(2)}, u32[]{:S(2)}) collective-permute-start(bf16[256,2048]{1,0:T(8,128)(2,1)S(1)} %bitcast.28), channel_id=1, source_target_pairs={{0,1},{1,0},{2,3},{3,2},{4,5},{5,4},{6,7},{7,6},{8,9},{9,8},{10,11... | collective-permute-start | bytes 3145736 | tf_op jit(solution)/shard_map/ppermute | solution.py:329
  90.8 2.4 %own_products.1 = (f32[256,256]{1,0:T(8,128)S(1)}, f32[256,1536]{1,0:T(8,128)S(1)}, f32[256,256]{1,0:T(8,128)S(1)}) custom-call(s32[1]{0:T(128)} %bitcast.4.core_ref, bf16[256,2048]{1,0:T(8,128)(2,1)S(1)} %bitcast.29, bf16[512,1536]{1,0:T(8,128)(2,1)S(1)} %bitcast.26, bf16[1536,256]{1,0:T(8,128)(2,1)S(1)} %copy-done), custom_call_target="tpu_custom_call" | custom-call | flops 2000000000 | bytes 1024 | tf_op jit(solution)/shard_map/own_products/pallas_call | solution.py:215
  93.5 4.4 %products.1 = (f32[4,96,384]{2,1,0:T(8,128)S(1)}, f32[4,192,384]{2,1,0:T(8,128)}, f32[256,256]{1,0:T(8,128)S(1)}) custom-call(s32[1]{0:T(128)} %bitcast.4.core_ref, bf16[256,2048]{1,0:T(8,128)(2,1)} %collective-permute-done.load_ref, bf16[512,1536]{1,0:T(8,128)(2,1)S(1)} %bitcast.27, bf16[1536,256]{1,0:T(8,128)(2,1)S(1)} %copy-done, ...), custom_call_target="tpu_custom_call" | custom-call | flops 3000000000 | bytes 1024 | tf_op jit(solution)/shard_map/products/pallas_call | solution.py:230
  98.0 14.7 %all_to_all.44 = f32[4,96,384]{2,1,0:T(8,128)S(1)} all-to-all(f32[4,96,384]{2,1,0:T(8,128)S(1)} %get-tuple-element.17), channel_id=1, replica_groups={{0,64,128,192},{256,320,384,448},{1,65,129,193},{257,321,385,449},{2,66..., dimensions={0} | all-to-all | bytes 1179648 | tf_op jit(solution)/shard_map/all_to_all | solution.py:334
  112.6 3.5 %all-to-all-start.6 = ((f32[4,192,384]{2,1,0:T(8,128)}), f32[4,192,384]{2,1,0:T(8,128)S(1)}, u32[]{:S(2)}, u32[]{:S(2)}) async-start(f32[4,192,384]{2,1,0:T(8,128)} %get-tuple-element.18), calls=%async_computation.6 | async-start | bytes 2359296 | tf_op jit(solution)/shard_map/all_to_all | solution.py:334
  116.2 8.2 %collective-permute-start.1 = (f32[96,384]{1,0:T(8,128)S(1)}, f32[96,384]{1,0:T(8,128)S(1)}, u32[]{:S(2)}, u32[]{:S(2)}) collective-permute-start(f32[96,384]{1,0:T(8,128)S(1)} %reduce_sum.28), channel_id=1, source_target_pairs={{0,256},{64,320},{128,384},{192,448},{256,0},{320,64},{384,128},{4... | collective-permute-start | bytes 442376 | tf_op jit(solution)/shard_map/ppermute | solution.py:340
  124.5 7.6 %all-to-all-done.6 = f32[4,192,384]{2,1,0:T(8,128)S(1)} async-done(((f32[4,192,384]{2,1,0:T(8,128)}), f32[4,192,384]{2,1,0:T(8,128)S(1)}, u32[]{:S(2)}, u32[]{:S(2)}) %all-to-all-start.6) | async-done | bytes 1179680 | tf_op jit(solution)/shard_map/all_to_all | solution.py:334
  132.2 8.2 %collective-permute-start.2 = (f32[192,384]{1,0:T(8,128)S(1)}, f32[192,384]{1,0:T(8,128)S(1)}, u32[]{:S(2)}, u32[]{:S(2)}) collective-permute-start(f32[192,384]{1,0:T(8,128)S(1)} %reduce_sum.29.refs_2_), channel_id=1, source_target_pairs={{0,256},{64,320},{128,384},{192,448},{256,0},{320,64},{384,128},{4... | collective-permute-start | bytes 884744 | tf_op jit(solution)/shard_map/ppermute | solution.py:342
  140.4 0.7 broadcast_in_dim.29
  141.1 3.5 %all-to-all-start.5 = ((f32[4,32,384]{2,1,0:T(8,128)}), f32[4,32,384]{2,1,0:T(8,128)S(1)}, u32[]{:S(2)}, u32[]{:S(2)}) async-start(f32[4,32,384]{2,1,0:T(8,128)} %broadcast_in_dim.29), calls=%async_computation.5 | async-start | bytes 393216 | tf_op jit(solution)/shard_map/all_to_all | solution.py:334
  144.7 6.1 %all-to-all-done.5.packed_ref = f32[4,32,384]{2,1,0:T(8,128)S(1)} async-done(((f32[4,32,384]{2,1,0:T(8,128)}), f32[4,32,384]{2,1,0:T(8,128)S(1)}, u32[]{:S(2)}, u32[]{:S(2)}) %all-to-all-start.5) | async-done | bytes 196640 | tf_op jit(solution)/shard_map/all_to_all | solution.py:334
  150.8 8.9 %inverse_factor.1.inverse_ref = f32[256,256]{1,0:T(8,128)S(1)} custom-call(f32[4,32,384]{2,1,0:T(8,128)S(1)} %all-to-all-done.5.packed_ref), custom_call_target="tpu_custom_call" | custom-call | flops 536870912 | bytes 1024 | tf_op jit(solution)/shard_map/inverse_factor/pallas_call | solution.py:124
  159.6 11.6 %collective-permute-done.2.refs_3_ = f32[192,384]{1,0:T(8,128)S(1)} collective-permute-done((f32[192,384]{1,0:T(8,128)S(1)}, f32[192,384]{1,0:T(8,128)S(1)}, u32[]{:S(2)}, u32[]{:S(2)}) %collective-permute-start.2) | collective-permute-done | bytes 294944 | tf_op jit(solution)/shard_map/ppermute | solution.py:342
  171.2 0.7 finished.1
  172.0 1.0 broadcast_in_dim.30
  173.0 3.5 %all-to-all-start.7 = ((f16[4,272,384]{2,1,0:T(8,128)(2,1)}), f16[4,272,384]{2,1,0:T(8,128)(2,1)S(1)}, u32[]{:S(2)}, u32[]{:S(2)}) async-start(f16[4,272,384]{2,1,0:T(8,128)(2,1)} %broadcast_in_dim.30), calls=%async_computation.7 | async-start | bytes 1671168 | tf_op jit(solution)/shard_map/all_to_all | solution.py:334
  177.4 0.9 copy.7
  178.2 11.1 %all-to-all-done.7 = f16[4,272,384]{2,1,0:T(8,128)(2,1)S(1)} async-done(((f16[4,272,384]{2,1,0:T(8,128)(2,1)}), f16[4,272,384]{2,1,0:T(8,128)(2,1)S(1)}, u32[]{:S(2)}, u32[]{:S(2)}) %all-to-all-start.7) | async-done | bytes 835616 | tf_op jit(solution)/shard_map/all_to_all | solution.py:334
  189.4 1.2 assembled.1
  (32 shorter events, 3.0 us)
Async XLA Ops:
  33.4 20.7 %copy-start = (bf16[1536,256]{1,0:T(8,128)(2,1)S(1)}, bf16[1536,256]{1,0:T(8,128)(2,1)}, u32[]{:S(2)}) copy-start(bf16[1536,256]{1,0:T(8,128)(2,1)} %sketch_ref.3) | copy-start | bytes 2359300
  54.1 34.7 %copy-start.3 = (bf16[8,1536]{1,0:T(8,128)(2,1)}, bf16[8,1536]{1,0:T(8,128)(2,1)S(1)}, u32[]{:S(2)}) copy-start(bf16[8,1536]{1,0:T(8,128)(2,1)S(1)} %fusion.2) | copy-start | bytes 73732
  88.8 4.7 %collective-permute-start = (bf16[256,2048]{1,0:T(8,128)(2,1)S(1)}, bf16[256,2048]{1,0:T(8,128)(2,1)}, u32[]{:S(2)}, u32[]{:S(2)}) collective-permute-start(bf16[256,2048]{1,0:T(8,128)(2,1)S(1)} %bitcast.28), channel_id=1, source_target_pairs={{0,1},{1,0},{2,3},{3,2},{4,5},{5,4},{6,7},{7,6},{8,9},{9,8},{10,11... | collective-permute-start | bytes 3145736 | tf_op jit(solution)/shard_map/ppermute | solution.py:329
  93.2 4.8 %copy-start.1 = (f32[256,256]{1,0:T(8,128)}, f32[256,256]{1,0:T(8,128)S(1)}, u32[]{:S(2)}) copy-start(f32[256,256]{1,0:T(8,128)S(1)} %get-tuple-element.14) | copy-start | bytes 786436
  112.6 19.4 %all-to-all-start.6 = ((f32[4,192,384]{2,1,0:T(8,128)}), f32[4,192,384]{2,1,0:T(8,128)S(1)}, u32[]{:S(2)}, u32[]{:S(2)}) async-start(f32[4,192,384]{2,1,0:T(8,128)} %get-tuple-element.18), calls=%async_computation.6 | async-start | bytes 2359296 | tf_op jit(solution)/shard_map/all_to_all | solution.py:334
  116.2 24.2 %collective-permute-start.1 = (f32[96,384]{1,0:T(8,128)S(1)}, f32[96,384]{1,0:T(8,128)S(1)}, u32[]{:S(2)}, u32[]{:S(2)}) collective-permute-start(f32[96,384]{1,0:T(8,128)S(1)} %reduce_sum.28), channel_id=1, source_target_pairs={{0,256},{64,320},{128,384},{192,448},{256,0},{320,64},{384,128},{4... | collective-permute-start | bytes 442376 | tf_op jit(solution)/shard_map/ppermute | solution.py:340
  132.2 39.0 %collective-permute-start.2 = (f32[192,384]{1,0:T(8,128)S(1)}, f32[192,384]{1,0:T(8,128)S(1)}, u32[]{:S(2)}, u32[]{:S(2)}) collective-permute-start(f32[192,384]{1,0:T(8,128)S(1)} %reduce_sum.29.refs_2_), channel_id=1, source_target_pairs={{0,256},{64,320},{128,384},{192,448},{256,0},{320,64},{384,128},{4... | collective-permute-start | bytes 884744 | tf_op jit(solution)/shard_map/ppermute | solution.py:342
  141.1 9.7 %all-to-all-start.5 = ((f32[4,32,384]{2,1,0:T(8,128)}), f32[4,32,384]{2,1,0:T(8,128)S(1)}, u32[]{:S(2)}, u32[]{:S(2)}) async-start(f32[4,32,384]{2,1,0:T(8,128)} %broadcast_in_dim.29), calls=%async_computation.5 | async-start | bytes 393216 | tf_op jit(solution)/shard_map/all_to_all | solution.py:334
  172.0 4.9 %copy-start.2 = (f32[256,256]{1,0:T(8,128)S(1)}, f32[256,256]{1,0:T(8,128)}, u32[]{:S(2)}) copy-start(f32[256,256]{1,0:T(8,128)} %copy-done.1) | copy-start | bytes 786436
  173.0 16.4 %all-to-all-start.7 = ((f16[4,272,384]{2,1,0:T(8,128)(2,1)}), f16[4,272,384]{2,1,0:T(8,128)(2,1)S(1)}, u32[]{:S(2)}, u32[]{:S(2)}) async-start(f16[4,272,384]{2,1,0:T(8,128)(2,1)} %broadcast_in_dim.30), calls=%async_computation.7 | async-start | bytes 1671168 | tf_op jit(solution)/shard_map/all_to_all | solution.py:334

commit v16 on v15

--- a/solution.py
+++ b/solution.py
@@ -29,6 +29,7 @@
     for y in range(YN) for n in range(NN) for c in range(CN)
 ]
 OTHER_CORE = [(i, i ^ 1) for i in range(64)]
+ALONG_X = [[(i, i ^ k) for i in range(8)] for k in range(XN)]
 OTHER_HALF = [(i, i ^ 4) for i in range(8)]
 X_GROUPS = [[h * XN + x for x in range(XN)] for h in range(2)]
 
@@ -191,12 +192,13 @@
 
 
 def products_kernel(
-    core_ref, load_ref, own_ref, sketch_ref, own_gram_ref, own_delta_ref,
+    place_ref, load_ref, own_ref, sketch_ref, own_gram_ref, own_delta_ref,
     first_ref, second_ref, range_ref,
 ):
     ff, rank = sketch_ref.shape
     block, slab = rank // XN, ff // XN
-    gram, delta = half_products(1 - core_ref[0], load_ref, own_ref, sketch_ref, range_ref)
+    core, x = place_ref[0], place_ref[1]
+    gram, delta = half_products(1 - core, load_ref, own_ref, sketch_ref, range_ref)
     gram += own_gram_ref[...]
     delta += own_delta_ref[...]
     for b in range(XN):
@@ -207,7 +209,7 @@
         packed = jnp.concatenate([kept[: block // 2], kept[block // 2 :]], axis=1)
         first_ref[b, : block // 2, :] = packed
         first_ref[b, block // 2 :, :] = delta[:FIRST, b * slab : (b + 1) * slab]
-        second_ref[b] = delta[FIRST:, b * slab : (b + 1) * slab]
+        second_ref[b ^ x] = delta[FIRST:, b * slab : (b + 1) * slab]
 
 
 def own_products(core, load, own, sketch):
@@ -223,7 +225,7 @@
     )(core, load, own, sketch)
 
 
-def products(core, load, own, sketch, own_gram, own_delta):
+def products(place, load, own, sketch, own_gram, own_delta):
     half, (ff, rank) = load.shape[0], sketch.shape
     first = (XN, rank // XN // 2 + FIRST, ff // XN)
     second = (XN, rank - FIRST, ff // XN)
@@ -235,7 +237,7 @@
         compiler_params=pltpu.CompilerParams(vmem_limit_bytes=32 * MIB),
         cost_estimate=pl.CostEstimate(flops=3 * 10**9, bytes_accessed=2**10, transcendentals=0),
         name="products",
-    )(core, load, own, sketch, own_gram, own_delta)
+    )(place, load, own, sketch, own_gram, own_delta)
 
 
 def finished_kernel(inverse_ref, *refs):
@@ -334,11 +336,11 @@
         return lax.all_to_all(blocks, "grp", 0, 0, axis_index_groups=X_GROUPS)
 
     own_gram, own_delta, own_range = own_products(core, load, own, sketch)
-    first, second, other_range = products(core, other, own, sketch, own_gram, own_delta)
-    first, second = to_owners(first), to_owners(second)
-    first = jnp.sum(first, axis=0)
+    place = jnp.concatenate([core, (lax.axis_index("grp") % XN).reshape(1)])
+    first, second, other_range = products(place, other, own, sketch, own_gram, own_delta)
+    first = jnp.sum(to_owners(first), axis=0)
     first_came = lax.ppermute(first, "grp", OTHER_HALF)
-    second = jnp.sum(second, axis=0)
+    second = second[0] + sum(lax.ppermute(second[k], "grp", ALONG_X[k]) for k in (2, 3, 1))
     second_came = lax.ppermute(second, "grp", OTHER_HALF)
     packed = rank // XN // 2
     gram = first[:packed] + first_came[:packed]

time: 192 us -> 187 us (0.974)
  the two profiles are of different devices: /device:TPU:32 before, /device:TPU:96 now
where the time goes in v16:
time: 187 us; the launch traced here: 186 us
  blocking collectives  84.3 us (45%)
  starting transfers between devices  41.1 us (22%)
  waiting for transfers between devices  32.1 us (17%)
  Pallas kernels  17.2 us (9%)
  local copies, waits for them, and re-layouts  6.8 us (4%)
    all_to_all x1, blocking collectives, per_device(): lax.all_to_all(jnp.concatenate([own, tag], axis=2), 'exp', 0, 0, axis_ind...  28.1 us
    all_to_all x1, blocking collectives, per_device(): lax.all_to_all(weighted(got), 'exp', 0, 0, axis_index_groups=FAR_GROUPS)  19.7 us
    all_to_all x1, blocking collectives, per_device(): lax.all_to_all(jnp.broadcast_to(load, (YN * NN, FN * piece, wide)), 'exp'...  18.6 us
    all_to_all x1, blocking collectives, per_device(): lax.all_to_all(jnp.broadcast_to(load, (FN, piece, wide)), 'exp', 0, 0, ax...  17.9 us
    all_to_all x3, waiting for transfers between devices, to_owners(): return lax.all_to_all(blocks, 'grp', 0, 0, axis_index_groups=X_GROUPS)  17.7 us
    all_to_all x3, starting transfers between devices, to_owners(): return lax.all_to_all(blocks, 'grp', 0, 0, axis_index_groups=X_GROUPS)  12.3 us
    ppermute x1, waiting for transfers between devices, per_device(): second_came = lax.ppermute(second, 'grp', OTHER_HALF)  10.7 us
    ppermute x3, starting transfers between devices, per_device(): lax.ppermute(second[k], 'grp', ALONG_X[k])  10.4 us
  transfers between devices with their start and end apart: 9, of which 5 were waited for; matrix products, arithmetic and copies ran while one was open for 2% of the time, Pallas kernels for 6%

profile of v16, /device:TPU:96, one launch (start us, length us, event | category | flops | bytes accessed | tf_op | source)
XLA Modules:
  0.0 186.2 jit_solution(4376270218053448899)
XLA Ops:
  1.3 1.6 copy.6
  3.1 28.1 %all_to_all.35.got_ref = bf16[16,32,1664]{2,1,0:T(8,128)(2,1)S(1)} all-to-all(bf16[16,32,1664]{2,1,0:T(8,128)(2,1)S(1)} %pad_maximum_fusion), channel_id=1, replica_groups={{0,2,16,18,32,34,48,50,1,3,17,19,33,35,49,51},{4,6,20,22,36,38,52,54,5,..., dimensions={0} | all-to-all | bytes 3407872 | tf_op jit(solution)/shard_map/all_to_all | solution.py:312
  31.7 19.7 %all_to_all.36 = f32[4,8,1664]{2,1,0:T(8,128)S(1)} all-to-all(f32[4,8,1664]{2,1,0:T(8,128)S(1)} %weighted.1), channel_id=1, replica_groups={{0,4,8,12},{1,5,9,13},{2,6,10,14},{3,7,11,15},{16,20,24,28},{17,21,25,2..., dimensions={0} | all-to-all | bytes 425984 | tf_op jit(solution)/shard_map/all_to_all | solution.py:316
  52.3 17.9 %all_to_all.37 = bf16[4,8,2048]{2,1,0:T(8,128)(2,1)S(1)} all-to-all(bf16[4,8,2048]{2,1,0:T(8,128)(2,1)S(1)} %broadcast_in_dim.27), channel_id=1, replica_groups={{0,4,8,12},{1,5,9,13},{2,6,10,14},{3,7,11,15},{16,20,24,28},{17,21,25,2..., dimensions={0} | all-to-all | bytes 262144 | tf_op jit(solution)/shard_map/all_to_all | solution.py:324
  70.3 18.6 %all_to_all.38 = bf16[8,32,2048]{2,1,0:T(8,128)(2,1)S(1)} all-to-all(bf16[8,32,2048]{2,1,0:T(8,128)(2,1)S(1)} %broadcast_in_dim.28), channel_id=1, replica_groups={{0,2,16,18,32,34,48,50},{1,3,17,19,33,35,49,51},{4,6,20,22,36,38,52,54}..., dimensions={0} | all-to-all | bytes 2097152 | tf_op jit(solution)/shard_map/all_to_all | solution.py:327
  88.9 1.9 %collective-permute-start = (bf16[256,2048]{1,0:T(8,128)(2,1)S(1)}, bf16[256,2048]{1,0:T(8,128)(2,1)}, u32[]{:S(2)}, u32[]{:S(2)}) collective-permute-start(bf16[256,2048]{1,0:T(8,128)(2,1)S(1)} %bitcast.37), channel_id=1, source_target_pairs={{0,1},{1,0},{2,3},{3,2},{4,5},{5,4},{6,7},{7,6},{8,9},{9,8},{10,11... | collective-permute-start | bytes 3145736 | tf_op jit(solution)/shard_map/ppermute | solution.py:331
  90.9 2.4 %own_products.1 = (f32[256,256]{1,0:T(8,128)S(1)}, f32[256,1536]{1,0:T(8,128)S(1)}, f32[256,256]{1,0:T(8,128)S(1)}) custom-call(s32[1]{0:T(128)} %bitcast.4.core_ref, bf16[256,2048]{1,0:T(8,128)(2,1)S(1)} %bitcast.38, bf16[512,1536]{1,0:T(8,128)(2,1)S(1)} %bitcast.35, bf16[1536,256]{1,0:T(8,128)(2,1)S(1)} %copy-done), custom_call_target="tpu_custom_call" | custom-call | flops 2000000000 | bytes 1024 | tf_op jit(solution)/shard_map/own_products/pallas_call | solution.py:217
  94.0 3.5 %products.1 = (f32[4,96,384]{2,1,0:T(8,128)S(1)}, f32[4,192,384]{2,1,0:T(8,128)S(1)}, f32[256,256]{1,0:T(8,128)S(1)}) custom-call(s32[2]{0:T(128)S(1)} %pad_add_fusion.place_ref, bf16[256,2048]{1,0:T(8,128)(2,1)} %collective-permute-done.load_ref, bf16[512,1536]{1,0:T(8,128)(2,1)S(1)} %bitcast.36, bf16[1536,256]{1,0:T(8,128)(2,1)S(1)} %copy-done, ...), custom_call_target="tpu_custom_call" | custom-call | flops 3000000000 | bytes 1024 | tf_op jit(solution)/shard_map/products/pallas_call | solution.py:232
  99.1 4.3 %all-to-all-start.4 = ((f32[4,96,384]{2,1,0:T(8,128)}), f32[4,96,384]{2,1,0:T(8,128)S(1)}, u32[]{:S(2)}, u32[]{:S(2)}) async-start(f32[4,96,384]{2,1,0:T(8,128)} %copy-done.1), calls=%async_computation.4 | async-start | bytes 1179648 | tf_op jit(solution)/shard_map/all_to_all | solution.py:336
  103.4 5.1 %collective-permute-start.3 = (f32[192,384]{1,0:T(8,128)S(1)}, f32[192,384]{1,0:T(8,128)S(1)}, u32[]{:S(2)}, u32[]{:S(2)}) collective-permute-start(f32[192,384]{1,0:T(8,128)S(1)} %get-tuple-element.25), channel_id=1, source_target_pairs={{0,192},{64,128},{128,64},{192,0},{256,448},{320,384},{384,320},{4... | collective-permute-start | bytes 884744 | tf_op jit(solution)/shard_map/ppermute | solution.py:343
  108.6 2.2 %collective-permute-start.4 = (f32[192,384]{1,0:T(8,128)S(1)}, f32[192,384]{1,0:T(8,128)S(1)}, u32[]{:S(2)}, u32[]{:S(2)}) collective-permute-start(f32[192,384]{1,0:T(8,128)S(1)} %get-tuple-element.26), channel_id=1, source_target_pairs={{0,64},{64,0},{128,192},{192,128},{256,320},{320,256},{384,448},{4... | collective-permute-start | bytes 884744 | tf_op jit(solution)/shard_map/ppermute | solution.py:343
  110.8 3.1 %collective-permute-start.2 = (f32[192,384]{1,0:T(8,128)S(1)}, f32[192,384]{1,0:T(8,128)}, u32[]{:S(2)}, u32[]{:S(2)}) collective-permute-start(f32[192,384]{1,0:T(8,128)S(1)} %get-tuple-element.27), channel_id=1, source_target_pairs={{0,128},{64,192},{128,0},{192,64},{256,384},{320,448},{384,256},{4... | collective-permute-start | bytes 884744 | tf_op jit(solution)/shard_map/ppermute | solution.py:343
  113.9 1.1 all-to-all-done.4
  115.0 8.2 %collective-permute-start.1 = (f32[96,384]{1,0:T(8,128)S(1)}, f32[96,384]{1,0:T(8,128)S(1)}, u32[]{:S(2)}, u32[]{:S(2)}) collective-permute-start(f32[96,384]{1,0:T(8,128)S(1)} %reduce_sum.19), channel_id=1, source_target_pairs={{0,256},{64,320},{128,384},{192,448},{256,0},{320,64},{384,128},{4... | collective-permute-start | bytes 442376 | tf_op jit(solution)/shard_map/ppermute | solution.py:342
  123.3 3.8 %collective-permute-done.2 = f32[192,384]{1,0:T(8,128)} collective-permute-done((f32[192,384]{1,0:T(8,128)S(1)}, f32[192,384]{1,0:T(8,128)}, u32[]{:S(2)}, u32[]{:S(2)}) %collective-permute-start.2) | collective-permute-done | bytes 294944 | tf_op jit(solution)/shard_map/ppermute | solution.py:343
  127.0 1.0 bitcast_add_fusion.refs_2_
  128.0 8.2 %collective-permute-start.5 = (f32[192,384]{1,0:T(8,128)S(1)}, f32[192,384]{1,0:T(8,128)S(1)}, u32[]{:S(2)}, u32[]{:S(2)}) collective-permute-start(f32[192,384]{1,0:T(8,128)S(1)} %bitcast_add_fusion.refs_2_), channel_id=1, source_target_pairs={{0,256},{64,320},{128,384},{192,448},{256,0},{320,64},{384,128},{4... | collective-permute-start | bytes 884744 | tf_op jit(solution)/shard_map/ppermute | solution.py:344
  137.0 3.5 %all-to-all-start.5 = ((f32[4,32,384]{2,1,0:T(8,128)}), f32[4,32,384]{2,1,0:T(8,128)S(1)}, u32[]{:S(2)}, u32[]{:S(2)}) async-start(f32[4,32,384]{2,1,0:T(8,128)} %broadcast_in_dim.29), calls=%async_computation.5 | async-start | bytes 393216 | tf_op jit(solution)/shard_map/all_to_all | solution.py:336
  140.6 6.1 %all-to-all-done.5.packed_ref = f32[4,32,384]{2,1,0:T(8,128)S(1)} async-done(((f32[4,32,384]{2,1,0:T(8,128)}), f32[4,32,384]{2,1,0:T(8,128)S(1)}, u32[]{:S(2)}, u32[]{:S(2)}) %all-to-all-start.5) | async-done | bytes 196640 | tf_op jit(solution)/shard_map/all_to_all | solution.py:336
  146.6 8.9 %inverse_factor.1.inverse_ref = f32[256,256]{1,0:T(8,128)S(1)} custom-call(f32[4,32,384]{2,1,0:T(8,128)S(1)} %all-to-all-done.5.packed_ref), custom_call_target="tpu_custom_call" | custom-call | flops 536870912 | bytes 1024 | tf_op jit(solution)/shard_map/inverse_factor/pallas_call | solution.py:125
  155.5 10.7 %collective-permute-done.5.refs_3_ = f32[192,384]{1,0:T(8,128)S(1)} collective-permute-done((f32[192,384]{1,0:T(8,128)S(1)}, f32[192,384]{1,0:T(8,128)S(1)}, u32[]{:S(2)}, u32[]{:S(2)}) %collective-permute-start.5) | collective-permute-done | bytes 294944 | tf_op jit(solution)/shard_map/ppermute | solution.py:344
  168.0 4.5 %all-to-all-start.6 = ((f16[4,272,384]{2,1,0:T(8,128)(2,1)}), f16[4,272,384]{2,1,0:T(8,128)(2,1)S(1)}, u32[]{:S(2)}, u32[]{:S(2)}) async-start(f16[4,272,384]{2,1,0:T(8,128)(2,1)} %broadcast_in_dim.30), calls=%async_computation.6 | async-start | bytes 1671168 | tf_op jit(solution)/shard_map/all_to_all | solution.py:336
  174.2 10.6 %all-to-all-done.6 = f16[4,272,384]{2,1,0:T(8,128)(2,1)S(1)} async-done(((f16[4,272,384]{2,1,0:T(8,128)(2,1)}), f16[4,272,384]{2,1,0:T(8,128)(2,1)S(1)}, u32[]{:S(2)}, u32[]{:S(2)}) %all-to-all-start.6) | async-done | bytes 835616 | tf_op jit(solution)/shard_map/all_to_all | solution.py:336
  184.9 1.2 assembled.1
  (45 shorter events, 8.3 us)
Async XLA Ops:
  31.2 20.4 %copy-start = (bf16[1536,256]{1,0:T(8,128)(2,1)S(1)}, bf16[1536,256]{1,0:T(8,128)(2,1)}, u32[]{:S(2)}) copy-start(bf16[1536,256]{1,0:T(8,128)(2,1)} %sketch_ref.3) | copy-start | bytes 2359300
  51.6 0.6 copy-start.6
  88.9 5.1 %collective-permute-start = (bf16[256,2048]{1,0:T(8,128)(2,1)S(1)}, bf16[256,2048]{1,0:T(8,128)(2,1)}, u32[]{:S(2)}, u32[]{:S(2)}) collective-permute-start(bf16[256,2048]{1,0:T(8,128)(2,1)S(1)} %bitcast.37), channel_id=1, source_target_pairs={{0,1},{1,0},{2,3},{3,2},{4,5},{5,4},{6,7},{7,6},{8,9},{9,8},{10,11... | collective-permute-start | bytes 3145736 | tf_op jit(solution)/shard_map/ppermute | solution.py:331
  93.3 0.7 copy-start.2
  97.6 0.8 copy-start.1
  98.4 0.7 copy-start.4
  99.1 15.9 %all-to-all-start.4 = ((f32[4,96,384]{2,1,0:T(8,128)}), f32[4,96,384]{2,1,0:T(8,128)S(1)}, u32[]{:S(2)}, u32[]{:S(2)}) async-start(f32[4,96,384]{2,1,0:T(8,128)} %copy-done.1), calls=%async_computation.4 | async-start | bytes 1179648 | tf_op jit(solution)/shard_map/all_to_all | solution.py:336
  103.4 19.8 %collective-permute-start.3 = (f32[192,384]{1,0:T(8,128)S(1)}, f32[192,384]{1,0:T(8,128)S(1)}, u32[]{:S(2)}, u32[]{:S(2)}) collective-permute-start(f32[192,384]{1,0:T(8,128)S(1)} %get-tuple-element.25), channel_id=1, source_target_pairs={{0,192},{64,128},{128,64},{192,0},{256,448},{320,384},{384,320},{4... | collective-permute-start | bytes 884744 | tf_op jit(solution)/shard_map/ppermute | solution.py:343
  108.6 14.7 %collective-permute-start.4 = (f32[192,384]{1,0:T(8,128)S(1)}, f32[192,384]{1,0:T(8,128)S(1)}, u32[]{:S(2)}, u32[]{:S(2)}) collective-permute-start(f32[192,384]{1,0:T(8,128)S(1)} %get-tuple-element.26), channel_id=1, source_target_pairs={{0,64},{64,0},{128,192},{192,128},{256,320},{320,256},{384,448},{4... | collective-permute-start | bytes 884744 | tf_op jit(solution)/shard_map/ppermute | solution.py:343
  110.8 16.3 %collective-permute-start.2 = (f32[192,384]{1,0:T(8,128)S(1)}, f32[192,384]{1,0:T(8,128)}, u32[]{:S(2)}, u32[]{:S(2)}) collective-permute-start(f32[192,384]{1,0:T(8,128)S(1)} %get-tuple-element.27), channel_id=1, source_target_pairs={{0,128},{64,192},{128,0},{192,64},{256,384},{320,448},{384,256},{4... | collective-permute-start | bytes 884744 | tf_op jit(solution)/shard_map/ppermute | solution.py:343
  115.0 21.3 %collective-permute-start.1 = (f32[96,384]{1,0:T(8,128)S(1)}, f32[96,384]{1,0:T(8,128)S(1)}, u32[]{:S(2)}, u32[]{:S(2)}) collective-permute-start(f32[96,384]{1,0:T(8,128)S(1)} %reduce_sum.19), channel_id=1, source_target_pairs={{0,256},{64,320},{128,384},{192,448},{256,0},{320,64},{384,128},{4... | collective-permute-start | bytes 442376 | tf_op jit(solution)/shard_map/ppermute | solution.py:342
  128.0 38.2 %collective-permute-start.5 = (f32[192,384]{1,0:T(8,128)S(1)}, f32[192,384]{1,0:T(8,128)S(1)}, u32[]{:S(2)}, u32[]{:S(2)}) collective-permute-start(f32[192,384]{1,0:T(8,128)S(1)} %bitcast_add_fusion.refs_2_), channel_id=1, source_target_pairs={{0,256},{64,320},{128,384},{192,448},{256,0},{320,64},{384,128},{4... | collective-permute-start | bytes 884744 | tf_op jit(solution)/shard_map/ppermute | solution.py:344
  137.0 9.7 %all-to-all-start.5 = ((f32[4,32,384]{2,1,0:T(8,128)}), f32[4,32,384]{2,1,0:T(8,128)S(1)}, u32[]{:S(2)}, u32[]{:S(2)}) async-start(f32[4,32,384]{2,1,0:T(8,128)} %broadcast_in_dim.29), calls=%async_computation.5 | async-start | bytes 393216 | tf_op jit(solution)/shard_map/all_to_all | solution.py:336
  166.9 5.5 %copy-start.5 = (f32[256,256]{1,0:T(8,128)S(1)}, f32[256,256]{1,0:T(8,128)}, u32[]{:S(2)}) copy-start(f32[256,256]{1,0:T(8,128)} %copy-done.4) | copy-start | bytes 786436
  167.0 5.9 %copy-start.3 = (f32[256,256]{1,0:T(8,128)S(1)}, f32[256,256]{1,0:T(8,128)}, u32[]{:S(2)}) copy-start(f32[256,256]{1,0:T(8,128)} %copy-done.2) | copy-start | bytes 786436
  168.0 16.8 %all-to-all-start.6 = ((f16[4,272,384]{2,1,0:T(8,128)(2,1)}), f16[4,272,384]{2,1,0:T(8,128)(2,1)S(1)}, u32[]{:S(2)}, u32[]{:S(2)}) async-start(f16[4,272,384]{2,1,0:T(8,128)(2,1)} %broadcast_in_dim.30), calls=%async_computation.6 | async-start | bytes 1671168 | tf_op jit(solution)/shard_map/all_to_all | solution.py:336

commit v17 on v16

--- a/solution.py
+++ b/solution.py
@@ -35,7 +35,7 @@
 
 PANEL, STEP = 64, 8
 TOP_POWER = 13
-FIRST = 64
+FIRST = 72
 FACTOR_COST = 2**29
 
 
@@ -192,13 +192,16 @@
 
 
 def products_kernel(
-    place_ref, load_ref, own_ref, sketch_ref, own_gram_ref, own_delta_ref,
+    place_ref, load_ref, own_ref, sketch_ref, own_gram_ref, own_delta_ref, own_range_ref,
     first_ref, second_ref, range_ref,
 ):
     ff, rank = sketch_ref.shape
     block, slab = rank // XN, ff // XN
     core, x = place_ref[0], place_ref[1]
-    gram, delta = half_products(1 - core, load_ref, own_ref, sketch_ref, range_ref)
+    range_ref[core] = own_range_ref[...]
+    gram, delta = half_products(
+        1 - core, load_ref, own_ref, sketch_ref, range_ref.at[1 - core]
+    )
     gram += own_gram_ref[...]
     delta += own_delta_ref[...]
     for b in range(XN):
@@ -225,19 +228,19 @@
     )(core, load, own, sketch)
 
 
-def products(place, load, own, sketch, own_gram, own_delta):
+def products(place, load, own, sketch, own_gram, own_delta, own_range):
     half, (ff, rank) = load.shape[0], sketch.shape
     first = (XN, rank // XN // 2 + FIRST, ff // XN)
     second = (XN, rank - FIRST, ff // XN)
     return pl.pallas_call(
         products_kernel,
-        out_shape=[jax.ShapeDtypeStruct(shape, F32) for shape in (first, second, (half, rank))],
-        in_specs=[SMEM] + [VMEM] * 5,
+        out_shape=[jax.ShapeDtypeStruct(shape, F32) for shape in (first, second, (CN, half, rank))],
+        in_specs=[SMEM] + [VMEM] * 6,
         out_specs=[VMEM] * 3,
         compiler_params=pltpu.CompilerParams(vmem_limit_bytes=32 * MIB),
         cost_estimate=pl.CostEstimate(flops=3 * 10**9, bytes_accessed=2**10, transcendentals=0),
         name="products",
-    )(place, load, own, sketch, own_gram, own_delta)
+    )(place, load, own, sketch, own_gram, own_delta, own_range)
 
 
 def finished_kernel(inverse_ref, *refs):
@@ -335,9 +338,9 @@
     def to_owners(blocks):
         return lax.all_to_all(blocks, "grp", 0, 0, axis_index_groups=X_GROUPS)
 
-    own_gram, own_delta, own_range = own_products(core, load, own, sketch)
+    held = own_products(core, load, own, sketch)
     place = jnp.concatenate([core, (lax.axis_index("grp") % XN).reshape(1)])
-    first, second, other_range = products(place, other, own, sketch, own_gram, own_delta)
+    first, second, range_rows = products(place, other, own, sketch, *held)
     first = jnp.sum(to_owners(first), axis=0)
     first_came = lax.ppermute(first, "grp", OTHER_HALF)
     second = second[0] + sum(lax.ppermute(second[k], "grp", ALONG_X[k]) for k in (2, 3, 1))
@@ -351,15 +354,10 @@
     blocks = to_owners(jnp.broadcast_to(block, (XN,) + block.shape))
     coeff = assembled(blocks.astype(F32))
 
-    scale = math.sqrt(rows * lax.axis_size("grp"))
-    halves = [
-        scale * lax.dot_general(half, inverse, (((1,), (1,)), ((), ())), precision=HIGHEST)
-        for half in (own_range, other_range)
-    ]
-    on_first = core[0] == 0
-    basis = jnp.stack(
-        [jnp.where(on_first, halves[i], halves[1 - i]) for i in range(CN)]
-    )
+    ortho = lax.dot_general(
+        range_rows.reshape(rows, rank), inverse, (((1,), (1,)), ((), ())), precision=HIGHEST
+    )
+    basis = ortho * math.sqrt(rows * lax.axis_size("grp"))
     basis = basis.reshape(CN, YN, NN, FN, piece, rank).transpose(1, 3, 2, 0, 4, 5)
     return (base_piece, basis.reshape(1, rows, rank), coeff[None])
 

time: 187 us -> 188 us (level)
  waiting for transfers between devices: 32.1 us -> 34.8 us
  transfers between devices with their start and end apart: 9 -> 9, of which waited for: 5 -> 6; matrix products, arithmetic and copies ran while one was open for 2% -> 2% of each run, Pallas kernels for 6% -> 6%
where the time goes in v17:
time: 188 us; the launch traced here: 187 us
  blocking collectives  84.3 us (45%)
  starting transfers between devices  40.1 us (21%)
  waiting for transfers between devices  34.8 us (19%)
  Pallas kernels  17.2 us (9%)
  local copies, waits for them, and re-layouts  6.05 us (3%)
    all_to_all x1, blocking collectives, per_device(): lax.all_to_all(jnp.concatenate([own, tag], axis=2), 'exp', 0, 0, axis_ind...  28.1 us
    all_to_all x1, blocking collectives, per_device(): lax.all_to_all(weighted(got), 'exp', 0, 0, axis_index_groups=FAR_GROUPS)  19.7 us
    all_to_all x3, waiting for transfers between devices, to_owners(): return lax.all_to_all(blocks, 'grp', 0, 0, axis_index_groups=X_GROUPS)  19.4 us
    all_to_all x1, blocking collectives, per_device(): lax.all_to_all(jnp.broadcast_to(load, (YN * NN, FN * piece, wide)), 'exp'...  18.6 us
    all_to_all x1, blocking collectives, per_device(): lax.all_to_all(jnp.broadcast_to(load, (FN, piece, wide)), 'exp', 0, 0, ax...  17.9 us
    ppermute x1, waiting for transfers between devices, per_device(): second_came = lax.ppermute(second, 'grp', OTHER_HALF)  12.1 us
    all_to_all x3, starting transfers between devices, to_owners(): return lax.all_to_all(blocks, 'grp', 0, 0, axis_index_groups=X_GROUPS)  11.3 us
    ppermute x3, starting transfers between devices, per_device(): lax.ppermute(second[k], 'grp', ALONG_X[k])  10.4 us
  transfers between devices with their start and end apart: 9, of which 6 were waited for; matrix products, arithmetic and copies ran while one was open for 2% of the time, Pallas kernels for 6%

profile of v17, /device:TPU:96, one launch (start us, length us, event | category | flops | bytes accessed | tf_op | source)
XLA Modules:
  0.0 186.9 jit_solution(5822820347656470119)
XLA Ops:
  1.3 1.6 copy.6
  3.1 28.1 %all_to_all.35.got_ref = bf16[16,32,1664]{2,1,0:T(8,128)(2,1)S(1)} all-to-all(bf16[16,32,1664]{2,1,0:T(8,128)(2,1)S(1)} %pad_maximum_fusion), channel_id=1, replica_groups={{0,2,16,18,32,34,48,50,1,3,17,19,33,35,49,51},{4,6,20,22,36,38,52,54,5,..., dimensions={0} | all-to-all | bytes 3407872 | tf_op jit(solution)/shard_map/all_to_all | solution.py:315
  31.7 19.7 %all_to_all.36 = f32[4,8,1664]{2,1,0:T(8,128)S(1)} all-to-all(f32[4,8,1664]{2,1,0:T(8,128)S(1)} %weighted.1), channel_id=1, replica_groups={{0,4,8,12},{1,5,9,13},{2,6,10,14},{3,7,11,15},{16,20,24,28},{17,21,25,2..., dimensions={0} | all-to-all | bytes 425984 | tf_op jit(solution)/shard_map/all_to_all | solution.py:319
  52.1 17.9 %all_to_all.37 = bf16[4,8,2048]{2,1,0:T(8,128)(2,1)S(1)} all-to-all(bf16[4,8,2048]{2,1,0:T(8,128)(2,1)S(1)} %broadcast_in_dim.27), channel_id=1, replica_groups={{0,4,8,12},{1,5,9,13},{2,6,10,14},{3,7,11,15},{16,20,24,28},{17,21,25,2..., dimensions={0} | all-to-all | bytes 262144 | tf_op jit(solution)/shard_map/all_to_all | solution.py:327
  70.1 18.6 %all_to_all.38 = bf16[8,32,2048]{2,1,0:T(8,128)(2,1)S(1)} all-to-all(bf16[8,32,2048]{2,1,0:T(8,128)(2,1)S(1)} %broadcast_in_dim.28), channel_id=1, replica_groups={{0,2,16,18,32,34,48,50},{1,3,17,19,33,35,49,51},{4,6,20,22,36,38,52,54}..., dimensions={0} | all-to-all | bytes 2097152 | tf_op jit(solution)/shard_map/all_to_all | solution.py:330
  88.8 1.9 %collective-permute-start = (bf16[256,2048]{1,0:T(8,128)(2,1)S(1)}, bf16[256,2048]{1,0:T(8,128)(2,1)}, u32[]{:S(2)}, u32[]{:S(2)}) collective-permute-start(bf16[256,2048]{1,0:T(8,128)(2,1)S(1)} %bitcast.35), channel_id=1, source_target_pairs={{0,1},{1,0},{2,3},{3,2},{4,5},{5,4},{6,7},{7,6},{8,9},{9,8},{10,11... | collective-permute-start | bytes 3145736 | tf_op jit(solution)/shard_map/ppermute | solution.py:334
  90.8 2.4 %own_products.1 = (f32[256,256]{1,0:T(8,128)S(1)}, f32[256,1536]{1,0:T(8,128)S(1)}, f32[256,256]{1,0:T(8,128)S(1)}) custom-call(s32[1]{0:T(128)} %bitcast.4.core_ref, bf16[256,2048]{1,0:T(8,128)(2,1)S(1)} %bitcast.36, bf16[512,1536]{1,0:T(8,128)(2,1)S(1)} %bitcast.33, bf16[1536,256]{1,0:T(8,128)(2,1)S(1)} %copy-done), custom_call_target="tpu_custom_call" | custom-call | flops 2000000000 | bytes 1024 | tf_op jit(solution)/shard_map/own_products/pallas_call | solution.py:220
  93.4 3.5 %products.1 = (f32[4,104,384]{2,1,0:T(8,128)S(1)}, f32[4,184,384]{2,1,0:T(8,128)S(1)}, f32[2,256,256]{2,1,0:T(8,128)S(1)}) custom-call(s32[2]{0:T(128)S(1)} %pad_add_fusion.place_ref, bf16[256,2048]{1,0:T(8,128)(2,1)} %collective-permute-done.load_ref, bf16[512,1536]{1,0:T(8,128)(2,1)S(1)} %bitcast.34, bf16[1536,256]{1,0:T(8,128)(2,1)S(1)} %copy-done, ...), custom_call_target="tpu_custom_call" | custom-call | flops 3000000000 | bytes 1024 | tf_op jit(solution)/shard_map/products/pallas_call | solution.py:235
  98.6 4.3 %all-to-all-start.4 = ((f32[4,104,384]{2,1,0:T(8,128)}), f32[4,104,384]{2,1,0:T(8,128)S(1)}, u32[]{:S(2)}, u32[]{:S(2)}) async-start(f32[4,104,384]{2,1,0:T(8,128)} %copy-done.1), calls=%async_computation.4 | async-start | bytes 1277952 | tf_op jit(solution)/shard_map/all_to_all | solution.py:339
  103.0 5.1 %collective-permute-start.3 = (f32[184,384]{1,0:T(8,128)S(1)}, f32[184,384]{1,0:T(8,128)S(1)}, u32[]{:S(2)}, u32[]{:S(2)}) collective-permute-start(f32[184,384]{1,0:T(8,128)S(1)} %get-tuple-element.25), channel_id=1, source_target_pairs={{0,192},{64,128},{128,64},{192,0},{256,448},{320,384},{384,320},{4... | collective-permute-start | bytes 847880 | tf_op jit(solution)/shard_map/ppermute | solution.py:346
  108.1 2.2 %collective-permute-start.4 = (f32[184,384]{1,0:T(8,128)S(1)}, f32[184,384]{1,0:T(8,128)S(1)}, u32[]{:S(2)}, u32[]{:S(2)}) collective-permute-start(f32[184,384]{1,0:T(8,128)S(1)} %get-tuple-element.26), channel_id=1, source_target_pairs={{0,64},{64,0},{128,192},{192,128},{256,320},{320,256},{384,448},{4... | collective-permute-start | bytes 847880 | tf_op jit(solution)/shard_map/ppermute | solution.py:346
  110.3 3.1 %collective-permute-start.2 = (f32[184,384]{1,0:T(8,128)S(1)}, f32[184,384]{1,0:T(8,128)}, u32[]{:S(2)}, u32[]{:S(2)}) collective-permute-start(f32[184,384]{1,0:T(8,128)S(1)} %get-tuple-element.27), channel_id=1, source_target_pairs={{0,128},{64,192},{128,0},{192,64},{256,384},{320,448},{384,256},{4... | collective-permute-start | bytes 847880 | tf_op jit(solution)/shard_map/ppermute | solution.py:346
  113.4 1.6 all-to-all-done.4
  115.1 8.2 %collective-permute-start.1 = (f32[104,384]{1,0:T(8,128)S(1)}, f32[104,384]{1,0:T(8,128)S(1)}, u32[]{:S(2)}, u32[]{:S(2)}) collective-permute-start(f32[104,384]{1,0:T(8,128)S(1)} %reduce_sum.19), channel_id=1, source_target_pairs={{0,256},{64,320},{128,384},{192,448},{256,0},{320,64},{384,128},{4... | collective-permute-start | bytes 479240 | tf_op jit(solution)/shard_map/ppermute | solution.py:345
  123.3 2.9 %collective-permute-done.2 = f32[184,384]{1,0:T(8,128)} collective-permute-done((f32[184,384]{1,0:T(8,128)S(1)}, f32[184,384]{1,0:T(8,128)}, u32[]{:S(2)}, u32[]{:S(2)}) %collective-permute-start.2) | collective-permute-done | bytes 282656 | tf_op jit(solution)/shard_map/ppermute | solution.py:346
  126.3 1.0 bitcast_add_fusion.refs_2_
  127.3 8.2 %collective-permute-start.5 = (f32[184,384]{1,0:T(8,128)S(1)}, f32[184,384]{1,0:T(8,128)S(1)}, u32[]{:S(2)}, u32[]{:S(2)}) collective-permute-start(f32[184,384]{1,0:T(8,128)S(1)} %bitcast_add_fusion.refs_2_), channel_id=1, source_target_pairs={{0,256},{64,320},{128,384},{192,448},{256,0},{320,64},{384,128},{4... | collective-permute-start | bytes 847880 | tf_op jit(solution)/shard_map/ppermute | solution.py:347
  136.3 3.5 %all-to-all-start.5 = ((f32[4,32,384]{2,1,0:T(8,128)}), f32[4,32,384]{2,1,0:T(8,128)S(1)}, u32[]{:S(2)}, u32[]{:S(2)}) async-start(f32[4,32,384]{2,1,0:T(8,128)} %broadcast_in_dim.29), calls=%async_computation.5 | async-start | bytes 393216 | tf_op jit(solution)/shard_map/all_to_all | solution.py:339
  139.9 6.1 %all-to-all-done.5.packed_ref = f32[4,32,384]{2,1,0:T(8,128)S(1)} async-done(((f32[4,32,384]{2,1,0:T(8,128)}), f32[4,32,384]{2,1,0:T(8,128)S(1)}, u32[]{:S(2)}, u32[]{:S(2)}) %all-to-all-start.5) | async-done | bytes 196640 | tf_op jit(solution)/shard_map/all_to_all | solution.py:339
  145.9 8.9 %inverse_factor.1.inverse_ref = f32[256,256]{1,0:T(8,128)S(1)} custom-call(f32[4,32,384]{2,1,0:T(8,128)S(1)} %all-to-all-done.5.packed_ref), custom_call_target="tpu_custom_call" | custom-call | flops 536870912 | bytes 1024 | tf_op jit(solution)/shard_map/inverse_factor/pallas_call | solution.py:125
  154.8 12.1 %collective-permute-done.5.refs_3_ = f32[184,384]{1,0:T(8,128)S(1)} collective-permute-done((f32[184,384]{1,0:T(8,128)S(1)}, f32[184,384]{1,0:T(8,128)S(1)}, u32[]{:S(2)}, u32[]{:S(2)}) %collective-permute-start.5) | collective-permute-done | bytes 282656 | tf_op jit(solution)/shard_map/ppermute | solution.py:347
  168.7 3.5 %all-to-all-start.6 = ((f16[4,272,384]{2,1,0:T(8,128)(2,1)}), f16[4,272,384]{2,1,0:T(8,128)(2,1)S(1)}, u32[]{:S(2)}, u32[]{:S(2)}) async-start(f16[4,272,384]{2,1,0:T(8,128)(2,1)} %broadcast_in_dim.30), calls=%async_computation.6 | async-start | bytes 1671168 | tf_op jit(solution)/shard_map/all_to_all | solution.py:339
  173.7 11.7 %all-to-all-done.6 = f16[4,272,384]{2,1,0:T(8,128)(2,1)S(1)} async-done(((f16[4,272,384]{2,1,0:T(8,128)(2,1)}), f16[4,272,384]{2,1,0:T(8,128)(2,1)S(1)}, u32[]{:S(2)}, u32[]{:S(2)}) %all-to-all-start.6) | async-done | bytes 835616 | tf_op jit(solution)/shard_map/all_to_all | solution.py:339
  185.5 1.2 assembled.1
  (39 shorter events, 7.6 us)
Async XLA Ops:
  31.2 20.4 %copy-start = (bf16[1536,256]{1,0:T(8,128)(2,1)S(1)}, bf16[1536,256]{1,0:T(8,128)(2,1)}, u32[]{:S(2)}) copy-start(bf16[1536,256]{1,0:T(8,128)(2,1)} %sketch_ref.3) | copy-start | bytes 2359300
  51.6 37.1 %copy-start.4 = (bf16[8,1536]{1,0:T(8,128)(2,1)}, bf16[8,1536]{1,0:T(8,128)(2,1)S(1)}, u32[]{:S(2)}) copy-start(bf16[8,1536]{1,0:T(8,128)(2,1)S(1)} %fusion.2) | copy-start | bytes 73732
  88.8 4.7 %collective-permute-start = (bf16[256,2048]{1,0:T(8,128)(2,1)S(1)}, bf16[256,2048]{1,0:T(8,128)(2,1)}, u32[]{:S(2)}, u32[]{:S(2)}) collective-permute-start(bf16[256,2048]{1,0:T(8,128)(2,1)S(1)} %bitcast.35), channel_id=1, source_target_pairs={{0,1},{1,0},{2,3},{3,2},{4,5},{5,4},{6,7},{7,6},{8,9},{9,8},{10,11... | collective-permute-start | bytes 3145736 | tf_op jit(solution)/shard_map/ppermute | solution.py:334
  97.0 0.8 copy-start.1
  97.8 0.8 copy-start.2
  98.6 16.5 %all-to-all-start.4 = ((f32[4,104,384]{2,1,0:T(8,128)}), f32[4,104,384]{2,1,0:T(8,128)S(1)}, u32[]{:S(2)}, u32[]{:S(2)}) async-start(f32[4,104,384]{2,1,0:T(8,128)} %copy-done.1), calls=%async_computation.4 | async-start | bytes 1277952 | tf_op jit(solution)/shard_map/all_to_all | solution.py:339
  103.0 20.4 %collective-permute-start.3 = (f32[184,384]{1,0:T(8,128)S(1)}, f32[184,384]{1,0:T(8,128)S(1)}, u32[]{:S(2)}, u32[]{:S(2)}) collective-permute-start(f32[184,384]{1,0:T(8,128)S(1)} %get-tuple-element.25), channel_id=1, source_target_pairs={{0,192},{64,128},{128,64},{192,0},{256,448},{320,384},{384,320},{4... | collective-permute-start | bytes 847880 | tf_op jit(solution)/shard_map/ppermute | solution.py:346
  108.1 15.2 %collective-permute-start.4 = (f32[184,384]{1,0:T(8,128)S(1)}, f32[184,384]{1,0:T(8,128)S(1)}, u32[]{:S(2)}, u32[]{:S(2)}) collective-permute-start(f32[184,384]{1,0:T(8,128)S(1)} %get-tuple-element.26), channel_id=1, source_target_pairs={{0,64},{64,0},{128,192},{192,128},{256,320},{320,256},{384,448},{4... | collective-permute-start | bytes 847880 | tf_op jit(solution)/shard_map/ppermute | solution.py:346
  110.3 16.0 %collective-permute-start.2 = (f32[184,384]{1,0:T(8,128)S(1)}, f32[184,384]{1,0:T(8,128)}, u32[]{:S(2)}, u32[]{:S(2)}) collective-permute-start(f32[184,384]{1,0:T(8,128)S(1)} %get-tuple-element.27), channel_id=1, source_target_pairs={{0,128},{64,192},{128,0},{192,64},{256,384},{320,448},{384,256},{4... | collective-permute-start | bytes 847880 | tf_op jit(solution)/shard_map/ppermute | solution.py:346
  115.1 20.5 %collective-permute-start.1 = (f32[104,384]{1,0:T(8,128)S(1)}, f32[104,384]{1,0:T(8,128)S(1)}, u32[]{:S(2)}, u32[]{:S(2)}) collective-permute-start(f32[104,384]{1,0:T(8,128)S(1)} %reduce_sum.19), channel_id=1, source_target_pairs={{0,256},{64,320},{128,384},{192,448},{256,0},{320,64},{384,128},{4... | collective-permute-start | bytes 479240 | tf_op jit(solution)/shard_map/ppermute | solution.py:345
  127.3 39.6 %collective-permute-start.5 = (f32[184,384]{1,0:T(8,128)S(1)}, f32[184,384]{1,0:T(8,128)S(1)}, u32[]{:S(2)}, u32[]{:S(2)}) collective-permute-start(f32[184,384]{1,0:T(8,128)S(1)} %bitcast_add_fusion.refs_2_), channel_id=1, source_target_pairs={{0,256},{64,320},{128,384},{192,448},{256,0},{320,64},{384,128},{4... | collective-permute-start | bytes 847880 | tf_op jit(solution)/shard_map/ppermute | solution.py:347
  136.3 9.7 %all-to-all-start.5 = ((f32[4,32,384]{2,1,0:T(8,128)}), f32[4,32,384]{2,1,0:T(8,128)S(1)}, u32[]{:S(2)}, u32[]{:S(2)}) async-start(f32[4,32,384]{2,1,0:T(8,128)} %broadcast_in_dim.29), calls=%async_computation.5 | async-start | bytes 393216 | tf_op jit(solution)/shard_map/all_to_all | solution.py:339
  167.7 4.5 %copy-start.3 = (f32[2,256,256]{2,1,0:T(8,128)S(1)}, f32[2,256,256]{2,1,0:T(8,128)}, u32[]{:S(2)}) copy-start(f32[2,256,256]{2,1,0:T(8,128)} %copy-done.2) | copy-start | bytes 1572868
  168.7 16.7 %all-to-all-start.6 = ((f16[4,272,384]{2,1,0:T(8,128)(2,1)}), f16[4,272,384]{2,1,0:T(8,128)(2,1)S(1)}, u32[]{:S(2)}, u32[]{:S(2)}) async-start(f16[4,272,384]{2,1,0:T(8,128)(2,1)} %broadcast_in_dim.30), calls=%async_computation.6 | async-start | bytes 1671168 | tf_op jit(solution)/shard_map/all_to_all | solution.py:339

commit v18 on v17

--- a/solution.py
+++ b/solution.py
@@ -35,7 +35,7 @@
 
 PANEL, STEP = 64, 8
 TOP_POWER = 13
-FIRST = 72
+FIRST = 64
 FACTOR_COST = 2**29
 
 

time: 188 us -> 186 us (0.989)
  waiting for transfers between devices: 34.8 us -> 32.7 us
where the time goes in v18:
time: 186 us
  blocking collectives  84.3 us (45%)
  starting transfers between devices  40.8 us (22%)
  waiting for transfers between devices  32.7 us (18%)
  Pallas kernels  17.2 us (9%)
  local copies, waits for them, and re-layouts  6.18 us (3%)
    all_to_all x1, blocking collectives, per_device(): lax.all_to_all(jnp.concatenate([own, tag], axis=2), 'exp', 0, 0, axis_ind...  28.1 us
    all_to_all x1, blocking collectives, per_device(): lax.all_to_all(weighted(got), 'exp', 0, 0, axis_index_groups=FAR_GROUPS)  19.7 us
    all_to_all x1, blocking collectives, per_device(): lax.all_to_all(jnp.broadcast_to(load, (YN * NN, FN * piece, wide)), 'exp'...  18.6 us
    all_to_all x3, waiting for transfers between devices, to_owners(): return lax.all_to_all(blocks, 'grp', 0, 0, axis_index_groups=X_GROUPS)  18.3 us
    all_to_all x1, blocking collectives, per_device(): lax.all_to_all(jnp.broadcast_to(load, (FN, piece, wide)), 'exp', 0, 0, ax...  17.9 us
    all_to_all x3, starting transfers between devices, to_owners(): return lax.all_to_all(blocks, 'grp', 0, 0, axis_index_groups=X_GROUPS)  12 us
    ppermute x1, waiting for transfers between devices, per_device(): second_came = lax.ppermute(second, 'grp', OTHER_HALF)  10.7 us
    ppermute x3, starting transfers between devices, per_device(): lax.ppermute(second[k], 'grp', ALONG_X[k])  10.4 us
  transfers between devices with their start and end apart: 9, of which 6 were waited for; matrix products, arithmetic and copies ran while one was open for 2% of the time, Pallas kernels for 6%

profile of v18, /device:TPU:96, one launch (start us, length us, event | category | flops | bytes accessed | tf_op | source)
XLA Modules:
  0.0 185.6 jit_solution(3767748519107180483)
XLA Ops:
  1.3 1.6 copy.6
  3.1 28.1 %all_to_all.35.got_ref = bf16[16,32,1664]{2,1,0:T(8,128)(2,1)S(1)} all-to-all(bf16[16,32,1664]{2,1,0:T(8,128)(2,1)S(1)} %pad_maximum_fusion), channel_id=1, replica_groups={{0,2,16,18,32,34,48,50,1,3,17,19,33,35,49,51},{4,6,20,22,36,38,52,54,5,..., dimensions={0} | all-to-all | bytes 3407872 | tf_op jit(solution)/shard_map/all_to_all | solution.py:315
  31.7 19.7 %all_to_all.36 = f32[4,8,1664]{2,1,0:T(8,128)S(1)} all-to-all(f32[4,8,1664]{2,1,0:T(8,128)S(1)} %weighted.1), channel_id=1, replica_groups={{0,4,8,12},{1,5,9,13},{2,6,10,14},{3,7,11,15},{16,20,24,28},{17,21,25,2..., dimensions={0} | all-to-all | bytes 425984 | tf_op jit(solution)/shard_map/all_to_all | solution.py:319
  52.3 17.9 %all_to_all.37 = bf16[4,8,2048]{2,1,0:T(8,128)(2,1)S(1)} all-to-all(bf16[4,8,2048]{2,1,0:T(8,128)(2,1)S(1)} %broadcast_in_dim.27), channel_id=1, replica_groups={{0,4,8,12},{1,5,9,13},{2,6,10,14},{3,7,11,15},{16,20,24,28},{17,21,25,2..., dimensions={0} | all-to-all | bytes 262144 | tf_op jit(solution)/shard_map/all_to_all | solution.py:327
  70.3 18.6 %all_to_all.38 = bf16[8,32,2048]{2,1,0:T(8,128)(2,1)S(1)} all-to-all(bf16[8,32,2048]{2,1,0:T(8,128)(2,1)S(1)} %broadcast_in_dim.28), channel_id=1, replica_groups={{0,2,16,18,32,34,48,50},{1,3,17,19,33,35,49,51},{4,6,20,22,36,38,52,54}..., dimensions={0} | all-to-all | bytes 2097152 | tf_op jit(solution)/shard_map/all_to_all | solution.py:330
  88.9 1.9 %collective-permute-start = (bf16[256,2048]{1,0:T(8,128)(2,1)S(1)}, bf16[256,2048]{1,0:T(8,128)(2,1)}, u32[]{:S(2)}, u32[]{:S(2)}) collective-permute-start(bf16[256,2048]{1,0:T(8,128)(2,1)S(1)} %bitcast.35), channel_id=1, source_target_pairs={{0,1},{1,0},{2,3},{3,2},{4,5},{5,4},{6,7},{7,6},{8,9},{9,8},{10,11... | collective-permute-start | bytes 3145736 | tf_op jit(solution)/shard_map/ppermute | solution.py:334
  90.9 2.4 %own_products.1 = (f32[256,256]{1,0:T(8,128)S(1)}, f32[256,1536]{1,0:T(8,128)S(1)}, f32[256,256]{1,0:T(8,128)S(1)}) custom-call(s32[1]{0:T(128)} %bitcast.4.core_ref, bf16[256,2048]{1,0:T(8,128)(2,1)S(1)} %bitcast.36, bf16[512,1536]{1,0:T(8,128)(2,1)S(1)} %bitcast.33, bf16[1536,256]{1,0:T(8,128)(2,1)S(1)} %copy-done), custom_call_target="tpu_custom_call" | custom-call | flops 2000000000 | bytes 1024 | tf_op jit(solution)/shard_map/own_products/pallas_call | solution.py:220
  93.6 3.5 %products.1 = (f32[4,96,384]{2,1,0:T(8,128)S(1)}, f32[4,192,384]{2,1,0:T(8,128)S(1)}, f32[2,256,256]{2,1,0:T(8,128)S(1)}) custom-call(s32[2]{0:T(128)S(1)} %pad_add_fusion.place_ref, bf16[256,2048]{1,0:T(8,128)(2,1)} %collective-permute-done.load_ref, bf16[512,1536]{1,0:T(8,128)(2,1)S(1)} %bitcast.34, bf16[1536,256]{1,0:T(8,128)(2,1)S(1)} %copy-done, ...), custom_call_target="tpu_custom_call" | custom-call | flops 3000000000 | bytes 1024 | tf_op jit(solution)/shard_map/products/pallas_call | solution.py:235
  98.7 4.3 %all-to-all-start.4 = ((f32[4,96,384]{2,1,0:T(8,128)}), f32[4,96,384]{2,1,0:T(8,128)S(1)}, u32[]{:S(2)}, u32[]{:S(2)}) async-start(f32[4,96,384]{2,1,0:T(8,128)} %copy-done.1), calls=%async_computation.4 | async-start | bytes 1179648 | tf_op jit(solution)/shard_map/all_to_all | solution.py:339
  103.1 5.1 %collective-permute-start.3 = (f32[192,384]{1,0:T(8,128)S(1)}, f32[192,384]{1,0:T(8,128)S(1)}, u32[]{:S(2)}, u32[]{:S(2)}) collective-permute-start(f32[192,384]{1,0:T(8,128)S(1)} %get-tuple-element.25), channel_id=1, source_target_pairs={{0,192},{64,128},{128,64},{192,0},{256,448},{320,384},{384,320},{4... | collective-permute-start | bytes 884744 | tf_op jit(solution)/shard_map/ppermute | solution.py:346
  108.2 2.2 %collective-permute-start.4 = (f32[192,384]{1,0:T(8,128)S(1)}, f32[192,384]{1,0:T(8,128)S(1)}, u32[]{:S(2)}, u32[]{:S(2)}) collective-permute-start(f32[192,384]{1,0:T(8,128)S(1)} %get-tuple-element.26), channel_id=1, source_target_pairs={{0,64},{64,0},{128,192},{192,128},{256,320},{320,256},{384,448},{4... | collective-permute-start | bytes 884744 | tf_op jit(solution)/shard_map/ppermute | solution.py:346
  110.4 3.1 %collective-permute-start.2 = (f32[192,384]{1,0:T(8,128)S(1)}, f32[192,384]{1,0:T(8,128)}, u32[]{:S(2)}, u32[]{:S(2)}) collective-permute-start(f32[192,384]{1,0:T(8,128)S(1)} %get-tuple-element.27), channel_id=1, source_target_pairs={{0,128},{64,192},{128,0},{192,64},{256,384},{320,448},{384,256},{4... | collective-permute-start | bytes 884744 | tf_op jit(solution)/shard_map/ppermute | solution.py:346
  113.5 1.1 all-to-all-done.4
  114.7 8.2 %collective-permute-start.1 = (f32[96,384]{1,0:T(8,128)S(1)}, f32[96,384]{1,0:T(8,128)S(1)}, u32[]{:S(2)}, u32[]{:S(2)}) collective-permute-start(f32[96,384]{1,0:T(8,128)S(1)} %reduce_sum.19), channel_id=1, source_target_pairs={{0,256},{64,320},{128,384},{192,448},{256,0},{320,64},{384,128},{4... | collective-permute-start | bytes 442376 | tf_op jit(solution)/shard_map/ppermute | solution.py:345
  122.9 3.5 %collective-permute-done.2 = f32[192,384]{1,0:T(8,128)} collective-permute-done((f32[192,384]{1,0:T(8,128)S(1)}, f32[192,384]{1,0:T(8,128)}, u32[]{:S(2)}, u32[]{:S(2)}) %collective-permute-start.2) | collective-permute-done | bytes 294944 | tf_op jit(solution)/shard_map/ppermute | solution.py:346
  126.4 1.0 bitcast_add_fusion.refs_2_
  127.4 8.2 %collective-permute-start.5 = (f32[192,384]{1,0:T(8,128)S(1)}, f32[192,384]{1,0:T(8,128)S(1)}, u32[]{:S(2)}, u32[]{:S(2)}) collective-permute-start(f32[192,384]{1,0:T(8,128)S(1)} %bitcast_add_fusion.refs_2_), channel_id=1, source_target_pairs={{0,256},{64,320},{128,384},{192,448},{256,0},{320,64},{384,128},{4... | collective-permute-start | bytes 884744 | tf_op jit(solution)/shard_map/ppermute | solution.py:347
  136.4 3.5 %all-to-all-start.5 = ((f32[4,32,384]{2,1,0:T(8,128)}), f32[4,32,384]{2,1,0:T(8,128)S(1)}, u32[]{:S(2)}, u32[]{:S(2)}) async-start(f32[4,32,384]{2,1,0:T(8,128)} %broadcast_in_dim.29), calls=%async_computation.5 | async-start | bytes 393216 | tf_op jit(solution)/shard_map/all_to_all | solution.py:339
  139.9 6.1 %all-to-all-done.5.packed_ref = f32[4,32,384]{2,1,0:T(8,128)S(1)} async-done(((f32[4,32,384]{2,1,0:T(8,128)}), f32[4,32,384]{2,1,0:T(8,128)S(1)}, u32[]{:S(2)}, u32[]{:S(2)}) %all-to-all-start.5) | async-done | bytes 196640 | tf_op jit(solution)/shard_map/all_to_all | solution.py:339
  146.0 8.9 %inverse_factor.1.inverse_ref = f32[256,256]{1,0:T(8,128)S(1)} custom-call(f32[4,32,384]{2,1,0:T(8,128)S(1)} %all-to-all-done.5.packed_ref), custom_call_target="tpu_custom_call" | custom-call | flops 536870912 | bytes 1024 | tf_op jit(solution)/shard_map/inverse_factor/pallas_call | solution.py:125
  154.9 10.7 %collective-permute-done.5.refs_3_ = f32[192,384]{1,0:T(8,128)S(1)} collective-permute-done((f32[192,384]{1,0:T(8,128)S(1)}, f32[192,384]{1,0:T(8,128)S(1)}, u32[]{:S(2)}, u32[]{:S(2)}) %collective-permute-start.5) | collective-permute-done | bytes 294944 | tf_op jit(solution)/shard_map/ppermute | solution.py:347
  167.4 4.1 %all-to-all-start.6 = ((f16[4,272,384]{2,1,0:T(8,128)(2,1)}), f16[4,272,384]{2,1,0:T(8,128)(2,1)S(1)}, u32[]{:S(2)}, u32[]{:S(2)}) async-start(f16[4,272,384]{2,1,0:T(8,128)(2,1)} %broadcast_in_dim.30), calls=%async_computation.6 | async-start | bytes 1671168 | tf_op jit(solution)/shard_map/all_to_all | solution.py:339
  173.0 11.1 %all-to-all-done.6 = f16[4,272,384]{2,1,0:T(8,128)(2,1)S(1)} async-done(((f16[4,272,384]{2,1,0:T(8,128)(2,1)}), f16[4,272,384]{2,1,0:T(8,128)(2,1)S(1)}, u32[]{:S(2)}, u32[]{:S(2)}) %all-to-all-start.6) | async-done | bytes 835616 | tf_op jit(solution)/shard_map/all_to_all | solution.py:339
  184.2 1.2 assembled.1
  (39 shorter events, 7.7 us)
Async XLA Ops:
  31.2 20.4 %copy-start = (bf16[1536,256]{1,0:T(8,128)(2,1)S(1)}, bf16[1536,256]{1,0:T(8,128)(2,1)}, u32[]{:S(2)}) copy-start(bf16[1536,256]{1,0:T(8,128)(2,1)} %sketch_ref.3) | copy-start | bytes 2359300
  51.6 0.6 copy-start.4
  88.9 4.7 %collective-permute-start = (bf16[256,2048]{1,0:T(8,128)(2,1)S(1)}, bf16[256,2048]{1,0:T(8,128)(2,1)}, u32[]{:S(2)}, u32[]{:S(2)}) collective-permute-start(bf16[256,2048]{1,0:T(8,128)(2,1)S(1)} %bitcast.35), channel_id=1, source_target_pairs={{0,1},{1,0},{2,3},{3,2},{4,5},{5,4},{6,7},{7,6},{8,9},{9,8},{10,11... | collective-permute-start | bytes 3145736 | tf_op jit(solution)/shard_map/ppermute | solution.py:334
  97.1 0.8 copy-start.1
  97.9 0.8 copy-start.2
  98.7 15.9 %all-to-all-start.4 = ((f32[4,96,384]{2,1,0:T(8,128)}), f32[4,96,384]{2,1,0:T(8,128)S(1)}, u32[]{:S(2)}, u32[]{:S(2)}) async-start(f32[4,96,384]{2,1,0:T(8,128)} %copy-done.1), calls=%async_computation.4 | async-start | bytes 1179648 | tf_op jit(solution)/shard_map/all_to_all | solution.py:339
  103.1 19.8 %collective-permute-start.3 = (f32[192,384]{1,0:T(8,128)S(1)}, f32[192,384]{1,0:T(8,128)S(1)}, u32[]{:S(2)}, u32[]{:S(2)}) collective-permute-start(f32[192,384]{1,0:T(8,128)S(1)} %get-tuple-element.25), channel_id=1, source_target_pairs={{0,192},{64,128},{128,64},{192,0},{256,448},{320,384},{384,320},{4... | collective-permute-start | bytes 884744 | tf_op jit(solution)/shard_map/ppermute | solution.py:346
  108.2 14.7 %collective-permute-start.4 = (f32[192,384]{1,0:T(8,128)S(1)}, f32[192,384]{1,0:T(8,128)S(1)}, u32[]{:S(2)}, u32[]{:S(2)}) collective-permute-start(f32[192,384]{1,0:T(8,128)S(1)} %get-tuple-element.26), channel_id=1, source_target_pairs={{0,64},{64,0},{128,192},{192,128},{256,320},{320,256},{384,448},{4... | collective-permute-start | bytes 884744 | tf_op jit(solution)/shard_map/ppermute | solution.py:346
  110.4 16.0 %collective-permute-start.2 = (f32[192,384]{1,0:T(8,128)S(1)}, f32[192,384]{1,0:T(8,128)}, u32[]{:S(2)}, u32[]{:S(2)}) collective-permute-start(f32[192,384]{1,0:T(8,128)S(1)} %get-tuple-element.27), channel_id=1, source_target_pairs={{0,128},{64,192},{128,0},{192,64},{256,384},{320,448},{384,256},{4... | collective-permute-start | bytes 884744 | tf_op jit(solution)/shard_map/ppermute | solution.py:346
  114.7 21.0 %collective-permute-start.1 = (f32[96,384]{1,0:T(8,128)S(1)}, f32[96,384]{1,0:T(8,128)S(1)}, u32[]{:S(2)}, u32[]{:S(2)}) collective-permute-start(f32[96,384]{1,0:T(8,128)S(1)} %reduce_sum.19), channel_id=1, source_target_pairs={{0,256},{64,320},{128,384},{192,448},{256,0},{320,64},{384,128},{4... | collective-permute-start | bytes 442376 | tf_op jit(solution)/shard_map/ppermute | solution.py:345
  127.4 38.2 %collective-permute-start.5 = (f32[192,384]{1,0:T(8,128)S(1)}, f32[192,384]{1,0:T(8,128)S(1)}, u32[]{:S(2)}, u32[]{:S(2)}) collective-permute-start(f32[192,384]{1,0:T(8,128)S(1)} %bitcast_add_fusion.refs_2_), channel_id=1, source_target_pairs={{0,256},{64,320},{128,384},{192,448},{256,0},{320,64},{384,128},{4... | collective-permute-start | bytes 884744 | tf_op jit(solution)/shard_map/ppermute | solution.py:347
  136.4 9.7 %all-to-all-start.5 = ((f32[4,32,384]{2,1,0:T(8,128)}), f32[4,32,384]{2,1,0:T(8,128)S(1)}, u32[]{:S(2)}, u32[]{:S(2)}) async-start(f32[4,32,384]{2,1,0:T(8,128)} %broadcast_in_dim.29), calls=%async_computation.5 | async-start | bytes 393216 | tf_op jit(solution)/shard_map/all_to_all | solution.py:339
  166.4 5.2 %copy-start.3 = (f32[2,256,256]{2,1,0:T(8,128)S(1)}, f32[2,256,256]{2,1,0:T(8,128)}, u32[]{:S(2)}) copy-start(f32[2,256,256]{2,1,0:T(8,128)} %copy-done.2) | copy-start | bytes 1572868
  167.4 16.7 %all-to-all-start.6 = ((f16[4,272,384]{2,1,0:T(8,128)(2,1)}), f16[4,272,384]{2,1,0:T(8,128)(2,1)S(1)}, u32[]{:S(2)}, u32[]{:S(2)}) async-start(f16[4,272,384]{2,1,0:T(8,128)(2,1)} %broadcast_in_dim.30), calls=%async_computation.6 | async-start | bytes 1671168 | tf_op jit(solution)/shard_map/all_to_all | solution.py:339
